TPU v7x, 512 devices: a whole 4x8x8 slice. The times are simulated.
512 devices in a mesh: grp: 16 (over x_lo, y), seq: 32 (over x_hi, z, core).
Axes of the slice: x: 4 (x_hi: 2, x_lo: 2; x = x_hi * 2 + x_lo), y: 8, z: 8, core: 2. Of those that a mesh axis runs over, the one named last changes fastest.
Arguments:
- tokens: bfloat16 [16, 12288, 1536], P('grp', 'seq'), may hold values from -32 to 32, as said below
- router: bfloat16 [1536, 512], P('grp'), may hold values from -1 to 1, as said below
- norm_gain: float32 [32, 1536], P('seq'), may hold values from 0.1 to 1.9
- w_in: bfloat16 [32, 1536, 6144], P('seq', None, 'grp'), may hold values from -0.15625 to 0.15625
- w_out: bfloat16 [32, 6144, 1536], P('seq', 'grp'), may hold values from -0.078125 to 0.078125
Outputs:
- output: bfloat16 [16, 12288, 1536], P('grp', 'seq')
Inputs may be any that keep to these rules, and one draw needn't show every extreme that they name: `tokens`: token features are real values. `router`: slot parameters are real values.
All inputs are finite; a program needn't handle non-finite values.
Results may differ from a plain program's by a relative error of at most 0.0075.
Values may be sent and summed in bfloat16 or wider, within the bound.
No kernel may reach another device: no remote copies, remote signals or barrier semaphores. Data moves between devices by JAX's collectives and lax.ppermute only.
A program may use at most 64 MiB of HBM per device.

v0:
```python
import math

import jax
import jax.numpy as jnp
from jax import lax
from jax.sharding import PartitionSpec as P


def laid_out(blocks, dim):
    blocks = jnp.moveaxis(blocks, 0, dim)
    lengths = blocks.shape
    return blocks.reshape(*lengths[:dim], lengths[dim] * lengths[dim + 1], *lengths[dim + 2 :])


def sent_to_all(value, axis):
    length = lax.axis_size(axis)
    return lax.all_to_all(
        jnp.broadcast_to(value[None], (length, *value.shape)), axis, 0, 0, tiled=True
    )


def collect(value, axis, dim):
    return laid_out(sent_to_all(value, axis), dim)


def in_one_piece(arrays, axis, split_dim, concat_dim, along):
    widths = [math.prod(a.shape[along:]) for a in arrays]
    both = jnp.concatenate(
        [a.reshape(*a.shape[:along], w) for a, w in zip(arrays, widths)], axis=along
    )
    out = lax.all_to_all(both, axis, split_axis=split_dim, concat_axis=concat_dim, tiled=True)
    blocks = jnp.split(out, [sum(widths[:k]) for k in range(1, len(widths))], axis=along)
    return tuple((b.reshape(*out.shape[:along], *a.shape[along:]) for a, b in zip(arrays, blocks)))


def split_up(value, dim, length):
    lengths = value.shape
    blocks = value.reshape(*lengths[:dim], length, lengths[dim] // length, *lengths[dim + 1 :])
    return jnp.moveaxis(blocks, dim, 0)


def sent_and_summed(value, axis, dim):
    length = lax.axis_size(axis)
    blocks = lax.all_to_all(split_up(value, dim, length), axis, 0, 0, tiled=True)
    return jnp.sum(blocks.astype(jnp.float32), axis=0)


def local(tokens, router, norm_gain, w_in, w_out):
    feats = tokens[0]
    width = feats.shape[1]
    slot_count = router.shape[1]
    columns = feats
    logits = jnp.dot(columns, collect(router, "grp", 0), preferred_element_type=jnp.float32)
    owners = lax.axis_size("seq")
    per_owner = slot_count // owners
    local_high = jnp.max(logits, axis=0)
    dispatch = jnp.exp(logits - local_high).astype(jnp.bfloat16)
    partial_sums = lax.dot_general(
        dispatch, feats, (((0,), (0,)), ((), ())), preferred_element_type=jnp.float32
    )
    received, source_highs = in_one_piece(
        (partial_sums.reshape(owners, per_owner, width), local_high.reshape(owners, per_owner)),
        "seq",
        0,
        0,
        2,
    )
    overall = jnp.max(source_highs, axis=0)
    pooled = jnp.sum(received * jnp.exp(source_highs - overall)[:, :, None], axis=0)
    mean_sq = jnp.mean(pooled * pooled, axis=-1, keepdims=True)
    normed = (pooled * lax.rsqrt(mean_sq + 1e-06) * norm_gain[0]).astype(jnp.bfloat16)
    hidden = jax.nn.gelu(
        jnp.dot(collect(normed, "grp", 0), w_in[0], preferred_element_type=jnp.float32)
    ).astype(jnp.bfloat16)
    partials = jnp.dot(hidden, w_out[0], preferred_element_type=jnp.float32)
    own_out = sent_and_summed(partials.astype(jnp.bfloat16), "grp", 0).astype(jnp.bfloat16)
    weights = jax.nn.softmax(logits, axis=1).astype(jnp.bfloat16)
    columns = weights
    mixed = jnp.dot(columns, collect(own_out, "seq", 0), preferred_element_type=jnp.float32)
    return (feats.astype(jnp.float32) + mixed).astype(jnp.bfloat16)[None]


def solution(mesh):
    in_specs = (
        P("grp", "seq", None),
        P("grp", None),
        P("seq", None),
        P("seq", None, "grp"),
        P("seq", "grp", None),
    )
    out_specs = P("grp", "seq", None)
    return jax.shard_map(local, mesh=mesh, in_specs=in_specs, out_specs=out_specs, check_vma=False)
```

profile of v0, /device:TPU:1, one launch (start us, length us, event | category | flops | bytes accessed | tf_op | source)
XLA Modules:
  0.0 254.8 jit_solution(14349199583496500161)
XLA Ops:
  0.0 0.0 copy-start
  0.0 1.1 broadcast_in_dim.8
  1.1 0.0 copy-start.1
  1.2 44.2 %all_to_all.25 = bf16[16,96,512]{2,1,0:T(8,128)(2,1)S(1)} all-to-all(bf16[16,96,512]{2,1,0:T(8,128)(2,1)S(1)} %broadcast_in_dim.8), channel_id=1, replica_groups=mesh['grp'=16,'seq'=32] {'grp'}, dimensions={0} | all-to-all | bytes 3145728 | tf_op jit(solution)/shard_map/all_to_all | solution.py:17
  45.4 0.0 copy-done.1
  45.4 0.9 fusion.36
  46.2 0.3 fusion.10
  46.5 0.1 fusion.25
  46.7 0.2 reshape_reshape.4
  46.9 0.2 copy.18
  47.1 2.2 fusion.6
  49.3 2.1 pad_maximum_fusion
  51.4 0.0 copy-start.3
  51.4 16.4 %all-to-all-start.1 = ((f32[32,16,1537]{2,1,0:T(8,128)}), f32[32,16,1537]{2,1,0:T(8,128)}, u32[]{:S(2)}, u32[]{:S(2)}) async-start(f32[32,16,1537]{2,1,0:T(8,128)} %pad_maximum_fusion), calls=%async_computation.1 | async-start | bytes 6815744 | tf_op jit(solution)/shard_map/all_to_all | solution.py:31
  67.7 0.0 copy-done.3
  67.8 79.3 %all-to-all-done.1 = f32[32,16,1537]{2,1,0:T(8,128)} async-done(((f32[32,16,1537]{2,1,0:T(8,128)}), f32[32,16,1537]{2,1,0:T(8,128)}, u32[]{:S(2)}, u32[]{:S(2)}) %all-to-all-start.1) | async-done | bytes 3147808 | tf_op jit(solution)/shard_map/all_to_all | solution.py:31
  147.0 1.1 slice_reduce_fusion
  148.2 0.2 copy.27
  148.3 0.1 exponential_bitcast_fusion
  148.4 0.1 copy.21
  148.5 2.2 fusion
  150.7 0.3 copy.25
  151.0 0.2 multiply_reduce_fusion
  151.2 0.3 multiply_convert_fusion
  151.5 0.1 copy.24
  151.6 0.1 broadcast_in_dim.9
  151.7 23.2 %all_to_all.26 = bf16[16,16,1536]{2,1,0:T(8,128)(2,1)S(1)} all-to-all(bf16[16,16,1536]{2,1,0:T(8,128)(2,1)S(1)} %broadcast_in_dim.9), channel_id=1, replica_groups=mesh['grp'=16,'seq'=32] {'grp'}, dimensions={0} | all-to-all | bytes 1572864 | tf_op jit(solution)/shard_map/all_to_all | solution.py:17
  174.9 0.0 copy-done
  174.9 2.4 convolution_convert_fusion
  177.2 25.3 %all_to_all.27 = bf16[16,16,1536]{2,1,0:T(8,128)(2,1)S(1)} all-to-all(bf16[16,16,1536]{2,1,0:T(8,128)(2,1)S(1)} %bitcast.40), channel_id=1, replica_groups=mesh['grp'=16,'seq'=32] {'grp'}, dimensions={0} | all-to-all | bytes 1572864 | tf_op jit(solution)/shard_map/all_to_all | solution.py:44
  202.6 0.1 reduce_sum.42
  202.7 0.2 broadcast_in_dim.10
  202.9 0.0 copy-start.2
  202.9 50.0 %all_to_all.28 = bf16[32,16,1536]{2,1,0:T(8,128)(2,1)S(1)} all-to-all(bf16[32,16,1536]{2,1,0:T(8,128)(2,1)S(1)} %broadcast_in_dim.10), channel_id=1, replica_groups=mesh['grp'=16,'seq'=32] {'seq'}, dimensions={0} | all-to-all | bytes 3145728 | tf_op jit(solution)/shard_map/all_to_all | solution.py:17
  252.9 0.0 copy-done.2
  252.9 1.9 fusion.2
  (2 shorter events, 0.0 us)
Async XLA Ops:
  0.0 174.9 %copy-start = (bf16[1,384,1536]{2,1,0:T(8,128)(2,1)S(1)}, bf16[1,384,1536]{2,1,0:T(8,128)(2,1)}, u32[]{:S(2)}) copy-start(bf16[1,384,1536]{2,1,0:T(8,128)(2,1)} %param.9) | copy-start | bytes 3538948
  1.1 44.2 %copy-start.1 = (bf16[1,384,1536]{2,1,0:T(8,128)(2,1)S(1)}, bf16[1,384,1536]{2,1,0:T(8,128)(2,1)}, u32[]{:S(2)}) copy-start(bf16[1,384,1536]{2,1,0:T(8,128)(2,1)} %param.5) | copy-start | bytes 3538948
  51.4 16.4 %copy-start.3 = (f32[1,1536]{1,0:T(1,128)S(1)}, f32[1,1536]{1,0:T(1,128)}, u32[]{:S(2)}) copy-start(f32[1,1536]{1,0:T(1,128)} %param.7) | copy-start | bytes 18436
  51.4 95.7 %all-to-all-start.1 = ((f32[32,16,1537]{2,1,0:T(8,128)}), f32[32,16,1537]{2,1,0:T(8,128)}, u32[]{:S(2)}, u32[]{:S(2)}) async-start(f32[32,16,1537]{2,1,0:T(8,128)} %pad_maximum_fusion), calls=%async_computation.1 | async-start | bytes 6815744 | tf_op jit(solution)/shard_map/all_to_all | solution.py:31
  202.9 50.0 %copy-start.2 = (bf16[1,384,1536]{2,1,0:T(8,128)(2,1)S(1)}, bf16[1,384,1536]{2,1,0:T(8,128)(2,1)}, u32[]{:S(2)}) copy-start(bf16[1,384,1536]{2,1,0:T(8,128)(2,1)} %param.5) | copy-start | bytes 3538948
where the time goes:
time: 256 us; the launch traced here: 255 us
  blocking collectives  143 us (56%)
  waiting for transfers between devices  79.3 us (31%)
  starting transfers between devices  16.4 us (6%)
  matrix products  7.37 us (3%)
  other arithmetic  6.47 us (3%)
    all_to_all x3, blocking collectives, sent_to_all(): lax.all_to_all(jnp.broadcast_to(value[None], (length, *value.shape)), axi...  117 us
    all_to_all x1, waiting for transfers between devices, in_one_piece(): lax.all_to_all(both, axis, split_axis=split_dim, concat_axis=concat_dim,...  79.3 us
    all_to_all x1, blocking collectives, sent_and_summed(): lax.all_to_all(split_up(value, dim, length), axis, 0, 0, tiled=True)  25.3 us
    all_to_all x1, starting transfers between devices, in_one_piece(): lax.all_to_all(both, axis, split_axis=split_dim, concat_axis=concat_dim,...  16.4 us
  transfers between devices with their start and end apart: 1, of which 1 were waited for; matrix products, arithmetic and copies ran while one was open for 0% of the time, Pallas kernels for 0%

commit v1 on v0

v1 whole, which is shorter than its diff:
```python
import jax
import jax.numpy as jnp
from jax import lax
from jax.sharding import Mesh, PartitionSpec as P

F32 = jnp.float32
BF16 = jnp.bfloat16
EXTRA = 128


def other(length=2):
    return [(k, k ^ 1) for k in range(length)]


def pieces(value):
    first = lax.reduce_precision(value, 8, 7)
    second = lax.reduce_precision(value - first, 8, 7)
    third = value - first - second
    return first, second, third


def with_pieces(body, columns):
    parts = [p[..., None] for column in columns for p in pieces(column)]
    fill = jnp.zeros((*body.shape[:-1], EXTRA - len(parts)), F32)
    return jnp.concatenate([body, *parts, fill], axis=-1).astype(BF16)


def piece_sum(block, which):
    part = block[..., 3 * which : 3 * which + 3].astype(F32)
    return part[..., 0] + part[..., 1] + part[..., 2]


def sent_to_all(value, axes):
    length = lax.axis_size(axes)
    return lax.all_to_all(
        jnp.broadcast_to(value[None], (length, *value.shape)), axes, 0, 0, tiled=True
    )


def local(tokens, router, norm_gain, w_in, w_out):
    feats = tokens[0]
    count, width = feats.shape
    slot_count = router.shape[1]
    owners = lax.axis_size(("xhi", "z"))
    per_owner = slot_count // (2 * owners)
    half = slot_count // 2
    core = lax.axis_index("core")

    partner_feats = lax.ppermute(feats, "core", other())
    partner_in = lax.ppermute(w_in[0], "xlo", other())
    partner_out = lax.ppermute(w_out[0], "xlo", other())

    row = lax.broadcasted_iota(jnp.int32, (slot_count, half), 0)
    col = lax.broadcasted_iota(jnp.int32, (slot_count, half), 1)
    wanted = (col // per_owner * 2 + core) * per_owner + col % per_owner
    pick = (row == wanted).astype(BF16)
    own_columns = jnp.dot(router, pick, preferred_element_type=F32).astype(BF16)
    columns = sent_to_all(own_columns, ("xlo", "y")).reshape(width, half)

    logits = jnp.dot(feats, columns, preferred_element_type=F32)
    partner_logits = jnp.dot(partner_feats, columns, preferred_element_type=F32)
    high = jnp.maximum(jnp.max(logits, axis=0), jnp.max(partner_logits, axis=0))
    dispatch = jnp.exp(logits - high).astype(BF16)
    partner_dispatch = jnp.exp(partner_logits - high).astype(BF16)
    dims = (((0,), (0,)), ((), ()))
    sums = lax.dot_general(dispatch, feats, dims, preferred_element_type=F32)
    sums += lax.dot_general(partner_dispatch, partner_feats, dims, preferred_element_type=F32)
    message = with_pieces(sums, [high]).reshape(owners, per_owner, width + EXTRA)
    received = lax.all_to_all(message, ("xhi", "z"), 0, 0, tiled=True)

    row_high = jnp.max(logits, axis=1)
    exps = jnp.exp(logits - row_high[:, None])
    row_sum = jnp.sum(exps, axis=1)
    partner_high = jnp.max(partner_logits, axis=1)
    partner_exps = jnp.exp(partner_logits - partner_high[:, None])
    answer = with_pieces(partner_exps, [partner_high, jnp.sum(partner_exps, axis=1)])
    answer = lax.ppermute(answer, "core", other())

    highs = piece_sum(received[:, :, width:], 0)
    overall = jnp.max(highs, axis=0)
    scale = jnp.exp(highs - overall)
    pooled = jnp.sum(received[:, :, :width].astype(F32) * scale[:, :, None], axis=0)
    mean_sq = jnp.mean(pooled * pooled, axis=-1, keepdims=True)
    slots = (pooled * lax.rsqrt(mean_sq + 1e-06) * norm_gain[0]).astype(BF16)

    rows = sent_to_all(slots, "y")
    groups = rows.shape[0]
    rows = rows.reshape(groups * per_owner, width)
    hidden = jax.nn.gelu(jnp.dot(rows, w_in[0], preferred_element_type=F32)).astype(BF16)
    hidden_b = jax.nn.gelu(jnp.dot(rows, partner_in, preferred_element_type=F32)).astype(BF16)
    partial = jnp.dot(hidden, w_out[0], preferred_element_type=F32)
    partial += jnp.dot(hidden_b, partner_out, preferred_element_type=F32)
    partial = partial.astype(BF16).reshape(groups, per_owner, width)
    blocks = lax.all_to_all(partial, "y", 0, 0, tiled=True)
    own_out = jnp.sum(blocks.astype(F32), axis=0).astype(BF16)

    outs = sent_to_all(own_out, ("xhi", "z")).reshape(half, width)
    outs_b = lax.ppermute(outs, "core", other())

    exps_b = answer[:, :half]
    row_high_b = piece_sum(answer[:, half:], 0)
    row_sum_b = piece_sum(answer[:, half:], 1)
    top = jnp.maximum(row_high, row_high_b)
    factor = jnp.exp(row_high - top)
    factor_b = jnp.exp(row_high_b - top)
    total = row_sum * factor + row_sum_b * factor_b
    mixed = jnp.dot(exps.astype(BF16), outs, preferred_element_type=F32) * (factor / total)[:, None]
    mixed += jnp.dot(exps_b, outs_b, preferred_element_type=F32) * (factor_b / total)[:, None]
    return (feats.astype(F32) + mixed).astype(BF16)[None]


def solution(mesh):
    fine = Mesh(mesh.devices.reshape(2, 8, 2, 8, 2), ("xlo", "y", "xhi", "z", "core"))
    grp, seq = ("xlo", "y"), ("xhi", "z", "core")
    in_specs = (P(grp, seq, None), P(grp, None), P(seq, None), P(seq, None, grp), P(seq, grp, None))
    return jax.shard_map(
        local, mesh=fine, in_specs=in_specs, out_specs=P(grp, seq, None), check_vma=False
    )
```

time: 256 us -> 177 us (0.69)
  blocking collectives: 143 us -> 37.4 us
  starting transfers between devices: 16.4 us -> 51.5 us
  waiting for transfers between devices: 79.3 us -> 64.3 us
  local copies, waits for them, and re-layouts: 2.5 us -> 8.39 us
  matrix products: 7.37 us -> 13.1 us
  other arithmetic: 6.47 us -> 1.06 us
    all_to_all x4 -> x2, blocking collectives: 143 us -> 37.4 us  [the longest x1 20.1 us: local(): blocks = lax.all_to_all(partial, 'y', 0, 0, tiled=True)]
    all_to_all x1 -> x3, waiting for transfers between devices: 79.3 us -> 43.1 us  [the longest x2 28.2 us: sent_to_all(): lax.all_to_all(jnp.broadcast_to(value[None], (length, *value.shape)), axe...]
    ppermute x0 -> x5, waiting for transfers between devices: none -> 21.2 us  [the longest x1 19.9 us: local(): partner_in = lax.ppermute(w_in[0], 'xlo', other())]
    ppermute x0 -> x5, starting transfers between devices: none -> 20.2 us  [the longest x1 6.74 us: local(): outs_b = lax.ppermute(outs, 'core', other())]
    all_to_all x1 -> x3, starting transfers between devices: 16.4 us -> 31.3 us  [the longest x2 17.2 us: sent_to_all(): lax.all_to_all(jnp.broadcast_to(value[None], (length, *value.shape)), axe...]
    dot_general x4 -> x9, matrix products: 7.37 us -> 13.1 us  [the longest x1 2.94 us: local(): lax.dot_general(partner_dispatch, partner_feats, dims, preferred_element_...]
    concatenate x0 -> x2, local copies, waits for them, and re-layouts: none -> 2.65 us  [with_pieces(): return jnp.concatenate([body, *parts, fill], axis=-1).astype(BF16)]
  transfers between devices with their start and end apart: 1 -> 8, of which waited for: 1 -> 5; matrix products, arithmetic and copies ran while one was open for 0% -> 3% of each run, Pallas kernels for 0% -> 0%
where the time goes in v1:
time: 177 us; the launch traced here: 176 us
  waiting for transfers between devices  64.3 us (36%)
  starting transfers between devices  51.5 us (29%)
  blocking collectives  37.4 us (21%)
  matrix products  13.1 us (7%)
  local copies, waits for them, and re-layouts  8.39 us (5%)
    all_to_all x2, waiting for transfers between devices, sent_to_all(): lax.all_to_all(jnp.broadcast_to(value[None], (length, *value.shape)), axe...  28.2 us
    all_to_all x1, blocking collectives, local(): blocks = lax.all_to_all(partial, 'y', 0, 0, tiled=True)  20.1 us
    ppermute x1, waiting for transfers between devices, local(): partner_in = lax.ppermute(w_in[0], 'xlo', other())  19.9 us
    all_to_all x1, blocking collectives, sent_to_all(): lax.all_to_all(jnp.broadcast_to(value[None], (length, *value.shape)), axe...  17.3 us
    all_to_all x2, starting transfers between devices, sent_to_all(): lax.all_to_all(jnp.broadcast_to(value[None], (length, *value.shape)), axe...  17.2 us
    all_to_all x1, waiting for transfers between devices, local(): received = lax.all_to_all(message, ('xhi', 'z'), 0, 0, tiled=True)  14.8 us
    all_to_all x1, starting transfers between devices, local(): received = lax.all_to_all(message, ('xhi', 'z'), 0, 0, tiled=True)  14 us
    ppermute x1, starting transfers between devices, local(): outs_b = lax.ppermute(outs, 'core', other())  6.74 us
  transfers between devices with their start and end apart: 8, of which 5 were waited for; matrix products, arithmetic and copies ran while one was open for 3% of the time, Pallas kernels for 0%

profile of v1, /device:TPU:1, one launch (start us, length us, event | category | flops | bytes accessed | tf_op | source)
XLA Modules:
  0.0 176.1 jit_solution(2057646489144412050)
XLA Ops:
  0.0 0.0 copy-start
  0.0 0.9 copy-done
  0.9 0.2 fusion.6
  1.1 0.0 copy-start.1
  1.2 1.0 broadcast_in_dim.12
  2.1 8.7 %all-to-all-start = ((bf16[16,96,256]{2,1,0:T(8,128)(2,1)}), bf16[16,96,256]{2,1,0:T(8,128)(2,1)S(1)}, u32[]{:S(2)}, u32[]{:S(2)}) async-start(bf16[16,96,256]{2,1,0:T(8,128)(2,1)} %broadcast_in_dim.12), calls=%async_computation | async-start | bytes 1572864 | tf_op jit(solution)/shard_map/all_to_all | solution.py:35
  10.8 3.7 %collective-permute-start = (bf16[384,1536]{1,0:T(8,128)(2,1)S(1)}, bf16[384,1536]{1,0:T(8,128)(2,1)}, u32[]{:S(2)}, u32[]{:S(2)}) collective-permute-start(bf16[384,1536]{1,0:T(8,128)(2,1)S(1)} %bitcast.42), channel_id=1, source_target_pairs={{0,1},{1,0},{2,3},{3,2},{4,5},{5,4},{6,7},{7,6},{8,9},{9,8},{10,11... | collective-permute-start | bytes 3538952 | tf_op jit(solution)/shard_map/ppermute | solution.py:49
  14.5 14.4 %all-to-all-done = bf16[16,96,256]{2,1,0:T(8,128)(2,1)S(1)} async-done(((bf16[16,96,256]{2,1,0:T(8,128)(2,1)}), bf16[16,96,256]{2,1,0:T(8,128)(2,1)S(1)}, u32[]{:S(2)}, u32[]{:S(2)}) %all-to-all-start) | async-done | bytes 786464 | tf_op jit(solution)/shard_map/all_to_all | solution.py:35
  29.0 0.6 fusion.84
  29.6 0.1 fusion.7
  29.7 0.0 collective-permute-done
  29.8 1.9 %fusion.85 = (f32[384]{0:T(512)S(1)}, f32[256,384]{1,0:T(8,128)S(1)}) fusion(bf16[1536,256]{1,0:T(8,128)(2,1)S(1)} %bitcast.44, bf16[384,1536]{1,0:T(8,128)(2,1)} %collective-permute-done), kind=kOutput, calls=%fused_computation.125 | convolution fusion | flops 302087808 | bytes 2360832 | tf_op jit(solution)/shard_map/dot_general | solution.py:61
  31.7 0.0 copy-start.2
  31.7 0.2 fusion.9
  31.8 0.6 copy-done.2
  32.4 0.6 fusion.38
  33.0 0.1 max.34
  33.1 0.2 copy.13
  33.3 0.8 copy.14
  34.1 0.8 copy.15
  34.9 2.9 %fusion.3 = bf16[256,1536]{1,0:T(8,128)(2,1)} fusion(f32[256,1536]{1,0:T(8,128)S(1)} %fusion.38, bf16[384,1536]{1,0:T(8,128)(2,1)} %collective-permute-done, f32[256,384]{1,0:T(8,128)} %copy-done.2, f32[256]{0:T(256)S(1)} %max.33), kind=kOutput, calls=%fused_computation.6 | convolution fusion | flops 302972928 | bytes 3933184 | tf_op jit(solution)/shard_map/dot_general | solution.py:67
  37.9 2.0 %concatenate.12 = bf16[16,16,1664]{2,1,0:T(8,128)(2,1)} concatenate(bf16[16,16,1536]{2,1,0:T(8,128)(2,1)} %bitcast.49, bf16[16,16,1]{2,1,0:T(8,128)(2,1)S(1)} %copy.13, bf16[16,16,1]{2,1,0:T(8,128)(2,1)} %copy.14, bf16[16,16,1]{2,1,0:T(8,128)(2,1)} %copy.15, bf16[16,16,125]{2,1,0:T(8,128)(2,1)S(1)} %broadcast_in_dim.13), dimensions={2} | concatenate | bytes 1703936 | tf_op jit(solution)/shard_map/concatenate | solution.py:25
  39.9 14.0 %all-to-all-start.1 = ((bf16[16,16,1664]{2,1,0:T(8,128)(2,1)}), bf16[16,16,1664]{2,1,0:T(8,128)(2,1)S(1)}, u32[]{:S(2)}, u32[]{:S(2)}) async-start(bf16[16,16,1664]{2,1,0:T(8,128)(2,1)} %concatenate.12), calls=%async_computation.1 | async-start | bytes 1703936 | tf_op jit(solution)/shard_map/all_to_all | solution.py:69
  54.0 1.9 %collective-permute-start.2 = (bf16[384,1536]{1,0:T(8,128)(2,1)}, bf16[384,1536]{1,0:T(8,128)(2,1)}, u32[]{:S(2)}, u32[]{:S(2)}) collective-permute-start(bf16[384,1536]{1,0:T(8,128)(2,1)} %bitcast.51), channel_id=1, source_target_pairs={{0,256},{256,0},{1,257},{257,1},{2,258},{258,2},{3,259},{259,3},{4... | collective-permute-start | bytes 3538952 | tf_op jit(solution)/shard_map/ppermute | solution.py:51
  55.9 3.4 %collective-permute-start.1 = (bf16[1536,384]{1,0:T(8,128)(2,1)}, bf16[1536,384]{1,0:T(8,128)(2,1)}, u32[]{:S(2)}, u32[]{:S(2)}) collective-permute-start(bf16[1536,384]{1,0:T(8,128)(2,1)} %bitcast.52), channel_id=1, source_target_pairs={{0,256},{256,0},{1,257},{257,1},{2,258},{258,2},{3,259},{259,3},{4... | collective-permute-start | bytes 3538952 | tf_op jit(solution)/shard_map/ppermute | solution.py:50
  59.3 14.8 %all-to-all-done.1 = bf16[16,16,1664]{2,1,0:T(8,128)(2,1)S(1)} async-done(((bf16[16,16,1664]{2,1,0:T(8,128)(2,1)}), bf16[16,16,1664]{2,1,0:T(8,128)(2,1)S(1)}, u32[]{:S(2)}, u32[]{:S(2)}) %all-to-all-start.1) | async-done | bytes 852000 | tf_op jit(solution)/shard_map/all_to_all | solution.py:69
  74.2 0.2 copy.20
  74.4 0.2 multiply_reduce_fusion
  74.6 0.3 copy.19
  74.9 0.2 multiply_reduce_fusion.1
  75.1 0.1 multiply_convert_fusion
  75.3 17.3 %all_to_all.25 = bf16[8,16,1536]{2,1,0:T(8,128)(2,1)S(1)} all-to-all(bf16[8,16,1536]{2,1,0:T(8,128)(2,1)S(1)} %broadcast_in_dim.14), channel_id=1, replica_groups=mesh['xlo'=2,'y'=8,'xhi'=2,'z'=8,'core'=2] {'y'}, dimensions={0} | all-to-all | bytes 786432 | tf_op jit(solution)/shard_map/all_to_all | solution.py:35
  92.5 2.3 %fusion.44 = f32[128,1536]{1,0:T(8,128)S(1)} fusion(bf16[1,384,1536]{2,1,0:T(8,128)(2,1)} %param.9, bf16[128,1536]{1,0:T(8,128)(2,1)S(1)} %bitcast.45, bf16[1,1536,384]{2,1,0:T(8,128)(2,1)} %param.8), kind=kOutput, calls=%fused_computation.56 | convolution fusion | flops 302432256 | bytes 3538944 | tf_op jit(solution)/shard_map/dot_general | solution.py:91
  94.9 0.0 collective-permute-done.2
  94.9 19.9 %collective-permute-done.1 = bf16[1536,384]{1,0:T(8,128)(2,1)} collective-permute-done((bf16[1536,384]{1,0:T(8,128)(2,1)}, bf16[1536,384]{1,0:T(8,128)(2,1)}, u32[]{:S(2)}, u32[]{:S(2)}) %collective-permute-start.1) | collective-permute-done | bytes 1179680 | tf_op jit(solution)/shard_map/ppermute | solution.py:50
  114.8 2.3 %fusion.5 = bf16[128,1536]{1,0:T(8,128)(2,1)S(1)} fusion(f32[128,1536]{1,0:T(8,128)S(1)} %fusion.44, bf16[384,1536]{1,0:T(8,128)(2,1)} %collective-permute-done.2, bf16[128,1536]{1,0:T(8,128)(2,1)S(1)} %bitcast.46, bf16[1536,384]{1,0:T(8,128)(2,1)} %collective-permute-done.1), kind=kOutput, calls=%fused_computation.9 | convolution fusion | flops 302825472 | bytes 3932160 | tf_op jit(solution)/shard_map/dot_general | solution.py:92
  117.2 20.1 %all_to_all.26 = bf16[8,16,1536]{2,1,0:T(8,128)(2,1)S(1)} all-to-all(bf16[8,16,1536]{2,1,0:T(8,128)(2,1)S(1)} %bitcast.50), channel_id=1, replica_groups=mesh['xlo'=2,'y'=8,'xhi'=2,'z'=8,'core'=2] {'y'}, dimensions={0} | all-to-all | bytes 786432 | tf_op jit(solution)/shard_map/all_to_all | solution.py:94
  137.3 0.1 reduce_sum.54
  137.4 1.0 broadcast_in_dim.15
  138.3 8.5 %all-to-all-start.4 = ((bf16[16,16,1536]{2,1,0:T(8,128)(2,1)}), bf16[16,16,1536]{2,1,0:T(8,128)(2,1)S(1)}, u32[]{:S(2)}, u32[]{:S(2)}) async-start(bf16[16,16,1536]{2,1,0:T(8,128)(2,1)} %broadcast_in_dim.15), calls=%async_computation.4 | async-start | bytes 1572864 | tf_op jit(solution)/shard_map/all_to_all | solution.py:35
  146.9 0.6 concatenate.13
  147.5 4.4 %collective-permute-start.3 = (bf16[384,384]{0,1:T(8,128)(2,1)S(1)}, bf16[384,384]{0,1:T(8,128)(2,1)S(1)}, u32[]{:S(2)}, u32[]{:S(2)}) collective-permute-start(bf16[384,384]{0,1:T(8,128)(2,1)S(1)} %concatenate.13), channel_id=1, source_target_pairs={{0,1},{1,0},{2,3},{3,2},{4,5},{5,4},{6,7},{7,6},{8,9},{9,8},{10,11... | collective-permute-start | bytes 884744 | tf_op jit(solution)/shard_map/ppermute | solution.py:77
  152.0 13.8 %all-to-all-done.4 = bf16[16,16,1536]{2,1,0:T(8,128)(2,1)S(1)} async-done(((bf16[16,16,1536]{2,1,0:T(8,128)(2,1)}), bf16[16,16,1536]{2,1,0:T(8,128)(2,1)S(1)}, u32[]{:S(2)}, u32[]{:S(2)}) %all-to-all-start.4) | async-done | bytes 786464 | tf_op jit(solution)/shard_map/all_to_all | solution.py:35
  165.8 6.7 %collective-permute-start.4 = (bf16[256,1536]{1,0:T(8,128)(2,1)S(1)}, bf16[256,1536]{1,0:T(8,128)(2,1)S(1)}, u32[]{:S(2)}, u32[]{:S(2)}) collective-permute-start(bf16[256,1536]{1,0:T(8,128)(2,1)S(1)} %bitcast.47), channel_id=1, source_target_pairs={{0,1},{1,0},{2,3},{3,2},{4,5},{5,4},{6,7},{7,6},{8,9},{9,8},{10,11... | collective-permute-start | bytes 2359304 | tf_op jit(solution)/shard_map/ppermute | solution.py:98
  172.5 0.0 collective-permute-done.3
  172.6 0.5 convolution_multiply_fusion.1
  173.1 1.3 collective-permute-done.4
  174.4 1.6 fusion.4
  (22 shorter events, 0.2 us)
Async XLA Ops:
  0.0 0.9 copy-start
  1.1 9.7 %copy-start.1 = (bf16[1,384,1536]{2,1,0:T(8,128)(2,1)S(1)}, bf16[1,384,1536]{2,1,0:T(8,128)(2,1)}, u32[]{:S(2)}) copy-start(bf16[1,384,1536]{2,1,0:T(8,128)(2,1)} %param.5) | copy-start | bytes 3538948
  2.1 26.9 %all-to-all-start = ((bf16[16,96,256]{2,1,0:T(8,128)(2,1)}), bf16[16,96,256]{2,1,0:T(8,128)(2,1)S(1)}, u32[]{:S(2)}, u32[]{:S(2)}) async-start(bf16[16,96,256]{2,1,0:T(8,128)(2,1)} %broadcast_in_dim.12), calls=%async_computation | async-start | bytes 1572864 | tf_op jit(solution)/shard_map/all_to_all | solution.py:35
  10.8 18.9 %collective-permute-start = (bf16[384,1536]{1,0:T(8,128)(2,1)S(1)}, bf16[384,1536]{1,0:T(8,128)(2,1)}, u32[]{:S(2)}, u32[]{:S(2)}) collective-permute-start(bf16[384,1536]{1,0:T(8,128)(2,1)S(1)} %bitcast.42), channel_id=1, source_target_pairs={{0,1},{1,0},{2,3},{3,2},{4,5},{5,4},{6,7},{7,6},{8,9},{9,8},{10,11... | collective-permute-start | bytes 3538952 | tf_op jit(solution)/shard_map/ppermute | solution.py:49
  31.7 0.7 copy-start.2
  39.9 19.4 %copy-start.3 = (f32[1,1536]{1,0:T(1,128)S(1)}, f32[1,1536]{1,0:T(1,128)}, u32[]{:S(2)}) copy-start(f32[1,1536]{1,0:T(1,128)} %param.7) | copy-start | bytes 18436
  39.9 34.2 %all-to-all-start.1 = ((bf16[16,16,1664]{2,1,0:T(8,128)(2,1)}), bf16[16,16,1664]{2,1,0:T(8,128)(2,1)S(1)}, u32[]{:S(2)}, u32[]{:S(2)}) async-start(bf16[16,16,1664]{2,1,0:T(8,128)(2,1)} %concatenate.12), calls=%async_computation.1 | async-start | bytes 1703936 | tf_op jit(solution)/shard_map/all_to_all | solution.py:69
  54.0 40.9 %collective-permute-start.2 = (bf16[384,1536]{1,0:T(8,128)(2,1)}, bf16[384,1536]{1,0:T(8,128)(2,1)}, u32[]{:S(2)}, u32[]{:S(2)}) collective-permute-start(bf16[384,1536]{1,0:T(8,128)(2,1)} %bitcast.51), channel_id=1, source_target_pairs={{0,256},{256,0},{1,257},{257,1},{2,258},{258,2},{3,259},{259,3},{4... | collective-permute-start | bytes 3538952 | tf_op jit(solution)/shard_map/ppermute | solution.py:51
  55.9 58.9 %collective-permute-start.1 = (bf16[1536,384]{1,0:T(8,128)(2,1)}, bf16[1536,384]{1,0:T(8,128)(2,1)}, u32[]{:S(2)}, u32[]{:S(2)}) collective-permute-start(bf16[1536,384]{1,0:T(8,128)(2,1)} %bitcast.52), channel_id=1, source_target_pairs={{0,256},{256,0},{1,257},{257,1},{2,258},{258,2},{3,259},{259,3},{4... | collective-permute-start | bytes 3538952 | tf_op jit(solution)/shard_map/ppermute | solution.py:50
  138.3 27.5 %all-to-all-start.4 = ((bf16[16,16,1536]{2,1,0:T(8,128)(2,1)}), bf16[16,16,1536]{2,1,0:T(8,128)(2,1)S(1)}, u32[]{:S(2)}, u32[]{:S(2)}) async-start(bf16[16,16,1536]{2,1,0:T(8,128)(2,1)} %broadcast_in_dim.15), calls=%async_computation.4 | async-start | bytes 1572864 | tf_op jit(solution)/shard_map/all_to_all | solution.py:35
  147.5 25.0 %collective-permute-start.3 = (bf16[384,384]{0,1:T(8,128)(2,1)S(1)}, bf16[384,384]{0,1:T(8,128)(2,1)S(1)}, u32[]{:S(2)}, u32[]{:S(2)}) collective-permute-start(bf16[384,384]{0,1:T(8,128)(2,1)S(1)} %concatenate.13), channel_id=1, source_target_pairs={{0,1},{1,0},{2,3},{3,2},{4,5},{5,4},{6,7},{7,6},{8,9},{9,8},{10,11... | collective-permute-start | bytes 884744 | tf_op jit(solution)/shard_map/ppermute | solution.py:77
  165.8 8.6 %collective-permute-start.4 = (bf16[256,1536]{1,0:T(8,128)(2,1)S(1)}, bf16[256,1536]{1,0:T(8,128)(2,1)S(1)}, u32[]{:S(2)}, u32[]{:S(2)}) collective-permute-start(bf16[256,1536]{1,0:T(8,128)(2,1)S(1)} %bitcast.47), channel_id=1, source_target_pairs={{0,1},{1,0},{2,3},{3,2},{4,5},{5,4},{6,7},{7,6},{8,9},{9,8},{10,11... | collective-permute-start | bytes 2359304 | tf_op jit(solution)/shard_map/ppermute | solution.py:98

commit v2 on v1

v2 whole, which is shorter than its diff:
```python
import functools

import jax
import jax.numpy as jnp
from jax import lax
from jax.experimental import pallas as pl
from jax.experimental.pallas import tpu as pltpu
from jax.sharding import Mesh, PartitionSpec as P

F32 = jnp.float32
BF16 = jnp.bfloat16
EXTRA = 128
VMEM = pl.BlockSpec(memory_space=pltpu.VMEM)
ANY = pl.BlockSpec(memory_space=pl.ANY)


def other(length=2):
    return [(k, k ^ 1) for k in range(length)]


def kernel_call(body, outs, flops, moved, specs, *args):
    return pl.pallas_call(
        body,
        out_shape=outs,
        in_specs=specs,
        out_specs=jax.tree.map(lambda _: VMEM, outs),
        compiler_params=pltpu.CompilerParams(vmem_limit_bytes=16 * 2**20),
        cost_estimate=pl.CostEstimate(flops=flops, bytes_accessed=moved, transcendentals=0),
    )(*args)


def split_off(value):
    wide = value * 65537.0
    return wide - (wide - value)


def in_lanes(columns):
    lane = lax.broadcasted_iota(jnp.int32, columns[0].shape, 1)
    packed = jnp.zeros(columns[0].shape, F32)
    for k, column in enumerate(columns):
        first = split_off(column)
        second = split_off(column - first)
        for j, piece in enumerate((first, second, column - first - second)):
            packed = jnp.where(lane == 3 * k + j, piece, packed)
    return packed.astype(BF16)


def dispatch_kernel(own_ref, partner_ref, columns_ref, dummy_ref, message_ref, own_logits_ref, partner_logits_ref):
    width = own_ref.shape[1]
    slots = columns_ref.shape[1]
    columns = columns_ref[...]
    for feats, logits_ref in ((own_ref, own_logits_ref), (partner_ref, partner_logits_ref)):
        logits_ref[...] = jnp.dot(feats[...], columns, preferred_element_type=F32)
    own_logits, partner_logits = own_logits_ref[...], partner_logits_ref[...]
    high = jnp.maximum(
        jnp.max(own_logits, axis=0, keepdims=True), jnp.max(partner_logits, axis=0, keepdims=True)
    )
    own = jnp.exp(own_logits - high).astype(BF16).T
    partner = jnp.exp(partner_logits - high).astype(BF16).T
    step = 512
    for start in range(0, width, step):
        part = slice(start, start + step)
        sums = jnp.dot(own, own_ref[:, part], preferred_element_type=F32)
        sums += jnp.dot(partner, partner_ref[:, part], preferred_element_type=F32)
        message_ref[:, part] = sums.astype(BF16)
    message_ref[:, width:] = in_lanes([jnp.broadcast_to(high, (EXTRA, slots)).T])


def softmax_kernel(own_logits_ref, partner_logits_ref, own_ref, answer_ref):
    for logits_ref, out_ref in ((own_logits_ref, own_ref), (partner_logits_ref, answer_ref)):
        logits = logits_ref[...]
        slots = logits.shape[1]
        high = jnp.max(logits, axis=1, keepdims=True)
        exps = jnp.exp(logits - high)
        total = jnp.sum(exps, axis=1, keepdims=True)
        out_ref[:, :slots] = exps.astype(BF16)
        lanes = (logits.shape[0], EXTRA)
        out_ref[:, slots:] = in_lanes([jnp.broadcast_to(high, lanes), jnp.broadcast_to(total, lanes)])


def pool_kernel(received_ref, gain_ref, slots_ref):
    width = gain_ref.shape[1]
    highs = jnp.sum(received_ref[:, :, width:].astype(F32), axis=-1, keepdims=True)
    overall = jnp.max(highs, axis=0, keepdims=True)
    scale = jnp.exp(highs - overall)
    pooled = received_ref[0, :, :width].astype(F32) * scale[0]
    for k in range(1, received_ref.shape[0]):
        pooled += received_ref[k, :, :width].astype(F32) * scale[k]
    mean_sq = jnp.mean(pooled * pooled, axis=-1, keepdims=True)
    slots = (pooled * lax.rsqrt(mean_sq + 1e-06) * gain_ref[...]).astype(BF16)
    for k in range(slots_ref.shape[0]):
        slots_ref[k] = slots


def expert_kernel(rows_ref, in_ref, early_ref, late_ref, out_ref, out_b_ref, partial_ref):
    rows = rows_ref[...].reshape(-1, rows_ref.shape[-1])
    hidden = jax.nn.gelu(jnp.dot(rows, in_ref[...], preferred_element_type=F32)).astype(BF16)
    cut = early_ref.shape[0]
    summed = jnp.dot(rows[:, :cut], early_ref[...], preferred_element_type=F32)
    summed += jnp.dot(rows[:, cut:], late_ref[...], preferred_element_type=F32)
    hidden_b = jax.nn.gelu(summed).astype(BF16)
    step = 512
    for start in range(0, rows.shape[1], step):
        part = slice(start, start + step)
        sums = jnp.dot(hidden, out_ref[:, part], preferred_element_type=F32)
        sums += jnp.dot(hidden_b, out_b_ref[:, part], preferred_element_type=F32)
        partial_ref[:, :, part] = sums.astype(BF16).reshape(*rows_ref.shape[:2], step)


def sum_kernel(blocks_ref, copies_ref):
    total = blocks_ref[0].astype(F32)
    for k in range(1, blocks_ref.shape[0]):
        total += blocks_ref[k].astype(F32)
    total = total.astype(BF16)
    for k in range(copies_ref.shape[0]):
        copies_ref[k] = total


def piece_sum(block, which):
    part = block[:, 3 * which : 3 * which + 3].astype(F32)
    return part[:, 0] + part[:, 1] + part[:, 2]


def sent_to_all(value, axes):
    length = lax.axis_size(axes)
    return lax.all_to_all(
        jnp.broadcast_to(value[None], (length, *value.shape)), axes, 0, 0, tiled=True
    )


def local(tokens, router, norm_gain, w_in, w_out):
    feats = tokens[0]
    count, width = feats.shape
    slot_count = router.shape[1]
    owners = lax.axis_size(("xhi", "z"))
    groups = lax.axis_size("y")
    per_owner = slot_count // (2 * owners)
    half = slot_count // 2
    core = lax.axis_index("core")
    hidden_units = w_in.shape[2]
    shape = jax.ShapeDtypeStruct

    cut = width * 2 // 3
    partner_early = lax.ppermute(w_in[0, :cut], "xlo", other())
    partner_late = lax.ppermute(w_in[0, cut:], "xlo", other())
    partner_out = lax.ppermute(w_out[0], "xlo", other())
    partner_feats = lax.ppermute(feats, "core", other())

    row = lax.broadcasted_iota(jnp.int32, (slot_count, half), 0)
    col = lax.broadcasted_iota(jnp.int32, (slot_count, half), 1)
    wanted = (col // per_owner * 2 + core) * per_owner + col % per_owner
    pick = (row == wanted).astype(BF16)
    own_columns = jnp.dot(router, pick, preferred_element_type=F32).astype(BF16)
    columns = sent_to_all(own_columns, ("xlo", "y")).reshape(width, half)

    message, logits, partner_logits = kernel_call(
        dispatch_kernel,
        (shape((half, width + EXTRA), BF16), shape((count, half), F32), shape((count, half), F32)),
        8 * count * width * half,
        2 * (2 * count * width + 2 * width * half),
        [VMEM, VMEM, VMEM, ANY],
        feats,
        partner_feats,
        columns,
        partner_early,
    )
    received = lax.all_to_all(
        message.reshape(owners, per_owner, width + EXTRA), ("xhi", "z"), 0, 0, tiled=True
    )

    weights, answer = kernel_call(
        softmax_kernel,
        (shape((count, half + EXTRA), BF16), shape((count, half + EXTRA), BF16)),
        16 * count * half,
        12 * count * half,
        [VMEM] * 2,
        logits,
        partner_logits,
    )
    weights_b = lax.ppermute(answer, "core", other())

    slots = kernel_call(
        pool_kernel,
        shape((groups, per_owner, width), BF16),
        4 * half * width,
        2 * half * width,
        [VMEM] * 2,
        received,
        norm_gain,
    )
    rows = lax.all_to_all(slots, "y", 0, 0, tiled=True)
    partial = kernel_call(
        expert_kernel,
        shape((groups, per_owner, width), BF16),
        8 * groups * per_owner * width * hidden_units,
        8 * width * hidden_units,
        [VMEM] * 6,
        rows,
        w_in[0],
        partner_early,
        partner_late,
        w_out[0],
        partner_out,
    )
    blocks = lax.all_to_all(partial, "y", 0, 0, tiled=True)
    copies = kernel_call(
        sum_kernel,
        shape((owners, per_owner, width), BF16),
        groups * per_owner * width,
        2 * half * width,
        [VMEM],
        blocks,
    )
    outs = lax.all_to_all(copies, ("xhi", "z"), 0, 0, tiled=True).reshape(half, width)
    outs_b = lax.ppermute(outs, "core", other())

    stats, stats_b = weights[:, half:], weights_b[:, half:]
    row_high, row_sum = piece_sum(stats, 0), piece_sum(stats, 1)
    row_high_b, row_sum_b = piece_sum(stats_b, 0), piece_sum(stats_b, 1)
    top = jnp.maximum(row_high, row_high_b)
    factor = jnp.exp(row_high - top)
    factor_b = jnp.exp(row_high_b - top)
    total = row_sum * factor + row_sum_b * factor_b
    mixed = jnp.dot(weights[:, :half], outs, preferred_element_type=F32) * (factor / total)[:, None]
    mixed += jnp.dot(weights_b[:, :half], outs_b, preferred_element_type=F32) * (factor_b / total)[:, None]
    return (feats.astype(F32) + mixed).astype(BF16)[None]


def solution(mesh):
    fine = Mesh(mesh.devices.reshape(2, 8, 2, 8, 2), ("xlo", "y", "xhi", "z", "core"))
    grp, seq = ("xlo", "y"), ("xhi", "z", "core")
    in_specs = (P(grp, seq, None), P(grp, None), P(seq, None), P(seq, None, grp), P(seq, grp, None))
    return jax.shard_map(
        local, mesh=fine, in_specs=in_specs, out_specs=P(grp, seq, None), check_vma=False
    )
```

time: 177 us -> 171 us (0.966)
  blocking collectives: 37.4 us -> 16.6 us
  matrix products: 13.1 us -> 2.29 us
  starting transfers between devices: 51.5 us -> 60.5 us
  waiting for transfers between devices: 64.3 us -> 71.7 us
  Pallas kernels: 0 us -> 6.76 us
  local copies, waits for them, and re-layouts: 8.39 us -> 11.1 us
    all_to_all x2 -> x1, waiting for transfers between devices: 28.2 us -> 0.01 us  [sent_to_all(): lax.all_to_all(jnp.broadcast_to(value[None], (length, *value.shape)), axe...]
    all_to_all x1 -> x3, waiting for transfers between devices: 14.8 us -> 34.1 us  [the longest x1 20.2 us: local(): lax.all_to_all(message.reshape(owners, per_owner, width + EXTRA), ('xhi',...]
    all_to_all x1 -> x0, blocking collectives: 17.3 us -> none  [sent_to_all(): lax.all_to_all(jnp.broadcast_to(value[None], (length, *value.shape)), axe...]
    ppermute x2 -> x3, waiting for transfers between devices: 19.9 us -> 37 us  [the longest x1 23.4 us: local(): partner_early = lax.ppermute(w_in[0, :cut], 'xlo', other())]
    all_to_all x1 -> x3, starting transfers between devices: 14 us -> 29.6 us  [the longest x1 12.4 us: local(): lax.all_to_all(message.reshape(owners, per_owner, width + EXTRA), ('xhi',...]
    dot_general x8 -> x2, matrix products: 12.9 us -> 2.05 us  [the longest x1 1.58 us: local(): jnp.dot(weights_b[:, :half], outs_b, preferred_element_type=F32)]
    all_to_all x2 -> x1, starting transfers between devices: 17.2 us -> 8.68 us  [sent_to_all(): lax.all_to_all(jnp.broadcast_to(value[None], (length, *value.shape)), axe...]
    unnamed x10 -> x34, local copies, waits for them, and re-layouts: 1.89 us -> 9.97 us
  transfers between devices with their start and end apart: 8 -> 10, of which waited for: 5 -> 5; matrix products, arithmetic and copies ran while one was open for 3% -> 1% of each run, Pallas kernels for 0% -> 1%
where the time goes in v2:
time: 171 us; the launch traced here: 170 us
  waiting for transfers between devices  71.7 us (42%)
  starting transfers between devices  60.5 us (35%)
  blocking collectives  16.6 us (10%)
  local copies, waits for them, and re-layouts  11.1 us (6%)
  Pallas kernels  6.76 us (4%)
  matrix products  2.29 us (1%)
    ppermute x1, waiting for transfers between devices, local(): partner_early = lax.ppermute(w_in[0, :cut], 'xlo', other())  23.4 us
    all_to_all x1, waiting for transfers between devices, local(): lax.all_to_all(message.reshape(owners, per_owner, width + EXTRA), ('xhi',...  20.2 us
    all_to_all x1, blocking collectives, local(): blocks = lax.all_to_all(partial, 'y', 0, 0, tiled=True)  16.6 us
    all_to_all x1, waiting for transfers between devices, local(): lax.all_to_all(copies, ('xhi', 'z'), 0, 0, tiled=True).reshape(half, width)  13.9 us
    ppermute x1, waiting for transfers between devices, local(): partner_late = lax.ppermute(w_in[0, cut:], 'xlo', other())  13.6 us
    all_to_all x1, starting transfers between devices, local(): lax.all_to_all(message.reshape(owners, per_owner, width + EXTRA), ('xhi',...  12.4 us
    all_to_all x1, starting transfers between devices, local(): lax.all_to_all(copies, ('xhi', 'z'), 0, 0, tiled=True).reshape(half, width)  11.7 us
    unnamed x34, local copies, waits for them, and re-layouts  9.97 us
  transfers between devices with their start and end apart: 10, of which 5 were waited for; matrix products, arithmetic and copies ran while one was open for 1% of the time, Pallas kernels for 1%

profile of v2, /device:TPU:1, one launch (start us, length us, event | category | flops | bytes accessed | tf_op | source)
XLA Modules:
  0.0 170.1 jit_solution(12285817245781489488)
XLA Ops:
  0.0 0.0 copy-start
  0.1 0.8 copy-done
  0.9 0.2 fusion.4
  1.1 1.0 broadcast_in_dim.4
  2.1 8.7 %all-to-all-start = ((bf16[16,96,256]{2,1,0:T(8,128)(2,1)}), bf16[16,96,256]{2,1,0:T(8,128)(2,1)S(1)}, u32[]{:S(2)}, u32[]{:S(2)}) async-start(bf16[16,96,256]{2,1,0:T(8,128)(2,1)} %broadcast_in_dim.4), calls=%async_computation | async-start | bytes 1572864 | tf_op jit(solution)/shard_map/all_to_all | solution.py:126
  10.8 3.7 %collective-permute-start = (bf16[384,1536]{1,0:T(8,128)(2,1)S(1)}, bf16[384,1536]{1,0:T(8,128)(2,1)S(1)}, u32[]{:S(2)}, u32[]{:S(2)}) collective-permute-start(bf16[384,1536]{1,0:T(8,128)(2,1)S(1)} %bitcast.21), channel_id=1, source_target_pairs={{0,1},{1,0},{2,3},{3,2},{4,5},{5,4},{6,7},{7,6},{8,9},{9,8},{10,11... | collective-permute-start | bytes 3538952 | tf_op jit(solution)/shard_map/ppermute | solution.py:147
  14.6 0.1 slice_bitcast_fusion
  14.6 3.5 %collective-permute-start.1 = (bf16[1024,384]{1,0:T(8,128)(2,1)S(1)}, bf16[1024,384]{1,0:T(8,128)(2,1)S(1)}, u32[]{:S(2)}, u32[]{:S(2)}) collective-permute-start(bf16[1024,384]{1,0:T(8,128)(2,1)S(1)} %slice_bitcast_fusion), channel_id=1, source_target_pairs={{0,256},{256,0},{1,257},{257,1},{2,258},{258,2},{3,259},{259,3},{4... | collective-permute-start | bytes 2359304 | tf_op jit(solution)/shard_map/ppermute | solution.py:144
  18.1 23.4 %collective-permute-done.1.dummy_ref.early_ref = bf16[1024,384]{1,0:T(8,128)(2,1)S(1)} collective-permute-done((bf16[1024,384]{1,0:T(8,128)(2,1)S(1)}, bf16[1024,384]{1,0:T(8,128)(2,1)S(1)}, u32[]{:S(2)}, u32[]{:S(2)}) %collective-permute-start.1) | collective-permute-done | bytes 786464 | tf_op jit(solution)/shard_map/ppermute | solution.py:144
  41.6 0.9 copy-done.7
  42.4 0.0 collective-permute-done.partner_ref
  42.5 1.0 copy-done.15
  43.5 0.0 all-to-all-done
  43.5 1.3 copy-done.4
  44.7 1.1 copy-done.8
  45.9 1.3 copy-done.16
  47.2 1.8 %shard_map.55 = (bf16[256,1664]{1,0:T(8,128)(2,1)S(1)}, f32[384,256]{1,0:T(8,128)S(1)}, f32[384,256]{1,0:T(8,128)S(1)}) custom-call(bf16[384,1536]{1,0:T(8,128)(2,1)S(1)} %bitcast.22, bf16[384,1536]{1,0:T(8,128)(2,1)S(1)} %copy-done.16, bf16[1536,256]{1,0:T(8,128)(2,1)S(1)} %bitcast.24, bf16[1024,384]{1,0:T(8,128)(2,1)S(1)} %copy-done.8), custom_call_target="tpu_custom_call" | custom-call | flops 1207959552 | bytes 3932160 | tf_op jit(solution)/shard_map/pallas_call | solution.py:22
  49.0 0.0 copy-start.6
  49.0 0.9 copy-done.6
  49.9 0.7 copy-done.10
  50.6 0.8 copy-done.12
  51.4 12.4 %all-to-all-start.1 = ((bf16[16,16,1664]{2,1,0:T(8,128)(2,1)}), bf16[16,16,1664]{2,1,0:T(8,128)(2,1)S(1)}, u32[]{:S(2)}, u32[]{:S(2)}) async-start(bf16[16,16,1664]{2,1,0:T(8,128)(2,1)} %bitcast.23), calls=%async_computation.1 | async-start | bytes 1703936 | tf_op jit(solution)/shard_map/all_to_all | solution.py:167
  63.8 1.9 %collective-permute-start.3 = (bf16[384,1536]{1,0:T(8,128)(2,1)S(1)}, bf16[384,1536]{1,0:T(8,128)(2,1)}, u32[]{:S(2)}, u32[]{:S(2)}) collective-permute-start(bf16[384,1536]{1,0:T(8,128)(2,1)S(1)} %bitcast.19), channel_id=1, source_target_pairs={{0,256},{256,0},{1,257},{257,1},{2,258},{258,2},{3,259},{259,3},{4... | collective-permute-start | bytes 3538952 | tf_op jit(solution)/shard_map/ppermute | solution.py:146
  65.7 20.2 %all-to-all-done.1.received_ref = bf16[16,16,1664]{2,1,0:T(8,128)(2,1)S(1)} async-done(((bf16[16,16,1664]{2,1,0:T(8,128)(2,1)}), bf16[16,16,1664]{2,1,0:T(8,128)(2,1)S(1)}, u32[]{:S(2)}, u32[]{:S(2)}) %all-to-all-start.1) | async-done | bytes 852000 | tf_op jit(solution)/shard_map/all_to_all | solution.py:167
  85.9 1.1 shard_map.57
  87.0 5.5 %all-to-all-start.2 = ((bf16[8,16,1536]{2,1,0:T(8,128)(2,1)}), bf16[8,16,1536]{2,1,0:T(8,128)(2,1)S(1)}, u32[]{:S(2)}, u32[]{:S(2)}) async-start(bf16[8,16,1536]{2,1,0:T(8,128)(2,1)} %shard_map.57), calls=%async_computation.2 | async-start | bytes 786432 | tf_op jit(solution)/shard_map/all_to_all | solution.py:191
  92.6 1.9 %collective-permute-start.2 = (bf16[512,384]{1,0:T(8,128)(2,1)S(1)}, bf16[512,384]{1,0:T(8,128)(2,1)S(1)}, u32[]{:S(2)}, u32[]{:S(2)}) collective-permute-start(bf16[512,384]{1,0:T(8,128)(2,1)S(1)} %slice_bitcast_fusion.1), channel_id=1, source_target_pairs={{0,256},{256,0},{1,257},{257,1},{2,258},{258,2},{3,259},{259,3},{4... | collective-permute-start | bytes 1179656 | tf_op jit(solution)/shard_map/ppermute | solution.py:145
  94.5 13.6 %collective-permute-done.2.late_ref = bf16[512,384]{1,0:T(8,128)(2,1)S(1)} collective-permute-done((bf16[512,384]{1,0:T(8,128)(2,1)S(1)}, bf16[512,384]{1,0:T(8,128)(2,1)S(1)}, u32[]{:S(2)}, u32[]{:S(2)}) %collective-permute-start.2) | collective-permute-done | bytes 393248 | tf_op jit(solution)/shard_map/ppermute | solution.py:145
  108.1 0.0 collective-permute-done.3.out_b_ref
  108.1 0.0 all-to-all-done.2.rows_ref
  108.1 1.1 copy-done.9
  109.2 2.4 %shard_map.58 = bf16[8,16,1536]{2,1,0:T(8,128)(2,1)S(1)} custom-call(bf16[8,16,1536]{2,1,0:T(8,128)(2,1)S(1)} %all-to-all-done.2.rows_ref, bf16[1536,384]{1,0:T(8,128)(2,1)S(1)} %bitcast.18, bf16[1024,384]{1,0:T(8,128)(2,1)S(1)} %copy-done.9, bf16[512,384]{1,0:T(8,128)(2,1)S(1)} %collective-permute-done.2.late_ref, bf16[384,1536]{1,0:T(8,128)(2,1)S(1)} %bitcast.20, ...), custom_call_target="tpu_custom_call" | custom-call | flops 603979776 | bytes 4718592 | tf_op jit(solution)/shard_map/pallas_call | solution.py:22
  111.6 16.6 %all_to_all.25.blocks_ref = bf16[8,16,1536]{2,1,0:T(8,128)(2,1)S(1)} all-to-all(bf16[8,16,1536]{2,1,0:T(8,128)(2,1)S(1)} %shard_map.58), channel_id=1, replica_groups=mesh['xlo'=2,'y'=8,'xhi'=2,'z'=8,'core'=2] {'y'}, dimensions={0} | all-to-all | bytes 786432 | tf_op jit(solution)/shard_map/all_to_all | solution.py:205
  128.2 1.0 shard_map.59
  129.2 11.7 %all-to-all-start.4 = ((bf16[16,16,1536]{2,1,0:T(8,128)(2,1)}), bf16[16,16,1536]{2,1,0:T(8,128)(2,1)S(1)}, u32[]{:S(2)}, u32[]{:S(2)}) async-start(bf16[16,16,1536]{2,1,0:T(8,128)(2,1)} %shard_map.59), calls=%async_computation.4 | async-start | bytes 1572864 | tf_op jit(solution)/shard_map/all_to_all | solution.py:214
  140.9 0.5 shard_map.56
  141.4 4.4 %collective-permute-start.4 = (bf16[384,384]{1,0:T(8,128)(2,1)S(1)}, bf16[384,384]{1,0:T(8,128)(2,1)S(1)}, u32[]{:S(2)}, u32[]{:S(2)}) collective-permute-start(bf16[384,384]{1,0:T(8,128)(2,1)S(1)} %get-tuple-element.14), channel_id=1, source_target_pairs={{0,1},{1,0},{2,3},{3,2},{4,5},{5,4},{6,7},{7,6},{8,9},{9,8},{10,11... | collective-permute-start | bytes 884744 | tf_op jit(solution)/shard_map/ppermute | solution.py:180
  145.9 0.1 slice_convert_fusion.3
  146.0 13.9 %all-to-all-done.4 = bf16[16,16,1536]{2,1,0:T(8,128)(2,1)S(1)} async-done(((bf16[16,16,1536]{2,1,0:T(8,128)(2,1)}), bf16[16,16,1536]{2,1,0:T(8,128)(2,1)S(1)}, u32[]{:S(2)}, u32[]{:S(2)}) %all-to-all-start.4) | async-done | bytes 786464 | tf_op jit(solution)/shard_map/all_to_all | solution.py:214
  159.8 6.7 %collective-permute-start.5 = (bf16[256,1536]{1,0:T(8,128)(2,1)S(1)}, bf16[256,1536]{1,0:T(8,128)(2,1)S(1)}, u32[]{:S(2)}, u32[]{:S(2)}) collective-permute-start(bf16[256,1536]{1,0:T(8,128)(2,1)S(1)} %bitcast.25), channel_id=1, source_target_pairs={{0,1},{1,0},{2,3},{3,2},{4,5},{5,4},{6,7},{7,6},{8,9},{9,8},{10,11... | collective-permute-start | bytes 2359304 | tf_op jit(solution)/shard_map/ppermute | solution.py:215
  166.6 0.0 collective-permute-done.4
  166.6 0.1 slice_convert_fusion.1
  166.7 0.5 fusion.18
  167.2 0.0 copy-start.5
  167.2 0.2 divide_reduce_fusion
  167.4 0.5 convolution_multiply_fusion.1
  167.9 0.6 collective-permute-done.5
  168.5 1.6 fusion.3
  (25 shorter events, 0.1 us)
Async XLA Ops:
  0.0 0.9 copy-start
  0.0 10.8 %copy-start.3 = (bf16[1,384,1536]{2,1,0:T(8,128)(2,1)S(1)}, bf16[1,384,1536]{2,1,0:T(8,128)(2,1)}, u32[]{:S(2)}) copy-start(bf16[1,384,1536]{2,1,0:T(8,128)(2,1)} %param.5) | copy-start | bytes 3538948
  0.0 14.5 %copy-start.1 = (bf16[1,1536,384]{2,1,0:T(8,128)(2,1)S(1)}, bf16[1,1536,384]{2,1,0:T(8,128)(2,1)}, u32[]{:S(2)}) copy-start(bf16[1,1536,384]{2,1,0:T(8,128)(2,1)} %param.8) | copy-start | bytes 3538948
  2.1 41.3 %all-to-all-start = ((bf16[16,96,256]{2,1,0:T(8,128)(2,1)}), bf16[16,96,256]{2,1,0:T(8,128)(2,1)S(1)}, u32[]{:S(2)}, u32[]{:S(2)}) async-start(bf16[16,96,256]{2,1,0:T(8,128)(2,1)} %broadcast_in_dim.4), calls=%async_computation | async-start | bytes 1572864 | tf_op jit(solution)/shard_map/all_to_all | solution.py:126
  10.8 31.6 %collective-permute-start = (bf16[384,1536]{1,0:T(8,128)(2,1)S(1)}, bf16[384,1536]{1,0:T(8,128)(2,1)S(1)}, u32[]{:S(2)}, u32[]{:S(2)}) collective-permute-start(bf16[384,1536]{1,0:T(8,128)(2,1)S(1)} %bitcast.21), channel_id=1, source_target_pairs={{0,1},{1,0},{2,3},{3,2},{4,5},{5,4},{6,7},{7,6},{8,9},{9,8},{10,11... | collective-permute-start | bytes 3538952 | tf_op jit(solution)/shard_map/ppermute | solution.py:147
  14.6 26.9 %collective-permute-start.1 = (bf16[1024,384]{1,0:T(8,128)(2,1)S(1)}, bf16[1024,384]{1,0:T(8,128)(2,1)S(1)}, u32[]{:S(2)}, u32[]{:S(2)}) collective-permute-start(bf16[1024,384]{1,0:T(8,128)(2,1)S(1)} %slice_bitcast_fusion), channel_id=1, source_target_pairs={{0,256},{256,0},{1,257},{257,1},{2,258},{258,2},{3,259},{259,3},{4... | collective-permute-start | bytes 2359304 | tf_op jit(solution)/shard_map/ppermute | solution.py:144
  41.6 0.9 copy-start.7
  42.5 1.0 copy-start.15
  43.5 1.3 copy-start.4
  44.7 1.1 copy-start.8
  45.9 1.3 copy-start.16
  47.1 16.6 %copy-start.2 = (bf16[1,384,1536]{2,1,0:T(8,128)(2,1)S(1)}, bf16[1,384,1536]{2,1,0:T(8,128)(2,1)}, u32[]{:S(2)}) copy-start(bf16[1,384,1536]{2,1,0:T(8,128)(2,1)} %param.9) | copy-start | bytes 3538948
  47.1 38.8 %copy-start.14 = (f32[1,1536]{1,0:T(1,128)S(1)}, f32[1,1536]{1,0:T(1,128)}, u32[]{:S(2)}) copy-start(f32[1,1536]{1,0:T(1,128)} %gain_ref.1) | copy-start | bytes 18436
  49.0 0.9 copy-start.6
  49.9 0.7 copy-start.10
  50.6 0.8 copy-start.12
  51.4 34.5 %all-to-all-start.1 = ((bf16[16,16,1664]{2,1,0:T(8,128)(2,1)}), bf16[16,16,1664]{2,1,0:T(8,128)(2,1)S(1)}, u32[]{:S(2)}, u32[]{:S(2)}) async-start(bf16[16,16,1664]{2,1,0:T(8,128)(2,1)} %bitcast.23), calls=%async_computation.1 | async-start | bytes 1703936 | tf_op jit(solution)/shard_map/all_to_all | solution.py:167
  63.8 44.3 %collective-permute-start.3 = (bf16[384,1536]{1,0:T(8,128)(2,1)S(1)}, bf16[384,1536]{1,0:T(8,128)(2,1)}, u32[]{:S(2)}, u32[]{:S(2)}) collective-permute-start(bf16[384,1536]{1,0:T(8,128)(2,1)S(1)} %bitcast.19), channel_id=1, source_target_pairs={{0,256},{256,0},{1,257},{257,1},{2,258},{258,2},{3,259},{259,3},{4... | collective-permute-start | bytes 3538952 | tf_op jit(solution)/shard_map/ppermute | solution.py:146
  87.0 21.0 %all-to-all-start.2 = ((bf16[8,16,1536]{2,1,0:T(8,128)(2,1)}), bf16[8,16,1536]{2,1,0:T(8,128)(2,1)S(1)}, u32[]{:S(2)}, u32[]{:S(2)}) async-start(bf16[8,16,1536]{2,1,0:T(8,128)(2,1)} %shard_map.57), calls=%async_computation.2 | async-start | bytes 786432 | tf_op jit(solution)/shard_map/all_to_all | solution.py:191
  92.6 15.5 %collective-permute-start.2 = (bf16[512,384]{1,0:T(8,128)(2,1)S(1)}, bf16[512,384]{1,0:T(8,128)(2,1)S(1)}, u32[]{:S(2)}, u32[]{:S(2)}) collective-permute-start(bf16[512,384]{1,0:T(8,128)(2,1)S(1)} %slice_bitcast_fusion.1), channel_id=1, source_target_pairs={{0,256},{256,0},{1,257},{257,1},{2,258},{258,2},{3,259},{259,3},{4... | collective-permute-start | bytes 1179656 | tf_op jit(solution)/shard_map/ppermute | solution.py:145
  108.1 1.1 copy-start.9
  111.6 29.3 %copy-start.11 = (f32[384,256]{1,0:T(8,128)S(1)}, f32[384,256]{1,0:T(8,128)}, u32[]{:S(2)}) copy-start(f32[384,256]{1,0:T(8,128)} %copy-done.10) | copy-start | bytes 1179652
  111.6 29.3 %copy-start.13 = (f32[384,256]{1,0:T(8,128)S(1)}, f32[384,256]{1,0:T(8,128)}, u32[]{:S(2)}) copy-start(f32[384,256]{1,0:T(8,128)} %copy-done.12) | copy-start | bytes 1179652
  129.2 30.6 %all-to-all-start.4 = ((bf16[16,16,1536]{2,1,0:T(8,128)(2,1)}), bf16[16,16,1536]{2,1,0:T(8,128)(2,1)S(1)}, u32[]{:S(2)}, u32[]{:S(2)}) async-start(bf16[16,16,1536]{2,1,0:T(8,128)(2,1)} %shard_map.59), calls=%async_computation.4 | async-start | bytes 1572864 | tf_op jit(solution)/shard_map/all_to_all | solution.py:214
  141.4 25.2 %collective-permute-start.4 = (bf16[384,384]{1,0:T(8,128)(2,1)S(1)}, bf16[384,384]{1,0:T(8,128)(2,1)S(1)}, u32[]{:S(2)}, u32[]{:S(2)}) collective-permute-start(bf16[384,384]{1,0:T(8,128)(2,1)S(1)} %get-tuple-element.14), channel_id=1, source_target_pairs={{0,1},{1,0},{2,3},{3,2},{4,5},{5,4},{6,7},{7,6},{8,9},{9,8},{10,11... | collective-permute-start | bytes 884744 | tf_op jit(solution)/shard_map/ppermute | solution.py:180
  159.8 8.6 %collective-permute-start.5 = (bf16[256,1536]{1,0:T(8,128)(2,1)S(1)}, bf16[256,1536]{1,0:T(8,128)(2,1)S(1)}, u32[]{:S(2)}, u32[]{:S(2)}) collective-permute-start(bf16[256,1536]{1,0:T(8,128)(2,1)S(1)} %bitcast.25), channel_id=1, source_target_pairs={{0,1},{1,0},{2,3},{3,2},{4,5},{5,4},{6,7},{7,6},{8,9},{9,8},{10,11... | collective-permute-start | bytes 2359304 | tf_op jit(solution)/shard_map/ppermute | solution.py:215
  167.2 1.3 copy-start.5

commit v3 on v2

--- a/solution.py
+++ b/solution.py
@@ -1,5 +1,3 @@
-import functools
-
 import jax
 import jax.numpy as jnp
 from jax import lax
@@ -11,22 +9,29 @@
 BF16 = jnp.bfloat16
 EXTRA = 128
 VMEM = pl.BlockSpec(memory_space=pltpu.VMEM)
-ANY = pl.BlockSpec(memory_space=pl.ANY)
+HBM = pl.BlockSpec(memory_space=pltpu.HBM)
 
 
 def other(length=2):
     return [(k, k ^ 1) for k in range(length)]
 
 
-def kernel_call(body, outs, flops, moved, specs, *args):
+def kernel_call(body, outs, flops, moved, specs, *args, out_specs=None, scratch=(), room=60):
     return pl.pallas_call(
         body,
         out_shape=outs,
         in_specs=specs,
-        out_specs=jax.tree.map(lambda _: VMEM, outs),
-        compiler_params=pltpu.CompilerParams(vmem_limit_bytes=16 * 2**20),
+        out_specs=jax.tree.map(lambda _: VMEM, outs) if out_specs is None else out_specs,
+        scratch_shapes=scratch,
+        compiler_params=pltpu.CompilerParams(vmem_limit_bytes=room * 2**20),
         cost_estimate=pl.CostEstimate(flops=flops, bytes_accessed=moved, transcendentals=0),
     )(*args)
+
+
+def started(source, target, semaphores, k):
+    copy = pltpu.make_async_copy(source, target, semaphores.at[k])
+    copy.start()
+    return copy
 
 
 def split_off(value):
@@ -45,12 +50,32 @@
     return packed.astype(BF16)
 
 
-def dispatch_kernel(own_ref, partner_ref, columns_ref, dummy_ref, message_ref, own_logits_ref, partner_logits_ref):
+def dispatch_kernel(
+    own_hbm,
+    partner_hbm,
+    columns_ref,
+    message_ref,
+    own_logits_hbm,
+    partner_logits_hbm,
+    own_ref,
+    partner_ref,
+    own_logits_ref,
+    partner_logits_ref,
+    semaphores,
+):
     width = own_ref.shape[1]
     slots = columns_ref.shape[1]
+    loads = [
+        started(own_hbm, own_ref, semaphores, 0),
+        started(partner_hbm, partner_ref, semaphores, 1),
+    ]
     columns = columns_ref[...]
-    for feats, logits_ref in ((own_ref, own_logits_ref), (partner_ref, partner_logits_ref)):
-        logits_ref[...] = jnp.dot(feats[...], columns, preferred_element_type=F32)
+    loads[0].wait()
+    own_logits_ref[...] = jnp.dot(own_ref[...], columns, preferred_element_type=F32)
+    stores = [started(own_logits_ref, own_logits_hbm, semaphores, 2)]
+    loads[1].wait()
+    partner_logits_ref[...] = jnp.dot(partner_ref[...], columns, preferred_element_type=F32)
+    stores.append(started(partner_logits_ref, partner_logits_hbm, semaphores, 3))
     own_logits, partner_logits = own_logits_ref[...], partner_logits_ref[...]
     high = jnp.maximum(
         jnp.max(own_logits, axis=0, keepdims=True), jnp.max(partner_logits, axis=0, keepdims=True)
@@ -64,6 +89,8 @@
         sums += jnp.dot(partner, partner_ref[:, part], preferred_element_type=F32)
         message_ref[:, part] = sums.astype(BF16)
     message_ref[:, width:] = in_lanes([jnp.broadcast_to(high, (EXTRA, slots)).T])
+    for copy in stores:
+        copy.wait()
 
 
 def softmax_kernel(own_logits_ref, partner_logits_ref, own_ref, answer_ref):
@@ -92,28 +119,48 @@
         slots_ref[k] = slots
 
 
-def expert_kernel(rows_ref, in_ref, early_ref, late_ref, out_ref, out_b_ref, partial_ref):
+def pack_kernel(in_hbm, out_hbm, packed_hbm, semaphores):
+    rows, units = in_hbm.shape
+    copies = [started(in_hbm, packed_hbm.at[pl.ds(0, rows)], semaphores, 0)]
+    for k in range(rows // units):
+        block = out_hbm.at[:, pl.ds(k * units, units)]
+        copies.append(started(block, packed_hbm.at[pl.ds(rows + k * units, units)], semaphores, k + 1))
+    for copy in copies:
+        copy.wait()
+
+
+def expert_kernel(
+    rows_ref, in_hbm, out_hbm, packed_hbm, partial_ref, in_ref, out_ref, in_b_ref, out_b_ref, semaphores
+):
     rows = rows_ref[...].reshape(-1, rows_ref.shape[-1])
+    width, units = in_ref.shape
+    loads = [
+        started(in_hbm, in_ref, semaphores, 0),
+        started(packed_hbm.at[pl.ds(0, width)], in_b_ref, semaphores, 1),
+        started(out_hbm, out_ref, semaphores, 2),
+        started(packed_hbm.at[pl.ds(width, width)], out_b_ref, semaphores, 3),
+    ]
+    loads[0].wait()
     hidden = jax.nn.gelu(jnp.dot(rows, in_ref[...], preferred_element_type=F32)).astype(BF16)
-    cut = early_ref.shape[0]
-    summed = jnp.dot(rows[:, :cut], early_ref[...], preferred_element_type=F32)
-    summed += jnp.dot(rows[:, cut:], late_ref[...], preferred_element_type=F32)
-    hidden_b = jax.nn.gelu(summed).astype(BF16)
-    step = 512
-    for start in range(0, rows.shape[1], step):
-        part = slice(start, start + step)
+    loads[1].wait()
+    hidden_b = jax.nn.gelu(jnp.dot(rows, in_b_ref[...], preferred_element_type=F32)).astype(BF16)
+    loads[2].wait()
+    loads[3].wait()
+    for start in range(0, width, units):
+        part = slice(start, start + units)
         sums = jnp.dot(hidden, out_ref[:, part], preferred_element_type=F32)
-        sums += jnp.dot(hidden_b, out_b_ref[:, part], preferred_element_type=F32)
-        partial_ref[:, :, part] = sums.astype(BF16).reshape(*rows_ref.shape[:2], step)
-
-
-def sum_kernel(blocks_ref, copies_ref):
+        sums += jnp.dot(hidden_b, out_b_ref[part, :], preferred_element_type=F32)
+        partial_ref[:, :, part] = sums.astype(BF16).reshape(*rows_ref.shape[:2], units)
+
+
+def sum_kernel(blocks_ref, copies_hbm, total_ref, semaphores):
     total = blocks_ref[0].astype(F32)
     for k in range(1, blocks_ref.shape[0]):
         total += blocks_ref[k].astype(F32)
-    total = total.astype(BF16)
-    for k in range(copies_ref.shape[0]):
-        copies_ref[k] = total
+    total_ref[...] = total.astype(BF16)
+    copies = [started(total_ref, copies_hbm.at[k], semaphores, k) for k in range(copies_hbm.shape[0])]
+    for copy in copies:
+        copy.wait()
 
 
 def piece_sum(block, which):
@@ -140,10 +187,18 @@
     hidden_units = w_in.shape[2]
     shape = jax.ShapeDtypeStruct
 
-    cut = width * 2 // 3
-    partner_early = lax.ppermute(w_in[0, :cut], "xlo", other())
-    partner_late = lax.ppermute(w_in[0, cut:], "xlo", other())
-    partner_out = lax.ppermute(w_out[0], "xlo", other())
+    packed = kernel_call(
+        pack_kernel,
+        shape((2 * width, hidden_units), BF16),
+        0,
+        8 * width * hidden_units,
+        [HBM] * 2,
+        w_in[0],
+        w_out[0],
+        out_specs=HBM,
+        scratch=[pltpu.SemaphoreType.DMA((1 + width // hidden_units,))],
+    )
+    partner_packed = lax.ppermute(packed, "xlo", other())
     partner_feats = lax.ppermute(feats, "core", other())
 
     row = lax.broadcasted_iota(jnp.int32, (slot_count, half), 0)
@@ -158,11 +213,18 @@
         (shape((half, width + EXTRA), BF16), shape((count, half), F32), shape((count, half), F32)),
         8 * count * width * half,
         2 * (2 * count * width + 2 * width * half),
-        [VMEM, VMEM, VMEM, ANY],
+        [HBM, HBM, VMEM],
         feats,
         partner_feats,
         columns,
-        partner_early,
+        out_specs=(VMEM, HBM, HBM),
+        scratch=[
+            pltpu.VMEM((count, width), BF16),
+            pltpu.VMEM((count, width), BF16),
+            pltpu.VMEM((count, half), F32),
+            pltpu.VMEM((count, half), F32),
+            pltpu.SemaphoreType.DMA((4,)),
+        ],
     )
     received = lax.all_to_all(
         message.reshape(owners, per_owner, width + EXTRA), ("xhi", "z"), 0, 0, tiled=True
@@ -187,6 +249,7 @@
         [VMEM] * 2,
         received,
         norm_gain,
+        room=16,
     )
     rows = lax.all_to_all(slots, "y", 0, 0, tiled=True)
     partial = kernel_call(
@@ -194,13 +257,19 @@
         shape((groups, per_owner, width), BF16),
         8 * groups * per_owner * width * hidden_units,
         8 * width * hidden_units,
-        [VMEM] * 6,
+        [VMEM, HBM, HBM, HBM],
         rows,
         w_in[0],
-        partner_early,
-        partner_late,
         w_out[0],
-        partner_out,
+        partner_packed,
+        scratch=[
+            pltpu.VMEM((width, hidden_units), BF16),
+            pltpu.VMEM((hidden_units, width), BF16),
+            pltpu.VMEM((width, hidden_units), BF16),
+            pltpu.VMEM((width, hidden_units), BF16),
+            pltpu.SemaphoreType.DMA((4,)),
+        ],
+        room=48,
     )
     blocks = lax.all_to_all(partial, "y", 0, 0, tiled=True)
     copies = kernel_call(
@@ -210,6 +279,9 @@
         2 * half * width,
         [VMEM],
         blocks,
+        out_specs=HBM,
+        scratch=[pltpu.VMEM((per_owner, width), BF16), pltpu.SemaphoreType.DMA((owners,))],
+        room=16,
     )
     outs = lax.all_to_all(copies, ("xhi", "z"), 0, 0, tiled=True).reshape(half, width)
     outs_b = lax.ppermute(outs, "core", other())

time: 171 us -> 232 us (1.36)
  Pallas kernels: 6.76 us -> 85.7 us
  blocking collectives: 16.6 us -> 69.2 us
  waiting for transfers between devices: 71.7 us -> 22.2 us
  starting transfers between devices: 60.5 us -> 47 us
  local copies, waits for them, and re-layouts: 11.1 us -> 3.13 us
    pallas_call x5 -> x6, Pallas kernels: 6.76 us -> 85.7 us  [kernel_call(): pl.pallas_call(body, out_shape=outs, in_specs=specs, out_specs=jax.tree.m...]
    all_to_all x0 -> x1, blocking collectives: none -> 55.1 us  [local(): lax.all_to_all(message.reshape(owners, per_owner, width + EXTRA), ('xhi',...]
    ppermute x3 -> x1, waiting for transfers between devices: 37 us -> 0.01 us  [local(): partner_packed = lax.ppermute(packed, 'xlo', other())]
    all_to_all x1 -> x0, waiting for transfers between devices: 20.2 us -> none  [local(): lax.all_to_all(message.reshape(owners, per_owner, width + EXTRA), ('xhi',...]
    all_to_all x1, waiting for transfers between devices: 0.01 us -> 13.6 us  [local(): rows = lax.all_to_all(slots, 'y', 0, 0, tiled=True)]
    all_to_all x1 -> x0, starting transfers between devices: 12.4 us -> none  [local(): lax.all_to_all(message.reshape(owners, per_owner, width + EXTRA), ('xhi',...]
    unnamed x34 -> x18, local copies, waits for them, and re-layouts: 9.97 us -> 2.16 us
    all_to_all x1, waiting for transfers between devices: 13.9 us -> 8.05 us  [local(): lax.all_to_all(copies, ('xhi', 'z'), 0, 0, tiled=True).reshape(half, width)]
  transfers between devices with their start and end apart: 10 -> 7, of which waited for: 5 -> 3; matrix products, arithmetic and copies ran while one was open for 1% -> 1% of each run, Pallas kernels for 1% -> 35%
where the time goes in v3:
time: 232 us
  Pallas kernels  85.7 us (37%)
  blocking collectives  69.2 us (30%)
  starting transfers between devices  47 us (20%)
  waiting for transfers between devices  22.2 us (10%)
  local copies, waits for them, and re-layouts  3.13 us (1%)
    pallas_call x6, Pallas kernels, kernel_call(): pl.pallas_call(body, out_shape=outs, in_specs=specs, out_specs=jax.tree.m...  85.7 us
    all_to_all x1, blocking collectives, local(): lax.all_to_all(message.reshape(owners, per_owner, width + EXTRA), ('xhi',...  55.1 us
    all_to_all x1, blocking collectives, local(): blocks = lax.all_to_all(partial, 'y', 0, 0, tiled=True)  14 us
    all_to_all x1, waiting for transfers between devices, local(): rows = lax.all_to_all(slots, 'y', 0, 0, tiled=True)  13.6 us
    all_to_all x1, starting transfers between devices, local(): lax.all_to_all(copies, ('xhi', 'z'), 0, 0, tiled=True).reshape(half, width)  10.4 us
    all_to_all x1, starting transfers between devices, sent_to_all(): lax.all_to_all(jnp.broadcast_to(value[None], (length, *value.shape)), axe...  8.68 us
    ppermute x1, starting transfers between devices, local(): outs_b = lax.ppermute(outs, 'core', other())  8.17 us
    all_to_all x1, waiting for transfers between devices, local(): lax.all_to_all(copies, ('xhi', 'z'), 0, 0, tiled=True).reshape(half, width)  8.05 us
  transfers between devices with their start and end apart: 7, of which 3 were waited for; matrix products, arithmetic and copies ran while one was open for 1% of the time, Pallas kernels for 35%

profile of v3, /device:TPU:1, one launch (start us, length us, event | category | flops | bytes accessed | tf_op | source)
XLA Modules:
  0.0 231.6 jit_solution(13422142171621661422)
XLA Ops:
  0.0 0.0 copy-start
  0.0 0.0 copy-start.4
  0.0 0.9 copy-done
  0.9 0.2 fusion.4
  1.1 1.0 broadcast_in_dim.4
  2.1 8.7 %all-to-all-start = ((bf16[16,96,256]{2,1,0:T(8,128)(2,1)}), bf16[16,96,256]{2,1,0:T(8,128)(2,1)S(1)}, u32[]{:S(2)}, u32[]{:S(2)}) async-start(bf16[16,96,256]{2,1,0:T(8,128)(2,1)} %broadcast_in_dim.4), calls=%async_computation | async-start | bytes 1572864 | tf_op jit(solution)/shard_map/all_to_all | solution.py:173
  10.8 0.0 copy-done.4
  10.8 3.7 %collective-permute-start = (bf16[384,1536]{1,0:T(8,128)(2,1)S(1)}, bf16[384,1536]{1,0:T(8,128)(2,1)S(1)}, u32[]{:S(2)}, u32[]{:S(2)}) collective-permute-start(bf16[384,1536]{1,0:T(8,128)(2,1)S(1)} %bitcast.21), channel_id=1, source_target_pairs={{0,1},{1,0},{2,3},{3,2},{4,5},{5,4},{6,7},{7,6},{8,9},{9,8},{10,11... | collective-permute-start | bytes 3538952 | tf_op jit(solution)/shard_map/ppermute | solution.py:202
  14.5 72.6 %shard_map.58 = bf16[3072,384]{1,0:T(8,128)(2,1)} custom-call(bf16[1536,384]{1,0:T(8,128)(2,1)} %bitcast.14, bf16[384,1536]{1,0:T(8,128)(2,1)} %bitcast.16), custom_call_target="tpu_custom_call" | custom-call | bytes 4718592 | tf_op jit(solution)/shard_map/pallas_call | solution.py:20
  87.2 3.5 %collective-permute-start.1 = (bf16[3072,384]{1,0:T(8,128)(2,1)}, bf16[3072,384]{1,0:T(8,128)(2,1)}, u32[]{:S(2)}, u32[]{:S(2)}) collective-permute-start(bf16[3072,384]{1,0:T(8,128)(2,1)} %shard_map.58), channel_id=1, source_target_pairs={{0,256},{256,0},{1,257},{257,1},{2,258},{258,2},{3,259},{259,3},{4... | collective-permute-start | bytes 7077896 | tf_op jit(solution)/shard_map/ppermute | solution.py:201
  90.7 0.0 collective-permute-done.partner_hbm
  90.7 0.0 copy-start.8
  90.7 0.0 all-to-all-done
  90.7 0.0 copy-start.6
  90.7 1.0 copy-done.8
  91.7 0.3 copy-done.6
  92.0 0.0 copy-start.3
  92.0 5.9 %shard_map.55 = (bf16[256,1664]{1,0:T(8,128)(2,1)}, f32[384,256]{1,0:T(8,128)}, f32[384,256]{1,0:T(8,128)}) custom-call(bf16[384,1536]{1,0:T(8,128)(2,1)} %bitcast.20, bf16[384,1536]{1,0:T(8,128)(2,1)} %copy-done.8, bf16[1536,256]{1,0:T(8,128)(2,1)} %bitcast.23), custom_call_target="tpu_custom_call" | custom-call | flops 1207959552 | bytes 3932160 | tf_op jit(solution)/shard_map/pallas_call | solution.py:20
  97.9 0.0 copy-start.1
  97.9 0.0 copy-start.2
  97.9 55.1 %all_to_all.25.received_ref = bf16[16,16,1664]{2,1,0:T(8,128)(2,1)S(1)} all-to-all(bf16[16,16,1664]{2,1,0:T(8,128)(2,1)} %bitcast.22), channel_id=1, replica_groups=mesh['xlo'=2,'y'=8,'xhi'=2,'z'=8,'core'=2] {'xhi','z'}, dimensions={0} | all-to-all | bytes 1703936 | tf_op jit(solution)/shard_map/all_to_all | solution.py:229
  153.0 0.0 copy-done.3
  153.0 1.1 shard_map.57
  154.2 6.4 %all-to-all-start.2 = ((bf16[8,16,1536]{2,1,0:T(8,128)(2,1)}), bf16[8,16,1536]{2,1,0:T(8,128)(2,1)S(1)}, u32[]{:S(2)}, u32[]{:S(2)}) async-start(bf16[8,16,1536]{2,1,0:T(8,128)(2,1)} %shard_map.57), calls=%async_computation.2 | async-start | bytes 786432 | tf_op jit(solution)/shard_map/all_to_all | solution.py:254
  160.5 0.0 collective-permute-done.1.packed_hbm
  160.5 13.6 %all-to-all-done.2.rows_ref = bf16[8,16,1536]{2,1,0:T(8,128)(2,1)S(1)} async-done(((bf16[8,16,1536]{2,1,0:T(8,128)(2,1)}), bf16[8,16,1536]{2,1,0:T(8,128)(2,1)S(1)}, u32[]{:S(2)}, u32[]{:S(2)}) %all-to-all-start.2) | async-done | bytes 393248 | tf_op jit(solution)/shard_map/all_to_all | solution.py:254
  174.1 0.0 copy-done.1
  174.1 0.0 copy-done.2
  174.1 2.7 %shard_map.59 = bf16[8,16,1536]{2,1,0:T(8,128)(2,1)S(1)} custom-call(bf16[8,16,1536]{2,1,0:T(8,128)(2,1)S(1)} %all-to-all-done.2.rows_ref, bf16[1536,384]{1,0:T(8,128)(2,1)S(1)} %bitcast.15, bf16[384,1536]{1,0:T(8,128)(2,1)S(1)} %bitcast.17, bf16[3072,384]{1,0:T(8,128)(2,1)} %collective-permute-done.1.packed_hbm), custom_call_target="tpu_custom_call" | custom-call | flops 603979776 | bytes 4718592 | tf_op jit(solution)/shard_map/pallas_call | solution.py:20
  176.8 14.0 %all_to_all.26.blocks_ref = bf16[8,16,1536]{2,1,0:T(8,128)(2,1)S(1)} all-to-all(bf16[8,16,1536]{2,1,0:T(8,128)(2,1)S(1)} %shard_map.59), channel_id=1, replica_groups=mesh['xlo'=2,'y'=8,'xhi'=2,'z'=8,'core'=2] {'y'}, dimensions={0} | all-to-all | bytes 786432 | tf_op jit(solution)/shard_map/all_to_all | solution.py:274
  190.8 1.1 shard_map.60
  191.9 10.4 %all-to-all-start.4 = ((bf16[16,16,1536]{2,1,0:T(8,128)(2,1)}), bf16[16,16,1536]{2,1,0:T(8,128)(2,1)S(1)}, u32[]{:S(2)}, u32[]{:S(2)}) async-start(bf16[16,16,1536]{2,1,0:T(8,128)(2,1)} %shard_map.60), calls=%async_computation.4 | async-start | bytes 1572864 | tf_op jit(solution)/shard_map/all_to_all | solution.py:286
  202.3 2.3 shard_map.56
  204.6 6.2 %collective-permute-start.2 = (bf16[384,384]{1,0:T(8,128)(2,1)}, bf16[384,384]{1,0:T(8,128)(2,1)S(1)}, u32[]{:S(2)}, u32[]{:S(2)}) collective-permute-start(bf16[384,384]{1,0:T(8,128)(2,1)} %get-tuple-element.14), channel_id=1, source_target_pairs={{0,1},{1,0},{2,3},{3,2},{4,5},{5,4},{6,7},{7,6},{8,9},{9,8},{10,11... | collective-permute-start | bytes 884744 | tf_op jit(solution)/shard_map/ppermute | solution.py:242
  210.8 0.0 copy-start.7
  210.8 1.1 slice_convert_fusion.3
  211.9 8.0 %all-to-all-done.4 = bf16[16,16,1536]{2,1,0:T(8,128)(2,1)S(1)} async-done(((bf16[16,16,1536]{2,1,0:T(8,128)(2,1)}), bf16[16,16,1536]{2,1,0:T(8,128)(2,1)S(1)}, u32[]{:S(2)}, u32[]{:S(2)}) %all-to-all-start.4) | async-done | bytes 786464 | tf_op jit(solution)/shard_map/all_to_all | solution.py:286
  220.0 8.2 %collective-permute-start.3 = (bf16[256,1536]{1,0:T(8,128)(2,1)S(1)}, bf16[256,1536]{1,0:T(8,128)(2,1)S(1)}, u32[]{:S(2)}, u32[]{:S(2)}) collective-permute-start(bf16[256,1536]{1,0:T(8,128)(2,1)S(1)} %bitcast.18), channel_id=1, source_target_pairs={{0,1},{1,0},{2,3},{3,2},{4,5},{5,4},{6,7},{7,6},{8,9},{9,8},{10,11... | collective-permute-start | bytes 2359304 | tf_op jit(solution)/shard_map/ppermute | solution.py:287
  228.1 0.0 collective-permute-done.2
  228.1 0.1 slice_convert_fusion.1
  228.2 0.5 fusion.18
  228.7 0.0 copy-start.5
  228.7 0.2 divide_reduce_fusion
  228.9 0.0 copy-done.7
  228.9 0.5 convolution_multiply_fusion.1
  229.4 0.6 collective-permute-done.3
  230.0 0.0 copy-done.5
  230.0 1.6 fusion.3
  (3 shorter events, 0.0 us)
Async XLA Ops:
  0.0 0.9 copy-start
  0.0 10.8 %copy-start.4 = (bf16[1,384,1536]{2,1,0:T(8,128)(2,1)S(1)}, bf16[1,384,1536]{2,1,0:T(8,128)(2,1)}, u32[]{:S(2)}) copy-start(bf16[1,384,1536]{2,1,0:T(8,128)(2,1)} %param.5) | copy-start | bytes 3538948
  2.1 88.6 %all-to-all-start = ((bf16[16,96,256]{2,1,0:T(8,128)(2,1)}), bf16[16,96,256]{2,1,0:T(8,128)(2,1)S(1)}, u32[]{:S(2)}, u32[]{:S(2)}) async-start(bf16[16,96,256]{2,1,0:T(8,128)(2,1)} %broadcast_in_dim.4), calls=%async_computation | async-start | bytes 1572864 | tf_op jit(solution)/shard_map/all_to_all | solution.py:173
  10.8 79.8 %collective-permute-start = (bf16[384,1536]{1,0:T(8,128)(2,1)S(1)}, bf16[384,1536]{1,0:T(8,128)(2,1)S(1)}, u32[]{:S(2)}, u32[]{:S(2)}) collective-permute-start(bf16[384,1536]{1,0:T(8,128)(2,1)S(1)} %bitcast.21), channel_id=1, source_target_pairs={{0,1},{1,0},{2,3},{3,2},{4,5},{5,4},{6,7},{7,6},{8,9},{9,8},{10,11... | collective-permute-start | bytes 3538952 | tf_op jit(solution)/shard_map/ppermute | solution.py:202
  87.2 73.4 %collective-permute-start.1 = (bf16[3072,384]{1,0:T(8,128)(2,1)}, bf16[3072,384]{1,0:T(8,128)(2,1)}, u32[]{:S(2)}, u32[]{:S(2)}) collective-permute-start(bf16[3072,384]{1,0:T(8,128)(2,1)} %shard_map.58), channel_id=1, source_target_pairs={{0,256},{256,0},{1,257},{257,1},{2,258},{258,2},{3,259},{259,3},{4... | collective-permute-start | bytes 7077896 | tf_op jit(solution)/shard_map/ppermute | solution.py:201
  90.7 1.0 copy-start.8
  90.7 1.3 copy-start.6
  92.0 61.1 %copy-start.3 = (f32[1,1536]{1,0:T(1,128)S(1)}, f32[1,1536]{1,0:T(1,128)}, u32[]{:S(2)}) copy-start(f32[1,1536]{1,0:T(1,128)} %gain_ref.1) | copy-start | bytes 18436
  97.9 76.2 %copy-start.1 = (bf16[1,1536,384]{2,1,0:T(8,128)(2,1)S(1)}, bf16[1,1536,384]{2,1,0:T(8,128)(2,1)}, u32[]{:S(2)}) copy-start(bf16[1,1536,384]{2,1,0:T(8,128)(2,1)} %param.8) | copy-start | bytes 3538948
  97.9 76.2 %copy-start.2 = (bf16[1,384,1536]{2,1,0:T(8,128)(2,1)S(1)}, bf16[1,384,1536]{2,1,0:T(8,128)(2,1)}, u32[]{:S(2)}) copy-start(bf16[1,384,1536]{2,1,0:T(8,128)(2,1)} %param.9) | copy-start | bytes 3538948
  154.2 19.9 %all-to-all-start.2 = ((bf16[8,16,1536]{2,1,0:T(8,128)(2,1)}), bf16[8,16,1536]{2,1,0:T(8,128)(2,1)S(1)}, u32[]{:S(2)}, u32[]{:S(2)}) async-start(bf16[8,16,1536]{2,1,0:T(8,128)(2,1)} %shard_map.57), calls=%async_computation.2 | async-start | bytes 786432 | tf_op jit(solution)/shard_map/all_to_all | solution.py:254
  191.9 28.1 %all-to-all-start.4 = ((bf16[16,16,1536]{2,1,0:T(8,128)(2,1)}), bf16[16,16,1536]{2,1,0:T(8,128)(2,1)S(1)}, u32[]{:S(2)}, u32[]{:S(2)}) async-start(bf16[16,16,1536]{2,1,0:T(8,128)(2,1)} %shard_map.60), calls=%async_computation.4 | async-start | bytes 1572864 | tf_op jit(solution)/shard_map/all_to_all | solution.py:286
  204.6 23.5 %collective-permute-start.2 = (bf16[384,384]{1,0:T(8,128)(2,1)}, bf16[384,384]{1,0:T(8,128)(2,1)S(1)}, u32[]{:S(2)}, u32[]{:S(2)}) collective-permute-start(bf16[384,384]{1,0:T(8,128)(2,1)} %get-tuple-element.14), channel_id=1, source_target_pairs={{0,1},{1,0},{2,3},{3,2},{4,5},{5,4},{6,7},{7,6},{8,9},{9,8},{10,11... | collective-permute-start | bytes 884744 | tf_op jit(solution)/shard_map/ppermute | solution.py:242
  210.8 18.2 %copy-start.7 = (bf16[384,384]{1,0:T(8,128)(2,1)S(1)}, bf16[384,384]{1,0:T(8,128)(2,1)}, u32[]{:S(2)}) copy-start(bf16[384,384]{1,0:T(8,128)(2,1)} %get-tuple-element.12) | copy-start | bytes 884740
  220.0 10.1 %collective-permute-start.3 = (bf16[256,1536]{1,0:T(8,128)(2,1)S(1)}, bf16[256,1536]{1,0:T(8,128)(2,1)S(1)}, u32[]{:S(2)}, u32[]{:S(2)}) collective-permute-start(bf16[256,1536]{1,0:T(8,128)(2,1)S(1)} %bitcast.18), channel_id=1, source_target_pairs={{0,1},{1,0},{2,3},{3,2},{4,5},{5,4},{6,7},{7,6},{8,9},{9,8},{10,11... | collective-permute-start | bytes 2359304 | tf_op jit(solution)/shard_map/ppermute | solution.py:287
  228.7 1.3 copy-start.5

commit v4 on v3

--- a/solution.py
+++ b/solution.py
@@ -23,7 +23,7 @@
         in_specs=specs,
         out_specs=jax.tree.map(lambda _: VMEM, outs) if out_specs is None else out_specs,
         scratch_shapes=scratch,
-        compiler_params=pltpu.CompilerParams(vmem_limit_bytes=room * 2**20),
+        compiler_params=pltpu.CompilerParams(vmem_limit_bytes=int(room * 2**20)),
         cost_estimate=pl.CostEstimate(flops=flops, bytes_accessed=moved, transcendentals=0),
     )(*args)
 
@@ -32,6 +32,12 @@
     copy = pltpu.make_async_copy(source, target, semaphores.at[k])
     copy.start()
     return copy
+
+
+def started_rows(source, target, semaphores, first, count):
+    rows = source.shape[0] // count
+    parts = [pl.ds(k * rows, rows) for k in range(count)]
+    return [started(source.at[p], target.at[p], semaphores, first + k) for k, p in enumerate(parts)]
 
 
 def split_off(value):
@@ -53,42 +59,49 @@
 def dispatch_kernel(
     own_hbm,
     partner_hbm,
-    columns_ref,
-    message_ref,
+    columns_hbm,
+    message_hbm,
     own_logits_hbm,
     partner_logits_hbm,
     own_ref,
     partner_ref,
+    columns_ref,
     own_logits_ref,
     partner_logits_ref,
+    message_ref,
     semaphores,
 ):
     width = own_ref.shape[1]
     slots = columns_ref.shape[1]
-    loads = [
-        started(own_hbm, own_ref, semaphores, 0),
-        started(partner_hbm, partner_ref, semaphores, 1),
-    ]
+    cuts = 4
+    first = started_rows(columns_hbm, columns_ref, semaphores, 15, cuts)
+    loads = started_rows(own_hbm, own_ref, semaphores, 0, cuts)
+    loads += started_rows(partner_hbm, partner_ref, semaphores, cuts, cuts)
+    for copy in first + loads[:cuts]:
+        copy.wait()
     columns = columns_ref[...]
-    loads[0].wait()
     own_logits_ref[...] = jnp.dot(own_ref[...], columns, preferred_element_type=F32)
-    stores = [started(own_logits_ref, own_logits_hbm, semaphores, 2)]
-    loads[1].wait()
+    stores = [started(own_logits_ref, own_logits_hbm, semaphores, 2 * cuts)]
+    for copy in loads[cuts:]:
+        copy.wait()
     partner_logits_ref[...] = jnp.dot(partner_ref[...], columns, preferred_element_type=F32)
-    stores.append(started(partner_logits_ref, partner_logits_hbm, semaphores, 3))
+    stores.append(started(partner_logits_ref, partner_logits_hbm, semaphores, 2 * cuts + 1))
     own_logits, partner_logits = own_logits_ref[...], partner_logits_ref[...]
     high = jnp.maximum(
         jnp.max(own_logits, axis=0, keepdims=True), jnp.max(partner_logits, axis=0, keepdims=True)
     )
+    message_ref[:, width:] = in_lanes([jnp.broadcast_to(high, (EXTRA, slots)).T])
+    last = pl.ds(width, EXTRA)
+    stores.append(started(message_ref.at[:, last], message_hbm.at[:, last], semaphores, 2 * cuts + 2))
     own = jnp.exp(own_logits - high).astype(BF16).T
     partner = jnp.exp(partner_logits - high).astype(BF16).T
-    step = 512
-    for start in range(0, width, step):
-        part = slice(start, start + step)
+    step = 384
+    for k in range(width // step):
+        part = pl.ds(k * step, step)
         sums = jnp.dot(own, own_ref[:, part], preferred_element_type=F32)
         sums += jnp.dot(partner, partner_ref[:, part], preferred_element_type=F32)
         message_ref[:, part] = sums.astype(BF16)
-    message_ref[:, width:] = in_lanes([jnp.broadcast_to(high, (EXTRA, slots)).T])
+        stores.append(started(message_ref.at[:, part], message_hbm.at[:, part], semaphores, 2 * cuts + 3 + k))
     for copy in stores:
         copy.wait()
 
@@ -105,7 +118,7 @@
         out_ref[:, slots:] = in_lanes([jnp.broadcast_to(high, lanes), jnp.broadcast_to(total, lanes)])
 
 
-def pool_kernel(received_ref, gain_ref, slots_ref):
+def pool_kernel(received_ref, gain_ref, copies_hbm, slots_ref, semaphores):
     width = gain_ref.shape[1]
     highs = jnp.sum(received_ref[:, :, width:].astype(F32), axis=-1, keepdims=True)
     overall = jnp.max(highs, axis=0, keepdims=True)
@@ -114,43 +127,49 @@
     for k in range(1, received_ref.shape[0]):
         pooled += received_ref[k, :, :width].astype(F32) * scale[k]
     mean_sq = jnp.mean(pooled * pooled, axis=-1, keepdims=True)
-    slots = (pooled * lax.rsqrt(mean_sq + 1e-06) * gain_ref[...]).astype(BF16)
-    for k in range(slots_ref.shape[0]):
-        slots_ref[k] = slots
-
-
-def pack_kernel(in_hbm, out_hbm, packed_hbm, semaphores):
-    rows, units = in_hbm.shape
-    copies = [started(in_hbm, packed_hbm.at[pl.ds(0, rows)], semaphores, 0)]
-    for k in range(rows // units):
-        block = out_hbm.at[:, pl.ds(k * units, units)]
-        copies.append(started(block, packed_hbm.at[pl.ds(rows + k * units, units)], semaphores, k + 1))
+    slots_ref[...] = (pooled * lax.rsqrt(mean_sq + 1e-06) * gain_ref[...]).astype(BF16)
+    copies = [started(slots_ref, copies_hbm.at[k], semaphores, k) for k in range(copies_hbm.shape[0])]
     for copy in copies:
         copy.wait()
 
 
+def follow_kernel(weights_hbm, before_hbm, weights_ref, semaphores):
+    for copy in started_rows(weights_hbm, weights_ref, semaphores, 0, semaphores.shape[0]):
+        copy.wait()
+
+
 def expert_kernel(
-    rows_ref, in_hbm, out_hbm, packed_hbm, partial_ref, in_ref, out_ref, in_b_ref, out_b_ref, semaphores
+    rows_ref,
+    in_hbm,
+    out_hbm,
+    in_b_hbm,
+    out_b_hbm,
+    partial_ref,
+    in_ref,
+    out_ref,
+    in_b_ref,
+    out_b_ref,
+    semaphores,
 ):
     rows = rows_ref[...].reshape(-1, rows_ref.shape[-1])
-    width, units = in_ref.shape
-    loads = [
-        started(in_hbm, in_ref, semaphores, 0),
-        started(packed_hbm.at[pl.ds(0, width)], in_b_ref, semaphores, 1),
-        started(out_hbm, out_ref, semaphores, 2),
-        started(packed_hbm.at[pl.ds(width, width)], out_b_ref, semaphores, 3),
-    ]
-    loads[0].wait()
+    width = rows.shape[1]
+    cuts = 4
+    pairs = ((in_hbm, in_ref), (in_b_hbm, in_b_ref), (out_hbm, out_ref), (out_b_hbm, out_b_ref))
+    loads = [started_rows(*pair, semaphores, cuts * k, cuts) for k, pair in enumerate(pairs)]
+    for copy in loads[0]:
+        copy.wait()
     hidden = jax.nn.gelu(jnp.dot(rows, in_ref[...], preferred_element_type=F32)).astype(BF16)
-    loads[1].wait()
+    for copy in loads[1]:
+        copy.wait()
     hidden_b = jax.nn.gelu(jnp.dot(rows, in_b_ref[...], preferred_element_type=F32)).astype(BF16)
-    loads[2].wait()
-    loads[3].wait()
-    for start in range(0, width, units):
-        part = slice(start, start + units)
+    for copy in loads[2] + loads[3]:
+        copy.wait()
+    step = 512
+    for k in range(width // step):
+        part = pl.ds(k * step, step)
         sums = jnp.dot(hidden, out_ref[:, part], preferred_element_type=F32)
-        sums += jnp.dot(hidden_b, out_b_ref[part, :], preferred_element_type=F32)
-        partial_ref[:, :, part] = sums.astype(BF16).reshape(*rows_ref.shape[:2], units)
+        sums += jnp.dot(hidden_b, out_b_ref[:, part], preferred_element_type=F32)
+        partial_ref[:, :, part] = sums.astype(BF16).reshape(*rows_ref.shape[:2], step)
 
 
 def sum_kernel(blocks_ref, copies_hbm, total_ref, semaphores):
@@ -187,18 +206,19 @@
     hidden_units = w_in.shape[2]
     shape = jax.ShapeDtypeStruct
 
-    packed = kernel_call(
-        pack_kernel,
-        shape((2 * width, hidden_units), BF16),
+    partner_in = lax.ppermute(w_in[0], "xlo", other())
+    out_later = kernel_call(
+        follow_kernel,
+        shape((hidden_units, width), BF16),
         0,
-        8 * width * hidden_units,
+        4 * width * hidden_units,
         [HBM] * 2,
-        w_in[0],
         w_out[0],
-        out_specs=HBM,
-        scratch=[pltpu.SemaphoreType.DMA((1 + width // hidden_units,))],
-    )
-    partner_packed = lax.ppermute(packed, "xlo", other())
+        partner_in,
+        scratch=[pltpu.SemaphoreType.DMA((4,))],
+        room=16,
+    )
+    partner_out = lax.ppermute(out_later, "xlo", other())
     partner_feats = lax.ppermute(feats, "core", other())
 
     row = lax.broadcasted_iota(jnp.int32, (slot_count, half), 0)
@@ -213,18 +233,21 @@
         (shape((half, width + EXTRA), BF16), shape((count, half), F32), shape((count, half), F32)),
         8 * count * width * half,
         2 * (2 * count * width + 2 * width * half),
-        [HBM, HBM, VMEM],
+        [HBM] * 3,
         feats,
         partner_feats,
         columns,
-        out_specs=(VMEM, HBM, HBM),
+        out_specs=(HBM, HBM, HBM),
         scratch=[
             pltpu.VMEM((count, width), BF16),
             pltpu.VMEM((count, width), BF16),
+            pltpu.VMEM((width, half), BF16),
             pltpu.VMEM((count, half), F32),
             pltpu.VMEM((count, half), F32),
-            pltpu.SemaphoreType.DMA((4,)),
+            pltpu.VMEM((half, width + EXTRA), BF16),
+            pltpu.SemaphoreType.DMA((19,)),
         ],
+        room=58,
     )
     received = lax.all_to_all(
         message.reshape(owners, per_owner, width + EXTRA), ("xhi", "z"), 0, 0, tiled=True
@@ -249,6 +272,8 @@
         [VMEM] * 2,
         received,
         norm_gain,
+        out_specs=HBM,
+        scratch=[pltpu.VMEM((per_owner, width), BF16), pltpu.SemaphoreType.DMA((groups,))],
         room=16,
     )
     rows = lax.all_to_all(slots, "y", 0, 0, tiled=True)
@@ -257,17 +282,18 @@
         shape((groups, per_owner, width), BF16),
         8 * groups * per_owner * width * hidden_units,
         8 * width * hidden_units,
-        [VMEM, HBM, HBM, HBM],
+        [VMEM, HBM, HBM, HBM, HBM],
         rows,
         w_in[0],
         w_out[0],
-        partner_packed,
+        partner_in,
+        partner_out,
         scratch=[
             pltpu.VMEM((width, hidden_units), BF16),
             pltpu.VMEM((hidden_units, width), BF16),
             pltpu.VMEM((width, hidden_units), BF16),
-            pltpu.VMEM((width, hidden_units), BF16),
-            pltpu.SemaphoreType.DMA((4,)),
+            pltpu.VMEM((hidden_units, width), BF16),
+            pltpu.SemaphoreType.DMA((16,)),
         ],
         room=48,
     )

time: 232 us -> 152 us (0.66)
  Pallas kernels: 85.7 us -> 13.6 us
  blocking collectives: 69.2 us -> 16.7 us
  waiting for transfers between devices: 22.2 us -> 49.3 us
  starting transfers between devices: 47 us -> 63.9 us
    pallas_call x6, Pallas kernels: 85.7 us -> 13.6 us  [kernel_call(): pl.pallas_call(body, out_shape=outs, in_specs=specs, out_specs=jax.tree.m...]
    all_to_all x1 -> x0, blocking collectives: 55.1 us -> none  [local(): lax.all_to_all(message.reshape(owners, per_owner, width + EXTRA), ('xhi',...]
    all_to_all x0 -> x1, waiting for transfers between devices: none -> 15.1 us  [local(): lax.all_to_all(message.reshape(owners, per_owner, width + EXTRA), ('xhi',...]
    all_to_all x0 -> x1, starting transfers between devices: none -> 13.9 us  [local(): lax.all_to_all(message.reshape(owners, per_owner, width + EXTRA), ('xhi',...]
    all_to_all x1, waiting for transfers between devices: 13.6 us -> 1.27 us  [local(): rows = lax.all_to_all(slots, 'y', 0, 0, tiled=True)]
    all_to_all x1, waiting for transfers between devices: 0.01 us -> 10.9 us  [sent_to_all(): lax.all_to_all(jnp.broadcast_to(value[None], (length, *value.shape)), axe...]
    ppermute x1 -> x2, waiting for transfers between devices: 0.01 us -> 10.2 us  [the longest x1 9.28 us: local(): partner_out = lax.ppermute(out_later, 'xlo', other())]
    all_to_all x1, starting transfers between devices: 10.4 us -> 13.9 us  [local(): lax.all_to_all(copies, ('xhi', 'z'), 0, 0, tiled=True).reshape(half, width)]
  transfers between devices with their start and end apart: 7 -> 9, of which waited for: 3 -> 7; matrix products, arithmetic and copies ran while one was open for 1% -> 2% of each run, Pallas kernels for 35% -> 6%
where the time goes in v4:
time: 152 us; the launch traced here: 151 us
  starting transfers between devices  63.9 us (42%)
  waiting for transfers between devices  49.3 us (32%)
  blocking collectives  16.7 us (11%)
  Pallas kernels  13.6 us (9%)
  local copies, waits for them, and re-layouts  3.45 us (2%)
  matrix products  2.28 us (1%)
  other arithmetic  1.91 us (1%)
    all_to_all x1, blocking collectives, local(): blocks = lax.all_to_all(partial, 'y', 0, 0, tiled=True)  16.7 us
    all_to_all x1, waiting for transfers between devices, local(): lax.all_to_all(message.reshape(owners, per_owner, width + EXTRA), ('xhi',...  15.1 us
    all_to_all x1, starting transfers between devices, local(): lax.all_to_all(copies, ('xhi', 'z'), 0, 0, tiled=True).reshape(half, width)  13.9 us
    all_to_all x1, starting transfers between devices, local(): lax.all_to_all(message.reshape(owners, per_owner, width + EXTRA), ('xhi',...  13.9 us
    pallas_call x6, Pallas kernels, kernel_call(): pl.pallas_call(body, out_shape=outs, in_specs=specs, out_specs=jax.tree.m...  13.6 us
    all_to_all x1, waiting for transfers between devices, local(): lax.all_to_all(copies, ('xhi', 'z'), 0, 0, tiled=True).reshape(half, width)  11.2 us
    all_to_all x1, waiting for transfers between devices, sent_to_all(): lax.all_to_all(jnp.broadcast_to(value[None], (length, *value.shape)), axe...  10.9 us
    ppermute x1, waiting for transfers between devices, local(): partner_out = lax.ppermute(out_later, 'xlo', other())  9.28 us
  transfers between devices with their start and end apart: 9, of which 7 were waited for; matrix products, arithmetic and copies ran while one was open for 2% of the time, Pallas kernels for 6%

profile of v4, /device:TPU:1, one launch (start us, length us, event | category | flops | bytes accessed | tf_op | source)
XLA Modules:
  0.0 151.4 jit_solution(3868597822807877693)
XLA Ops:
  0.0 0.0 copy-start
  0.0 0.0 copy-start.4
  0.0 0.9 copy-done
  0.9 0.2 fusion.4
  1.1 1.0 broadcast_in_dim.4
  2.1 8.7 %all-to-all-start = ((bf16[16,96,256]{2,1,0:T(8,128)(2,1)}), bf16[16,96,256]{2,1,0:T(8,128)(2,1)S(1)}, u32[]{:S(2)}, u32[]{:S(2)}) async-start(bf16[16,96,256]{2,1,0:T(8,128)(2,1)} %broadcast_in_dim.4), calls=%async_computation | async-start | bytes 1572864 | tf_op jit(solution)/shard_map/all_to_all | solution.py:192
  10.8 0.0 copy-done.4
  10.8 3.7 %collective-permute-start = (bf16[384,1536]{1,0:T(8,128)(2,1)S(1)}, bf16[384,1536]{1,0:T(8,128)(2,1)}, u32[]{:S(2)}, u32[]{:S(2)}) collective-permute-start(bf16[384,1536]{1,0:T(8,128)(2,1)S(1)} %bitcast.19), channel_id=1, source_target_pairs={{0,1},{1,0},{2,3},{3,2},{4,5},{5,4},{6,7},{7,6},{8,9},{9,8},{10,11... | collective-permute-start | bytes 3538952 | tf_op jit(solution)/shard_map/ppermute | solution.py:222
  14.5 3.5 %collective-permute-start.1 = (bf16[1536,384]{1,0:T(8,128)(2,1)}, bf16[1536,384]{1,0:T(8,128)(2,1)S(1)}, u32[]{:S(2)}, u32[]{:S(2)}) collective-permute-start(bf16[1536,384]{1,0:T(8,128)(2,1)} %bitcast.4.in_hbm), channel_id=1, source_target_pairs={{0,256},{256,0},{1,257},{257,1},{2,258},{258,2},{3,259},{259,3},{4... | collective-permute-start | bytes 3538952 | tf_op jit(solution)/shard_map/ppermute | solution.py:209
  18.0 0.0 collective-permute-done.partner_hbm
  18.0 10.9 %all-to-all-done = bf16[16,96,256]{2,1,0:T(8,128)(2,1)S(1)} async-done(((bf16[16,96,256]{2,1,0:T(8,128)(2,1)}), bf16[16,96,256]{2,1,0:T(8,128)(2,1)S(1)}, u32[]{:S(2)}, u32[]{:S(2)}) %all-to-all-start) | async-done | bytes 786464 | tf_op jit(solution)/shard_map/all_to_all | solution.py:192
  29.0 0.0 copy-start.6
  29.0 0.9 copy-done.6
  29.8 5.2 %shard_map.55 = (bf16[256,1664]{1,0:T(8,128)(2,1)}, f32[384,256]{1,0:T(8,128)}, f32[384,256]{1,0:T(8,128)}) custom-call(bf16[384,1536]{1,0:T(8,128)(2,1)} %bitcast.18, bf16[384,1536]{1,0:T(8,128)(2,1)} %collective-permute-done.partner_hbm, bf16[1536,256]{1,0:T(8,128)(2,1)} %bitcast.21), custom_call_target="tpu_custom_call" | custom-call | flops 1207959552 | bytes 3932160 | tf_op jit(solution)/shard_map/pallas_call | solution.py:20
  35.1 0.0 copy-start.3
  35.1 13.9 %all-to-all-start.1 = ((bf16[16,16,1664]{2,1,0:T(8,128)(2,1)}), bf16[16,16,1664]{2,1,0:T(8,128)(2,1)S(1)}, u32[]{:S(2)}, u32[]{:S(2)}) async-start(bf16[16,16,1664]{2,1,0:T(8,128)(2,1)} %bitcast.20), calls=%async_computation.1 | async-start | bytes 1703936 | tf_op jit(solution)/shard_map/all_to_all | solution.py:252
  49.0 0.9 collective-permute-done.1.before_hbm.in_b_hbm
  49.9 0.0 copy-done.1
  49.9 1.3 shard_map.58
  51.2 2.9 %collective-permute-start.2 = (bf16[384,1536]{1,0:T(8,128)(2,1)}, bf16[384,1536]{1,0:T(8,128)(2,1)}, u32[]{:S(2)}, u32[]{:S(2)}) collective-permute-start(bf16[384,1536]{1,0:T(8,128)(2,1)} %shard_map.58), channel_id=1, source_target_pairs={{0,256},{256,0},{1,257},{257,1},{2,258},{258,2},{3,259},{259,3},{4... | collective-permute-start | bytes 3538952 | tf_op jit(solution)/shard_map/ppermute | solution.py:221
  54.1 15.1 %all-to-all-done.1.received_ref = bf16[16,16,1664]{2,1,0:T(8,128)(2,1)S(1)} async-done(((bf16[16,16,1664]{2,1,0:T(8,128)(2,1)}), bf16[16,16,1664]{2,1,0:T(8,128)(2,1)S(1)}, u32[]{:S(2)}, u32[]{:S(2)}) %all-to-all-start.1) | async-done | bytes 852000 | tf_op jit(solution)/shard_map/all_to_all | solution.py:252
  69.2 0.0 copy-done.3
  69.2 0.9 shard_map.57
  70.2 0.0 copy-start.2
  70.2 0.7 copy-done.2
  70.9 6.5 %all-to-all-start.2 = ((bf16[8,16,1536]{2,1,0:T(8,128)(2,1)}), bf16[8,16,1536]{2,1,0:T(8,128)(2,1)S(1)}, u32[]{:S(2)}, u32[]{:S(2)}) async-start(bf16[8,16,1536]{2,1,0:T(8,128)(2,1)} %copy-done.2), calls=%async_computation.2 | async-start | bytes 786432 | tf_op jit(solution)/shard_map/all_to_all | solution.py:279
  77.4 9.3 %collective-permute-done.2.out_b_hbm = bf16[384,1536]{1,0:T(8,128)(2,1)} collective-permute-done((bf16[384,1536]{1,0:T(8,128)(2,1)}, bf16[384,1536]{1,0:T(8,128)(2,1)}, u32[]{:S(2)}, u32[]{:S(2)}) %collective-permute-start.2) | collective-permute-done | bytes 1179680 | tf_op jit(solution)/shard_map/ppermute | solution.py:221
  86.7 1.3 all-to-all-done.2.rows_ref
  88.0 2.8 %shard_map.59 = bf16[8,16,1536]{2,1,0:T(8,128)(2,1)S(1)} custom-call(bf16[8,16,1536]{2,1,0:T(8,128)(2,1)S(1)} %all-to-all-done.2.rows_ref, bf16[1536,384]{1,0:T(8,128)(2,1)} %bitcast.4.in_hbm, bf16[384,1536]{1,0:T(8,128)(2,1)S(1)} %bitcast.15, bf16[1536,384]{1,0:T(8,128)(2,1)S(1)} %collective-permute-done.1.before_hbm.in_b_hbm, ...), custom_call_target="tpu_custom_call" | custom-call | flops 603979776 | bytes 4718592 | tf_op jit(solution)/shard_map/pallas_call | solution.py:20
  90.8 16.7 %all_to_all.25.blocks_ref = bf16[8,16,1536]{2,1,0:T(8,128)(2,1)S(1)} all-to-all(bf16[8,16,1536]{2,1,0:T(8,128)(2,1)S(1)} %shard_map.59), channel_id=1, replica_groups=mesh['xlo'=2,'y'=8,'xhi'=2,'z'=8,'core'=2] {'y'}, dimensions={0} | all-to-all | bytes 786432 | tf_op jit(solution)/shard_map/all_to_all | solution.py:300
  107.5 1.1 shard_map.60
  108.5 13.9 %all-to-all-start.4 = ((bf16[16,16,1536]{2,1,0:T(8,128)(2,1)}), bf16[16,16,1536]{2,1,0:T(8,128)(2,1)S(1)}, u32[]{:S(2)}, u32[]{:S(2)}) async-start(bf16[16,16,1536]{2,1,0:T(8,128)(2,1)} %shard_map.60), calls=%async_computation.4 | async-start | bytes 1572864 | tf_op jit(solution)/shard_map/all_to_all | solution.py:312
  122.5 2.3 %shard_map.56 = (bf16[384,384]{1,0:T(8,128)(2,1)}, bf16[384,384]{1,0:T(8,128)(2,1)}) custom-call(f32[384,256]{1,0:T(8,128)} %get-tuple-element.10.own_logits_ref, f32[384,256]{1,0:T(8,128)} %get-tuple-element.11.partner_logits_ref), custom_call_target="tpu_custom_call" | custom-call | flops 1572864 | bytes 1179648 | tf_op jit(solution)/shard_map/pallas_call | solution.py:20
  124.8 4.3 %collective-permute-start.3 = (bf16[384,384]{1,0:T(8,128)(2,1)}, bf16[384,384]{1,0:T(8,128)(2,1)S(1)}, u32[]{:S(2)}, u32[]{:S(2)}) collective-permute-start(bf16[384,384]{1,0:T(8,128)(2,1)} %get-tuple-element.14), channel_id=1, source_target_pairs={{0,1},{1,0},{2,3},{3,2},{4,5},{5,4},{6,7},{7,6},{8,9},{9,8},{10,11... | collective-permute-start | bytes 884744 | tf_op jit(solution)/shard_map/ppermute | solution.py:265
  129.1 0.0 copy-start.7
  129.1 1.1 slice_convert_fusion.3
  130.2 11.2 %all-to-all-done.4 = bf16[16,16,1536]{2,1,0:T(8,128)(2,1)S(1)} async-done(((bf16[16,16,1536]{2,1,0:T(8,128)(2,1)}), bf16[16,16,1536]{2,1,0:T(8,128)(2,1)S(1)}, u32[]{:S(2)}, u32[]{:S(2)}) %all-to-all-start.4) | async-done | bytes 786464 | tf_op jit(solution)/shard_map/all_to_all | solution.py:312
  141.4 6.5 %collective-permute-start.4 = (bf16[256,1536]{1,0:T(8,128)(2,1)S(1)}, bf16[256,1536]{1,0:T(8,128)(2,1)S(1)}, u32[]{:S(2)}, u32[]{:S(2)}) collective-permute-start(bf16[256,1536]{1,0:T(8,128)(2,1)S(1)} %bitcast.16), channel_id=1, source_target_pairs={{0,1},{1,0},{2,3},{3,2},{4,5},{5,4},{6,7},{7,6},{8,9},{9,8},{10,11... | collective-permute-start | bytes 2359304 | tf_op jit(solution)/shard_map/ppermute | solution.py:313
  147.9 0.0 collective-permute-done.3
  147.9 0.1 slice_convert_fusion.1
  148.0 0.5 fusion.18
  148.5 0.0 copy-start.5
  148.5 0.2 divide_reduce_fusion
  148.7 0.0 copy-done.7
  148.7 0.5 convolution_multiply_fusion.1
  149.2 0.6 collective-permute-done.4
  149.8 0.0 copy-done.5
  149.8 1.6 %fusion.3 = bf16[1,384,1536]{2,1,0:T(8,128)(2,1)} fusion(f32[384,1536]{1,0:T(8,128)S(1)} %convolution_multiply_fusion.1, bf16[256,1536]{1,0:T(8,128)(2,1)S(1)} %collective-permute-done.4, f32[384]{0:T(512)S(1)} %get-tuple-element.15, bf16[384,384]{1,0:T(8,128)(2,1)S(1)} %collective-permute-done.3, bf16[1,384,1536]{2,1,0:T(8,128)(2,1)S(1)} %copy-done.5), kind=kOutput, calls=%fused_computation.5 | convolution fusion | flops 304939008 | bytes 5703680 | tf_op jit(solution)/shard_map/dot_general | solution.py:323
  (4 shorter events, 0.0 us)
Async XLA Ops:
  0.0 0.9 copy-start
  0.0 10.8 %copy-start.4 = (bf16[1,384,1536]{2,1,0:T(8,128)(2,1)S(1)}, bf16[1,384,1536]{2,1,0:T(8,128)(2,1)}, u32[]{:S(2)}) copy-start(bf16[1,384,1536]{2,1,0:T(8,128)(2,1)} %param.5) | copy-start | bytes 3538948
  2.1 26.9 %all-to-all-start = ((bf16[16,96,256]{2,1,0:T(8,128)(2,1)}), bf16[16,96,256]{2,1,0:T(8,128)(2,1)S(1)}, u32[]{:S(2)}, u32[]{:S(2)}) async-start(bf16[16,96,256]{2,1,0:T(8,128)(2,1)} %broadcast_in_dim.4), calls=%async_computation | async-start | bytes 1572864 | tf_op jit(solution)/shard_map/all_to_all | solution.py:192
  10.8 7.2 %collective-permute-start = (bf16[384,1536]{1,0:T(8,128)(2,1)S(1)}, bf16[384,1536]{1,0:T(8,128)(2,1)}, u32[]{:S(2)}, u32[]{:S(2)}) collective-permute-start(bf16[384,1536]{1,0:T(8,128)(2,1)S(1)} %bitcast.19), channel_id=1, source_target_pairs={{0,1},{1,0},{2,3},{3,2},{4,5},{5,4},{6,7},{7,6},{8,9},{9,8},{10,11... | collective-permute-start | bytes 3538952 | tf_op jit(solution)/shard_map/ppermute | solution.py:222
  14.5 35.4 %collective-permute-start.1 = (bf16[1536,384]{1,0:T(8,128)(2,1)}, bf16[1536,384]{1,0:T(8,128)(2,1)S(1)}, u32[]{:S(2)}, u32[]{:S(2)}) collective-permute-start(bf16[1536,384]{1,0:T(8,128)(2,1)} %bitcast.4.in_hbm), channel_id=1, source_target_pairs={{0,256},{256,0},{1,257},{257,1},{2,258},{258,2},{3,259},{259,3},{4... | collective-permute-start | bytes 3538952 | tf_op jit(solution)/shard_map/ppermute | solution.py:209
  29.0 0.9 copy-start.6
  29.8 20.1 %copy-start.1 = (bf16[1,384,1536]{2,1,0:T(8,128)(2,1)S(1)}, bf16[1,384,1536]{2,1,0:T(8,128)(2,1)}, u32[]{:S(2)}) copy-start(bf16[1,384,1536]{2,1,0:T(8,128)(2,1)} %param.9) | copy-start | bytes 3538948
  35.1 34.1 %copy-start.3 = (f32[1,1536]{1,0:T(1,128)S(1)}, f32[1,1536]{1,0:T(1,128)}, u32[]{:S(2)}) copy-start(f32[1,1536]{1,0:T(1,128)} %gain_ref.1) | copy-start | bytes 18436
  35.1 34.1 %all-to-all-start.1 = ((bf16[16,16,1664]{2,1,0:T(8,128)(2,1)}), bf16[16,16,1664]{2,1,0:T(8,128)(2,1)S(1)}, u32[]{:S(2)}, u32[]{:S(2)}) async-start(bf16[16,16,1664]{2,1,0:T(8,128)(2,1)} %bitcast.20), calls=%async_computation.1 | async-start | bytes 1703936 | tf_op jit(solution)/shard_map/all_to_all | solution.py:252
  51.2 35.5 %collective-permute-start.2 = (bf16[384,1536]{1,0:T(8,128)(2,1)}, bf16[384,1536]{1,0:T(8,128)(2,1)}, u32[]{:S(2)}, u32[]{:S(2)}) collective-permute-start(bf16[384,1536]{1,0:T(8,128)(2,1)} %shard_map.58), channel_id=1, source_target_pairs={{0,256},{256,0},{1,257},{257,1},{2,258},{258,2},{3,259},{259,3},{4... | collective-permute-start | bytes 3538952 | tf_op jit(solution)/shard_map/ppermute | solution.py:221
  70.2 0.7 copy-start.2
  70.9 17.1 %all-to-all-start.2 = ((bf16[8,16,1536]{2,1,0:T(8,128)(2,1)}), bf16[8,16,1536]{2,1,0:T(8,128)(2,1)S(1)}, u32[]{:S(2)}, u32[]{:S(2)}) async-start(bf16[8,16,1536]{2,1,0:T(8,128)(2,1)} %copy-done.2), calls=%async_computation.2 | async-start | bytes 786432 | tf_op jit(solution)/shard_map/all_to_all | solution.py:279
  108.5 32.9 %all-to-all-start.4 = ((bf16[16,16,1536]{2,1,0:T(8,128)(2,1)}), bf16[16,16,1536]{2,1,0:T(8,128)(2,1)S(1)}, u32[]{:S(2)}, u32[]{:S(2)}) async-start(bf16[16,16,1536]{2,1,0:T(8,128)(2,1)} %shard_map.60), calls=%async_computation.4 | async-start | bytes 1572864 | tf_op jit(solution)/shard_map/all_to_all | solution.py:312
  124.8 23.1 %collective-permute-start.3 = (bf16[384,384]{1,0:T(8,128)(2,1)}, bf16[384,384]{1,0:T(8,128)(2,1)S(1)}, u32[]{:S(2)}, u32[]{:S(2)}) collective-permute-start(bf16[384,384]{1,0:T(8,128)(2,1)} %get-tuple-element.14), channel_id=1, source_target_pairs={{0,1},{1,0},{2,3},{3,2},{4,5},{5,4},{6,7},{7,6},{8,9},{9,8},{10,11... | collective-permute-start | bytes 884744 | tf_op jit(solution)/shard_map/ppermute | solution.py:265
  129.1 19.6 %copy-start.7 = (bf16[384,384]{1,0:T(8,128)(2,1)S(1)}, bf16[384,384]{1,0:T(8,128)(2,1)}, u32[]{:S(2)}) copy-start(bf16[384,384]{1,0:T(8,128)(2,1)} %get-tuple-element.12) | copy-start | bytes 884740
  141.4 8.4 %collective-permute-start.4 = (bf16[256,1536]{1,0:T(8,128)(2,1)S(1)}, bf16[256,1536]{1,0:T(8,128)(2,1)S(1)}, u32[]{:S(2)}, u32[]{:S(2)}) collective-permute-start(bf16[256,1536]{1,0:T(8,128)(2,1)S(1)} %bitcast.16), channel_id=1, source_target_pairs={{0,1},{1,0},{2,3},{3,2},{4,5},{5,4},{6,7},{7,6},{8,9},{9,8},{10,11... | collective-permute-start | bytes 2359304 | tf_op jit(solution)/shard_map/ppermute | solution.py:313
  148.5 1.3 copy-start.5

commit v5 on v4

v5 whole, which is shorter than its diff:
```python
import jax
import jax.numpy as jnp
from jax import lax
from jax.experimental import pallas as pl
from jax.experimental.pallas import tpu as pltpu
from jax.sharding import Mesh, PartitionSpec as P

F32 = jnp.float32
BF16 = jnp.bfloat16
EXTRA = 128
Z = ("zh", "zl")
VMEM = pl.BlockSpec(memory_space=pltpu.VMEM)
HBM = pl.BlockSpec(memory_space=pltpu.HBM)


def other(length=2):
    return [(k, k ^ 1) for k in range(length)]


def kernel_call(body, outs, flops, moved, specs, *args, out_specs=None, scratch=(), room=60):
    return pl.pallas_call(
        body,
        out_shape=outs,
        in_specs=specs,
        out_specs=jax.tree.map(lambda _: VMEM, outs) if out_specs is None else out_specs,
        scratch_shapes=scratch,
        compiler_params=pltpu.CompilerParams(vmem_limit_bytes=int(room * 2**20)),
        cost_estimate=pl.CostEstimate(flops=flops, bytes_accessed=moved, transcendentals=0),
    )(*args)


def started(source, target, semaphores, k):
    copy = pltpu.make_async_copy(source, target, semaphores.at[k])
    copy.start()
    return copy


def started_rows(source, target, semaphores, first, count):
    rows = source.shape[0] // count
    parts = [pl.ds(k * rows, rows) for k in range(count)]
    return [started(source.at[p], target.at[p], semaphores, first + k) for k, p in enumerate(parts)]


def split_off(value):
    wide = value * 65537.0
    return wide - (wide - value)


def in_lanes(columns):
    lane = lax.broadcasted_iota(jnp.int32, columns[0].shape, 1)
    packed = jnp.zeros(columns[0].shape, F32)
    for k, column in enumerate(columns):
        first = split_off(column)
        second = split_off(column - first)
        for j, piece in enumerate((first, second, column - first - second)):
            packed = jnp.where(lane == 3 * k + j, piece, packed)
    return packed.astype(BF16)


def dispatch_kernel(*refs):
    sources, refs = refs[:7], refs[7:]
    message_hbm, logits_hbm, columns_ref, *feats = refs[:9]
    logits_ref, message_ref, semaphores = refs[9:]
    width, slots = columns_ref.shape
    targets = [columns_ref, *feats]
    loads = [started(source, target, semaphores, k) for k, (source, target) in enumerate(zip(sources, targets))]
    loads[0].wait()
    columns = columns_ref[...]
    offset, high, rows = 0, None, []
    for load, feats_ref in zip(loads[1:], feats):
        load.wait()
        part = slice(offset, offset + feats_ref.shape[0])
        logits = jnp.dot(feats_ref[...], columns, preferred_element_type=F32)
        logits_ref[part, :] = logits
        top = jnp.max(logits, axis=0, keepdims=True)
        high = top if high is None else jnp.maximum(high, top)
        offset += feats_ref.shape[0]
        rows.append(part)
    stores = [started(logits_ref, logits_hbm, semaphores, 7)]
    message_ref[:, width:] = in_lanes([jnp.broadcast_to(high, (EXTRA, slots)).T])
    last = pl.ds(width, EXTRA)
    stores.append(started(message_ref.at[:, last], message_hbm.at[:, last], semaphores, 8))
    dispatch = [jnp.exp(logits_ref[part, :] - high).astype(BF16).T for part in rows]
    step = 512
    for k in range(width // step):
        part = pl.ds(k * step, step)
        sums = jnp.dot(dispatch[0], feats[0][:, part], preferred_element_type=F32)
        for one, feats_ref in zip(dispatch[1:], feats[1:]):
            sums += jnp.dot(one, feats_ref[:, part], preferred_element_type=F32)
        message_ref[:, part] = sums.astype(BF16)
        stores.append(started(message_ref.at[:, part], message_hbm.at[:, part], semaphores, 9 + k))
    for copy in stores:
        copy.wait()


def exps_kernel(logits_ref, own_ref, answer_ref):
    rows, slots = own_ref.shape[0], logits_ref.shape[1]
    for k, out_ref in enumerate((own_ref, answer_ref)):
        logits = logits_ref[k * rows : (k + 1) * rows, :]
        high = jnp.max(logits, axis=1, keepdims=True)
        exps = jnp.exp(logits - high)
        total = jnp.sum(exps, axis=1, keepdims=True)
        out_ref[:, :slots] = exps.astype(BF16)
        lanes = (rows, EXTRA)
        out_ref[:, slots:] = in_lanes([jnp.broadcast_to(high, lanes), jnp.broadcast_to(total, lanes)])


def weights_kernel(side_ref, own_ref, core_ref, low_ref, up_ref, own_weights_ref, core_weights_ref):
    rows, wide = low_ref.shape[0] * 2, own_ref.shape[1]
    slots = wide - EXTRA
    half = rows // 2
    side = side_ref[0]
    for k, given_ref in enumerate((low_ref, up_ref)):
        part = slice(k * half, (k + 1) * half)
        blocks = [own_ref[part, :], core_ref[part, :], given_ref[:, :wide], given_ref[:, wide:]]
        lane = lax.broadcasted_iota(jnp.int32, (half, EXTRA), 1)
        stats = [block[:, slots:].astype(F32) for block in blocks]
        highs = [jnp.sum(jnp.where(lane < 3, s, 0.0), axis=1, keepdims=True) for s in stats]
        sums = [jnp.sum(jnp.where(lane < 3, 0.0, s), axis=1, keepdims=True) for s in stats]
        top = jnp.maximum(jnp.maximum(highs[0], highs[1]), jnp.maximum(highs[2], highs[3]))
        factors = [jnp.exp(high - top) for high in highs]
        total = sums[0] * factors[0] + sums[1] * factors[1] + sums[2] * factors[2] + sums[3] * factors[3]
        scaled = [
            (block[:, :slots].astype(F32) * (factor / total)).astype(BF16)
            for block, factor in zip(blocks, factors)
        ]
        here = pl.ds(pl.multiple_of(side * slots, slots), slots)
        there = pl.ds(pl.multiple_of((1 - side) * slots, slots), slots)
        own_weights_ref[part, here] = scaled[0]
        core_weights_ref[part, here] = scaled[1]
        own_weights_ref[part, there] = scaled[2]
        core_weights_ref[part, there] = scaled[3]


def pool_kernel(received_ref, gain_ref, copies_hbm, slots_ref, semaphores):
    width = gain_ref.shape[1]
    highs = jnp.sum(received_ref[:, :, width:].astype(F32), axis=-1, keepdims=True)
    overall = jnp.max(highs, axis=0, keepdims=True)
    scale = jnp.exp(highs - overall)
    pooled = received_ref[0, :, :width].astype(F32) * scale[0]
    for k in range(1, received_ref.shape[0]):
        pooled += received_ref[k, :, :width].astype(F32) * scale[k]
    mean_sq = jnp.mean(pooled * pooled, axis=-1, keepdims=True)
    slots_ref[...] = (pooled * lax.rsqrt(mean_sq + 1e-06) * gain_ref[...]).astype(BF16)
    copies = [started(slots_ref, copies_hbm.at[k], semaphores, k) for k in range(copies_hbm.shape[0])]
    for copy in copies:
        copy.wait()


def follow_kernel(weights_hbm, before_hbm, weights_ref, semaphores):
    for copy in started_rows(weights_hbm, weights_ref, semaphores, 0, semaphores.shape[0]):
        copy.wait()


def expert_kernel(
    rows_ref,
    in_hbm,
    out_hbm,
    in_b_hbm,
    out_b_hbm,
    before_hbm,
    partial_ref,
    in_ref,
    out_ref,
    in_b_ref,
    out_b_ref,
    semaphores,
):
    rows = rows_ref[...].reshape(-1, rows_ref.shape[-1])
    width = rows.shape[1]
    cuts = 4
    pairs = ((in_hbm, in_ref), (in_b_hbm, in_b_ref), (out_hbm, out_ref), (out_b_hbm, out_b_ref))
    loads = [started_rows(*pair, semaphores, cuts * k, cuts) for k, pair in enumerate(pairs)]
    for copy in loads[0]:
        copy.wait()
    hidden = jax.nn.gelu(jnp.dot(rows, in_ref[...], preferred_element_type=F32)).astype(BF16)
    for copy in loads[1]:
        copy.wait()
    hidden_b = jax.nn.gelu(jnp.dot(rows, in_b_ref[...], preferred_element_type=F32)).astype(BF16)
    for copy in loads[2] + loads[3]:
        copy.wait()
    step = 512
    for k in range(width // step):
        part = pl.ds(k * step, step)
        sums = jnp.dot(hidden, out_ref[:, part], preferred_element_type=F32)
        sums += jnp.dot(hidden_b, out_b_ref[:, part], preferred_element_type=F32)
        partial_ref[:, :, part] = sums.astype(BF16).reshape(*rows_ref.shape[:2], step)


def sum_kernel(blocks_ref, before_hbm, copies_hbm, total_ref, semaphores):
    total = blocks_ref[0].astype(F32)
    for k in range(1, blocks_ref.shape[0]):
        total += blocks_ref[k].astype(F32)
    total_ref[...] = total.astype(BF16)
    copies = [started(total_ref, copies_hbm.at[k], semaphores, k) for k in range(copies_hbm.shape[0])]
    for copy in copies:
        copy.wait()


def sent_to_all(value, axes):
    length = lax.axis_size(axes)
    return lax.all_to_all(
        jnp.broadcast_to(value[None], (length, *value.shape)), axes, 0, 0, tiled=True
    )


def local(tokens, router, norm_gain, w_in, w_out):
    feats = tokens[0]
    count, width = feats.shape
    slot_count = router.shape[1]
    depth = lax.axis_size(Z)
    owners = lax.axis_size(("xhi", "zh"))
    groups = lax.axis_size("y")
    per_owner = slot_count // (4 * owners)
    quarter = slot_count // 4
    core, side = lax.axis_index("core"), lax.axis_index("zl")
    hidden_units = w_in.shape[2]
    shape = jax.ShapeDtypeStruct
    up = [(k, (k + 1) % depth) for k in range(depth)]
    down = [(k, (k - 1) % depth) for k in range(depth)]

    middle = count // 2
    above = lax.ppermute(feats[:middle], Z, down)
    below = lax.ppermute(feats[middle:], Z, up)
    mine = [feats, above, below]
    theirs = [lax.ppermute(block, "core", other()) for block in mine]

    row = lax.broadcasted_iota(jnp.int32, (slot_count, quarter), 0)
    col = lax.broadcasted_iota(jnp.int32, (slot_count, quarter), 1)
    wanted = (col // per_owner * 4 + side * 2 + core) * per_owner + col % per_owner
    pick = (row == wanted).astype(BF16)
    own_columns = jnp.dot(router, pick, preferred_element_type=F32).astype(BF16)
    columns = sent_to_all(own_columns, ("xlo", "y")).reshape(width, quarter)

    in_later = kernel_call(
        follow_kernel,
        shape((width, hidden_units), BF16),
        0,
        4 * width * hidden_units,
        [HBM] * 2,
        w_in[0],
        columns,
        scratch=[pltpu.SemaphoreType.DMA((4,))],
        room=16,
    )
    partner_in = lax.ppermute(in_later, "xlo", other())
    out_later = kernel_call(
        follow_kernel,
        shape((hidden_units, width), BF16),
        0,
        4 * width * hidden_units,
        [HBM] * 2,
        w_out[0],
        partner_in,
        scratch=[pltpu.SemaphoreType.DMA((4,))],
        room=16,
    )
    partner_out = lax.ppermute(out_later, "xlo", other())

    message, logits = kernel_call(
        dispatch_kernel,
        (shape((quarter, width + EXTRA), BF16), shape((4 * count, quarter), F32)),
        16 * count * width * quarter,
        2 * (4 * count * width + 2 * width * quarter),
        [HBM] * 7,
        columns,
        *mine,
        *theirs,
        out_specs=(HBM, HBM),
        scratch=[
            pltpu.VMEM((width, quarter), BF16),
            *[pltpu.VMEM(block.shape, BF16) for block in mine + theirs],
            pltpu.VMEM((4 * count, quarter), F32),
            pltpu.VMEM((quarter, width + EXTRA), BF16),
            pltpu.SemaphoreType.DMA((12,)),
        ],
        room=58,
    )
    received = lax.all_to_all(
        message.reshape(owners, per_owner, width + EXTRA), ("xhi", "zh"), 0, 0, tiled=True
    )

    exps, answer = kernel_call(
        exps_kernel,
        (shape((2 * count, quarter + EXTRA), BF16), shape((2 * count, quarter + EXTRA), BF16)),
        64 * count * quarter,
        32 * count * quarter,
        [VMEM],
        logits,
        room=12,
    )
    exps_b = lax.ppermute(answer, "core", other())
    first, second = slice(count, count + middle), slice(count + middle, 2 * count)
    low = lax.ppermute(jnp.concatenate([exps[first], exps_b[first]], axis=1), Z, up)
    high = lax.ppermute(jnp.concatenate([exps[second], exps_b[second]], axis=1), Z, down)
    weights, weights_b = kernel_call(
        weights_kernel,
        (shape((count, 2 * quarter), BF16), shape((count, 2 * quarter), BF16)),
        32 * count * quarter,
        16 * count * quarter,
        [pl.BlockSpec(memory_space=pltpu.SMEM), VMEM, VMEM, VMEM, VMEM],
        jnp.full((1,), side, jnp.int32),
        exps[:count],
        exps_b[:count],
        low,
        high,
        room=12,
    )

    slots = kernel_call(
        pool_kernel,
        shape((groups, per_owner, width), BF16),
        4 * quarter * width,
        2 * quarter * width,
        [VMEM] * 2,
        received,
        norm_gain,
        out_specs=HBM,
        scratch=[pltpu.VMEM((per_owner, width), BF16), pltpu.SemaphoreType.DMA((groups,))],
        room=16,
    )
    rows = lax.all_to_all(slots, "y", 0, 0, tiled=True)
    partial = kernel_call(
        expert_kernel,
        shape((groups, per_owner, width), BF16),
        8 * groups * per_owner * width * hidden_units,
        8 * width * hidden_units,
        [VMEM, HBM, HBM, HBM, HBM, HBM],
        rows,
        w_in[0],
        w_out[0],
        partner_in,
        partner_out,
        exps_b,
        scratch=[
            pltpu.VMEM((width, hidden_units), BF16),
            pltpu.VMEM((hidden_units, width), BF16),
            pltpu.VMEM((width, hidden_units), BF16),
            pltpu.VMEM((hidden_units, width), BF16),
            pltpu.SemaphoreType.DMA((16,)),
        ],
        room=48,
    )
    blocks = lax.all_to_all(partial, "y", 0, 0, tiled=True)
    copies = kernel_call(
        sum_kernel,
        shape((2 * owners, per_owner, width), BF16),
        groups * per_owner * width,
        4 * quarter * width,
        [VMEM, HBM],
        blocks,
        weights,
        out_specs=HBM,
        scratch=[pltpu.VMEM((per_owner, width), BF16), pltpu.SemaphoreType.DMA((2 * owners,))],
        room=16,
    )
    outs = lax.all_to_all(copies, ("zl", "xhi", "zh"), 0, 0, tiled=True).reshape(2 * quarter, width)
    outs_b = lax.ppermute(outs, "core", other())

    mixed = jnp.dot(weights, outs, preferred_element_type=F32)
    mixed += jnp.dot(weights_b, outs_b, preferred_element_type=F32)
    return (feats.astype(F32) + mixed).astype(BF16)[None]


def solution(mesh):
    names = ("xlo", "y", "xhi", "zh", "zl", "core")
    fine = Mesh(mesh.devices.reshape(2, 8, 2, 4, 2, 2), names)
    grp, seq = names[:2], names[2:]
    in_specs = (P(grp, seq, None), P(grp, None), P(seq, None), P(seq, None, grp), P(seq, grp, None))
    return jax.shard_map(
        local, mesh=fine, in_specs=in_specs, out_specs=P(grp, seq, None), check_vma=False
    )
```

time: 152 us -> 157 us (1.033); the launches traced: 151 us -> 154 us
  waiting for transfers between devices: 49.3 us -> 28.4 us
  starting transfers between devices: 63.9 us -> 73.1 us
  blocking collectives: 16.7 us -> 25 us
  local copies, waits for them, and re-layouts: 3.45 us -> 9.28 us
  Pallas kernels: 13.6 us -> 16.1 us
  other arithmetic: 1.91 us -> 0.05 us
    ppermute x3 -> x9, starting transfers between devices: 11.5 us -> 37.3 us  [the longest x3 11 us: local(): theirs = [lax.ppermute(block, 'core', other()) for block in mine]]
    ppermute x3 -> x9, waiting for transfers between devices: 0.89 us -> 14.4 us  [the longest x1 4.66 us: local(): lax.ppermute(jnp.concatenate([exps[first], exps_b[first]], axis=1), Z, up)]
    all_to_all x1, waiting for transfers between devices: 11.2 us -> 0.01 us  [local(): blocks = lax.all_to_all(partial, 'y', 0, 0, tiled=True)]
    all_to_all x1, waiting for transfers between devices: 10.9 us -> 0.01 us  [sent_to_all(): lax.all_to_all(jnp.broadcast_to(value[None], (length, *value.shape)), axe...]
    all_to_all x1, starting transfers between devices: 13.9 us -> 3.73 us  [local(): lax.all_to_all(message.reshape(owners, per_owner, width + EXTRA), ('xhi',...]
    all_to_all x1, waiting for transfers between devices: 15.1 us -> 5.81 us  [local(): lax.all_to_all(message.reshape(owners, per_owner, width + EXTRA), ('xhi',...]
    all_to_all x1, blocking collectives: 16.7 us -> 25 us  [local(): lax.all_to_all(copies, ('zl', 'xhi', 'zh'), 0, 0, tiled=True)]
    all_to_all x1, starting transfers between devices: 13.9 us -> 6.27 us  [local(): blocks = lax.all_to_all(partial, 'y', 0, 0, tiled=True)]
  transfers between devices with their start and end apart: 9 -> 15, of which waited for: 7 -> 11; matrix products, arithmetic and copies ran while one was open for 2% -> 1% of each run, Pallas kernels for 6% -> 7%
where the time goes in v5:
time: 157 us; the launch traced here: 154 us
  starting transfers between devices  73.1 us (47%)
  waiting for transfers between devices  28.4 us (18%)
  blocking collectives  25 us (16%)
  Pallas kernels  16.1 us (10%)
  local copies, waits for them, and re-layouts  9.28 us (6%)
  matrix products  2.17 us (1%)
    all_to_all x1, blocking collectives, local(): lax.all_to_all(copies, ('zl', 'xhi', 'zh'), 0, 0, tiled=True)  25 us
    pallas_call x8, Pallas kernels, kernel_call(): pl.pallas_call(body, out_shape=outs, in_specs=specs, out_specs=jax.tree.m...  16.1 us
    ppermute x3, starting transfers between devices, local(): theirs = [lax.ppermute(block, 'core', other()) for block in mine]  11 us
    ppermute x1, starting transfers between devices, local(): above = lax.ppermute(feats[:middle], Z, down)  10.7 us
    all_to_all x1, starting transfers between devices, sent_to_all(): lax.all_to_all(jnp.broadcast_to(value[None], (length, *value.shape)), axe...  8.68 us
    ppermute x1, starting transfers between devices, local(): outs_b = lax.ppermute(outs, 'core', other())  7.13 us
    all_to_all x1, starting transfers between devices, local(): rows = lax.all_to_all(slots, 'y', 0, 0, tiled=True)  6.7 us
    unnamed x30, local copies, waits for them, and re-layouts  6.39 us
  transfers between devices with their start and end apart: 15, of which 11 were waited for; matrix products, arithmetic and copies ran while one was open for 1% of the time, Pallas kernels for 7%

profile of v5, /device:TPU:1, one launch (start us, length us, event | category | flops | bytes accessed | tf_op | source)
XLA Modules:
  0.0 154.4 jit_solution(2014837059547016604)
XLA Ops:
  0.0 0.9 copy-done
  0.9 0.2 fusion.3
  1.1 0.8 broadcast_in_dim.13
  1.9 8.7 %all-to-all-start = ((bf16[16,96,128]{2,1,0:T(8,128)(2,1)}), bf16[16,96,128]{2,1,0:T(8,128)(2,1)S(1)}, u32[]{:S(2)}, u32[]{:S(2)}) async-start(bf16[16,96,128]{2,1,0:T(8,128)(2,1)} %broadcast_in_dim.13), calls=%async_computation | async-start | bytes 786432 | tf_op jit(solution)/shard_map/all_to_all | solution.py:202
  10.6 1.1 slice_bitcast_fusion
  11.7 10.7 %collective-permute-start = (bf16[192,1536]{1,0:T(8,128)(2,1)}, bf16[192,1536]{1,0:T(8,128)(2,1)S(1)}, u32[]{:S(2)}, u32[]{:S(2)}) collective-permute-start(bf16[192,1536]{1,0:T(8,128)(2,1)} %get-tuple-element.18), channel_id=1, source_target_pairs={{0,14},{2,0},{4,2},{6,4},{8,6},{10,8},{12,10},{14,12},{1,15},{3,1}... | collective-permute-start | bytes 1769480 | tf_op jit(solution)/shard_map/ppermute | solution.py:223
  22.4 1.9 %collective-permute-start.1 = (bf16[192,1536]{1,0:T(8,128)(2,1)}, bf16[192,1536]{1,0:T(8,128)(2,1)}, u32[]{:S(2)}, u32[]{:S(2)}) collective-permute-start(bf16[192,1536]{1,0:T(8,128)(2,1)} %get-tuple-element.17), channel_id=1, source_target_pairs={{0,2},{2,4},{4,6},{6,8},{8,10},{10,12},{12,14},{14,0},{1,3},{3,5},... | collective-permute-start | bytes 1769480 | tf_op jit(solution)/shard_map/ppermute | solution.py:224
  24.3 3.1 %collective-permute-start.2 = (bf16[384,1536]{1,0:T(8,128)(2,1)S(1)}, bf16[384,1536]{1,0:T(8,128)(2,1)}, u32[]{:S(2)}, u32[]{:S(2)}) collective-permute-start(bf16[384,1536]{1,0:T(8,128)(2,1)S(1)} %bitcast.28), channel_id=1, source_target_pairs={{0,1},{1,0},{2,3},{3,2},{4,5},{5,4},{6,7},{7,6},{8,9},{9,8},{10,11... | collective-permute-start | bytes 3538952 | tf_op jit(solution)/shard_map/ppermute | solution.py:226
  27.5 1.3 shard_map.59
  28.8 3.6 %collective-permute-start.8 = (bf16[1536,384]{1,0:T(8,128)(2,1)}, bf16[1536,384]{1,0:T(8,128)(2,1)S(1)}, u32[]{:S(2)}, u32[]{:S(2)}) collective-permute-start(bf16[1536,384]{1,0:T(8,128)(2,1)} %shard_map.59), channel_id=1, source_target_pairs={{0,256},{256,0},{1,257},{257,1},{2,258},{258,2},{3,259},{259,3},{4... | collective-permute-start | bytes 3538952 | tf_op jit(solution)/shard_map/ppermute | solution.py:246
  32.4 2.0 %collective-permute-done.refs_2_ = bf16[192,1536]{1,0:T(8,128)(2,1)S(1)} collective-permute-done((bf16[192,1536]{1,0:T(8,128)(2,1)}, bf16[192,1536]{1,0:T(8,128)(2,1)S(1)}, u32[]{:S(2)}, u32[]{:S(2)}) %collective-permute-start) | collective-permute-done | bytes 589856 | tf_op jit(solution)/shard_map/ppermute | solution.py:223
  34.3 3.8 %collective-permute-start.3 = (bf16[192,1536]{1,0:T(8,128)(2,1)S(1)}, bf16[192,1536]{1,0:T(8,128)(2,1)S(1)}, u32[]{:S(2)}, u32[]{:S(2)}) collective-permute-start(bf16[192,1536]{1,0:T(8,128)(2,1)S(1)} %collective-permute-done.refs_2_), channel_id=1, source_target_pairs={{0,1},{1,0},{2,3},{3,2},{4,5},{5,4},{6,7},{7,6},{8,9},{9,8},{10,11... | collective-permute-start | bytes 1769480 | tf_op jit(solution)/shard_map/ppermute | solution.py:226
  38.1 1.3 collective-permute-done.1.refs_3_
  39.4 4.1 %collective-permute-start.4 = (bf16[192,1536]{1,0:T(8,128)(2,1)}, bf16[192,1536]{1,0:T(8,128)(2,1)S(1)}, u32[]{:S(2)}, u32[]{:S(2)}) collective-permute-start(bf16[192,1536]{1,0:T(8,128)(2,1)} %collective-permute-done.1.refs_3_), channel_id=1, source_target_pairs={{0,1},{1,0},{2,3},{3,2},{4,5},{5,4},{6,7},{7,6},{8,9},{9,8},{10,11... | collective-permute-start | bytes 1769480 | tf_op jit(solution)/shard_map/ppermute | solution.py:226
  43.5 1.8 %collective-permute-done.4.refs_6_ = bf16[192,1536]{1,0:T(8,128)(2,1)S(1)} collective-permute-done((bf16[192,1536]{1,0:T(8,128)(2,1)}, bf16[192,1536]{1,0:T(8,128)(2,1)S(1)}, u32[]{:S(2)}, u32[]{:S(2)}) %collective-permute-start.4) | collective-permute-done | bytes 589856 | tf_op jit(solution)/shard_map/ppermute | solution.py:226
  45.3 0.8 copy-done.14
  46.1 6.6 %shard_map.55 = (bf16[128,1664]{1,0:T(8,128)(2,1)}, f32[1536,128]{1,0:T(8,128)}) custom-call(bf16[1536,128]{1,0:T(8,128)(2,1)} %bitcast.26, bf16[384,1536]{1,0:T(8,128)(2,1)} %bitcast.27, bf16[192,1536]{1,0:T(8,128)(2,1)} %copy-done.12, bf16[192,1536]{1,0:T(8,128)(2,1)} %collective-permute-done.1.refs_3_, bf16[384,1536]{1,0:T(8,128)(2,1)} %collective-permute-done.2.refs_4_, ...), custom_call_target="tpu_custom_call" | custom-call | flops 1207959552 | bytes 5505024 | tf_op jit(solution)/shard_map/pallas_call | solution.py:21
  52.7 3.7 %all-to-all-start.1 = ((bf16[8,16,1664]{2,1,0:T(8,128)(2,1)}), bf16[8,16,1664]{2,1,0:T(8,128)(2,1)S(1)}, u32[]{:S(2)}, u32[]{:S(2)}) async-start(bf16[8,16,1664]{2,1,0:T(8,128)(2,1)} %bitcast.31), calls=%async_computation.1 | async-start | bytes 851968 | tf_op jit(solution)/shard_map/all_to_all | solution.py:279
  56.4 2.4 %collective-permute-done.8.before_hbm.in_b_hbm = bf16[1536,384]{1,0:T(8,128)(2,1)S(1)} collective-permute-done((bf16[1536,384]{1,0:T(8,128)(2,1)}, bf16[1536,384]{1,0:T(8,128)(2,1)S(1)}, u32[]{:S(2)}, u32[]{:S(2)}) %collective-permute-start.8) | collective-permute-done | bytes 1179680 | tf_op jit(solution)/shard_map/ppermute | solution.py:246
  58.8 1.3 shard_map.60
  60.1 3.2 %collective-permute-start.9 = (bf16[384,1536]{1,0:T(8,128)(2,1)}, bf16[384,1536]{1,0:T(8,128)(2,1)}, u32[]{:S(2)}, u32[]{:S(2)}) collective-permute-start(bf16[384,1536]{1,0:T(8,128)(2,1)} %shard_map.60), channel_id=1, source_target_pairs={{0,256},{256,0},{1,257},{257,1},{2,258},{258,2},{3,259},{259,3},{4... | collective-permute-start | bytes 3538952 | tf_op jit(solution)/shard_map/ppermute | solution.py:258
  63.3 5.8 %all-to-all-done.1.received_ref = bf16[8,16,1664]{2,1,0:T(8,128)(2,1)S(1)} async-done(((bf16[8,16,1664]{2,1,0:T(8,128)(2,1)}), bf16[8,16,1664]{2,1,0:T(8,128)(2,1)S(1)}, u32[]{:S(2)}, u32[]{:S(2)}) %all-to-all-start.1) | async-done | bytes 426016 | tf_op jit(solution)/shard_map/all_to_all | solution.py:279
  69.2 0.9 shard_map.58
  70.0 0.7 copy-done.5
  70.8 6.7 %all-to-all-start.2 = ((bf16[8,16,1536]{2,1,0:T(8,128)(2,1)}), bf16[8,16,1536]{2,1,0:T(8,128)(2,1)S(1)}, u32[]{:S(2)}, u32[]{:S(2)}) async-start(bf16[8,16,1536]{2,1,0:T(8,128)(2,1)} %copy-done.5), calls=%async_computation.2 | async-start | bytes 786432 | tf_op jit(solution)/shard_map/all_to_all | solution.py:322
  77.5 1.1 copy-done.6
  78.6 0.8 shard_map.56
  79.4 0.8 copy-done.7
  80.1 4.6 %collective-permute-start.5 = (bf16[768,256]{1,0:T(8,128)(2,1)S(1)}, bf16[768,256]{1,0:T(8,128)(2,1)S(1)}, u32[]{:S(2)}, u32[]{:S(2)}) collective-permute-start(bf16[768,256]{1,0:T(8,128)(2,1)S(1)} %get-tuple-element.13), channel_id=1, source_target_pairs={{0,1},{1,0},{2,3},{3,2},{4,5},{5,4},{6,7},{7,6},{8,9},{9,8},{10,11... | collective-permute-start | bytes 1179656 | tf_op jit(solution)/shard_map/ppermute | solution.py:292
  84.8 1.3 collective-permute-done.5.before_hbm
  86.1 2.9 %all-to-all-done.2.rows_ref = bf16[8,16,1536]{2,1,0:T(8,128)(2,1)S(1)} async-done(((bf16[8,16,1536]{2,1,0:T(8,128)(2,1)}), bf16[8,16,1536]{2,1,0:T(8,128)(2,1)S(1)}, u32[]{:S(2)}, u32[]{:S(2)}) %all-to-all-start.2) | async-done | bytes 393248 | tf_op jit(solution)/shard_map/all_to_all | solution.py:322
  89.0 3.4 %collective-permute-done.9.out_b_hbm = bf16[384,1536]{1,0:T(8,128)(2,1)} collective-permute-done((bf16[384,1536]{1,0:T(8,128)(2,1)}, bf16[384,1536]{1,0:T(8,128)(2,1)}, u32[]{:S(2)}, u32[]{:S(2)}) %collective-permute-start.9) | collective-permute-done | bytes 1179680 | tf_op jit(solution)/shard_map/ppermute | solution.py:258
  92.4 1.3 copy-done.3
  93.7 3.4 %shard_map.61 = bf16[8,16,1536]{2,1,0:T(8,128)(2,1)} custom-call(bf16[8,16,1536]{2,1,0:T(8,128)(2,1)S(1)} %all-to-all-done.2.rows_ref, bf16[1536,384]{1,0:T(8,128)(2,1)S(1)} %bitcast.24, bf16[384,1536]{1,0:T(8,128)(2,1)S(1)} %bitcast.22, bf16[1536,384]{1,0:T(8,128)(2,1)S(1)} %collective-permute-done.8.before_hbm.in_b_hbm, ...), custom_call_target="tpu_custom_call" | custom-call | flops 603979776 | bytes 4718592 | tf_op jit(solution)/shard_map/pallas_call | solution.py:21
  97.1 6.3 %all-to-all-start.3 = ((bf16[8,16,1536]{2,1,0:T(8,128)(2,1)}), bf16[8,16,1536]{2,1,0:T(8,128)(2,1)S(1)}, u32[]{:S(2)}, u32[]{:S(2)}) async-start(bf16[8,16,1536]{2,1,0:T(8,128)(2,1)} %shard_map.61), calls=%async_computation.3 | async-start | bytes 786432 | tf_op jit(solution)/shard_map/all_to_all | solution.py:344
  103.4 1.0 fusion.16
  104.4 3.7 %collective-permute-start.7 = (bf16[192,512]{1,0:T(8,128)(2,1)S(1)}, bf16[192,512]{1,0:T(8,128)(2,1)S(1)}, u32[]{:S(2)}, u32[]{:S(2)}) collective-permute-start(bf16[192,512]{1,0:T(8,128)(2,1)S(1)} %pad_maximum_fusion.1), channel_id=1, source_target_pairs={{0,14},{2,0},{4,2},{6,4},{8,6},{10,8},{12,10},{14,12},{1,15},{3,1}... | collective-permute-start | bytes 589832 | tf_op jit(solution)/shard_map/ppermute | solution.py:295
  108.1 1.9 %collective-permute-start.6 = (bf16[192,512]{1,0:T(8,128)(2,1)S(1)}, bf16[192,512]{1,0:T(8,128)(2,1)S(1)}, u32[]{:S(2)}, u32[]{:S(2)}) collective-permute-start(bf16[192,512]{1,0:T(8,128)(2,1)S(1)} %pad_maximum_fusion), channel_id=1, source_target_pairs={{0,2},{2,4},{4,6},{6,8},{8,10},{10,12},{12,14},{14,0},{1,3},{3,5},... | collective-permute-start | bytes 589832 | tf_op jit(solution)/shard_map/ppermute | solution.py:294
  110.1 1.0 collective-permute-done.7.up_ref
  111.1 4.7 %collective-permute-done.6.low_ref = bf16[192,512]{1,0:T(8,128)(2,1)S(1)} collective-permute-done((bf16[192,512]{1,0:T(8,128)(2,1)S(1)}, bf16[192,512]{1,0:T(8,128)(2,1)S(1)}, u32[]{:S(2)}, u32[]{:S(2)}) %collective-permute-start.6) | collective-permute-done | bytes 196640 | tf_op jit(solution)/shard_map/ppermute | solution.py:294
  115.8 0.6 shard_map.57
  116.4 1.2 shard_map.62
  117.6 25.0 %all_to_all.25 = bf16[16,16,1536]{2,1,0:T(8,128)(2,1)S(1)} all-to-all(bf16[16,16,1536]{2,1,0:T(8,128)(2,1)S(1)} %shard_map.62), channel_id=1, replica_groups=mesh['xlo'=2,'y'=8,'xhi'=2,'zh'=4,'zl'=2,'core'=2] {'zl','xhi','zh'}, dimensions={0} | all-to-all | bytes 1572864 | tf_op jit(solution)/shard_map/all_to_all | solution.py:357
  142.6 7.1 %collective-permute-start.10 = (bf16[256,1536]{1,0:T(8,128)(2,1)S(1)}, bf16[256,1536]{1,0:T(8,128)(2,1)S(1)}, u32[]{:S(2)}, u32[]{:S(2)}) collective-permute-start(bf16[256,1536]{1,0:T(8,128)(2,1)S(1)} %bitcast.29), channel_id=1, source_target_pairs={{0,1},{1,0},{2,3},{3,2},{4,5},{5,4},{6,7},{7,6},{8,9},{9,8},{10,11... | collective-permute-start | bytes 2359304 | tf_op jit(solution)/shard_map/ppermute | solution.py:358
  149.7 1.9 %collective-permute-done.10 = bf16[256,1536]{1,0:T(8,128)(2,1)S(1)} collective-permute-done((bf16[256,1536]{1,0:T(8,128)(2,1)S(1)}, bf16[256,1536]{1,0:T(8,128)(2,1)S(1)}, u32[]{:S(2)}, u32[]{:S(2)}) %collective-permute-start.10) | collective-permute-done | bytes 786464 | tf_op jit(solution)/shard_map/ppermute | solution.py:358
  151.6 0.5 fusion.18
  152.1 0.8 copy-done.11
  152.9 1.5 fusion.2
  (35 shorter events, 0.1 us)
Async XLA Ops:
  0.0 0.9 copy-start
  0.0 10.6 %copy-start.10 = (bf16[1,384,1536]{2,1,0:T(8,128)(2,1)S(1)}, bf16[1,384,1536]{2,1,0:T(8,128)(2,1)}, u32[]{:S(2)}) copy-start(bf16[1,384,1536]{2,1,0:T(8,128)(2,1)} %param.5) | copy-start | bytes 3538948
  1.9 25.6 %all-to-all-start = ((bf16[16,96,128]{2,1,0:T(8,128)(2,1)}), bf16[16,96,128]{2,1,0:T(8,128)(2,1)S(1)}, u32[]{:S(2)}, u32[]{:S(2)}) async-start(bf16[16,96,128]{2,1,0:T(8,128)(2,1)} %broadcast_in_dim.13), calls=%async_computation | async-start | bytes 786432 | tf_op jit(solution)/shard_map/all_to_all | solution.py:202
  10.6 16.9 %copy-start.2 = (bf16[1,1536,384]{2,1,0:T(8,128)(2,1)S(1)}, bf16[1,1536,384]{2,1,0:T(8,128)(2,1)}, u32[]{:S(2)}) copy-start(bf16[1,1536,384]{2,1,0:T(8,128)(2,1)} %param.8) | copy-start | bytes 3538948
  11.7 22.6 %collective-permute-start = (bf16[192,1536]{1,0:T(8,128)(2,1)}, bf16[192,1536]{1,0:T(8,128)(2,1)S(1)}, u32[]{:S(2)}, u32[]{:S(2)}) collective-permute-start(bf16[192,1536]{1,0:T(8,128)(2,1)} %get-tuple-element.18), channel_id=1, source_target_pairs={{0,14},{2,0},{4,2},{6,4},{8,6},{10,8},{12,10},{14,12},{1,15},{3,1}... | collective-permute-start | bytes 1769480 | tf_op jit(solution)/shard_map/ppermute | solution.py:223
  22.4 17.0 %collective-permute-start.1 = (bf16[192,1536]{1,0:T(8,128)(2,1)}, bf16[192,1536]{1,0:T(8,128)(2,1)}, u32[]{:S(2)}, u32[]{:S(2)}) collective-permute-start(bf16[192,1536]{1,0:T(8,128)(2,1)} %get-tuple-element.17), channel_id=1, source_target_pairs={{0,2},{2,4},{4,6},{6,8},{8,10},{10,12},{12,14},{14,0},{1,3},{3,5},... | collective-permute-start | bytes 1769480 | tf_op jit(solution)/shard_map/ppermute | solution.py:224
  24.3 21.0 %collective-permute-start.2 = (bf16[384,1536]{1,0:T(8,128)(2,1)S(1)}, bf16[384,1536]{1,0:T(8,128)(2,1)}, u32[]{:S(2)}, u32[]{:S(2)}) collective-permute-start(bf16[384,1536]{1,0:T(8,128)(2,1)S(1)} %bitcast.28), channel_id=1, source_target_pairs={{0,1},{1,0},{2,3},{3,2},{4,5},{5,4},{6,7},{7,6},{8,9},{9,8},{10,11... | collective-permute-start | bytes 3538952 | tf_op jit(solution)/shard_map/ppermute | solution.py:226
  27.5 1.3 copy-start.4
  28.8 30.0 %collective-permute-start.8 = (bf16[1536,384]{1,0:T(8,128)(2,1)}, bf16[1536,384]{1,0:T(8,128)(2,1)S(1)}, u32[]{:S(2)}, u32[]{:S(2)}) collective-permute-start(bf16[1536,384]{1,0:T(8,128)(2,1)} %shard_map.59), channel_id=1, source_target_pairs={{0,256},{256,0},{1,257},{257,1},{2,258},{258,2},{3,259},{259,3},{4... | collective-permute-start | bytes 3538952 | tf_op jit(solution)/shard_map/ppermute | solution.py:246
  34.3 10.9 %copy-start.12 = (bf16[192,1536]{1,0:T(8,128)(2,1)}, bf16[192,1536]{1,0:T(8,128)(2,1)S(1)}, u32[]{:S(2)}) copy-start(bf16[192,1536]{1,0:T(8,128)(2,1)S(1)} %collective-permute-done.refs_2_) | copy-start | bytes 1769476
  34.3 9.1 %collective-permute-start.3 = (bf16[192,1536]{1,0:T(8,128)(2,1)S(1)}, bf16[192,1536]{1,0:T(8,128)(2,1)S(1)}, u32[]{:S(2)}, u32[]{:S(2)}) collective-permute-start(bf16[192,1536]{1,0:T(8,128)(2,1)S(1)} %collective-permute-done.refs_2_), channel_id=1, source_target_pairs={{0,1},{1,0},{2,3},{3,2},{4,5},{5,4},{6,7},{7,6},{8,9},{9,8},{10,11... | collective-permute-start | bytes 1769480 | tf_op jit(solution)/shard_map/ppermute | solution.py:226
  39.4 5.9 %collective-permute-start.4 = (bf16[192,1536]{1,0:T(8,128)(2,1)}, bf16[192,1536]{1,0:T(8,128)(2,1)S(1)}, u32[]{:S(2)}, u32[]{:S(2)}) collective-permute-start(bf16[192,1536]{1,0:T(8,128)(2,1)} %collective-permute-done.1.refs_3_), channel_id=1, source_target_pairs={{0,1},{1,0},{2,3},{3,2},{4,5},{5,4},{6,7},{7,6},{8,9},{9,8},{10,11... | collective-permute-start | bytes 1769480 | tf_op jit(solution)/shard_map/ppermute | solution.py:226
  43.4 1.8 %copy-start.13 = (bf16[192,1536]{1,0:T(8,128)(2,1)}, bf16[192,1536]{1,0:T(8,128)(2,1)S(1)}, u32[]{:S(2)}) copy-start(bf16[192,1536]{1,0:T(8,128)(2,1)S(1)} %collective-permute-done.3.refs_5_) | copy-start | bytes 1769476
  45.3 0.8 copy-start.14
  46.1 12.7 %copy-start.1 = (bf16[1,384,1536]{2,1,0:T(8,128)(2,1)S(1)}, bf16[1,384,1536]{2,1,0:T(8,128)(2,1)}, u32[]{:S(2)}) copy-start(bf16[1,384,1536]{2,1,0:T(8,128)(2,1)} %param.9) | copy-start | bytes 3538948
  52.7 16.5 %all-to-all-start.1 = ((bf16[8,16,1664]{2,1,0:T(8,128)(2,1)}), bf16[8,16,1664]{2,1,0:T(8,128)(2,1)S(1)}, u32[]{:S(2)}, u32[]{:S(2)}) async-start(bf16[8,16,1664]{2,1,0:T(8,128)(2,1)} %bitcast.31), calls=%async_computation.1 | async-start | bytes 851968 | tf_op jit(solution)/shard_map/all_to_all | solution.py:279
  58.8 10.4 %copy-start.9 = (f32[1,1536]{1,0:T(1,128)S(1)}, f32[1,1536]{1,0:T(1,128)}, u32[]{:S(2)}) copy-start(f32[1,1536]{1,0:T(1,128)} %gain_ref.1) | copy-start | bytes 18436
  60.1 32.3 %collective-permute-start.9 = (bf16[384,1536]{1,0:T(8,128)(2,1)}, bf16[384,1536]{1,0:T(8,128)(2,1)}, u32[]{:S(2)}, u32[]{:S(2)}) collective-permute-start(bf16[384,1536]{1,0:T(8,128)(2,1)} %shard_map.60), channel_id=1, source_target_pairs={{0,256},{256,0},{1,257},{257,1},{2,258},{258,2},{3,259},{259,3},{4... | collective-permute-start | bytes 3538952 | tf_op jit(solution)/shard_map/ppermute | solution.py:258
  70.0 0.8 copy-start.5
  70.8 18.2 %all-to-all-start.2 = ((bf16[8,16,1536]{2,1,0:T(8,128)(2,1)}), bf16[8,16,1536]{2,1,0:T(8,128)(2,1)S(1)}, u32[]{:S(2)}, u32[]{:S(2)}) async-start(bf16[8,16,1536]{2,1,0:T(8,128)(2,1)} %copy-done.5), calls=%async_computation.2 | async-start | bytes 786432 | tf_op jit(solution)/shard_map/all_to_all | solution.py:322
  77.5 1.1 copy-start.6
  79.4 0.8 copy-start.7
  80.1 5.9 %collective-permute-start.5 = (bf16[768,256]{1,0:T(8,128)(2,1)S(1)}, bf16[768,256]{1,0:T(8,128)(2,1)S(1)}, u32[]{:S(2)}, u32[]{:S(2)}) collective-permute-start(bf16[768,256]{1,0:T(8,128)(2,1)S(1)} %get-tuple-element.13), channel_id=1, source_target_pairs={{0,1},{1,0},{2,3},{3,2},{4,5},{5,4},{6,7},{7,6},{8,9},{9,8},{10,11... | collective-permute-start | bytes 1179656 | tf_op jit(solution)/shard_map/ppermute | solution.py:292
  92.4 1.3 copy-start.3
  97.1 13.0 %copy-start.8 = (bf16[768,256]{1,0:T(8,128)(2,1)S(1)}, bf16[768,256]{1,0:T(8,128)(2,1)}, u32[]{:S(2)}) copy-start(bf16[768,256]{1,0:T(8,128)(2,1)} %copy-done.7) | copy-start | bytes 1179652
  97.1 19.2 %all-to-all-start.3 = ((bf16[8,16,1536]{2,1,0:T(8,128)(2,1)}), bf16[8,16,1536]{2,1,0:T(8,128)(2,1)S(1)}, u32[]{:S(2)}, u32[]{:S(2)}) async-start(bf16[8,16,1536]{2,1,0:T(8,128)(2,1)} %shard_map.61), calls=%async_computation.3 | async-start | bytes 786432 | tf_op jit(solution)/shard_map/all_to_all | solution.py:344
  104.4 6.7 %collective-permute-start.7 = (bf16[192,512]{1,0:T(8,128)(2,1)S(1)}, bf16[192,512]{1,0:T(8,128)(2,1)S(1)}, u32[]{:S(2)}, u32[]{:S(2)}) collective-permute-start(bf16[192,512]{1,0:T(8,128)(2,1)S(1)} %pad_maximum_fusion.1), channel_id=1, source_target_pairs={{0,14},{2,0},{4,2},{6,4},{8,6},{10,8},{12,10},{14,12},{1,15},{3,1}... | collective-permute-start | bytes 589832 | tf_op jit(solution)/shard_map/ppermute | solution.py:295
  108.1 7.6 %collective-permute-start.6 = (bf16[192,512]{1,0:T(8,128)(2,1)S(1)}, bf16[192,512]{1,0:T(8,128)(2,1)S(1)}, u32[]{:S(2)}, u32[]{:S(2)}) collective-permute-start(bf16[192,512]{1,0:T(8,128)(2,1)S(1)} %pad_maximum_fusion), channel_id=1, source_target_pairs={{0,2},{2,4},{4,6},{6,8},{8,10},{10,12},{12,14},{14,0},{1,3},{3,5},... | collective-permute-start | bytes 589832 | tf_op jit(solution)/shard_map/ppermute | solution.py:294
  142.6 9.0 %collective-permute-start.10 = (bf16[256,1536]{1,0:T(8,128)(2,1)S(1)}, bf16[256,1536]{1,0:T(8,128)(2,1)S(1)}, u32[]{:S(2)}, u32[]{:S(2)}) collective-permute-start(bf16[256,1536]{1,0:T(8,128)(2,1)S(1)} %bitcast.29), channel_id=1, source_target_pairs={{0,1},{1,0},{2,3},{3,2},{4,5},{5,4},{6,7},{7,6},{8,9},{9,8},{10,11... | collective-permute-start | bytes 2359304 | tf_op jit(solution)/shard_map/ppermute | solution.py:358
  151.6 1.3 copy-start.11

commit v6 on v5

--- a/solution.py
+++ b/solution.py
@@ -59,8 +59,8 @@
 
 def dispatch_kernel(*refs):
     sources, refs = refs[:7], refs[7:]
-    message_hbm, logits_hbm, columns_ref, *feats = refs[:9]
-    logits_ref, message_ref, semaphores = refs[9:]
+    message_hbm, columns_ref, *feats = refs[:8]
+    logits_ref, message_ref, semaphores = refs[8:]
     width, slots = columns_ref.shape
     targets = [columns_ref, *feats]
     loads = [started(source, target, semaphores, k) for k, (source, target) in enumerate(zip(sources, targets))]
@@ -76,10 +76,9 @@
         high = top if high is None else jnp.maximum(high, top)
         offset += feats_ref.shape[0]
         rows.append(part)
-    stores = [started(logits_ref, logits_hbm, semaphores, 7)]
     message_ref[:, width:] = in_lanes([jnp.broadcast_to(high, (EXTRA, slots)).T])
     last = pl.ds(width, EXTRA)
-    stores.append(started(message_ref.at[:, last], message_hbm.at[:, last], semaphores, 8))
+    stores = [started(message_ref.at[:, last], message_hbm.at[:, last], semaphores, 7)]
     dispatch = [jnp.exp(logits_ref[part, :] - high).astype(BF16).T for part in rows]
     step = 512
     for k in range(width // step):
@@ -88,21 +87,28 @@
         for one, feats_ref in zip(dispatch[1:], feats[1:]):
             sums += jnp.dot(one, feats_ref[:, part], preferred_element_type=F32)
         message_ref[:, part] = sums.astype(BF16)
-        stores.append(started(message_ref.at[:, part], message_hbm.at[:, part], semaphores, 9 + k))
+        stores.append(started(message_ref.at[:, part], message_hbm.at[:, part], semaphores, 8 + k))
     for copy in stores:
         copy.wait()
 
 
-def exps_kernel(logits_ref, own_ref, answer_ref):
-    rows, slots = own_ref.shape[0], logits_ref.shape[1]
+def exps_kernel(columns_ref, *refs):
+    feats, (own_ref, answer_ref) = refs[:6], refs[6:]
+    columns = columns_ref[...]
+    slots = columns.shape[1]
     for k, out_ref in enumerate((own_ref, answer_ref)):
-        logits = logits_ref[k * rows : (k + 1) * rows, :]
-        high = jnp.max(logits, axis=1, keepdims=True)
-        exps = jnp.exp(logits - high)
-        total = jnp.sum(exps, axis=1, keepdims=True)
-        out_ref[:, :slots] = exps.astype(BF16)
-        lanes = (rows, EXTRA)
-        out_ref[:, slots:] = in_lanes([jnp.broadcast_to(high, lanes), jnp.broadcast_to(total, lanes)])
+        offset = 0
+        for feats_ref in feats[3 * k : 3 * k + 3]:
+            rows = feats_ref.shape[0]
+            part = slice(offset, offset + rows)
+            offset += rows
+            logits = jnp.dot(feats_ref[...], columns, preferred_element_type=F32)
+            high = jnp.max(logits, axis=1, keepdims=True)
+            exps = jnp.exp(logits - high)
+            total = jnp.sum(exps, axis=1, keepdims=True)
+            out_ref[part, :slots] = exps.astype(BF16)
+            lanes = (rows, EXTRA)
+            out_ref[part, slots:] = in_lanes([jnp.broadcast_to(high, lanes), jnp.broadcast_to(total, lanes)])
 
 
 def weights_kernel(side_ref, own_ref, core_ref, low_ref, up_ref, own_weights_ref, core_weights_ref):
@@ -147,43 +153,17 @@
         copy.wait()
 
 
-def follow_kernel(weights_hbm, before_hbm, weights_ref, semaphores):
-    for copy in started_rows(weights_hbm, weights_ref, semaphores, 0, semaphores.shape[0]):
-        copy.wait()
-
-
-def expert_kernel(
-    rows_ref,
-    in_hbm,
-    out_hbm,
-    in_b_hbm,
-    out_b_hbm,
-    before_hbm,
-    partial_ref,
-    in_ref,
-    out_ref,
-    in_b_ref,
-    out_b_ref,
-    semaphores,
-):
+def expert_kernel(rows_ref, in_hbm, out_hbm, before_hbm, partial_ref, in_ref, out_ref, semaphores):
     rows = rows_ref[...].reshape(-1, rows_ref.shape[-1])
     width = rows.shape[1]
-    cuts = 4
-    pairs = ((in_hbm, in_ref), (in_b_hbm, in_b_ref), (out_hbm, out_ref), (out_b_hbm, out_b_ref))
-    loads = [started_rows(*pair, semaphores, cuts * k, cuts) for k, pair in enumerate(pairs)]
-    for copy in loads[0]:
-        copy.wait()
+    loads = [started(in_hbm, in_ref, semaphores, 0), started(out_hbm, out_ref, semaphores, 1)]
+    loads[0].wait()
     hidden = jax.nn.gelu(jnp.dot(rows, in_ref[...], preferred_element_type=F32)).astype(BF16)
-    for copy in loads[1]:
-        copy.wait()
-    hidden_b = jax.nn.gelu(jnp.dot(rows, in_b_ref[...], preferred_element_type=F32)).astype(BF16)
-    for copy in loads[2] + loads[3]:
-        copy.wait()
+    loads[1].wait()
     step = 512
     for k in range(width // step):
         part = pl.ds(k * step, step)
         sums = jnp.dot(hidden, out_ref[:, part], preferred_element_type=F32)
-        sums += jnp.dot(hidden_b, out_b_ref[:, part], preferred_element_type=F32)
         partial_ref[:, :, part] = sums.astype(BF16).reshape(*rows_ref.shape[:2], step)
 
 
@@ -210,7 +190,7 @@
     slot_count = router.shape[1]
     depth = lax.axis_size(Z)
     owners = lax.axis_size(("xhi", "zh"))
-    groups = lax.axis_size("y")
+    groups = lax.axis_size(("xlo", "y"))
     per_owner = slot_count // (4 * owners)
     quarter = slot_count // 4
     core, side = lax.axis_index("core"), lax.axis_index("zl")
@@ -232,47 +212,22 @@
     own_columns = jnp.dot(router, pick, preferred_element_type=F32).astype(BF16)
     columns = sent_to_all(own_columns, ("xlo", "y")).reshape(width, quarter)
 
-    in_later = kernel_call(
-        follow_kernel,
-        shape((width, hidden_units), BF16),
-        0,
-        4 * width * hidden_units,
-        [HBM] * 2,
-        w_in[0],
-        columns,
-        scratch=[pltpu.SemaphoreType.DMA((4,))],
-        room=16,
-    )
-    partner_in = lax.ppermute(in_later, "xlo", other())
-    out_later = kernel_call(
-        follow_kernel,
-        shape((hidden_units, width), BF16),
-        0,
-        4 * width * hidden_units,
-        [HBM] * 2,
-        w_out[0],
-        partner_in,
-        scratch=[pltpu.SemaphoreType.DMA((4,))],
-        room=16,
-    )
-    partner_out = lax.ppermute(out_later, "xlo", other())
-
-    message, logits = kernel_call(
+    message = kernel_call(
         dispatch_kernel,
-        (shape((quarter, width + EXTRA), BF16), shape((4 * count, quarter), F32)),
+        shape((quarter, width + EXTRA), BF16),
         16 * count * width * quarter,
         2 * (4 * count * width + 2 * width * quarter),
         [HBM] * 7,
         columns,
         *mine,
         *theirs,
-        out_specs=(HBM, HBM),
+        out_specs=HBM,
         scratch=[
             pltpu.VMEM((width, quarter), BF16),
             *[pltpu.VMEM(block.shape, BF16) for block in mine + theirs],
             pltpu.VMEM((4 * count, quarter), F32),
             pltpu.VMEM((quarter, width + EXTRA), BF16),
-            pltpu.SemaphoreType.DMA((12,)),
+            pltpu.SemaphoreType.DMA((11,)),
         ],
         room=58,
     )
@@ -283,11 +238,13 @@
     exps, answer = kernel_call(
         exps_kernel,
         (shape((2 * count, quarter + EXTRA), BF16), shape((2 * count, quarter + EXTRA), BF16)),
-        64 * count * quarter,
-        32 * count * quarter,
-        [VMEM],
-        logits,
-        room=12,
+        8 * count * width * quarter,
+        8 * count * width,
+        [VMEM] * 7,
+        columns,
+        *mine,
+        *theirs,
+        room=58,
     )
     exps_b = lax.ppermute(answer, "core", other())
     first, second = slice(count, count + middle), slice(count + middle, 2 * count)
@@ -319,29 +276,25 @@
         scratch=[pltpu.VMEM((per_owner, width), BF16), pltpu.SemaphoreType.DMA((groups,))],
         room=16,
     )
-    rows = lax.all_to_all(slots, "y", 0, 0, tiled=True)
+    rows = lax.all_to_all(slots, ("xlo", "y"), 0, 0, tiled=True)
     partial = kernel_call(
         expert_kernel,
         shape((groups, per_owner, width), BF16),
-        8 * groups * per_owner * width * hidden_units,
-        8 * width * hidden_units,
-        [VMEM, HBM, HBM, HBM, HBM, HBM],
+        4 * groups * per_owner * width * hidden_units,
+        4 * width * hidden_units,
+        [VMEM, HBM, HBM, HBM],
         rows,
         w_in[0],
         w_out[0],
-        partner_in,
-        partner_out,
         exps_b,
         scratch=[
             pltpu.VMEM((width, hidden_units), BF16),
             pltpu.VMEM((hidden_units, width), BF16),
-            pltpu.VMEM((width, hidden_units), BF16),
-            pltpu.VMEM((hidden_units, width), BF16),
-            pltpu.SemaphoreType.DMA((16,)),
+            pltpu.SemaphoreType.DMA((2,)),
         ],
         room=48,
     )
-    blocks = lax.all_to_all(partial, "y", 0, 0, tiled=True)
+    blocks = lax.all_to_all(partial, ("xlo", "y"), 0, 0, tiled=True)
     copies = kernel_call(
         sum_kernel,
         shape((2 * owners, per_owner, width), BF16),

time: 157 us -> 162 us (1.032); the launches traced: 154 us -> 161 us
  blocking collectives: 25 us -> 48.9 us
  starting transfers between devices: 73.1 us -> 58.8 us
  local copies, waits for them, and re-layouts: 9.28 us -> 6.49 us
    all_to_all x0 -> x1, blocking collectives: none -> 21.4 us  [local(): lax.all_to_all(message.reshape(owners, per_owner, width + EXTRA), ('xhi',...]
    all_to_all x1, waiting for transfers between devices: 0.01 us -> 7.15 us  [sent_to_all(): lax.all_to_all(jnp.broadcast_to(value[None], (length, *value.shape)), axe...]
    ppermute x2 -> x0, starting transfers between devices: 6.8 us -> none  [the longest x1 3.55 us: local(): partner_in = lax.ppermute(in_later, 'xlo', other())]
    ppermute x2 -> x0, waiting for transfers between devices: 5.76 us -> none  [the longest x1 3.4 us: local(): partner_out = lax.ppermute(out_later, 'xlo', other())]
    all_to_all x3 -> x2, starting transfers between devices: 16.7 us -> 12.2 us  [the longest x1 6.91 us: local(): blocks = lax.all_to_all(partial, ('xlo', 'y'), 0, 0, tiled=True)]
    ppermute x1, waiting for transfers between devices: 0.98 us -> 5.23 us  [local(): lax.ppermute(jnp.concatenate([exps[second], exps_b[second]], axis=1), Z,...]
    ppermute x3, starting transfers between devices: 11 us -> 7.42 us  [local(): theirs = [lax.ppermute(block, 'core', other()) for block in mine]]
    ppermute x1, waiting for transfers between devices: 4.66 us -> 1.34 us  [local(): lax.ppermute(jnp.concatenate([exps[first], exps_b[first]], axis=1), Z, up)]
  transfers between devices with their start and end apart: 15 -> 12, of which waited for: 11 -> 7; matrix products, arithmetic and copies ran while one was open for 1% -> 1% of each run, Pallas kernels for 7% -> 3%
where the time goes in v6:
time: 162 us; the launch traced here: 161 us
  starting transfers between devices  58.8 us (36%)
  blocking collectives  48.9 us (30%)
  waiting for transfers between devices  27.3 us (17%)
  Pallas kernels  17.3 us (11%)
  local copies, waits for them, and re-layouts  6.49 us (4%)
  matrix products  2.17 us (1%)
    all_to_all x1, blocking collectives, local(): lax.all_to_all(copies, ('zl', 'xhi', 'zh'), 0, 0, tiled=True)  27.5 us
    all_to_all x1, blocking collectives, local(): lax.all_to_all(message.reshape(owners, per_owner, width + EXTRA), ('xhi',...  21.4 us
    pallas_call x6, Pallas kernels, kernel_call(): pl.pallas_call(body, out_shape=outs, in_specs=specs, out_specs=jax.tree.m...  17.3 us
    ppermute x1, starting transfers between devices, local(): above = lax.ppermute(feats[:middle], Z, down)  8.59 us
    all_to_all x1, starting transfers between devices, sent_to_all(): lax.all_to_all(jnp.broadcast_to(value[None], (length, *value.shape)), axe...  7.85 us
    ppermute x3, starting transfers between devices, local(): theirs = [lax.ppermute(block, 'core', other()) for block in mine]  7.42 us
    all_to_all x1, waiting for transfers between devices, sent_to_all(): lax.all_to_all(jnp.broadcast_to(value[None], (length, *value.shape)), axe...  7.15 us
    ppermute x1, starting transfers between devices, local(): outs_b = lax.ppermute(outs, 'core', other())  7.12 us
  transfers between devices with their start and end apart: 12, of which 7 were waited for; matrix products, arithmetic and copies ran while one was open for 1% of the time, Pallas kernels for 3%

profile of v6, /device:TPU:1, one launch (start us, length us, event | category | flops | bytes accessed | tf_op | source)
XLA Modules:
  0.0 161.4 jit_solution(296853440439528748)
XLA Ops:
  0.0 0.0 copy-start
  0.0 2.4 %slice_bitcast_fusion = (bf16[192,1536]{1,0:T(8,128)(2,1)}, bf16[192,1536]{1,0:T(8,128)(2,1)}) fusion(bf16[1,384,1536]{2,1,0:T(8,128)(2,1)} %param.5), kind=kLoop, calls=%fused_computation.6 | loop fusion | bytes 2359296 | tf_op jit(solution)/shard_map/slice | solution.py:204
  2.4 4.8 %collective-permute-start.1 = (bf16[192,1536]{1,0:T(8,128)(2,1)}, bf16[192,1536]{1,0:T(8,128)(2,1)S(1)}, u32[]{:S(2)}, u32[]{:S(2)}) collective-permute-start(bf16[192,1536]{1,0:T(8,128)(2,1)} %get-tuple-element.13), channel_id=1, source_target_pairs={{0,2},{2,4},{4,6},{6,8},{8,10},{10,12},{12,14},{14,0},{1,3},{3,5},... | collective-permute-start | bytes 1769480 | tf_op jit(solution)/shard_map/ppermute | solution.py:204
  7.3 8.6 %collective-permute-start = (bf16[192,1536]{1,0:T(8,128)(2,1)}, bf16[192,1536]{1,0:T(8,128)(2,1)}, u32[]{:S(2)}, u32[]{:S(2)}) collective-permute-start(bf16[192,1536]{1,0:T(8,128)(2,1)} %get-tuple-element.14), channel_id=1, source_target_pairs={{0,14},{2,0},{4,2},{6,4},{8,6},{10,8},{12,10},{14,12},{1,15},{3,1}... | collective-permute-start | bytes 1769480 | tf_op jit(solution)/shard_map/ppermute | solution.py:203
  15.9 0.0 copy-done.4
  15.9 2.9 %collective-permute-start.2 = (bf16[384,1536]{1,0:T(8,128)(2,1)S(1)}, bf16[384,1536]{1,0:T(8,128)(2,1)S(1)}, u32[]{:S(2)}, u32[]{:S(2)}) collective-permute-start(bf16[384,1536]{1,0:T(8,128)(2,1)S(1)} %bitcast.25), channel_id=1, source_target_pairs={{0,1},{1,0},{2,3},{3,2},{4,5},{5,4},{6,7},{7,6},{8,9},{9,8},{10,11... | collective-permute-start | bytes 3538952 | tf_op jit(solution)/shard_map/ppermute | solution.py:206
  18.8 0.0 copy-done
  18.8 0.2 fusion.3
  19.0 0.8 broadcast_in_dim.13
  19.8 7.9 %all-to-all-start = ((bf16[16,96,128]{2,1,0:T(8,128)(2,1)}), bf16[16,96,128]{2,1,0:T(8,128)(2,1)S(1)}, u32[]{:S(2)}, u32[]{:S(2)}) async-start(bf16[16,96,128]{2,1,0:T(8,128)(2,1)} %broadcast_in_dim.13), calls=%async_computation | async-start | bytes 786432 | tf_op jit(solution)/shard_map/all_to_all | solution.py:182
  27.7 0.0 collective-permute-done.1.refs_2_.refs_3_
  27.7 2.6 %collective-permute-start.4 = (bf16[192,1536]{1,0:T(8,128)(2,1)S(1)}, bf16[192,1536]{1,0:T(8,128)(2,1)}, u32[]{:S(2)}, u32[]{:S(2)}) collective-permute-start(bf16[192,1536]{1,0:T(8,128)(2,1)S(1)} %collective-permute-done.1.refs_2_.refs_3_), channel_id=1, source_target_pairs={{0,1},{1,0},{2,3},{3,2},{4,5},{5,4},{6,7},{7,6},{8,9},{9,8},{10,11... | collective-permute-start | bytes 1769480 | tf_op jit(solution)/shard_map/ppermute | solution.py:206
  30.3 0.0 collective-permute-done.refs_1_.refs_2_
  30.3 1.9 %collective-permute-start.3 = (bf16[192,1536]{1,0:T(8,128)(2,1)}, bf16[192,1536]{1,0:T(8,128)(2,1)}, u32[]{:S(2)}, u32[]{:S(2)}) collective-permute-start(bf16[192,1536]{1,0:T(8,128)(2,1)} %collective-permute-done.refs_1_.refs_2_), channel_id=1, source_target_pairs={{0,1},{1,0},{2,3},{3,2},{4,5},{5,4},{6,7},{7,6},{8,9},{9,8},{10,11... | collective-permute-start | bytes 1769480 | tf_op jit(solution)/shard_map/ppermute | solution.py:206
  32.3 7.2 %all-to-all-done = bf16[16,96,128]{2,1,0:T(8,128)(2,1)S(1)} async-done(((bf16[16,96,128]{2,1,0:T(8,128)(2,1)}), bf16[16,96,128]{2,1,0:T(8,128)(2,1)S(1)}, u32[]{:S(2)}, u32[]{:S(2)}) %all-to-all-start) | async-done | bytes 393248 | tf_op jit(solution)/shard_map/all_to_all | solution.py:182
  39.4 0.0 collective-permute-done.4.refs_5_.refs_6_
  39.4 0.0 collective-permute-done.3.refs_4_.refs_5_
  39.4 0.0 collective-permute-done.2.refs_3_.refs_4_
  39.4 0.0 copy-start.6
  39.5 0.7 copy-done.7
  40.2 0.4 copy-done.6
  40.6 6.5 %shard_map.57 = bf16[128,1664]{1,0:T(8,128)(2,1)} custom-call(bf16[1536,128]{1,0:T(8,128)(2,1)} %bitcast.26, bf16[384,1536]{1,0:T(8,128)(2,1)} %bitcast.23, bf16[192,1536]{1,0:T(8,128)(2,1)} %collective-permute-done.refs_1_.refs_2_, bf16[192,1536]{1,0:T(8,128)(2,1)} %copy-done.8, bf16[384,1536]{1,0:T(8,128)(2,1)} %copy-done.6, ...), custom_call_target="tpu_custom_call" | custom-call | flops 1207959552 | bytes 5505024 | tf_op jit(solution)/shard_map/pallas_call | solution.py:21
  47.1 21.4 %all_to_all.25.received_ref = bf16[8,16,1664]{2,1,0:T(8,128)(2,1)S(1)} all-to-all(bf16[8,16,1664]{2,1,0:T(8,128)(2,1)} %bitcast.30), channel_id=1, replica_groups=mesh['xlo'=2,'y'=8,'xhi'=2,'zh'=4,'zl'=2,'core'=2] {'xhi','zh'}, dimensions={0} | all-to-all | bytes 851968 | tf_op jit(solution)/shard_map/all_to_all | solution.py:234
  68.6 0.0 copy-done.3
  68.6 1.3 shard_map.58
  69.9 5.3 %all-to-all-start.2 = ((bf16[16,16,1536]{2,1,0:T(8,128)(2,1)}), bf16[16,16,1536]{2,1,0:T(8,128)(2,1)S(1)}, u32[]{:S(2)}, u32[]{:S(2)}) async-start(bf16[16,16,1536]{2,1,0:T(8,128)(2,1)} %shard_map.58), calls=%async_computation.2 | async-start | bytes 1572864 | tf_op jit(solution)/shard_map/all_to_all | solution.py:279
  75.2 0.0 copy-start.1
  75.2 5.0 %shard_map.55 = (bf16[768,256]{1,0:T(8,128)(2,1)}, bf16[768,256]{1,0:T(8,128)(2,1)}) custom-call(bf16[1536,128]{1,0:T(8,128)(2,1)} %bitcast.27, bf16[384,1536]{1,0:T(8,128)(2,1)} %bitcast.24, bf16[192,1536]{1,0:T(8,128)(2,1)} %collective-permute-done.refs_1_.refs_2_, bf16[192,1536]{1,0:T(8,128)(2,1)} %copy-done.8, bf16[384,1536]{1,0:T(8,128)(2,1)} %copy-done.6, ...), custom_call_target="tpu_custom_call" | custom-call | flops 603979776 | bytes 4718592 | tf_op jit(solution)/shard_map/pallas_call | solution.py:21
  80.2 4.3 %collective-permute-start.5 = (bf16[768,256]{1,0:T(8,128)(2,1)}, bf16[768,256]{1,0:T(8,128)(2,1)S(1)}, u32[]{:S(2)}, u32[]{:S(2)}) collective-permute-start(bf16[768,256]{1,0:T(8,128)(2,1)} %get-tuple-element.10), channel_id=1, source_target_pairs={{0,1},{1,0},{2,3},{3,2},{4,5},{5,4},{6,7},{7,6},{8,9},{9,8},{10,11... | collective-permute-start | bytes 1179656 | tf_op jit(solution)/shard_map/ppermute | solution.py:249
  84.5 1.5 collective-permute-done.5.before_hbm
  86.0 6.6 %all-to-all-done.2.rows_ref = bf16[16,16,1536]{2,1,0:T(8,128)(2,1)S(1)} async-done(((bf16[16,16,1536]{2,1,0:T(8,128)(2,1)}), bf16[16,16,1536]{2,1,0:T(8,128)(2,1)S(1)}, u32[]{:S(2)}, u32[]{:S(2)}) %all-to-all-start.2) | async-done | bytes 786464 | tf_op jit(solution)/shard_map/all_to_all | solution.py:279
  92.6 1.3 copy-done.2
  93.9 2.6 %shard_map.59 = bf16[16,16,1536]{2,1,0:T(8,128)(2,1)} custom-call(bf16[16,16,1536]{2,1,0:T(8,128)(2,1)S(1)} %all-to-all-done.2.rows_ref, bf16[1536,384]{1,0:T(8,128)(2,1)S(1)} %bitcast.21, bf16[384,1536]{1,0:T(8,128)(2,1)S(1)} %bitcast.22, bf16[768,256]{1,0:T(8,128)(2,1)S(1)} %collective-permute-done.5.before_hbm), custom_call_target="tpu_custom_call" | custom-call | flops 603979776 | bytes 2359296 | tf_op jit(solution)/shard_map/pallas_call | solution.py:21
  96.6 6.9 %all-to-all-start.3 = ((bf16[16,16,1536]{2,1,0:T(8,128)(2,1)}), bf16[16,16,1536]{2,1,0:T(8,128)(2,1)S(1)}, u32[]{:S(2)}, u32[]{:S(2)}) async-start(bf16[16,16,1536]{2,1,0:T(8,128)(2,1)} %shard_map.59), calls=%async_computation.3 | async-start | bytes 1572864 | tf_op jit(solution)/shard_map/all_to_all | solution.py:297
  103.5 0.0 copy-done.9
  103.6 1.9 %collective-permute-start.6 = (bf16[192,512]{1,0:T(8,128)(2,1)S(1)}, bf16[192,512]{1,0:T(8,128)(2,1)S(1)}, u32[]{:S(2)}, u32[]{:S(2)}) collective-permute-start(bf16[192,512]{1,0:T(8,128)(2,1)S(1)} %pad_maximum_fusion), channel_id=1, source_target_pairs={{0,2},{2,4},{4,6},{6,8},{8,10},{10,12},{12,14},{14,0},{1,3},{3,5},... | collective-permute-start | bytes 589832 | tf_op jit(solution)/shard_map/ppermute | solution.py:251
  105.5 4.6 %collective-permute-start.7 = (bf16[192,512]{1,0:T(8,128)(2,1)S(1)}, bf16[192,512]{1,0:T(8,128)(2,1)S(1)}, u32[]{:S(2)}, u32[]{:S(2)}) collective-permute-start(bf16[192,512]{1,0:T(8,128)(2,1)S(1)} %pad_maximum_fusion.1), channel_id=1, source_target_pairs={{0,14},{2,0},{4,2},{6,4},{8,6},{10,8},{12,10},{14,12},{1,15},{3,1}... | collective-permute-start | bytes 589832 | tf_op jit(solution)/shard_map/ppermute | solution.py:252
  110.1 1.3 collective-permute-done.6.low_ref
  111.5 5.2 %collective-permute-done.7.up_ref = bf16[192,512]{1,0:T(8,128)(2,1)S(1)} collective-permute-done((bf16[192,512]{1,0:T(8,128)(2,1)S(1)}, bf16[192,512]{1,0:T(8,128)(2,1)S(1)}, u32[]{:S(2)}, u32[]{:S(2)}) %collective-permute-start.7) | collective-permute-done | bytes 196640 | tf_op jit(solution)/shard_map/ppermute | solution.py:252
  116.7 0.6 shard_map.56
  117.3 3.5 %all-to-all-done.3.blocks_ref = bf16[16,16,1536]{2,1,0:T(8,128)(2,1)S(1)} async-done(((bf16[16,16,1536]{2,1,0:T(8,128)(2,1)}), bf16[16,16,1536]{2,1,0:T(8,128)(2,1)S(1)}, u32[]{:S(2)}, u32[]{:S(2)}) %all-to-all-start.3) | async-done | bytes 786464 | tf_op jit(solution)/shard_map/all_to_all | solution.py:297
  120.8 1.3 shard_map.60
  122.1 27.5 %all_to_all.26 = bf16[16,16,1536]{2,1,0:T(8,128)(2,1)S(1)} all-to-all(bf16[16,16,1536]{2,1,0:T(8,128)(2,1)S(1)} %shard_map.60), channel_id=1, replica_groups=mesh['xlo'=2,'y'=8,'xhi'=2,'zh'=4,'zl'=2,'core'=2] {'zl','xhi','zh'}, dimensions={0} | all-to-all | bytes 1572864 | tf_op jit(solution)/shard_map/all_to_all | solution.py:310
  149.6 7.1 %collective-permute-start.8 = (bf16[256,1536]{1,0:T(8,128)(2,1)S(1)}, bf16[256,1536]{1,0:T(8,128)(2,1)S(1)}, u32[]{:S(2)}, u32[]{:S(2)}) collective-permute-start(bf16[256,1536]{1,0:T(8,128)(2,1)S(1)} %bitcast.28), channel_id=1, source_target_pairs={{0,1},{1,0},{2,3},{3,2},{4,5},{5,4},{6,7},{7,6},{8,9},{9,8},{10,11... | collective-permute-start | bytes 2359304 | tf_op jit(solution)/shard_map/ppermute | solution.py:311
  156.7 1.9 %collective-permute-done.8 = bf16[256,1536]{1,0:T(8,128)(2,1)S(1)} collective-permute-done((bf16[256,1536]{1,0:T(8,128)(2,1)S(1)}, bf16[256,1536]{1,0:T(8,128)(2,1)S(1)}, u32[]{:S(2)}, u32[]{:S(2)}) %collective-permute-start.8) | collective-permute-done | bytes 786464 | tf_op jit(solution)/shard_map/ppermute | solution.py:311
  158.6 0.5 fusion.18
  159.1 0.8 copy-done.5
  159.9 1.5 fusion.2
  (18 shorter events, 0.1 us)
Async XLA Ops:
  0.0 18.8 %copy-start = (bf16[96,512]{1,0:T(8,128)(2,1)S(1)}, bf16[96,512]{1,0:T(8,128)(2,1)}, u32[]{:S(2)}) copy-start(bf16[96,512]{1,0:T(8,128)(2,1)} %param.6) | copy-start | bytes 294916
  0.0 15.9 %copy-start.4 = (bf16[1,384,1536]{2,1,0:T(8,128)(2,1)S(1)}, bf16[1,384,1536]{2,1,0:T(8,128)(2,1)}, u32[]{:S(2)}) copy-start(bf16[1,384,1536]{2,1,0:T(8,128)(2,1)} %param.5) | copy-start | bytes 3538948
  2.4 25.2 %collective-permute-start.1 = (bf16[192,1536]{1,0:T(8,128)(2,1)}, bf16[192,1536]{1,0:T(8,128)(2,1)S(1)}, u32[]{:S(2)}, u32[]{:S(2)}) collective-permute-start(bf16[192,1536]{1,0:T(8,128)(2,1)} %get-tuple-element.13), channel_id=1, source_target_pairs={{0,2},{2,4},{4,6},{6,8},{8,10},{10,12},{12,14},{14,0},{1,3},{3,5},... | collective-permute-start | bytes 1769480 | tf_op jit(solution)/shard_map/ppermute | solution.py:204
  7.3 23.1 %collective-permute-start = (bf16[192,1536]{1,0:T(8,128)(2,1)}, bf16[192,1536]{1,0:T(8,128)(2,1)}, u32[]{:S(2)}, u32[]{:S(2)}) collective-permute-start(bf16[192,1536]{1,0:T(8,128)(2,1)} %get-tuple-element.14), channel_id=1, source_target_pairs={{0,14},{2,0},{4,2},{6,4},{8,6},{10,8},{12,10},{14,12},{1,15},{3,1}... | collective-permute-start | bytes 1769480 | tf_op jit(solution)/shard_map/ppermute | solution.py:203
  15.9 23.6 %collective-permute-start.2 = (bf16[384,1536]{1,0:T(8,128)(2,1)S(1)}, bf16[384,1536]{1,0:T(8,128)(2,1)S(1)}, u32[]{:S(2)}, u32[]{:S(2)}) collective-permute-start(bf16[384,1536]{1,0:T(8,128)(2,1)S(1)} %bitcast.25), channel_id=1, source_target_pairs={{0,1},{1,0},{2,3},{3,2},{4,5},{5,4},{6,7},{7,6},{8,9},{9,8},{10,11... | collective-permute-start | bytes 3538952 | tf_op jit(solution)/shard_map/ppermute | solution.py:206
  19.8 19.6 %all-to-all-start = ((bf16[16,96,128]{2,1,0:T(8,128)(2,1)}), bf16[16,96,128]{2,1,0:T(8,128)(2,1)S(1)}, u32[]{:S(2)}, u32[]{:S(2)}) async-start(bf16[16,96,128]{2,1,0:T(8,128)(2,1)} %broadcast_in_dim.13), calls=%async_computation | async-start | bytes 786432 | tf_op jit(solution)/shard_map/all_to_all | solution.py:182
  27.7 11.8 %copy-start.8 = (bf16[192,1536]{1,0:T(8,128)(2,1)}, bf16[192,1536]{1,0:T(8,128)(2,1)S(1)}, u32[]{:S(2)}) copy-start(bf16[192,1536]{1,0:T(8,128)(2,1)S(1)} %collective-permute-done.1.refs_2_.refs_3_) | copy-start | bytes 1769476
  27.7 11.7 %collective-permute-start.4 = (bf16[192,1536]{1,0:T(8,128)(2,1)S(1)}, bf16[192,1536]{1,0:T(8,128)(2,1)}, u32[]{:S(2)}, u32[]{:S(2)}) collective-permute-start(bf16[192,1536]{1,0:T(8,128)(2,1)S(1)} %collective-permute-done.1.refs_2_.refs_3_), channel_id=1, source_target_pairs={{0,1},{1,0},{2,3},{3,2},{4,5},{5,4},{6,7},{7,6},{8,9},{9,8},{10,11... | collective-permute-start | bytes 1769480 | tf_op jit(solution)/shard_map/ppermute | solution.py:206
  30.3 9.1 %collective-permute-start.3 = (bf16[192,1536]{1,0:T(8,128)(2,1)}, bf16[192,1536]{1,0:T(8,128)(2,1)}, u32[]{:S(2)}, u32[]{:S(2)}) collective-permute-start(bf16[192,1536]{1,0:T(8,128)(2,1)} %collective-permute-done.refs_1_.refs_2_), channel_id=1, source_target_pairs={{0,1},{1,0},{2,3},{3,2},{4,5},{5,4},{6,7},{7,6},{8,9},{9,8},{10,11... | collective-permute-start | bytes 1769480 | tf_op jit(solution)/shard_map/ppermute | solution.py:206
  39.4 0.7 copy-start.7
  39.4 1.1 copy-start.6
  40.6 28.0 %copy-start.3 = (f32[1,1536]{1,0:T(1,128)S(1)}, f32[1,1536]{1,0:T(1,128)}, u32[]{:S(2)}) copy-start(f32[1,1536]{1,0:T(1,128)} %gain_ref.1) | copy-start | bytes 18436
  69.9 22.8 %all-to-all-start.2 = ((bf16[16,16,1536]{2,1,0:T(8,128)(2,1)}), bf16[16,16,1536]{2,1,0:T(8,128)(2,1)S(1)}, u32[]{:S(2)}, u32[]{:S(2)}) async-start(bf16[16,16,1536]{2,1,0:T(8,128)(2,1)} %shard_map.58), calls=%async_computation.2 | async-start | bytes 1572864 | tf_op jit(solution)/shard_map/all_to_all | solution.py:279
  75.2 17.5 %copy-start.1 = (bf16[1,1536,384]{2,1,0:T(8,128)(2,1)S(1)}, bf16[1,1536,384]{2,1,0:T(8,128)(2,1)}, u32[]{:S(2)}) copy-start(bf16[1,1536,384]{2,1,0:T(8,128)(2,1)} %param.8) | copy-start | bytes 3538948
  80.2 5.8 %collective-permute-start.5 = (bf16[768,256]{1,0:T(8,128)(2,1)}, bf16[768,256]{1,0:T(8,128)(2,1)S(1)}, u32[]{:S(2)}, u32[]{:S(2)}) collective-permute-start(bf16[768,256]{1,0:T(8,128)(2,1)} %get-tuple-element.10), channel_id=1, source_target_pairs={{0,1},{1,0},{2,3},{3,2},{4,5},{5,4},{6,7},{7,6},{8,9},{9,8},{10,11... | collective-permute-start | bytes 1179656 | tf_op jit(solution)/shard_map/ppermute | solution.py:249
  92.6 1.3 copy-start.2
  96.6 6.9 %copy-start.9 = (bf16[768,256]{1,0:T(8,128)(2,1)S(1)}, bf16[768,256]{1,0:T(8,128)(2,1)}, u32[]{:S(2)}) copy-start(bf16[768,256]{1,0:T(8,128)(2,1)} %get-tuple-element.9) | copy-start | bytes 1179652
  96.6 24.3 %all-to-all-start.3 = ((bf16[16,16,1536]{2,1,0:T(8,128)(2,1)}), bf16[16,16,1536]{2,1,0:T(8,128)(2,1)S(1)}, u32[]{:S(2)}, u32[]{:S(2)}) async-start(bf16[16,16,1536]{2,1,0:T(8,128)(2,1)} %shard_map.59), calls=%async_computation.3 | async-start | bytes 1572864 | tf_op jit(solution)/shard_map/all_to_all | solution.py:297
  103.6 7.9 %collective-permute-start.6 = (bf16[192,512]{1,0:T(8,128)(2,1)S(1)}, bf16[192,512]{1,0:T(8,128)(2,1)S(1)}, u32[]{:S(2)}, u32[]{:S(2)}) collective-permute-start(bf16[192,512]{1,0:T(8,128)(2,1)S(1)} %pad_maximum_fusion), channel_id=1, source_target_pairs={{0,2},{2,4},{4,6},{6,8},{8,10},{10,12},{12,14},{14,0},{1,3},{3,5},... | collective-permute-start | bytes 589832 | tf_op jit(solution)/shard_map/ppermute | solution.py:251
  105.5 11.2 %collective-permute-start.7 = (bf16[192,512]{1,0:T(8,128)(2,1)S(1)}, bf16[192,512]{1,0:T(8,128)(2,1)S(1)}, u32[]{:S(2)}, u32[]{:S(2)}) collective-permute-start(bf16[192,512]{1,0:T(8,128)(2,1)S(1)} %pad_maximum_fusion.1), channel_id=1, source_target_pairs={{0,14},{2,0},{4,2},{6,4},{8,6},{10,8},{12,10},{14,12},{1,15},{3,1}... | collective-permute-start | bytes 589832 | tf_op jit(solution)/shard_map/ppermute | solution.py:252
  149.6 9.0 %collective-permute-start.8 = (bf16[256,1536]{1,0:T(8,128)(2,1)S(1)}, bf16[256,1536]{1,0:T(8,128)(2,1)S(1)}, u32[]{:S(2)}, u32[]{:S(2)}) collective-permute-start(bf16[256,1536]{1,0:T(8,128)(2,1)S(1)} %bitcast.28), channel_id=1, source_target_pairs={{0,1},{1,0},{2,3},{3,2},{4,5},{5,4},{6,7},{7,6},{8,9},{9,8},{10,11... | collective-permute-start | bytes 2359304 | tf_op jit(solution)/shard_map/ppermute | solution.py:311
  158.6 1.3 copy-start.5

commit v7 on v6

--- a/solution.py
+++ b/solution.py
@@ -8,6 +8,7 @@
 F32 = jnp.float32
 BF16 = jnp.bfloat16
 EXTRA = 128
+Y = ("yh", "yl")
 Z = ("zh", "zl")
 VMEM = pl.BlockSpec(memory_space=pltpu.VMEM)
 HBM = pl.BlockSpec(memory_space=pltpu.HBM)
@@ -153,17 +154,24 @@
         copy.wait()
 
 
-def expert_kernel(rows_ref, in_hbm, out_hbm, before_hbm, partial_ref, in_ref, out_ref, semaphores):
+def expert_kernel(rows_ref, *refs):
+    sources, before_hbm, partial_ref, targets, semaphores = refs[:6], refs[6], refs[7], refs[8:14], refs[14]
     rows = rows_ref[...].reshape(-1, rows_ref.shape[-1])
     width = rows.shape[1]
-    loads = [started(in_hbm, in_ref, semaphores, 0), started(out_hbm, out_ref, semaphores, 1)]
-    loads[0].wait()
-    hidden = jax.nn.gelu(jnp.dot(rows, in_ref[...], preferred_element_type=F32)).astype(BF16)
-    loads[1].wait()
+    loads = [started(source, target, semaphores, k) for k, (source, target) in enumerate(zip(sources, targets))]
+    hidden = []
+    for load, in_ref in zip(loads[:3], targets[:3]):
+        load.wait()
+        one = jnp.dot(rows, in_ref[...], preferred_element_type=F32)
+        hidden.append(jax.nn.gelu(one).astype(BF16))
+    for load in loads[3:]:
+        load.wait()
     step = 512
     for k in range(width // step):
         part = pl.ds(k * step, step)
-        sums = jnp.dot(hidden, out_ref[:, part], preferred_element_type=F32)
+        sums = jnp.dot(hidden[0], targets[3][:, part], preferred_element_type=F32)
+        sums += jnp.dot(hidden[1], targets[4][:, part], preferred_element_type=F32)
+        sums += jnp.dot(hidden[2], targets[5][:, part], preferred_element_type=F32)
         partial_ref[:, :, part] = sums.astype(BF16).reshape(*rows_ref.shape[:2], step)
 
 
@@ -190,7 +198,7 @@
     slot_count = router.shape[1]
     depth = lax.axis_size(Z)
     owners = lax.axis_size(("xhi", "zh"))
-    groups = lax.axis_size(("xlo", "y"))
+    groups = lax.axis_size(("xlo", "yh"))
     per_owner = slot_count // (4 * owners)
     quarter = slot_count // 4
     core, side = lax.axis_index("core"), lax.axis_index("zl")
@@ -205,12 +213,20 @@
     mine = [feats, above, below]
     theirs = [lax.ppermute(block, "core", other()) for block in mine]
 
+    ring = lax.axis_size(Y)
+    most = [(2 * k + c, (k + 2 * c - 1) % ring * 2 + c) for k in range(ring) for c in range(2)]
+    least = [(2 * k + c, (k + 1 - 2 * c) % ring * 2 + c) for k in range(ring) for c in range(2)]
+    cut = hidden_units * 2 // 3
+    pairs = [(slice(0, cut), most), (slice(cut, hidden_units), least)]
+    given_in = [w_in[0]] + [lax.ppermute(w_in[0, :, part], (*Y, "core"), perm) for part, perm in pairs]
+    given_out = [w_out[0]] + [lax.ppermute(w_out[0, part], (*Y, "core"), perm) for part, perm in pairs]
+
     row = lax.broadcasted_iota(jnp.int32, (slot_count, quarter), 0)
     col = lax.broadcasted_iota(jnp.int32, (slot_count, quarter), 1)
     wanted = (col // per_owner * 4 + side * 2 + core) * per_owner + col % per_owner
     pick = (row == wanted).astype(BF16)
     own_columns = jnp.dot(router, pick, preferred_element_type=F32).astype(BF16)
-    columns = sent_to_all(own_columns, ("xlo", "y")).reshape(width, quarter)
+    columns = sent_to_all(own_columns, ("xlo", *Y)).reshape(width, quarter)
 
     message = kernel_call(
         dispatch_kernel,
@@ -276,25 +292,24 @@
         scratch=[pltpu.VMEM((per_owner, width), BF16), pltpu.SemaphoreType.DMA((groups,))],
         room=16,
     )
-    rows = lax.all_to_all(slots, ("xlo", "y"), 0, 0, tiled=True)
+    rows = lax.all_to_all(slots, ("xlo", "yh"), 0, 0, tiled=True)
     partial = kernel_call(
         expert_kernel,
         shape((groups, per_owner, width), BF16),
-        4 * groups * per_owner * width * hidden_units,
-        4 * width * hidden_units,
-        [VMEM, HBM, HBM, HBM],
+        8 * groups * per_owner * width * hidden_units,
+        8 * width * hidden_units,
+        [VMEM, HBM, HBM, HBM, HBM, HBM, HBM, HBM],
         rows,
-        w_in[0],
-        w_out[0],
+        *given_in,
+        *given_out,
         exps_b,
         scratch=[
-            pltpu.VMEM((width, hidden_units), BF16),
-            pltpu.VMEM((hidden_units, width), BF16),
-            pltpu.SemaphoreType.DMA((2,)),
+            *[pltpu.VMEM(block.shape, BF16) for block in given_in + given_out],
+            pltpu.SemaphoreType.DMA((6,)),
         ],
         room=48,
     )
-    blocks = lax.all_to_all(partial, ("xlo", "y"), 0, 0, tiled=True)
+    blocks = lax.all_to_all(partial, ("xlo", "yh"), 0, 0, tiled=True)
     copies = kernel_call(
         sum_kernel,
         shape((2 * owners, per_owner, width), BF16),
@@ -316,9 +331,9 @@
 
 
 def solution(mesh):
-    names = ("xlo", "y", "xhi", "zh", "zl", "core")
-    fine = Mesh(mesh.devices.reshape(2, 8, 2, 4, 2, 2), names)
-    grp, seq = names[:2], names[2:]
+    names = ("xlo", "yh", "yl", "xhi", "zh", "zl", "core")
+    fine = Mesh(mesh.devices.reshape(2, 4, 2, 2, 4, 2, 2), names)
+    grp, seq = names[:3], names[3:]
     in_specs = (P(grp, seq, None), P(grp, None), P(seq, None), P(seq, None, grp), P(seq, grp, None))
     return jax.shard_map(
         local, mesh=fine, in_specs=in_specs, out_specs=P(grp, seq, None), check_vma=False

time: 162 us -> 153 us (0.944); the launches traced: 161 us -> 151 us
  blocking collectives: 48.9 us -> 22.4 us
  starting transfers between devices: 58.8 us -> 82.9 us
  waiting for transfers between devices: 27.3 us -> 14 us
  local copies, waits for them, and re-layouts: 6.49 us -> 11 us
    all_to_all x1 -> x0, blocking collectives: 21.4 us -> none  [local(): lax.all_to_all(message.reshape(owners, per_owner, width + EXTRA), ('xhi',...]
    ppermute x0 -> x4, starting transfers between devices: none -> 15 us  [the longest x2 8.58 us: local(): lax.ppermute(w_in[0, :, part], (*Y, 'core'), perm)]
    all_to_all x2 -> x3, waiting for transfers between devices: 10.2 us -> 2.9 us  [the longest x1 2.89 us: local(): lax.all_to_all(message.reshape(owners, per_owner, width + EXTRA), ('xhi',...]
    all_to_all x1, waiting for transfers between devices: 7.15 us -> 0.25 us  [sent_to_all(): lax.all_to_all(jnp.broadcast_to(value[None], (length, *value.shape)), axe...]
    all_to_all x2 -> x3, starting transfers between devices: 12.2 us -> 18.4 us  [the longest x1 7.14 us: local(): blocks = lax.all_to_all(partial, ('xlo', 'yh'), 0, 0, tiled=True)]
    all_to_all x1, blocking collectives: 27.5 us -> 22.4 us  [local(): lax.all_to_all(copies, ('zl', 'xhi', 'zh'), 0, 0, tiled=True)]
    ppermute x1, starting transfers between devices: 8.59 us -> 11.6 us  [local(): above = lax.ppermute(feats[:middle], Z, down)]
    ppermute x1, starting transfers between devices: 4.82 us -> 1.92 us  [local(): below = lax.ppermute(feats[middle:], Z, up)]
  transfers between devices with their start and end apart: 12 -> 17, of which waited for: 7 -> 7; matrix products, arithmetic and copies ran while one was open for 1% -> 3% of each run, Pallas kernels for 3% -> 9%
where the time goes in v7:
time: 153 us; the launch traced here: 151 us
  starting transfers between devices  82.9 us (54%)
  blocking collectives  22.4 us (15%)
  Pallas kernels  17.7 us (12%)
  waiting for transfers between devices  14 us (9%)
  local copies, waits for them, and re-layouts  11 us (7%)
  matrix products  2.17 us (1%)
    all_to_all x1, blocking collectives, local(): lax.all_to_all(copies, ('zl', 'xhi', 'zh'), 0, 0, tiled=True)  22.4 us
    pallas_call x6, Pallas kernels, kernel_call(): pl.pallas_call(body, out_shape=outs, in_specs=specs, out_specs=jax.tree.m...  17.7 us
    ppermute x1, starting transfers between devices, local(): above = lax.ppermute(feats[:middle], Z, down)  11.6 us
    ppermute x3, starting transfers between devices, local(): theirs = [lax.ppermute(block, 'core', other()) for block in mine]  8.83 us
    ppermute x2, starting transfers between devices, local(): lax.ppermute(w_in[0, :, part], (*Y, 'core'), perm)  8.58 us
    all_to_all x1, starting transfers between devices, sent_to_all(): lax.all_to_all(jnp.broadcast_to(value[None], (length, *value.shape)), axe...  7.85 us
    ppermute x1, starting transfers between devices, local(): outs_b = lax.ppermute(outs, 'core', other())  7.15 us
    all_to_all x1, starting transfers between devices, local(): blocks = lax.all_to_all(partial, ('xlo', 'yh'), 0, 0, tiled=True)  7.14 us
  transfers between devices with their start and end apart: 17, of which 7 were waited for; matrix products, arithmetic and copies ran while one was open for 3% of the time, Pallas kernels for 9%

profile of v7, /device:TPU:1, one launch (start us, length us, event | category | flops | bytes accessed | tf_op | source)
XLA Modules:
  0.0 150.7 jit_solution(17138726017392666468)
XLA Ops:
  0.0 2.5 %slice_bitcast_fusion.2 = (bf16[192,1536]{1,0:T(8,128)(2,1)}, bf16[192,1536]{1,0:T(8,128)(2,1)}) fusion(bf16[1,384,1536]{2,1,0:T(8,128)(2,1)} %param.5), kind=kLoop, calls=%fused_computation.8 | loop fusion | bytes 2359296 | tf_op jit(solution)/shard_map/slice | solution.py:212
  2.5 11.6 %collective-permute-start = (bf16[192,1536]{1,0:T(8,128)(2,1)}, bf16[192,1536]{1,0:T(8,128)(2,1)S(1)}, u32[]{:S(2)}, u32[]{:S(2)}) collective-permute-start(bf16[192,1536]{1,0:T(8,128)(2,1)} %get-tuple-element.14), channel_id=1, source_target_pairs={{0,14},{2,0},{4,2},{6,4},{8,6},{10,8},{12,10},{14,12},{1,15},{3,1}... | collective-permute-start | bytes 1769480 | tf_op jit(solution)/shard_map/ppermute | solution.py:211
  14.1 1.9 %collective-permute-start.1 = (bf16[192,1536]{1,0:T(8,128)(2,1)}, bf16[192,1536]{1,0:T(8,128)(2,1)}, u32[]{:S(2)}, u32[]{:S(2)}) collective-permute-start(bf16[192,1536]{1,0:T(8,128)(2,1)} %get-tuple-element.13), channel_id=1, source_target_pairs={{0,2},{2,4},{4,6},{6,8},{8,10},{10,12},{12,14},{14,0},{1,3},{3,5},... | collective-permute-start | bytes 1769480 | tf_op jit(solution)/shard_map/ppermute | solution.py:212
  16.0 2.9 %collective-permute-start.2 = (bf16[384,1536]{1,0:T(8,128)(2,1)S(1)}, bf16[384,1536]{1,0:T(8,128)(2,1)}, u32[]{:S(2)}, u32[]{:S(2)}) collective-permute-start(bf16[384,1536]{1,0:T(8,128)(2,1)S(1)} %bitcast.33), channel_id=1, source_target_pairs={{0,1},{1,0},{2,3},{3,2},{4,5},{5,4},{6,7},{7,6},{8,9},{9,8},{10,11... | collective-permute-start | bytes 3538952 | tf_op jit(solution)/shard_map/ppermute | solution.py:214
  19.0 0.2 fusion.3
  19.2 0.8 broadcast_in_dim.13
  20.0 7.9 %all-to-all-start = ((bf16[16,96,128]{2,1,0:T(8,128)(2,1)}), bf16[16,96,128]{2,1,0:T(8,128)(2,1)S(1)}, u32[]{:S(2)}, u32[]{:S(2)}) async-start(bf16[16,96,128]{2,1,0:T(8,128)(2,1)} %broadcast_in_dim.13), calls=%async_computation | async-start | bytes 786432 | tf_op jit(solution)/shard_map/all_to_all | solution.py:190
  27.8 0.0 collective-permute-done.refs_1_.refs_2_
  27.9 2.2 %collective-permute-start.3 = (bf16[192,1536]{1,0:T(8,128)(2,1)S(1)}, bf16[192,1536]{1,0:T(8,128)(2,1)}, u32[]{:S(2)}, u32[]{:S(2)}) collective-permute-start(bf16[192,1536]{1,0:T(8,128)(2,1)S(1)} %collective-permute-done.refs_1_.refs_2_), channel_id=1, source_target_pairs={{0,1},{1,0},{2,3},{3,2},{4,5},{5,4},{6,7},{7,6},{8,9},{9,8},{10,11... | collective-permute-start | bytes 1769480 | tf_op jit(solution)/shard_map/ppermute | solution.py:214
  30.1 1.3 collective-permute-done.1.refs_2_.refs_3_
  31.4 3.8 %collective-permute-start.4 = (bf16[192,1536]{1,0:T(8,128)(2,1)}, bf16[192,1536]{1,0:T(8,128)(2,1)}, u32[]{:S(2)}, u32[]{:S(2)}) collective-permute-start(bf16[192,1536]{1,0:T(8,128)(2,1)} %collective-permute-done.1.refs_2_.refs_3_), channel_id=1, source_target_pairs={{0,1},{1,0},{2,3},{3,2},{4,5},{5,4},{6,7},{7,6},{8,9},{9,8},{10,11... | collective-permute-start | bytes 1769480 | tf_op jit(solution)/shard_map/ppermute | solution.py:214
  35.2 1.0 slice_bitcast_fusion
  36.1 3.2 %collective-permute-start.10 = (bf16[256,1536]{1,0:T(8,128)(2,1)}, bf16[256,1536]{1,0:T(8,128)(2,1)}, u32[]{:S(2)}, u32[]{:S(2)}) collective-permute-start(bf16[256,1536]{1,0:T(8,128)(2,1)} %slice_bitcast_fusion), channel_id=1, source_target_pairs={{0,224},{1,33},{32,0},{33,65},{64,32},{65,97},{96,64},{97,129},{12... | collective-permute-start | bytes 2359304 | tf_op jit(solution)/shard_map/ppermute | solution.py:222
  39.3 0.3 all-to-all-done
  39.6 0.0 collective-permute-done.2.refs_3_.refs_4_
  39.6 0.7 copy-done.9
  40.3 6.6 %shard_map.57 = bf16[128,1664]{1,0:T(8,128)(2,1)} custom-call(bf16[1536,128]{1,0:T(8,128)(2,1)} %bitcast.34, bf16[384,1536]{1,0:T(8,128)(2,1)} %bitcast.31, bf16[192,1536]{1,0:T(8,128)(2,1)} %copy-done.10, bf16[192,1536]{1,0:T(8,128)(2,1)} %collective-permute-done.1.refs_2_.refs_3_, bf16[384,1536]{1,0:T(8,128)(2,1)} %collective-permute-done.2.refs_3_.refs_4_, ...), custom_call_target="tpu_custom_call" | custom-call | flops 1207959552 | bytes 5505024 | tf_op jit(solution)/shard_map/pallas_call | solution.py:22
  46.9 5.2 %all-to-all-start.1 = ((bf16[8,16,1664]{2,1,0:T(8,128)(2,1)}), bf16[8,16,1664]{2,1,0:T(8,128)(2,1)S(1)}, u32[]{:S(2)}, u32[]{:S(2)}) async-start(bf16[8,16,1664]{2,1,0:T(8,128)(2,1)} %bitcast.38), calls=%async_computation.1 | async-start | bytes 851968 | tf_op jit(solution)/shard_map/all_to_all | solution.py:250
  52.1 0.0 copy-start.6
  52.1 0.9 slice_bitcast_fusion.1
  53.1 3.3 %collective-permute-start.8 = (bf16[1536,256]{1,0:T(8,128)(2,1)}, bf16[1536,256]{1,0:T(8,128)(2,1)}, u32[]{:S(2)}, u32[]{:S(2)}) collective-permute-start(bf16[1536,256]{1,0:T(8,128)(2,1)} %slice_bitcast_fusion.1), channel_id=1, source_target_pairs={{0,224},{1,33},{32,0},{33,65},{64,32},{65,97},{96,64},{97,129},{12... | collective-permute-start | bytes 2359304 | tf_op jit(solution)/shard_map/ppermute | solution.py:221
  56.3 0.8 slice_bitcast_fusion.4
  57.2 3.3 %collective-permute-start.11 = (bf16[128,1536]{1,0:T(8,128)(2,1)}, bf16[128,1536]{1,0:T(8,128)(2,1)}, u32[]{:S(2)}, u32[]{:S(2)}) collective-permute-start(bf16[128,1536]{1,0:T(8,128)(2,1)} %slice_bitcast_fusion.4), channel_id=1, source_target_pairs={{0,32},{1,225},{32,64},{33,1},{64,96},{65,33},{96,128},{97,65},{12... | collective-permute-start | bytes 1179656 | tf_op jit(solution)/shard_map/ppermute | solution.py:222
  60.4 2.9 %all-to-all-done.1.received_ref = bf16[8,16,1664]{2,1,0:T(8,128)(2,1)S(1)} async-done(((bf16[8,16,1664]{2,1,0:T(8,128)(2,1)}), bf16[8,16,1664]{2,1,0:T(8,128)(2,1)S(1)}, u32[]{:S(2)}, u32[]{:S(2)}) %all-to-all-start.1) | async-done | bytes 426016 | tf_op jit(solution)/shard_map/all_to_all | solution.py:250
  63.3 0.9 shard_map.58
  64.2 0.7 copy-done.3
  65.0 6.1 %all-to-all-start.2 = ((bf16[8,16,1536]{2,1,0:T(8,128)(2,1)}), bf16[8,16,1536]{2,1,0:T(8,128)(2,1)S(1)}, u32[]{:S(2)}, u32[]{:S(2)}) async-start(bf16[8,16,1536]{2,1,0:T(8,128)(2,1)} %copy-done.3), calls=%async_computation.2 | async-start | bytes 786432 | tf_op jit(solution)/shard_map/all_to_all | solution.py:295
  71.0 5.3 %collective-permute-start.9 = (bf16[1536,128]{1,0:T(8,128)(2,1)S(1)}, bf16[1536,128]{1,0:T(8,128)(2,1)S(1)}, u32[]{:S(2)}, u32[]{:S(2)}) collective-permute-start(bf16[1536,128]{1,0:T(8,128)(2,1)S(1)} %slice_bitcast_fusion.5), channel_id=1, source_target_pairs={{0,32},{1,225},{32,64},{33,1},{64,96},{65,33},{96,128},{97,65},{12... | collective-permute-start | bytes 1179656 | tf_op jit(solution)/shard_map/ppermute | solution.py:221
  76.4 4.9 %shard_map.55 = (bf16[768,256]{1,0:T(8,128)(2,1)}, bf16[768,256]{1,0:T(8,128)(2,1)}) custom-call(bf16[1536,128]{1,0:T(8,128)(2,1)} %bitcast.35, bf16[384,1536]{1,0:T(8,128)(2,1)} %bitcast.32, bf16[192,1536]{1,0:T(8,128)(2,1)} %copy-done.10, bf16[192,1536]{1,0:T(8,128)(2,1)} %collective-permute-done.1.refs_2_.refs_3_, ...), custom_call_target="tpu_custom_call" | custom-call | flops 603979776 | bytes 4718592 | tf_op jit(solution)/shard_map/pallas_call | solution.py:22
  81.3 3.3 %collective-permute-start.5 = (bf16[768,256]{1,0:T(8,128)(2,1)}, bf16[768,256]{1,0:T(8,128)(2,1)S(1)}, u32[]{:S(2)}, u32[]{:S(2)}) collective-permute-start(bf16[768,256]{1,0:T(8,128)(2,1)} %get-tuple-element.10), channel_id=1, source_target_pairs={{0,1},{1,0},{2,3},{3,2},{4,5},{5,4},{6,7},{7,6},{8,9},{9,8},{10,11... | collective-permute-start | bytes 1179656 | tf_op jit(solution)/shard_map/ppermute | solution.py:265
  84.6 1.6 %collective-permute-done.9.refs_2_ = bf16[1536,128]{1,0:T(8,128)(2,1)S(1)} collective-permute-done((bf16[1536,128]{1,0:T(8,128)(2,1)S(1)}, bf16[1536,128]{1,0:T(8,128)(2,1)S(1)}, u32[]{:S(2)}, u32[]{:S(2)}) %collective-permute-start.9) | collective-permute-done | bytes 393248 | tf_op jit(solution)/shard_map/ppermute | solution.py:221
  86.2 0.7 copy-done.4
  87.0 1.0 copy-done.5
  88.0 3.5 %shard_map.59 = bf16[8,16,1536]{2,1,0:T(8,128)(2,1)} custom-call(bf16[8,16,1536]{2,1,0:T(8,128)(2,1)S(1)} %all-to-all-done.2.rows_ref, bf16[1536,384]{1,0:T(8,128)(2,1)S(1)} %bitcast.29, bf16[1536,256]{1,0:T(8,128)(2,1)} %collective-permute-done.8.refs_1_, bf16[1536,128]{1,0:T(8,128)(2,1)S(1)} %copy-done.5, bf16[384,1536]{1,0:T(8,128)(2,1)S(1)} %bitcast.30, ...), custom_call_target="tpu_custom_call" | custom-call | flops 603979776 | bytes 4718592 | tf_op jit(solution)/shard_map/pallas_call | solution.py:22
  91.5 7.1 %all-to-all-start.3 = ((bf16[8,16,1536]{2,1,0:T(8,128)(2,1)}), bf16[8,16,1536]{2,1,0:T(8,128)(2,1)S(1)}, u32[]{:S(2)}, u32[]{:S(2)}) async-start(bf16[8,16,1536]{2,1,0:T(8,128)(2,1)} %shard_map.59), calls=%async_computation.3 | async-start | bytes 786432 | tf_op jit(solution)/shard_map/all_to_all | solution.py:312
  98.6 1.0 fusion.16
  99.6 6.4 %collective-permute-start.7 = (bf16[192,512]{1,0:T(8,128)(2,1)S(1)}, bf16[192,512]{1,0:T(8,128)(2,1)S(1)}, u32[]{:S(2)}, u32[]{:S(2)}) collective-permute-start(bf16[192,512]{1,0:T(8,128)(2,1)S(1)} %pad_maximum_fusion.1), channel_id=1, source_target_pairs={{0,14},{2,0},{4,2},{6,4},{8,6},{10,8},{12,10},{14,12},{1,15},{3,1}... | collective-permute-start | bytes 589832 | tf_op jit(solution)/shard_map/ppermute | solution.py:268
  106.0 2.4 %collective-permute-start.6 = (bf16[192,512]{1,0:T(8,128)(2,1)S(1)}, bf16[192,512]{1,0:T(8,128)(2,1)S(1)}, u32[]{:S(2)}, u32[]{:S(2)}) collective-permute-start(bf16[192,512]{1,0:T(8,128)(2,1)S(1)} %pad_maximum_fusion), channel_id=1, source_target_pairs={{0,2},{2,4},{4,6},{6,8},{8,10},{10,12},{12,14},{14,0},{1,3},{3,5},... | collective-permute-start | bytes 589832 | tf_op jit(solution)/shard_map/ppermute | solution.py:267
  108.6 2.6 %collective-permute-done.7.up_ref = bf16[192,512]{1,0:T(8,128)(2,1)S(1)} collective-permute-done((bf16[192,512]{1,0:T(8,128)(2,1)S(1)}, bf16[192,512]{1,0:T(8,128)(2,1)S(1)}, u32[]{:S(2)}, u32[]{:S(2)}) %collective-permute-start.7) | collective-permute-done | bytes 196640 | tf_op jit(solution)/shard_map/ppermute | solution.py:268
  111.2 3.4 %collective-permute-done.6.low_ref = bf16[192,512]{1,0:T(8,128)(2,1)S(1)} collective-permute-done((bf16[192,512]{1,0:T(8,128)(2,1)S(1)}, bf16[192,512]{1,0:T(8,128)(2,1)S(1)}, u32[]{:S(2)}, u32[]{:S(2)}) %collective-permute-start.6) | collective-permute-done | bytes 196640 | tf_op jit(solution)/shard_map/ppermute | solution.py:267
  114.6 0.6 shard_map.56
  115.2 1.2 shard_map.60
  116.4 22.4 %all_to_all.25 = bf16[16,16,1536]{2,1,0:T(8,128)(2,1)S(1)} all-to-all(bf16[16,16,1536]{2,1,0:T(8,128)(2,1)S(1)} %shard_map.60), channel_id=1, replica_groups=mesh['xlo'=2,'yh'=4,'yl'=2,'xhi'=2,'zh'=4,'zl'=2,'core'=2] {'zl','xhi','..., dimensions={0} | all-to-all | bytes 1572864 | tf_op jit(solution)/shard_map/all_to_all | solution.py:325
  138.8 7.1 %collective-permute-start.12 = (bf16[256,1536]{1,0:T(8,128)(2,1)S(1)}, bf16[256,1536]{1,0:T(8,128)(2,1)S(1)}, u32[]{:S(2)}, u32[]{:S(2)}) collective-permute-start(bf16[256,1536]{1,0:T(8,128)(2,1)S(1)} %bitcast.36), channel_id=1, source_target_pairs={{0,1},{1,0},{2,3},{3,2},{4,5},{5,4},{6,7},{7,6},{8,9},{9,8},{10,11... | collective-permute-start | bytes 2359304 | tf_op jit(solution)/shard_map/ppermute | solution.py:326
  146.0 1.9 %collective-permute-done.12 = bf16[256,1536]{1,0:T(8,128)(2,1)S(1)} collective-permute-done((bf16[256,1536]{1,0:T(8,128)(2,1)S(1)}, bf16[256,1536]{1,0:T(8,128)(2,1)S(1)}, u32[]{:S(2)}, u32[]{:S(2)}) %collective-permute-start.12) | collective-permute-done | bytes 786464 | tf_op jit(solution)/shard_map/ppermute | solution.py:326
  147.9 0.5 fusion.18
  148.4 0.8 copy-done.8
  149.2 1.5 fusion.2
  (35 shorter events, 0.2 us)
Async XLA Ops:
  0.0 18.9 %copy-start = (bf16[96,512]{1,0:T(8,128)(2,1)S(1)}, bf16[96,512]{1,0:T(8,128)(2,1)}, u32[]{:S(2)}) copy-start(bf16[96,512]{1,0:T(8,128)(2,1)} %param.6) | copy-start | bytes 294916
  0.0 16.0 %copy-start.7 = (bf16[1,384,1536]{2,1,0:T(8,128)(2,1)S(1)}, bf16[1,384,1536]{2,1,0:T(8,128)(2,1)}, u32[]{:S(2)}) copy-start(bf16[1,384,1536]{2,1,0:T(8,128)(2,1)} %param.5) | copy-start | bytes 3538948
  2.5 32.7 %copy-start.2 = (bf16[1,384,1536]{2,1,0:T(8,128)(2,1)S(1)}, bf16[1,384,1536]{2,1,0:T(8,128)(2,1)}, u32[]{:S(2)}) copy-start(bf16[1,384,1536]{2,1,0:T(8,128)(2,1)} %param.9) | copy-start | bytes 3538948
  2.5 25.4 %collective-permute-start = (bf16[192,1536]{1,0:T(8,128)(2,1)}, bf16[192,1536]{1,0:T(8,128)(2,1)S(1)}, u32[]{:S(2)}, u32[]{:S(2)}) collective-permute-start(bf16[192,1536]{1,0:T(8,128)(2,1)} %get-tuple-element.14), channel_id=1, source_target_pairs={{0,14},{2,0},{4,2},{6,4},{8,6},{10,8},{12,10},{14,12},{1,15},{3,1}... | collective-permute-start | bytes 1769480 | tf_op jit(solution)/shard_map/ppermute | solution.py:211
  14.1 17.3 %collective-permute-start.1 = (bf16[192,1536]{1,0:T(8,128)(2,1)}, bf16[192,1536]{1,0:T(8,128)(2,1)}, u32[]{:S(2)}, u32[]{:S(2)}) collective-permute-start(bf16[192,1536]{1,0:T(8,128)(2,1)} %get-tuple-element.13), channel_id=1, source_target_pairs={{0,2},{2,4},{4,6},{6,8},{8,10},{10,12},{12,14},{14,0},{1,3},{3,5},... | collective-permute-start | bytes 1769480 | tf_op jit(solution)/shard_map/ppermute | solution.py:212
  16.0 23.6 %collective-permute-start.2 = (bf16[384,1536]{1,0:T(8,128)(2,1)S(1)}, bf16[384,1536]{1,0:T(8,128)(2,1)}, u32[]{:S(2)}, u32[]{:S(2)}) collective-permute-start(bf16[384,1536]{1,0:T(8,128)(2,1)S(1)} %bitcast.33), channel_id=1, source_target_pairs={{0,1},{1,0},{2,3},{3,2},{4,5},{5,4},{6,7},{7,6},{8,9},{9,8},{10,11... | collective-permute-start | bytes 3538952 | tf_op jit(solution)/shard_map/ppermute | solution.py:214
  20.0 19.6 %all-to-all-start = ((bf16[16,96,128]{2,1,0:T(8,128)(2,1)}), bf16[16,96,128]{2,1,0:T(8,128)(2,1)S(1)}, u32[]{:S(2)}, u32[]{:S(2)}) async-start(bf16[16,96,128]{2,1,0:T(8,128)(2,1)} %broadcast_in_dim.13), calls=%async_computation | async-start | bytes 786432 | tf_op jit(solution)/shard_map/all_to_all | solution.py:190
  27.8 11.8 %copy-start.10 = (bf16[192,1536]{1,0:T(8,128)(2,1)}, bf16[192,1536]{1,0:T(8,128)(2,1)S(1)}, u32[]{:S(2)}) copy-start(bf16[192,1536]{1,0:T(8,128)(2,1)S(1)} %collective-permute-done.refs_1_.refs_2_) | copy-start | bytes 1769476
  27.9 11.7 %collective-permute-start.3 = (bf16[192,1536]{1,0:T(8,128)(2,1)S(1)}, bf16[192,1536]{1,0:T(8,128)(2,1)}, u32[]{:S(2)}, u32[]{:S(2)}) collective-permute-start(bf16[192,1536]{1,0:T(8,128)(2,1)S(1)} %collective-permute-done.refs_1_.refs_2_), channel_id=1, source_target_pairs={{0,1},{1,0},{2,3},{3,2},{4,5},{5,4},{6,7},{7,6},{8,9},{9,8},{10,11... | collective-permute-start | bytes 1769480 | tf_op jit(solution)/shard_map/ppermute | solution.py:214
  31.4 8.2 %collective-permute-start.4 = (bf16[192,1536]{1,0:T(8,128)(2,1)}, bf16[192,1536]{1,0:T(8,128)(2,1)}, u32[]{:S(2)}, u32[]{:S(2)}) collective-permute-start(bf16[192,1536]{1,0:T(8,128)(2,1)} %collective-permute-done.1.refs_2_.refs_3_), channel_id=1, source_target_pairs={{0,1},{1,0},{2,3},{3,2},{4,5},{5,4},{6,7},{7,6},{8,9},{9,8},{10,11... | collective-permute-start | bytes 1769480 | tf_op jit(solution)/shard_map/ppermute | solution.py:214
  36.1 50.8 %collective-permute-start.10 = (bf16[256,1536]{1,0:T(8,128)(2,1)}, bf16[256,1536]{1,0:T(8,128)(2,1)}, u32[]{:S(2)}, u32[]{:S(2)}) collective-permute-start(bf16[256,1536]{1,0:T(8,128)(2,1)} %slice_bitcast_fusion), channel_id=1, source_target_pairs={{0,224},{1,33},{32,0},{33,65},{64,32},{65,97},{96,64},{97,129},{12... | collective-permute-start | bytes 2359304 | tf_op jit(solution)/shard_map/ppermute | solution.py:222
  39.6 0.7 copy-start.9
  40.3 11.8 %copy-start.1 = (bf16[1,1536,384]{2,1,0:T(8,128)(2,1)S(1)}, bf16[1,1536,384]{2,1,0:T(8,128)(2,1)}, u32[]{:S(2)}) copy-start(bf16[1,1536,384]{2,1,0:T(8,128)(2,1)} %param.8) | copy-start | bytes 3538948
  46.9 16.4 %all-to-all-start.1 = ((bf16[8,16,1664]{2,1,0:T(8,128)(2,1)}), bf16[8,16,1664]{2,1,0:T(8,128)(2,1)S(1)}, u32[]{:S(2)}, u32[]{:S(2)}) async-start(bf16[8,16,1664]{2,1,0:T(8,128)(2,1)} %bitcast.38), calls=%async_computation.1 | async-start | bytes 851968 | tf_op jit(solution)/shard_map/all_to_all | solution.py:250
  52.1 11.2 %copy-start.6 = (f32[1,1536]{1,0:T(1,128)S(1)}, f32[1,1536]{1,0:T(1,128)}, u32[]{:S(2)}) copy-start(f32[1,1536]{1,0:T(1,128)} %gain_ref.1) | copy-start | bytes 18436
  53.1 33.9 %collective-permute-start.8 = (bf16[1536,256]{1,0:T(8,128)(2,1)}, bf16[1536,256]{1,0:T(8,128)(2,1)}, u32[]{:S(2)}, u32[]{:S(2)}) collective-permute-start(bf16[1536,256]{1,0:T(8,128)(2,1)} %slice_bitcast_fusion.1), channel_id=1, source_target_pairs={{0,224},{1,33},{32,0},{33,65},{64,32},{65,97},{96,64},{97,129},{12... | collective-permute-start | bytes 2359304 | tf_op jit(solution)/shard_map/ppermute | solution.py:221
  57.2 27.4 %collective-permute-start.11 = (bf16[128,1536]{1,0:T(8,128)(2,1)}, bf16[128,1536]{1,0:T(8,128)(2,1)}, u32[]{:S(2)}, u32[]{:S(2)}) collective-permute-start(bf16[128,1536]{1,0:T(8,128)(2,1)} %slice_bitcast_fusion.4), channel_id=1, source_target_pairs={{0,32},{1,225},{32,64},{33,1},{64,96},{65,33},{96,128},{97,65},{12... | collective-permute-start | bytes 1179656 | tf_op jit(solution)/shard_map/ppermute | solution.py:222
  64.2 0.8 copy-start.3
  65.0 22.0 %all-to-all-start.2 = ((bf16[8,16,1536]{2,1,0:T(8,128)(2,1)}), bf16[8,16,1536]{2,1,0:T(8,128)(2,1)S(1)}, u32[]{:S(2)}, u32[]{:S(2)}) async-start(bf16[8,16,1536]{2,1,0:T(8,128)(2,1)} %copy-done.3), calls=%async_computation.2 | async-start | bytes 786432 | tf_op jit(solution)/shard_map/all_to_all | solution.py:295
  71.0 15.2 %collective-permute-start.9 = (bf16[1536,128]{1,0:T(8,128)(2,1)S(1)}, bf16[1536,128]{1,0:T(8,128)(2,1)S(1)}, u32[]{:S(2)}, u32[]{:S(2)}) collective-permute-start(bf16[1536,128]{1,0:T(8,128)(2,1)S(1)} %slice_bitcast_fusion.5), channel_id=1, source_target_pairs={{0,32},{1,225},{32,64},{33,1},{64,96},{65,33},{96,128},{97,65},{12... | collective-permute-start | bytes 1179656 | tf_op jit(solution)/shard_map/ppermute | solution.py:221
  81.3 5.7 %collective-permute-start.5 = (bf16[768,256]{1,0:T(8,128)(2,1)}, bf16[768,256]{1,0:T(8,128)(2,1)S(1)}, u32[]{:S(2)}, u32[]{:S(2)}) collective-permute-start(bf16[768,256]{1,0:T(8,128)(2,1)} %get-tuple-element.10), channel_id=1, source_target_pairs={{0,1},{1,0},{2,3},{3,2},{4,5},{5,4},{6,7},{7,6},{8,9},{9,8},{10,11... | collective-permute-start | bytes 1179656 | tf_op jit(solution)/shard_map/ppermute | solution.py:265
  86.2 0.7 copy-start.4
  87.0 1.0 copy-start.5
  91.5 17.0 %copy-start.11 = (bf16[768,256]{1,0:T(8,128)(2,1)S(1)}, bf16[768,256]{1,0:T(8,128)(2,1)}, u32[]{:S(2)}) copy-start(bf16[768,256]{1,0:T(8,128)(2,1)} %get-tuple-element.9) | copy-start | bytes 1179652
  91.5 23.7 %all-to-all-start.3 = ((bf16[8,16,1536]{2,1,0:T(8,128)(2,1)}), bf16[8,16,1536]{2,1,0:T(8,128)(2,1)S(1)}, u32[]{:S(2)}, u32[]{:S(2)}) async-start(bf16[8,16,1536]{2,1,0:T(8,128)(2,1)} %shard_map.59), calls=%async_computation.3 | async-start | bytes 786432 | tf_op jit(solution)/shard_map/all_to_all | solution.py:312
  99.6 11.5 %collective-permute-start.7 = (bf16[192,512]{1,0:T(8,128)(2,1)S(1)}, bf16[192,512]{1,0:T(8,128)(2,1)S(1)}, u32[]{:S(2)}, u32[]{:S(2)}) collective-permute-start(bf16[192,512]{1,0:T(8,128)(2,1)S(1)} %pad_maximum_fusion.1), channel_id=1, source_target_pairs={{0,14},{2,0},{4,2},{6,4},{8,6},{10,8},{12,10},{14,12},{1,15},{3,1}... | collective-permute-start | bytes 589832 | tf_op jit(solution)/shard_map/ppermute | solution.py:268
  106.0 8.6 %collective-permute-start.6 = (bf16[192,512]{1,0:T(8,128)(2,1)S(1)}, bf16[192,512]{1,0:T(8,128)(2,1)S(1)}, u32[]{:S(2)}, u32[]{:S(2)}) collective-permute-start(bf16[192,512]{1,0:T(8,128)(2,1)S(1)} %pad_maximum_fusion), channel_id=1, source_target_pairs={{0,2},{2,4},{4,6},{6,8},{8,10},{10,12},{12,14},{14,0},{1,3},{3,5},... | collective-permute-start | bytes 589832 | tf_op jit(solution)/shard_map/ppermute | solution.py:267
  138.8 9.0 %collective-permute-start.12 = (bf16[256,1536]{1,0:T(8,128)(2,1)S(1)}, bf16[256,1536]{1,0:T(8,128)(2,1)S(1)}, u32[]{:S(2)}, u32[]{:S(2)}) collective-permute-start(bf16[256,1536]{1,0:T(8,128)(2,1)S(1)} %bitcast.36), channel_id=1, source_target_pairs={{0,1},{1,0},{2,3},{3,2},{4,5},{5,4},{6,7},{7,6},{8,9},{9,8},{10,11... | collective-permute-start | bytes 2359304 | tf_op jit(solution)/shard_map/ppermute | solution.py:326
  147.9 1.3 copy-start.8

commit v8 on v7

--- a/solution.py
+++ b/solution.py
@@ -93,50 +93,20 @@
         copy.wait()
 
 
-def exps_kernel(columns_ref, *refs):
-    feats, (own_ref, answer_ref) = refs[:6], refs[6:]
-    columns = columns_ref[...]
-    slots = columns.shape[1]
-    for k, out_ref in enumerate((own_ref, answer_ref)):
-        offset = 0
-        for feats_ref in feats[3 * k : 3 * k + 3]:
-            rows = feats_ref.shape[0]
-            part = slice(offset, offset + rows)
-            offset += rows
-            logits = jnp.dot(feats_ref[...], columns, preferred_element_type=F32)
-            high = jnp.max(logits, axis=1, keepdims=True)
-            exps = jnp.exp(logits - high)
-            total = jnp.sum(exps, axis=1, keepdims=True)
-            out_ref[part, :slots] = exps.astype(BF16)
-            lanes = (rows, EXTRA)
-            out_ref[part, slots:] = in_lanes([jnp.broadcast_to(high, lanes), jnp.broadcast_to(total, lanes)])
-
-
-def weights_kernel(side_ref, own_ref, core_ref, low_ref, up_ref, own_weights_ref, core_weights_ref):
-    rows, wide = low_ref.shape[0] * 2, own_ref.shape[1]
-    slots = wide - EXTRA
-    half = rows // 2
-    side = side_ref[0]
-    for k, given_ref in enumerate((low_ref, up_ref)):
-        part = slice(k * half, (k + 1) * half)
-        blocks = [own_ref[part, :], core_ref[part, :], given_ref[:, :wide], given_ref[:, wide:]]
-        lane = lax.broadcasted_iota(jnp.int32, (half, EXTRA), 1)
-        stats = [block[:, slots:].astype(F32) for block in blocks]
-        highs = [jnp.sum(jnp.where(lane < 3, s, 0.0), axis=1, keepdims=True) for s in stats]
-        sums = [jnp.sum(jnp.where(lane < 3, 0.0, s), axis=1, keepdims=True) for s in stats]
-        top = jnp.maximum(jnp.maximum(highs[0], highs[1]), jnp.maximum(highs[2], highs[3]))
-        factors = [jnp.exp(high - top) for high in highs]
-        total = sums[0] * factors[0] + sums[1] * factors[1] + sums[2] * factors[2] + sums[3] * factors[3]
-        scaled = [
-            (block[:, :slots].astype(F32) * (factor / total)).astype(BF16)
-            for block, factor in zip(blocks, factors)
-        ]
-        here = pl.ds(pl.multiple_of(side * slots, slots), slots)
-        there = pl.ds(pl.multiple_of((1 - side) * slots, slots), slots)
-        own_weights_ref[part, here] = scaled[0]
-        core_weights_ref[part, here] = scaled[1]
-        own_weights_ref[part, there] = scaled[2]
-        core_weights_ref[part, there] = scaled[3]
+def weights_kernel(side_ref, feats_ref, here_ref, there_ref, here_b_ref, there_b_ref, own_ref, core_ref):
+    slots = here_ref.shape[1]
+    feats, side = feats_ref[...], side_ref[0]
+    columns = (here_ref, there_ref, here_b_ref, there_b_ref)
+    logits = [jnp.dot(feats, ref[...], preferred_element_type=F32) for ref in columns]
+    tops = [jnp.max(one, axis=1, keepdims=True) for one in logits]
+    top = jnp.maximum(jnp.maximum(tops[0], tops[1]), jnp.maximum(tops[2], tops[3]))
+    exps = [jnp.exp(one - top) for one in logits]
+    sums = [jnp.sum(one, axis=1, keepdims=True) for one in exps]
+    scale = 1.0 / (sums[0] + sums[1] + sums[2] + sums[3])
+    here = pl.ds(pl.multiple_of(side * slots, slots), slots)
+    there = pl.ds(pl.multiple_of((1 - side) * slots, slots), slots)
+    for k, (ref, place) in enumerate(((own_ref, here), (own_ref, there), (core_ref, here), (core_ref, there))):
+        ref[:, place] = (exps[k] * scale).astype(BF16)
 
 
 def pool_kernel(received_ref, gain_ref, copies_hbm, slots_ref, semaphores):
@@ -155,7 +125,7 @@
 
 
 def expert_kernel(rows_ref, *refs):
-    sources, before_hbm, partial_ref, targets, semaphores = refs[:6], refs[6], refs[7], refs[8:14], refs[14]
+    sources, partial_ref, targets, semaphores = refs[:6], refs[8], refs[9:15], refs[15]
     rows = rows_ref[...].reshape(-1, rows_ref.shape[-1])
     width = rows.shape[1]
     loads = [started(source, target, semaphores, k) for k, (source, target) in enumerate(zip(sources, targets))]
@@ -211,7 +181,7 @@
     above = lax.ppermute(feats[:middle], Z, down)
     below = lax.ppermute(feats[middle:], Z, up)
     mine = [feats, above, below]
-    theirs = [lax.ppermute(block, "core", other()) for block in mine]
+    theirs = [lax.ppermute(block, "core", other()) for block in (feats, above, below)]
 
     ring = lax.axis_size(Y)
     most = [(2 * k + c, (k + 2 * c - 1) % ring * 2 + c) for k in range(ring) for c in range(2)]
@@ -251,33 +221,22 @@
         message.reshape(owners, per_owner, width + EXTRA), ("xhi", "zh"), 0, 0, tiled=True
     )
 
-    exps, answer = kernel_call(
-        exps_kernel,
-        (shape((2 * count, quarter + EXTRA), BF16), shape((2 * count, quarter + EXTRA), BF16)),
-        8 * count * width * quarter,
-        8 * count * width,
-        [VMEM] * 7,
-        columns,
-        *mine,
-        *theirs,
-        room=58,
-    )
-    exps_b = lax.ppermute(answer, "core", other())
-    first, second = slice(count, count + middle), slice(count + middle, 2 * count)
-    low = lax.ppermute(jnp.concatenate([exps[first], exps_b[first]], axis=1), Z, up)
-    high = lax.ppermute(jnp.concatenate([exps[second], exps_b[second]], axis=1), Z, down)
+    columns_b = lax.ppermute(columns, "core", other())
+    far = lax.ppermute(columns, Z, down)
+    far_b = lax.ppermute(columns_b, Z, up)
     weights, weights_b = kernel_call(
         weights_kernel,
         (shape((count, 2 * quarter), BF16), shape((count, 2 * quarter), BF16)),
-        32 * count * quarter,
-        16 * count * quarter,
-        [pl.BlockSpec(memory_space=pltpu.SMEM), VMEM, VMEM, VMEM, VMEM],
+        8 * count * width * quarter,
+        2 * count * width + 8 * width * quarter,
+        [pl.BlockSpec(memory_space=pltpu.SMEM), *[VMEM] * 5],
         jnp.full((1,), side, jnp.int32),
-        exps[:count],
-        exps_b[:count],
-        low,
-        high,
-        room=12,
+        feats,
+        columns,
+        far,
+        columns_b,
+        far_b,
+        room=58,
     )
 
     slots = kernel_call(
@@ -298,16 +257,17 @@
         shape((groups, per_owner, width), BF16),
         8 * groups * per_owner * width * hidden_units,
         8 * width * hidden_units,
-        [VMEM, HBM, HBM, HBM, HBM, HBM, HBM, HBM],
+        [VMEM, *[HBM] * 8],
         rows,
         *given_in,
         *given_out,
-        exps_b,
+        far,
+        far_b,
         scratch=[
             *[pltpu.VMEM(block.shape, BF16) for block in given_in + given_out],
             pltpu.SemaphoreType.DMA((6,)),
         ],
-        room=48,
+        room=50,
     )
     blocks = lax.all_to_all(partial, ("xlo", "yh"), 0, 0, tiled=True)
     copies = kernel_call(

time: 153 us -> 160 us (1.046)
  waiting for transfers between devices: 14 us -> 19.9 us
  blocking collectives: 22.4 us -> 27.9 us
  starting transfers between devices: 82.9 us -> 79.1 us
    all_to_all x1, waiting for transfers between devices: 0.01 us -> 5.63 us  [local(): blocks = lax.all_to_all(partial, ('xlo', 'yh'), 0, 0, tiled=True)]
    all_to_all x1, blocking collectives: 22.4 us -> 27.9 us  [local(): lax.all_to_all(copies, ('zl', 'xhi', 'zh'), 0, 0, tiled=True)]
    ppermute x6, waiting for transfers between devices: 6.06 us -> 10.7 us  [the longest x1 6.95 us: local(): far = lax.ppermute(columns, Z, down)]
    all_to_all x1, starting transfers between devices: 7.14 us -> 3.46 us  [local(): blocks = lax.all_to_all(partial, ('xlo', 'yh'), 0, 0, tiled=True)]
    all_to_all x1, waiting for transfers between devices: 2.89 us -> 0.01 us  [local(): lax.all_to_all(message.reshape(owners, per_owner, width + EXTRA), ('xhi',...]
    all_to_all x1, starting transfers between devices: 6.06 us -> 4.44 us  [local(): rows = lax.all_to_all(slots, ('xlo', 'yh'), 0, 0, tiled=True)]
    pallas_call x6 -> x5, Pallas kernels: 17.7 us -> 16.9 us  [kernel_call(): pl.pallas_call(body, out_shape=outs, in_specs=specs, out_specs=jax.tree.m...]
    unnamed x24 -> x28, local copies, waits for them, and re-layouts: 4.01 us -> 3.76 us
  transfers between devices with their start and end apart: 17 -> 17, of which waited for: 7 -> 6; matrix products, arithmetic and copies ran while one was open for 3% -> 3% of each run, Pallas kernels for 9% -> 8%
where the time goes in v8:
time: 160 us; the launch traced here: 157 us
  starting transfers between devices  79.1 us (49%)
  blocking collectives  27.9 us (17%)
  waiting for transfers between devices  19.9 us (12%)
  Pallas kernels  16.9 us (11%)
  local copies, waits for them, and re-layouts  10.9 us (7%)
  matrix products  2.16 us (1%)
    all_to_all x1, blocking collectives, local(): lax.all_to_all(copies, ('zl', 'xhi', 'zh'), 0, 0, tiled=True)  27.9 us
    pallas_call x5, Pallas kernels, kernel_call(): pl.pallas_call(body, out_shape=outs, in_specs=specs, out_specs=jax.tree.m...  16.9 us
    ppermute x1, starting transfers between devices, local(): above = lax.ppermute(feats[:middle], Z, down)  11.6 us
    ppermute x3, starting transfers between devices, local(): lax.ppermute(block, 'core', other())  8.83 us
    ppermute x2, starting transfers between devices, local(): lax.ppermute(w_in[0, :, part], (*Y, 'core'), perm)  8.59 us
    all_to_all x1, starting transfers between devices, sent_to_all(): lax.all_to_all(jnp.broadcast_to(value[None], (length, *value.shape)), axe...  7.9 us
    ppermute x1, starting transfers between devices, local(): outs_b = lax.ppermute(outs, 'core', other())  7.12 us
    ppermute x1, waiting for transfers between devices, local(): far = lax.ppermute(columns, Z, down)  6.95 us
  transfers between devices with their start and end apart: 17, of which 6 were waited for; matrix products, arithmetic and copies ran while one was open for 3% of the time, Pallas kernels for 8%

profile of v8, /device:TPU:1, one launch (start us, length us, event | category | flops | bytes accessed | tf_op | source)
XLA Modules:
  0.0 157.3 jit_solution(9367151020471106141)
XLA Ops:
  0.0 2.5 %slice_bitcast_fusion.2 = (bf16[192,1536]{1,0:T(8,128)(2,1)}, bf16[192,1536]{1,0:T(8,128)(2,1)}) fusion(bf16[1,384,1536]{2,1,0:T(8,128)(2,1)} %param.5), kind=kLoop, calls=%fused_computation.8 | loop fusion | bytes 2359296 | tf_op jit(solution)/shard_map/slice | solution.py:182
  2.5 11.6 %collective-permute-start.3 = (bf16[192,1536]{1,0:T(8,128)(2,1)}, bf16[192,1536]{1,0:T(8,128)(2,1)S(1)}, u32[]{:S(2)}, u32[]{:S(2)}) collective-permute-start(bf16[192,1536]{1,0:T(8,128)(2,1)} %get-tuple-element.10), channel_id=1, source_target_pairs={{0,14},{2,0},{4,2},{6,4},{8,6},{10,8},{12,10},{14,12},{1,15},{3,1}... | collective-permute-start | bytes 1769480 | tf_op jit(solution)/shard_map/ppermute | solution.py:181
  14.1 1.9 %collective-permute-start.4 = (bf16[192,1536]{1,0:T(8,128)(2,1)}, bf16[192,1536]{1,0:T(8,128)(2,1)}, u32[]{:S(2)}, u32[]{:S(2)}) collective-permute-start(bf16[192,1536]{1,0:T(8,128)(2,1)} %get-tuple-element.9), channel_id=1, source_target_pairs={{0,2},{2,4},{4,6},{6,8},{8,10},{10,12},{12,14},{14,0},{1,3},{3,5},... | collective-permute-start | bytes 1769480 | tf_op jit(solution)/shard_map/ppermute | solution.py:182
  16.0 2.9 %collective-permute-start.5 = (bf16[384,1536]{1,0:T(8,128)(2,1)S(1)}, bf16[384,1536]{1,0:T(8,128)(2,1)}, u32[]{:S(2)}, u32[]{:S(2)}) collective-permute-start(bf16[384,1536]{1,0:T(8,128)(2,1)S(1)} %bitcast.31), channel_id=1, source_target_pairs={{0,1},{1,0},{2,3},{3,2},{4,5},{5,4},{6,7},{7,6},{8,9},{9,8},{10,11... | collective-permute-start | bytes 3538952 | tf_op jit(solution)/shard_map/ppermute | solution.py:184
  19.0 0.2 fusion.3
  19.2 0.8 broadcast_in_dim.13
  20.0 7.9 %all-to-all-start = ((bf16[16,96,128]{2,1,0:T(8,128)(2,1)}), bf16[16,96,128]{2,1,0:T(8,128)(2,1)}, u32[]{:S(2)}, u32[]{:S(2)}) async-start(bf16[16,96,128]{2,1,0:T(8,128)(2,1)} %broadcast_in_dim.13), calls=%async_computation | async-start | bytes 786432 | tf_op jit(solution)/shard_map/all_to_all | solution.py:160
  27.9 2.2 %collective-permute-start.6 = (bf16[192,1536]{1,0:T(8,128)(2,1)S(1)}, bf16[192,1536]{1,0:T(8,128)(2,1)}, u32[]{:S(2)}, u32[]{:S(2)}) collective-permute-start(bf16[192,1536]{1,0:T(8,128)(2,1)S(1)} %collective-permute-done.3.refs_2_), channel_id=1, source_target_pairs={{0,1},{1,0},{2,3},{3,2},{4,5},{5,4},{6,7},{7,6},{8,9},{9,8},{10,11... | collective-permute-start | bytes 1769480 | tf_op jit(solution)/shard_map/ppermute | solution.py:184
  30.1 1.3 collective-permute-done.4.refs_3_
  31.4 3.8 %collective-permute-start.7 = (bf16[192,1536]{1,0:T(8,128)(2,1)}, bf16[192,1536]{1,0:T(8,128)(2,1)}, u32[]{:S(2)}, u32[]{:S(2)}) collective-permute-start(bf16[192,1536]{1,0:T(8,128)(2,1)} %collective-permute-done.4.refs_3_), channel_id=1, source_target_pairs={{0,1},{1,0},{2,3},{3,2},{4,5},{5,4},{6,7},{7,6},{8,9},{9,8},{10,11... | collective-permute-start | bytes 1769480 | tf_op jit(solution)/shard_map/ppermute | solution.py:184
  35.2 0.9 slice_bitcast_fusion
  36.1 3.2 %collective-permute-start.10 = (bf16[256,1536]{1,0:T(8,128)(2,1)}, bf16[256,1536]{1,0:T(8,128)(2,1)S(1)}, u32[]{:S(2)}, u32[]{:S(2)}) collective-permute-start(bf16[256,1536]{1,0:T(8,128)(2,1)} %slice_bitcast_fusion), channel_id=1, source_target_pairs={{0,224},{1,33},{32,0},{33,65},{64,32},{65,97},{96,64},{97,129},{12... | collective-permute-start | bytes 2359304 | tf_op jit(solution)/shard_map/ppermute | solution.py:192
  39.3 0.4 all-to-all-done
  39.7 0.0 collective-permute-done.6.refs_5_
  39.7 0.0 collective-permute-done.7.refs_6_
  39.7 0.0 copy-start.10
  39.7 6.6 %shard_map.56 = bf16[128,1664]{1,0:T(8,128)(2,1)} custom-call(bf16[1536,128]{1,0:T(8,128)(2,1)} %bitcast.3.here_ref.refs_0_, bf16[384,1536]{1,0:T(8,128)(2,1)} %bitcast.29, bf16[192,1536]{1,0:T(8,128)(2,1)} %copy-done.12, bf16[192,1536]{1,0:T(8,128)(2,1)} %collective-permute-done.4.refs_3_, bf16[384,1536]{1,0:T(8,128)(2,1)} %collective-permute-done.5.refs_4_, ...), custom_call_target="tpu_custom_call" | custom-call | flops 1207959552 | bytes 5505024 | tf_op jit(solution)/shard_map/pallas_call | solution.py:22
  46.3 5.2 %all-to-all-start.1 = ((bf16[8,16,1664]{2,1,0:T(8,128)(2,1)}), bf16[8,16,1664]{2,1,0:T(8,128)(2,1)S(1)}, u32[]{:S(2)}, u32[]{:S(2)}) async-start(bf16[8,16,1664]{2,1,0:T(8,128)(2,1)} %bitcast.36), calls=%async_computation.1 | async-start | bytes 851968 | tf_op jit(solution)/shard_map/all_to_all | solution.py:220
  51.5 0.0 copy-start.7
  51.5 0.9 slice_bitcast_fusion.1
  52.4 3.3 %collective-permute-start.8 = (bf16[1536,256]{1,0:T(8,128)(2,1)}, bf16[1536,256]{1,0:T(8,128)(2,1)S(1)}, u32[]{:S(2)}, u32[]{:S(2)}) collective-permute-start(bf16[1536,256]{1,0:T(8,128)(2,1)} %slice_bitcast_fusion.1), channel_id=1, source_target_pairs={{0,224},{1,33},{32,0},{33,65},{64,32},{65,97},{96,64},{97,129},{12... | collective-permute-start | bytes 2359304 | tf_op jit(solution)/shard_map/ppermute | solution.py:191
  55.7 1.0 slice_bitcast_fusion.4
  56.8 3.3 %collective-permute-start.11 = (bf16[128,1536]{1,0:T(8,128)(2,1)S(1)}, bf16[128,1536]{1,0:T(8,128)(2,1)S(1)}, u32[]{:S(2)}, u32[]{:S(2)}) collective-permute-start(bf16[128,1536]{1,0:T(8,128)(2,1)S(1)} %slice_bitcast_fusion.4), channel_id=1, source_target_pairs={{0,32},{1,225},{32,64},{33,1},{64,96},{65,33},{96,128},{97,65},{12... | collective-permute-start | bytes 1179656 | tf_op jit(solution)/shard_map/ppermute | solution.py:192
  60.0 4.3 %collective-permute-start.1 = (bf16[1536,128]{1,0:T(8,128)(2,1)}, bf16[1536,128]{1,0:T(8,128)(2,1)}, u32[]{:S(2)}, u32[]{:S(2)}) collective-permute-start(bf16[1536,128]{1,0:T(8,128)(2,1)} %bitcast.3.here_ref.refs_0_), channel_id=1, source_target_pairs={{0,1},{1,0},{2,3},{3,2},{4,5},{5,4},{6,7},{7,6},{8,9},{9,8},{10,11... | collective-permute-start | bytes 1179656 | tf_op jit(solution)/shard_map/ppermute | solution.py:224
  64.4 1.1 shard_map.57
  65.5 4.4 %all-to-all-start.2 = ((bf16[8,16,1536]{2,1,0:T(8,128)(2,1)}), bf16[8,16,1536]{2,1,0:T(8,128)(2,1)S(1)}, u32[]{:S(2)}, u32[]{:S(2)}) async-start(bf16[8,16,1536]{2,1,0:T(8,128)(2,1)} %shard_map.57), calls=%async_computation.2 | async-start | bytes 786432 | tf_op jit(solution)/shard_map/all_to_all | solution.py:254
  69.9 1.0 slice_bitcast_fusion.5
  70.9 5.3 %collective-permute-start.9 = (bf16[1536,128]{1,0:T(8,128)(2,1)S(1)}, bf16[1536,128]{1,0:T(8,128)(2,1)S(1)}, u32[]{:S(2)}, u32[]{:S(2)}) collective-permute-start(bf16[1536,128]{1,0:T(8,128)(2,1)S(1)} %slice_bitcast_fusion.5), channel_id=1, source_target_pairs={{0,32},{1,225},{32,64},{33,1},{64,96},{65,33},{96,128},{97,65},{12... | collective-permute-start | bytes 1179656 | tf_op jit(solution)/shard_map/ppermute | solution.py:191
  76.3 6.9 %collective-permute-start = (bf16[1536,128]{1,0:T(8,128)(2,1)}, bf16[1536,128]{1,0:T(8,128)(2,1)S(1)}, u32[]{:S(2)}, u32[]{:S(2)}) collective-permute-start(bf16[1536,128]{1,0:T(8,128)(2,1)} %bitcast.3.here_ref.refs_0_), channel_id=1, source_target_pairs={{0,14},{2,0},{4,2},{6,4},{8,6},{10,8},{12,10},{14,12},{1,15},{3,1}... | collective-permute-start | bytes 1179656 | tf_op jit(solution)/shard_map/ppermute | solution.py:225
  83.2 2.4 %collective-permute-start.2 = (bf16[1536,128]{1,0:T(8,128)(2,1)}, bf16[1536,128]{1,0:T(8,128)(2,1)S(1)}, u32[]{:S(2)}, u32[]{:S(2)}) collective-permute-start(bf16[1536,128]{1,0:T(8,128)(2,1)} %collective-permute-done.1.here_b_ref), channel_id=1, source_target_pairs={{0,2},{2,4},{4,6},{6,8},{8,10},{10,12},{12,14},{14,0},{1,3},{3,5},... | collective-permute-start | bytes 1179656 | tf_op jit(solution)/shard_map/ppermute | solution.py:226
  85.6 0.0 collective-permute-done.9.refs_2_
  85.6 0.7 copy-done.5
  86.4 6.9 %collective-permute-done.there_ref.refs_6_ = bf16[1536,128]{1,0:T(8,128)(2,1)S(1)} collective-permute-done((bf16[1536,128]{1,0:T(8,128)(2,1)}, bf16[1536,128]{1,0:T(8,128)(2,1)S(1)}, u32[]{:S(2)}, u32[]{:S(2)}) %collective-permute-start) | collective-permute-done | bytes 393248 | tf_op jit(solution)/shard_map/ppermute | solution.py:225
  93.3 3.8 %collective-permute-done.2.there_b_ref.refs_7_ = bf16[1536,128]{1,0:T(8,128)(2,1)S(1)} collective-permute-done((bf16[1536,128]{1,0:T(8,128)(2,1)}, bf16[1536,128]{1,0:T(8,128)(2,1)S(1)}, u32[]{:S(2)}, u32[]{:S(2)}) %collective-permute-start.2) | collective-permute-done | bytes 393248 | tf_op jit(solution)/shard_map/ppermute | solution.py:226
  97.1 1.1 copy-done.6
  98.2 3.8 %shard_map.58 = bf16[8,16,1536]{2,1,0:T(8,128)(2,1)} custom-call(bf16[8,16,1536]{2,1,0:T(8,128)(2,1)S(1)} %all-to-all-done.2.rows_ref, bf16[1536,384]{1,0:T(8,128)(2,1)} %bitcast.32, bf16[1536,256]{1,0:T(8,128)(2,1)S(1)} %collective-permute-done.8.refs_1_, bf16[1536,128]{1,0:T(8,128)(2,1)S(1)} %copy-done.6, bf16[384,1536]{1,0:T(8,128)(2,1)} %bitcast.33, ...), custom_call_target="tpu_custom_call" | custom-call | flops 603979776 | bytes 4718592 | tf_op jit(solution)/shard_map/pallas_call | solution.py:22
  102.1 3.5 %all-to-all-start.3 = ((bf16[8,16,1536]{2,1,0:T(8,128)(2,1)}), bf16[8,16,1536]{2,1,0:T(8,128)(2,1)S(1)}, u32[]{:S(2)}, u32[]{:S(2)}) async-start(bf16[8,16,1536]{2,1,0:T(8,128)(2,1)} %shard_map.58), calls=%async_computation.3 | async-start | bytes 786432 | tf_op jit(solution)/shard_map/all_to_all | solution.py:272
  105.5 4.2 %shard_map.55 = (bf16[384,256]{1,0:T(8,128)(2,1)}, bf16[384,256]{1,0:T(8,128)(2,1)}) custom-call(s32[1]{0:T(128)} %bitcast.1.side_ref, bf16[384,1536]{1,0:T(8,128)(2,1)} %bitcast.30, bf16[1536,128]{1,0:T(8,128)(2,1)} %bitcast.3.here_ref.refs_0_, bf16[1536,128]{1,0:T(8,128)(2,1)} %copy-done.1, bf16[1536,128]{1,0:T(8,128)(2,1)} %collective-permute-done.1.here_b_ref, ...), custom_call_target="tpu_custom_call" | custom-call | flops 603979776 | bytes 2752512 | tf_op jit(solution)/shard_map/pallas_call | solution.py:22
  109.7 5.6 %all-to-all-done.3.blocks_ref = bf16[8,16,1536]{2,1,0:T(8,128)(2,1)S(1)} async-done(((bf16[8,16,1536]{2,1,0:T(8,128)(2,1)}), bf16[8,16,1536]{2,1,0:T(8,128)(2,1)S(1)}, u32[]{:S(2)}, u32[]{:S(2)}) %all-to-all-start.3) | async-done | bytes 393248 | tf_op jit(solution)/shard_map/all_to_all | solution.py:272
  115.3 0.9 copy-done.3
  116.3 1.2 shard_map.59
  117.5 27.9 %all_to_all.25 = bf16[16,16,1536]{2,1,0:T(8,128)(2,1)S(1)} all-to-all(bf16[16,16,1536]{2,1,0:T(8,128)(2,1)S(1)} %shard_map.59), channel_id=1, replica_groups=mesh['xlo'=2,'yh'=4,'yl'=2,'xhi'=2,'zh'=4,'zl'=2,'core'=2] {'zl','xhi','..., dimensions={0} | all-to-all | bytes 1572864 | tf_op jit(solution)/shard_map/all_to_all | solution.py:285
  145.4 7.1 %collective-permute-start.12 = (bf16[256,1536]{1,0:T(8,128)(2,1)S(1)}, bf16[256,1536]{1,0:T(8,128)(2,1)S(1)}, u32[]{:S(2)}, u32[]{:S(2)}) collective-permute-start(bf16[256,1536]{1,0:T(8,128)(2,1)S(1)} %bitcast.34), channel_id=1, source_target_pairs={{0,1},{1,0},{2,3},{3,2},{4,5},{5,4},{6,7},{7,6},{8,9},{9,8},{10,11... | collective-permute-start | bytes 2359304 | tf_op jit(solution)/shard_map/ppermute | solution.py:286
  152.6 1.9 %collective-permute-done.12 = bf16[256,1536]{1,0:T(8,128)(2,1)S(1)} collective-permute-done((bf16[256,1536]{1,0:T(8,128)(2,1)S(1)}, bf16[256,1536]{1,0:T(8,128)(2,1)S(1)}, u32[]{:S(2)}, u32[]{:S(2)}) %collective-permute-start.12) | collective-permute-done | bytes 786464 | tf_op jit(solution)/shard_map/ppermute | solution.py:286
  154.5 0.5 fusion.16
  154.9 0.5 copy-done.4
  155.4 0.5 copy-done.9
  155.8 1.5 fusion.2
  (32 shorter events, 0.1 us)
Async XLA Ops:
  0.0 19.0 %copy-start = (bf16[96,512]{1,0:T(8,128)(2,1)S(1)}, bf16[96,512]{1,0:T(8,128)(2,1)}, u32[]{:S(2)}) copy-start(bf16[96,512]{1,0:T(8,128)(2,1)} %param.6) | copy-start | bytes 294916
  0.0 16.0 %copy-start.8 = (bf16[1,384,1536]{2,1,0:T(8,128)(2,1)S(1)}, bf16[1,384,1536]{2,1,0:T(8,128)(2,1)}, u32[]{:S(2)}) copy-start(bf16[1,384,1536]{2,1,0:T(8,128)(2,1)} %param.5) | copy-start | bytes 3538948
  2.5 32.7 %copy-start.11 = (bf16[1,384,1536]{2,1,0:T(8,128)(2,1)S(1)}, bf16[1,384,1536]{2,1,0:T(8,128)(2,1)}, u32[]{:S(2)}) copy-start(bf16[1,384,1536]{2,1,0:T(8,128)(2,1)} %param.9) | copy-start | bytes 3538948
  2.5 25.4 %collective-permute-start.3 = (bf16[192,1536]{1,0:T(8,128)(2,1)}, bf16[192,1536]{1,0:T(8,128)(2,1)S(1)}, u32[]{:S(2)}, u32[]{:S(2)}) collective-permute-start(bf16[192,1536]{1,0:T(8,128)(2,1)} %get-tuple-element.10), channel_id=1, source_target_pairs={{0,14},{2,0},{4,2},{6,4},{8,6},{10,8},{12,10},{14,12},{1,15},{3,1}... | collective-permute-start | bytes 1769480 | tf_op jit(solution)/shard_map/ppermute | solution.py:181
  14.1 17.3 %collective-permute-start.4 = (bf16[192,1536]{1,0:T(8,128)(2,1)}, bf16[192,1536]{1,0:T(8,128)(2,1)}, u32[]{:S(2)}, u32[]{:S(2)}) collective-permute-start(bf16[192,1536]{1,0:T(8,128)(2,1)} %get-tuple-element.9), channel_id=1, source_target_pairs={{0,2},{2,4},{4,6},{6,8},{8,10},{10,12},{12,14},{14,0},{1,3},{3,5},... | collective-permute-start | bytes 1769480 | tf_op jit(solution)/shard_map/ppermute | solution.py:182
  16.0 23.6 %collective-permute-start.5 = (bf16[384,1536]{1,0:T(8,128)(2,1)S(1)}, bf16[384,1536]{1,0:T(8,128)(2,1)}, u32[]{:S(2)}, u32[]{:S(2)}) collective-permute-start(bf16[384,1536]{1,0:T(8,128)(2,1)S(1)} %bitcast.31), channel_id=1, source_target_pairs={{0,1},{1,0},{2,3},{3,2},{4,5},{5,4},{6,7},{7,6},{8,9},{9,8},{10,11... | collective-permute-start | bytes 3538952 | tf_op jit(solution)/shard_map/ppermute | solution.py:184
  20.0 19.7 %all-to-all-start = ((bf16[16,96,128]{2,1,0:T(8,128)(2,1)}), bf16[16,96,128]{2,1,0:T(8,128)(2,1)}, u32[]{:S(2)}, u32[]{:S(2)}) async-start(bf16[16,96,128]{2,1,0:T(8,128)(2,1)} %broadcast_in_dim.13), calls=%async_computation | async-start | bytes 786432 | tf_op jit(solution)/shard_map/all_to_all | solution.py:160
  27.9 11.8 %copy-start.12 = (bf16[192,1536]{1,0:T(8,128)(2,1)}, bf16[192,1536]{1,0:T(8,128)(2,1)S(1)}, u32[]{:S(2)}) copy-start(bf16[192,1536]{1,0:T(8,128)(2,1)S(1)} %collective-permute-done.3.refs_2_) | copy-start | bytes 1769476
  27.9 11.8 %collective-permute-start.6 = (bf16[192,1536]{1,0:T(8,128)(2,1)S(1)}, bf16[192,1536]{1,0:T(8,128)(2,1)}, u32[]{:S(2)}, u32[]{:S(2)}) collective-permute-start(bf16[192,1536]{1,0:T(8,128)(2,1)S(1)} %collective-permute-done.3.refs_2_), channel_id=1, source_target_pairs={{0,1},{1,0},{2,3},{3,2},{4,5},{5,4},{6,7},{7,6},{8,9},{9,8},{10,11... | collective-permute-start | bytes 1769480 | tf_op jit(solution)/shard_map/ppermute | solution.py:184
  31.4 8.3 %collective-permute-start.7 = (bf16[192,1536]{1,0:T(8,128)(2,1)}, bf16[192,1536]{1,0:T(8,128)(2,1)}, u32[]{:S(2)}, u32[]{:S(2)}) collective-permute-start(bf16[192,1536]{1,0:T(8,128)(2,1)} %collective-permute-done.4.refs_3_), channel_id=1, source_target_pairs={{0,1},{1,0},{2,3},{3,2},{4,5},{5,4},{6,7},{7,6},{8,9},{9,8},{10,11... | collective-permute-start | bytes 1769480 | tf_op jit(solution)/shard_map/ppermute | solution.py:184
  36.1 50.3 %collective-permute-start.10 = (bf16[256,1536]{1,0:T(8,128)(2,1)}, bf16[256,1536]{1,0:T(8,128)(2,1)S(1)}, u32[]{:S(2)}, u32[]{:S(2)}) collective-permute-start(bf16[256,1536]{1,0:T(8,128)(2,1)} %slice_bitcast_fusion), channel_id=1, source_target_pairs={{0,224},{1,33},{32,0},{33,65},{64,32},{65,97},{96,64},{97,129},{12... | collective-permute-start | bytes 2359304 | tf_op jit(solution)/shard_map/ppermute | solution.py:192
  39.7 11.8 %copy-start.10 = (bf16[1,1536,384]{2,1,0:T(8,128)(2,1)S(1)}, bf16[1,1536,384]{2,1,0:T(8,128)(2,1)}, u32[]{:S(2)}) copy-start(bf16[1,1536,384]{2,1,0:T(8,128)(2,1)} %param.8) | copy-start | bytes 3538948
  46.3 18.0 %all-to-all-start.1 = ((bf16[8,16,1664]{2,1,0:T(8,128)(2,1)}), bf16[8,16,1664]{2,1,0:T(8,128)(2,1)S(1)}, u32[]{:S(2)}, u32[]{:S(2)}) async-start(bf16[8,16,1664]{2,1,0:T(8,128)(2,1)} %bitcast.36), calls=%async_computation.1 | async-start | bytes 851968 | tf_op jit(solution)/shard_map/all_to_all | solution.py:220
  51.5 12.9 %copy-start.7 = (f32[1,1536]{1,0:T(1,128)S(1)}, f32[1,1536]{1,0:T(1,128)}, u32[]{:S(2)}) copy-start(f32[1,1536]{1,0:T(1,128)} %gain_ref.1) | copy-start | bytes 18436
  52.4 33.9 %collective-permute-start.8 = (bf16[1536,256]{1,0:T(8,128)(2,1)}, bf16[1536,256]{1,0:T(8,128)(2,1)S(1)}, u32[]{:S(2)}, u32[]{:S(2)}) collective-permute-start(bf16[1536,256]{1,0:T(8,128)(2,1)} %slice_bitcast_fusion.1), channel_id=1, source_target_pairs={{0,224},{1,33},{32,0},{33,65},{64,32},{65,97},{96,64},{97,129},{12... | collective-permute-start | bytes 2359304 | tf_op jit(solution)/shard_map/ppermute | solution.py:191
  56.8 19.5 %collective-permute-start.11 = (bf16[128,1536]{1,0:T(8,128)(2,1)S(1)}, bf16[128,1536]{1,0:T(8,128)(2,1)S(1)}, u32[]{:S(2)}, u32[]{:S(2)}) collective-permute-start(bf16[128,1536]{1,0:T(8,128)(2,1)S(1)} %slice_bitcast_fusion.4), channel_id=1, source_target_pairs={{0,32},{1,225},{32,64},{33,1},{64,96},{65,33},{96,128},{97,65},{12... | collective-permute-start | bytes 1179656 | tf_op jit(solution)/shard_map/ppermute | solution.py:192
  60.0 23.2 %collective-permute-start.1 = (bf16[1536,128]{1,0:T(8,128)(2,1)}, bf16[1536,128]{1,0:T(8,128)(2,1)}, u32[]{:S(2)}, u32[]{:S(2)}) collective-permute-start(bf16[1536,128]{1,0:T(8,128)(2,1)} %bitcast.3.here_ref.refs_0_), channel_id=1, source_target_pairs={{0,1},{1,0},{2,3},{3,2},{4,5},{5,4},{6,7},{7,6},{8,9},{9,8},{10,11... | collective-permute-start | bytes 1179656 | tf_op jit(solution)/shard_map/ppermute | solution.py:224
  65.5 31.6 %all-to-all-start.2 = ((bf16[8,16,1536]{2,1,0:T(8,128)(2,1)}), bf16[8,16,1536]{2,1,0:T(8,128)(2,1)S(1)}, u32[]{:S(2)}, u32[]{:S(2)}) async-start(bf16[8,16,1536]{2,1,0:T(8,128)(2,1)} %shard_map.57), calls=%async_computation.2 | async-start | bytes 786432 | tf_op jit(solution)/shard_map/all_to_all | solution.py:254
  70.9 14.7 %collective-permute-start.9 = (bf16[1536,128]{1,0:T(8,128)(2,1)S(1)}, bf16[1536,128]{1,0:T(8,128)(2,1)S(1)}, u32[]{:S(2)}, u32[]{:S(2)}) collective-permute-start(bf16[1536,128]{1,0:T(8,128)(2,1)S(1)} %slice_bitcast_fusion.5), channel_id=1, source_target_pairs={{0,32},{1,225},{32,64},{33,1},{64,96},{65,33},{96,128},{97,65},{12... | collective-permute-start | bytes 1179656 | tf_op jit(solution)/shard_map/ppermute | solution.py:191
  76.3 17.0 %collective-permute-start = (bf16[1536,128]{1,0:T(8,128)(2,1)}, bf16[1536,128]{1,0:T(8,128)(2,1)S(1)}, u32[]{:S(2)}, u32[]{:S(2)}) collective-permute-start(bf16[1536,128]{1,0:T(8,128)(2,1)} %bitcast.3.here_ref.refs_0_), channel_id=1, source_target_pairs={{0,14},{2,0},{4,2},{6,4},{8,6},{10,8},{12,10},{14,12},{1,15},{3,1}... | collective-permute-start | bytes 1179656 | tf_op jit(solution)/shard_map/ppermute | solution.py:225
  83.2 13.9 %collective-permute-start.2 = (bf16[1536,128]{1,0:T(8,128)(2,1)}, bf16[1536,128]{1,0:T(8,128)(2,1)S(1)}, u32[]{:S(2)}, u32[]{:S(2)}) collective-permute-start(bf16[1536,128]{1,0:T(8,128)(2,1)} %collective-permute-done.1.here_b_ref), channel_id=1, source_target_pairs={{0,2},{2,4},{4,6},{6,8},{8,10},{10,12},{12,14},{14,0},{1,3},{3,5},... | collective-permute-start | bytes 1179656 | tf_op jit(solution)/shard_map/ppermute | solution.py:226
  85.6 0.7 copy-start.5
  93.3 8.7 %copy-start.1 = (bf16[1536,128]{1,0:T(8,128)(2,1)}, bf16[1536,128]{1,0:T(8,128)(2,1)S(1)}, u32[]{:S(2)}) copy-start(bf16[1536,128]{1,0:T(8,128)(2,1)S(1)} %collective-permute-done.there_ref.refs_6_) | copy-start | bytes 1179652
  97.1 5.0 %copy-start.2 = (bf16[1536,128]{1,0:T(8,128)(2,1)}, bf16[1536,128]{1,0:T(8,128)(2,1)S(1)}, u32[]{:S(2)}) copy-start(bf16[1536,128]{1,0:T(8,128)(2,1)S(1)} %collective-permute-done.2.there_b_ref.refs_7_) | copy-start | bytes 1179652
  97.1 1.1 copy-start.6
  102.1 13.3 %all-to-all-start.3 = ((bf16[8,16,1536]{2,1,0:T(8,128)(2,1)}), bf16[8,16,1536]{2,1,0:T(8,128)(2,1)S(1)}, u32[]{:S(2)}, u32[]{:S(2)}) async-start(bf16[8,16,1536]{2,1,0:T(8,128)(2,1)} %shard_map.58), calls=%async_computation.3 | async-start | bytes 786432 | tf_op jit(solution)/shard_map/all_to_all | solution.py:272
  115.3 0.9 copy-start.3
  116.3 38.2 %copy-start.13 = (bf16[384,256]{1,0:T(8,128)(2,1)S(1)}, bf16[384,256]{1,0:T(8,128)(2,1)}, u32[]{:S(2)}) copy-start(bf16[384,256]{1,0:T(8,128)(2,1)} %get-tuple-element.8) | copy-start | bytes 589828
  145.4 9.0 %collective-permute-start.12 = (bf16[256,1536]{1,0:T(8,128)(2,1)S(1)}, bf16[256,1536]{1,0:T(8,128)(2,1)S(1)}, u32[]{:S(2)}, u32[]{:S(2)}) collective-permute-start(bf16[256,1536]{1,0:T(8,128)(2,1)S(1)} %bitcast.34), channel_id=1, source_target_pairs={{0,1},{1,0},{2,3},{3,2},{4,5},{5,4},{6,7},{7,6},{8,9},{9,8},{10,11... | collective-permute-start | bytes 2359304 | tf_op jit(solution)/shard_map/ppermute | solution.py:286
  154.5 0.9 copy-start.4
  154.5 1.4 copy-start.9

commit v9 on v4

--- a/solution.py
+++ b/solution.py
@@ -8,6 +8,7 @@
 F32 = jnp.float32
 BF16 = jnp.bfloat16
 EXTRA = 128
+Y = ("yh", "yl")
 VMEM = pl.BlockSpec(memory_space=pltpu.VMEM)
 HBM = pl.BlockSpec(memory_space=pltpu.HBM)
 
@@ -57,42 +58,26 @@
 
 
 def dispatch_kernel(
-    own_hbm,
-    partner_hbm,
-    columns_hbm,
-    message_hbm,
-    own_logits_hbm,
-    partner_logits_hbm,
-    own_ref,
-    partner_ref,
-    columns_ref,
-    own_logits_ref,
-    partner_logits_ref,
-    message_ref,
-    semaphores,
+    columns_hbm, own_hbm, partner_hbm, message_hbm, columns_ref, own_ref, partner_ref, message_ref, semaphores
 ):
-    width = own_ref.shape[1]
-    slots = columns_ref.shape[1]
-    cuts = 4
-    first = started_rows(columns_hbm, columns_ref, semaphores, 15, cuts)
-    loads = started_rows(own_hbm, own_ref, semaphores, 0, cuts)
-    loads += started_rows(partner_hbm, partner_ref, semaphores, cuts, cuts)
-    for copy in first + loads[:cuts]:
-        copy.wait()
+    width, slots = columns_ref.shape
+    loads = [
+        started(columns_hbm, columns_ref, semaphores, 0),
+        started(own_hbm, own_ref, semaphores, 1),
+        started(partner_hbm, partner_ref, semaphores, 2),
+    ]
+    loads[0].wait()
     columns = columns_ref[...]
-    own_logits_ref[...] = jnp.dot(own_ref[...], columns, preferred_element_type=F32)
-    stores = [started(own_logits_ref, own_logits_hbm, semaphores, 2 * cuts)]
-    for copy in loads[cuts:]:
-        copy.wait()
-    partner_logits_ref[...] = jnp.dot(partner_ref[...], columns, preferred_element_type=F32)
-    stores.append(started(partner_logits_ref, partner_logits_hbm, semaphores, 2 * cuts + 1))
-    own_logits, partner_logits = own_logits_ref[...], partner_logits_ref[...]
+    loads[1].wait()
+    own_logits = jnp.dot(own_ref[...], columns, preferred_element_type=F32)
+    loads[2].wait()
+    partner_logits = jnp.dot(partner_ref[...], columns, preferred_element_type=F32)
     high = jnp.maximum(
         jnp.max(own_logits, axis=0, keepdims=True), jnp.max(partner_logits, axis=0, keepdims=True)
     )
     message_ref[:, width:] = in_lanes([jnp.broadcast_to(high, (EXTRA, slots)).T])
     last = pl.ds(width, EXTRA)
-    stores.append(started(message_ref.at[:, last], message_hbm.at[:, last], semaphores, 2 * cuts + 2))
+    stores = [started(message_ref.at[:, last], message_hbm.at[:, last], semaphores, 3)]
     own = jnp.exp(own_logits - high).astype(BF16).T
     partner = jnp.exp(partner_logits - high).astype(BF16).T
     step = 384
@@ -101,14 +86,15 @@
         sums = jnp.dot(own, own_ref[:, part], preferred_element_type=F32)
         sums += jnp.dot(partner, partner_ref[:, part], preferred_element_type=F32)
         message_ref[:, part] = sums.astype(BF16)
-        stores.append(started(message_ref.at[:, part], message_hbm.at[:, part], semaphores, 2 * cuts + 3 + k))
+        stores.append(started(message_ref.at[:, part], message_hbm.at[:, part], semaphores, 4 + k))
     for copy in stores:
         copy.wait()
 
 
-def softmax_kernel(own_logits_ref, partner_logits_ref, own_ref, answer_ref):
-    for logits_ref, out_ref in ((own_logits_ref, own_ref), (partner_logits_ref, answer_ref)):
-        logits = logits_ref[...]
+def softmax_kernel(columns_ref, own_feats_ref, partner_feats_ref, own_ref, answer_ref):
+    columns = columns_ref[...]
+    for feats_ref, out_ref in ((own_feats_ref, own_ref), (partner_feats_ref, answer_ref)):
+        logits = jnp.dot(feats_ref[...], columns, preferred_element_type=F32)
         slots = logits.shape[1]
         high = jnp.max(logits, axis=1, keepdims=True)
         exps = jnp.exp(logits - high)
@@ -133,42 +119,24 @@
         copy.wait()
 
 
-def follow_kernel(weights_hbm, before_hbm, weights_ref, semaphores):
-    for copy in started_rows(weights_hbm, weights_ref, semaphores, 0, semaphores.shape[0]):
-        copy.wait()
-
-
-def expert_kernel(
-    rows_ref,
-    in_hbm,
-    out_hbm,
-    in_b_hbm,
-    out_b_hbm,
-    partial_ref,
-    in_ref,
-    out_ref,
-    in_b_ref,
-    out_b_ref,
-    semaphores,
-):
+def expert_kernel(rows_ref, *refs):
+    sources, partial_ref, targets, semaphores = refs[:6], refs[6], refs[7:13], refs[13]
     rows = rows_ref[...].reshape(-1, rows_ref.shape[-1])
     width = rows.shape[1]
-    cuts = 4
-    pairs = ((in_hbm, in_ref), (in_b_hbm, in_b_ref), (out_hbm, out_ref), (out_b_hbm, out_b_ref))
-    loads = [started_rows(*pair, semaphores, cuts * k, cuts) for k, pair in enumerate(pairs)]
-    for copy in loads[0]:
-        copy.wait()
-    hidden = jax.nn.gelu(jnp.dot(rows, in_ref[...], preferred_element_type=F32)).astype(BF16)
-    for copy in loads[1]:
-        copy.wait()
-    hidden_b = jax.nn.gelu(jnp.dot(rows, in_b_ref[...], preferred_element_type=F32)).astype(BF16)
-    for copy in loads[2] + loads[3]:
-        copy.wait()
+    loads = [started(source, target, semaphores, k) for k, (source, target) in enumerate(zip(sources, targets))]
+    hidden = []
+    for load, in_ref in zip(loads[:3], targets[:3]):
+        load.wait()
+        one = jnp.dot(rows, in_ref[...], preferred_element_type=F32)
+        hidden.append(jax.nn.gelu(one).astype(BF16))
+    for load in loads[3:]:
+        load.wait()
     step = 512
     for k in range(width // step):
         part = pl.ds(k * step, step)
-        sums = jnp.dot(hidden, out_ref[:, part], preferred_element_type=F32)
-        sums += jnp.dot(hidden_b, out_b_ref[:, part], preferred_element_type=F32)
+        sums = jnp.dot(hidden[0], targets[3][:, part], preferred_element_type=F32)
+        sums += jnp.dot(hidden[1], targets[4][:, part], preferred_element_type=F32)
+        sums += jnp.dot(hidden[2], targets[5][:, part], preferred_element_type=F32)
         partial_ref[:, :, part] = sums.astype(BF16).reshape(*rows_ref.shape[:2], step)
 
 
@@ -199,55 +167,48 @@
     count, width = feats.shape
     slot_count = router.shape[1]
     owners = lax.axis_size(("xhi", "z"))
-    groups = lax.axis_size("y")
+    groups = lax.axis_size(("xlo", "yh"))
     per_owner = slot_count // (2 * owners)
     half = slot_count // 2
     core = lax.axis_index("core")
     hidden_units = w_in.shape[2]
     shape = jax.ShapeDtypeStruct
 
-    partner_in = lax.ppermute(w_in[0], "xlo", other())
-    out_later = kernel_call(
-        follow_kernel,
-        shape((hidden_units, width), BF16),
-        0,
-        4 * width * hidden_units,
-        [HBM] * 2,
-        w_out[0],
-        partner_in,
-        scratch=[pltpu.SemaphoreType.DMA((4,))],
-        room=16,
-    )
-    partner_out = lax.ppermute(out_later, "xlo", other())
     partner_feats = lax.ppermute(feats, "core", other())
+
+    ring = lax.axis_size(Y)
+    most = [(2 * k + c, (k + 2 * c - 1) % ring * 2 + c) for k in range(ring) for c in range(2)]
+    least = [(2 * k + c, (k + 1 - 2 * c) % ring * 2 + c) for k in range(ring) for c in range(2)]
+    cut = hidden_units * 2 // 3
+    pairs = [(slice(0, cut), most), (slice(cut, hidden_units), least)]
+    given_in = [w_in[0]] + [lax.ppermute(w_in[0, :, part], (*Y, "core"), perm) for part, perm in pairs]
+    given_out = [w_out[0]] + [lax.ppermute(w_out[0, part], (*Y, "core"), perm) for part, perm in pairs]
 
     row = lax.broadcasted_iota(jnp.int32, (slot_count, half), 0)
     col = lax.broadcasted_iota(jnp.int32, (slot_count, half), 1)
     wanted = (col // per_owner * 2 + core) * per_owner + col % per_owner
     pick = (row == wanted).astype(BF16)
     own_columns = jnp.dot(router, pick, preferred_element_type=F32).astype(BF16)
-    columns = sent_to_all(own_columns, ("xlo", "y")).reshape(width, half)
-
-    message, logits, partner_logits = kernel_call(
+    columns = sent_to_all(own_columns, ("xlo", *Y)).reshape(width, half)
+
+    message = kernel_call(
         dispatch_kernel,
-        (shape((half, width + EXTRA), BF16), shape((count, half), F32), shape((count, half), F32)),
+        shape((half, width + EXTRA), BF16),
         8 * count * width * half,
         2 * (2 * count * width + 2 * width * half),
         [HBM] * 3,
+        columns,
         feats,
         partner_feats,
-        columns,
-        out_specs=(HBM, HBM, HBM),
+        out_specs=HBM,
         scratch=[
+            pltpu.VMEM((width, half), BF16),
             pltpu.VMEM((count, width), BF16),
             pltpu.VMEM((count, width), BF16),
-            pltpu.VMEM((width, half), BF16),
-            pltpu.VMEM((count, half), F32),
-            pltpu.VMEM((count, half), F32),
             pltpu.VMEM((half, width + EXTRA), BF16),
-            pltpu.SemaphoreType.DMA((19,)),
+            pltpu.SemaphoreType.DMA((8,)),
         ],
-        room=58,
+        room=50,
     )
     received = lax.all_to_all(
         message.reshape(owners, per_owner, width + EXTRA), ("xhi", "z"), 0, 0, tiled=True
@@ -256,11 +217,13 @@
     weights, answer = kernel_call(
         softmax_kernel,
         (shape((count, half + EXTRA), BF16), shape((count, half + EXTRA), BF16)),
-        16 * count * half,
-        12 * count * half,
-        [VMEM] * 2,
-        logits,
-        partner_logits,
+        4 * count * width * half,
+        4 * count * width,
+        [VMEM] * 3,
+        columns,
+        feats,
+        partner_feats,
+        room=58,
     )
     weights_b = lax.ppermute(answer, "core", other())
 
@@ -276,28 +239,23 @@
         scratch=[pltpu.VMEM((per_owner, width), BF16), pltpu.SemaphoreType.DMA((groups,))],
         room=16,
     )
-    rows = lax.all_to_all(slots, "y", 0, 0, tiled=True)
+    rows = lax.all_to_all(slots, ("xlo", "yh"), 0, 0, tiled=True)
     partial = kernel_call(
         expert_kernel,
         shape((groups, per_owner, width), BF16),
         8 * groups * per_owner * width * hidden_units,
         8 * width * hidden_units,
-        [VMEM, HBM, HBM, HBM, HBM],
+        [VMEM, *[HBM] * 6],
         rows,
-        w_in[0],
-        w_out[0],
-        partner_in,
-        partner_out,
+        *given_in,
+        *given_out,
         scratch=[
-            pltpu.VMEM((width, hidden_units), BF16),
-            pltpu.VMEM((hidden_units, width), BF16),
-            pltpu.VMEM((width, hidden_units), BF16),
-            pltpu.VMEM((hidden_units, width), BF16),
-            pltpu.SemaphoreType.DMA((16,)),
+            *[pltpu.VMEM(block.shape, BF16) for block in given_in + given_out],
+            pltpu.SemaphoreType.DMA((6,)),
         ],
-        room=48,
-    )
-    blocks = lax.all_to_all(partial, "y", 0, 0, tiled=True)
+        room=50,
+    )
+    blocks = lax.all_to_all(partial, ("xlo", "yh"), 0, 0, tiled=True)
     copies = kernel_call(
         sum_kernel,
         shape((owners, per_owner, width), BF16),
@@ -325,8 +283,8 @@
 
 
 def solution(mesh):
-    fine = Mesh(mesh.devices.reshape(2, 8, 2, 8, 2), ("xlo", "y", "xhi", "z", "core"))
-    grp, seq = ("xlo", "y"), ("xhi", "z", "core")
+    fine = Mesh(mesh.devices.reshape(2, 4, 2, 2, 8, 2), ("xlo", "yh", "yl", "xhi", "z", "core"))
+    grp, seq = ("xlo", *Y), ("xhi", "z", "core")
     in_specs = (P(grp, seq, None), P(grp, None), P(seq, None), P(seq, None, grp), P(seq, grp, None))
     return jax.shard_map(
         local, mesh=fine, in_specs=in_specs, out_specs=P(grp, seq, None), check_vma=False

time: 152 us -> 154 us (1.013)
  waiting for transfers between devices: 49.3 us -> 38 us
  local copies, waits for them, and re-layouts: 3.45 us -> 9.54 us
  starting transfers between devices: 63.9 us -> 68.6 us
  blocking collectives: 16.7 us -> 19.5 us
    all_to_all x1, waiting for transfers between devices: 15.1 us -> 5.9 us  [local(): lax.all_to_all(message.reshape(owners, per_owner, width + EXTRA), ('xhi',...]
    ppermute x2 -> x4, starting transfers between devices: 6.37 us -> 14.7 us  [the longest x2 9.09 us: local(): lax.ppermute(w_out[0, part], (*Y, 'core'), perm)]
    all_to_all x1, starting transfers between devices: 13.9 us -> 7.04 us  [local(): lax.all_to_all(copies, ('xhi', 'z'), 0, 0, tiled=True).reshape(half, width)]
    squeeze x0 -> x4, local copies, waits for them, and re-layouts: none -> 6.2 us  [the longest x2 3.12 us: local(): w_in[0, :, part]]
    all_to_all x1, blocking collectives: 16.7 us -> 19.5 us  [local(): blocks = lax.all_to_all(partial, ('xlo', 'yh'), 0, 0, tiled=True)]
    ppermute x1, waiting for transfers between devices: 0.01 us -> 2.45 us  [local(): partner_feats = lax.ppermute(feats, 'core', other())]
    all_to_all x1, waiting for transfers between devices: 11.2 us -> 8.84 us  [local(): lax.all_to_all(copies, ('xhi', 'z'), 0, 0, tiled=True).reshape(half, width)]
    ppermute x1, starting transfers between devices: 6.47 us -> 8.34 us  [local(): outs_b = lax.ppermute(outs, 'core', other())]
  transfers between devices with their start and end apart: 9 -> 11, of which waited for: 7 -> 5; matrix products, arithmetic and copies ran while one was open for 2% -> 5% of each run, Pallas kernels for 6% -> 3%
where the time goes in v9:
time: 154 us; the launch traced here: 153 us
  starting transfers between devices  68.6 us (45%)
  waiting for transfers between devices  38 us (25%)
  blocking collectives  19.5 us (13%)
  Pallas kernels  13.3 us (9%)
  local copies, waits for them, and re-layouts  9.54 us (6%)
  matrix products  2.29 us (1%)
  other arithmetic  1.85 us (1%)
    all_to_all x1, blocking collectives, local(): blocks = lax.all_to_all(partial, ('xlo', 'yh'), 0, 0, tiled=True)  19.5 us
    all_to_all x1, starting transfers between devices, local(): lax.all_to_all(message.reshape(owners, per_owner, width + EXTRA), ('xhi',...  13.9 us
    pallas_call x5, Pallas kernels, kernel_call(): pl.pallas_call(body, out_shape=outs, in_specs=specs, out_specs=jax.tree.m...  13.3 us
    all_to_all x1, waiting for transfers between devices, sent_to_all(): lax.all_to_all(jnp.broadcast_to(value[None], (length, *value.shape)), axe...  12 us
    ppermute x2, starting transfers between devices, local(): lax.ppermute(w_out[0, part], (*Y, 'core'), perm)  9.09 us
    all_to_all x1, waiting for transfers between devices, local(): lax.all_to_all(copies, ('xhi', 'z'), 0, 0, tiled=True).reshape(half, width)  8.84 us
    ppermute x2, waiting for transfers between devices, local(): lax.ppermute(w_out[0, part], (*Y, 'core'), perm)  8.8 us
    all_to_all x1, starting transfers between devices, sent_to_all(): lax.all_to_all(jnp.broadcast_to(value[None], (length, *value.shape)), axe...  8.68 us
  transfers between devices with their start and end apart: 11, of which 5 were waited for; matrix products, arithmetic and copies ran while one was open for 5% of the time, Pallas kernels for 3%

profile of v9, /device:TPU:1, one launch (start us, length us, event | category | flops | bytes accessed | tf_op | source)
XLA Modules:
  0.0 153.3 jit_solution(12946186696121109482)
XLA Ops:
  0.0 0.0 copy-start
  0.0 0.9 copy-done
  0.9 0.2 fusion.4
  1.1 1.0 broadcast_in_dim.4
  2.1 8.7 %all-to-all-start = ((bf16[16,96,256]{2,1,0:T(8,128)(2,1)}), bf16[16,96,256]{2,1,0:T(8,128)(2,1)S(1)}, u32[]{:S(2)}, u32[]{:S(2)}) async-start(bf16[16,96,256]{2,1,0:T(8,128)(2,1)} %broadcast_in_dim.4), calls=%async_computation | async-start | bytes 1572864 | tf_op jit(solution)/shard_map/all_to_all | solution.py:160
  10.8 0.0 copy-done.1
  10.8 3.7 %collective-permute-start = (bf16[384,1536]{1,0:T(8,128)(2,1)S(1)}, bf16[384,1536]{1,0:T(8,128)(2,1)S(1)}, u32[]{:S(2)}, u32[]{:S(2)}) collective-permute-start(bf16[384,1536]{1,0:T(8,128)(2,1)S(1)} %bitcast.23), channel_id=1, source_target_pairs={{0,1},{1,0},{2,3},{3,2},{4,5},{5,4},{6,7},{7,6},{8,9},{9,8},{10,11... | collective-permute-start | bytes 3538952 | tf_op jit(solution)/shard_map/ppermute | solution.py:177
  14.5 2.5 %collective-permute-done.partner_feats_ref.partner_hbm = bf16[384,1536]{1,0:T(8,128)(2,1)S(1)} collective-permute-done((bf16[384,1536]{1,0:T(8,128)(2,1)S(1)}, bf16[384,1536]{1,0:T(8,128)(2,1)S(1)}, u32[]{:S(2)}, u32[]{:S(2)}) %collective-permute-start) | collective-permute-done | bytes 1179680 | tf_op jit(solution)/shard_map/ppermute | solution.py:177
  17.0 12.0 %all-to-all-done = bf16[16,96,256]{2,1,0:T(8,128)(2,1)S(1)} async-done(((bf16[16,96,256]{2,1,0:T(8,128)(2,1)}), bf16[16,96,256]{2,1,0:T(8,128)(2,1)S(1)}, u32[]{:S(2)}, u32[]{:S(2)}) %all-to-all-start) | async-done | bytes 786464 | tf_op jit(solution)/shard_map/all_to_all | solution.py:160
  29.0 4.2 %shard_map.56 = bf16[256,1664]{1,0:T(8,128)(2,1)S(1)} custom-call(bf16[1536,256]{1,0:T(8,128)(2,1)S(1)} %bitcast.25, bf16[384,1536]{1,0:T(8,128)(2,1)S(1)} %bitcast.24, bf16[384,1536]{1,0:T(8,128)(2,1)S(1)} %collective-permute-done.partner_feats_ref.partner_hbm), custom_call_target="tpu_custom_call" | custom-call | flops 1207959552 | bytes 3932160 | tf_op jit(solution)/shard_map/pallas_call | solution.py:21
  33.2 0.9 copy-done.5
  34.1 13.9 %all-to-all-start.1 = ((bf16[16,16,1664]{2,1,0:T(8,128)(2,1)}), bf16[16,16,1664]{2,1,0:T(8,128)(2,1)S(1)}, u32[]{:S(2)}, u32[]{:S(2)}) async-start(bf16[16,16,1664]{2,1,0:T(8,128)(2,1)} %bitcast.27), calls=%async_computation.1 | async-start | bytes 1703936 | tf_op jit(solution)/shard_map/all_to_all | solution.py:213
  48.0 0.0 copy-start.6
  48.0 2.1 %slice_bitcast_fusion.1 = bf16[1536,256]{1,0:T(8,128)(2,1)} fusion(bf16[1,1536,384]{2,1,0:T(8,128)(2,1)} %param.8), kind=kLoop, calls=%fused_computation.9 | loop fusion | bytes 1572864 | tf_op jit(solution)/shard_map/squeeze | solution.py:184
  50.1 2.6 %collective-permute-start.1 = (bf16[1536,256]{1,0:T(8,128)(2,1)}, bf16[1536,256]{1,0:T(8,128)(2,1)S(1)}, u32[]{:S(2)}, u32[]{:S(2)}) collective-permute-start(bf16[1536,256]{1,0:T(8,128)(2,1)} %slice_bitcast_fusion.1), channel_id=1, source_target_pairs={{0,224},{1,33},{32,0},{33,65},{64,32},{65,97},{96,64},{97,129},{12... | collective-permute-start | bytes 2359304 | tf_op jit(solution)/shard_map/ppermute | solution.py:184
  52.7 2.1 %slice_bitcast_fusion = bf16[256,1536]{1,0:T(8,128)(2,1)} fusion(bf16[1,384,1536]{2,1,0:T(8,128)(2,1)} %param.9), kind=kLoop, calls=%fused_computation.8 | loop fusion | bytes 1572864 | tf_op jit(solution)/shard_map/squeeze | solution.py:185
  54.7 3.5 %collective-permute-start.3 = (bf16[256,1536]{1,0:T(8,128)(2,1)}, bf16[256,1536]{1,0:T(8,128)(2,1)S(1)}, u32[]{:S(2)}, u32[]{:S(2)}) collective-permute-start(bf16[256,1536]{1,0:T(8,128)(2,1)} %slice_bitcast_fusion), channel_id=1, source_target_pairs={{0,224},{1,33},{32,0},{33,65},{64,32},{65,97},{96,64},{97,129},{12... | collective-permute-start | bytes 2359304 | tf_op jit(solution)/shard_map/ppermute | solution.py:185
  58.2 1.0 slice_bitcast_fusion.3
  59.2 3.0 %collective-permute-start.2 = (bf16[1536,128]{1,0:T(8,128)(2,1)S(1)}, bf16[1536,128]{1,0:T(8,128)(2,1)S(1)}, u32[]{:S(2)}, u32[]{:S(2)}) collective-permute-start(bf16[1536,128]{1,0:T(8,128)(2,1)S(1)} %slice_bitcast_fusion.3), channel_id=1, source_target_pairs={{0,32},{1,225},{32,64},{33,1},{64,96},{65,33},{96,128},{97,65},{12... | collective-permute-start | bytes 1179656 | tf_op jit(solution)/shard_map/ppermute | solution.py:184
  62.3 5.9 %all-to-all-done.1.received_ref = bf16[16,16,1664]{2,1,0:T(8,128)(2,1)S(1)} async-done(((bf16[16,16,1664]{2,1,0:T(8,128)(2,1)}), bf16[16,16,1664]{2,1,0:T(8,128)(2,1)S(1)}, u32[]{:S(2)}, u32[]{:S(2)}) %all-to-all-start.1) | async-done | bytes 852000 | tf_op jit(solution)/shard_map/all_to_all | solution.py:213
  68.2 1.2 shard_map.57
  69.4 7.4 %all-to-all-start.2 = ((bf16[8,16,1536]{2,1,0:T(8,128)(2,1)}), bf16[8,16,1536]{2,1,0:T(8,128)(2,1)S(1)}, u32[]{:S(2)}, u32[]{:S(2)}) async-start(bf16[8,16,1536]{2,1,0:T(8,128)(2,1)} %shard_map.57), calls=%async_computation.2 | async-start | bytes 786432 | tf_op jit(solution)/shard_map/all_to_all | solution.py:242
  76.7 1.0 slice_bitcast_fusion.2
  77.7 5.6 %collective-permute-start.4 = (bf16[128,1536]{1,0:T(8,128)(2,1)S(1)}, bf16[128,1536]{1,0:T(8,128)(2,1)S(1)}, u32[]{:S(2)}, u32[]{:S(2)}) collective-permute-start(bf16[128,1536]{1,0:T(8,128)(2,1)S(1)} %slice_bitcast_fusion.2), channel_id=1, source_target_pairs={{0,32},{1,225},{32,64},{33,1},{64,96},{65,33},{96,128},{97,65},{12... | collective-permute-start | bytes 1179656 | tf_op jit(solution)/shard_map/ppermute | solution.py:185
  83.4 0.0 collective-permute-done.2.refs_2_
  83.4 8.8 %collective-permute-done.4.refs_5_ = bf16[128,1536]{1,0:T(8,128)(2,1)S(1)} collective-permute-done((bf16[128,1536]{1,0:T(8,128)(2,1)S(1)}, bf16[128,1536]{1,0:T(8,128)(2,1)S(1)}, u32[]{:S(2)}, u32[]{:S(2)}) %collective-permute-start.4) | collective-permute-done | bytes 393248 | tf_op jit(solution)/shard_map/ppermute | solution.py:185
  92.2 0.0 collective-permute-done.1.refs_1_
  92.2 0.0 collective-permute-done.3.refs_4_
  92.2 0.0 all-to-all-done.2.rows_ref
  92.2 3.0 %shard_map.58 = bf16[8,16,1536]{2,1,0:T(8,128)(2,1)S(1)} custom-call(bf16[8,16,1536]{2,1,0:T(8,128)(2,1)S(1)} %all-to-all-done.2.rows_ref, bf16[1536,384]{1,0:T(8,128)(2,1)} %bitcast.28, bf16[1536,256]{1,0:T(8,128)(2,1)S(1)} %collective-permute-done.1.refs_1_, bf16[1536,128]{1,0:T(8,128)(2,1)S(1)} %collective-permute-done.2.refs_2_, ...), custom_call_target="tpu_custom_call" | custom-call | flops 603979776 | bytes 4718592 | tf_op jit(solution)/shard_map/pallas_call | solution.py:21
  95.3 19.5 %all_to_all.25.blocks_ref = bf16[8,16,1536]{2,1,0:T(8,128)(2,1)S(1)} all-to-all(bf16[8,16,1536]{2,1,0:T(8,128)(2,1)S(1)} %shard_map.58), channel_id=1, replica_groups=mesh['xlo'=2,'yh'=4,'yl'=2,'xhi'=2,'z'=8,'core'=2] {'xlo','yh'}, dimensions={0} | all-to-all | bytes 786432 | tf_op jit(solution)/shard_map/all_to_all | solution.py:258
  114.7 1.1 shard_map.59
  115.8 7.0 %all-to-all-start.4 = ((bf16[16,16,1536]{2,1,0:T(8,128)(2,1)}), bf16[16,16,1536]{2,1,0:T(8,128)(2,1)S(1)}, u32[]{:S(2)}, u32[]{:S(2)}) async-start(bf16[16,16,1536]{2,1,0:T(8,128)(2,1)} %shard_map.59), calls=%async_computation.4 | async-start | bytes 1572864 | tf_op jit(solution)/shard_map/all_to_all | solution.py:270
  122.9 3.8 %shard_map.55 = (bf16[384,384]{1,0:T(8,128)(2,1)}, bf16[384,384]{1,0:T(8,128)(2,1)}) custom-call(bf16[1536,256]{1,0:T(8,128)(2,1)} %bitcast.26, bf16[384,1536]{1,0:T(8,128)(2,1)} %bitcast.22, bf16[384,1536]{1,0:T(8,128)(2,1)} %copy-done.4), custom_call_target="tpu_custom_call" | custom-call | flops 603979776 | bytes 2359296 | tf_op jit(solution)/shard_map/pallas_call | solution.py:21
  126.7 4.8 %collective-permute-start.5 = (bf16[384,384]{1,0:T(8,128)(2,1)}, bf16[384,384]{1,0:T(8,128)(2,1)S(1)}, u32[]{:S(2)}, u32[]{:S(2)}) collective-permute-start(bf16[384,384]{1,0:T(8,128)(2,1)} %get-tuple-element.8), channel_id=1, source_target_pairs={{0,1},{1,0},{2,3},{3,2},{4,5},{5,4},{6,7},{7,6},{8,9},{9,8},{10,11... | collective-permute-start | bytes 884744 | tf_op jit(solution)/shard_map/ppermute | solution.py:228
  131.5 8.8 %all-to-all-done.4 = bf16[16,16,1536]{2,1,0:T(8,128)(2,1)S(1)} async-done(((bf16[16,16,1536]{2,1,0:T(8,128)(2,1)}), bf16[16,16,1536]{2,1,0:T(8,128)(2,1)S(1)}, u32[]{:S(2)}, u32[]{:S(2)}) %all-to-all-start.4) | async-done | bytes 786464 | tf_op jit(solution)/shard_map/all_to_all | solution.py:270
  140.4 8.3 %collective-permute-start.6 = (bf16[256,1536]{1,0:T(8,128)(2,1)S(1)}, bf16[256,1536]{1,0:T(8,128)(2,1)S(1)}, u32[]{:S(2)}, u32[]{:S(2)}) collective-permute-start(bf16[256,1536]{1,0:T(8,128)(2,1)S(1)} %bitcast.30), channel_id=1, source_target_pairs={{0,1},{1,0},{2,3},{3,2},{4,5},{5,4},{6,7},{7,6},{8,9},{9,8},{10,11... | collective-permute-start | bytes 2359304 | tf_op jit(solution)/shard_map/ppermute | solution.py:271
  148.7 1.1 slice_convert_fusion.3
  149.8 0.0 collective-permute-done.5
  149.8 0.1 slice_convert_fusion.1
  149.9 0.5 fusion.18
  150.4 0.0 copy-start.2
  150.4 0.2 divide_reduce_fusion.1
  150.6 0.0 collective-permute-done.6
  150.6 0.5 convolution_multiply_fusion
  151.1 0.6 copy-done.2
  151.7 0.0 copy-done.7
  151.7 1.6 %fusion.3 = bf16[1,384,1536]{2,1,0:T(8,128)(2,1)} fusion(f32[384,1536]{1,0:T(8,128)S(1)} %convolution_multiply_fusion, bf16[256,1536]{1,0:T(8,128)(2,1)S(1)} %bitcast.31, f32[384]{0:T(512)S(1)} %get-tuple-element.9, bf16[384,384]{1,0:T(8,128)(2,1)S(1)} %copy-done.7, bf16[1,384,1536]{2,1,0:T(8,128)(2,1)S(1)} %copy-done.2), kind=kOutput, calls=%fused_computation.5 | convolution fusion | flops 304939008 | bytes 5703680 | tf_op jit(solution)/shard_map/dot_general | solution.py:280
  (11 shorter events, 0.0 us)
Async XLA Ops:
  0.0 0.9 copy-start
  0.0 10.8 %copy-start.1 = (bf16[1,384,1536]{2,1,0:T(8,128)(2,1)S(1)}, bf16[1,384,1536]{2,1,0:T(8,128)(2,1)}, u32[]{:S(2)}) copy-start(bf16[1,384,1536]{2,1,0:T(8,128)(2,1)} %param.5) | copy-start | bytes 3538948
  2.1 26.9 %all-to-all-start = ((bf16[16,96,256]{2,1,0:T(8,128)(2,1)}), bf16[16,96,256]{2,1,0:T(8,128)(2,1)S(1)}, u32[]{:S(2)}, u32[]{:S(2)}) async-start(bf16[16,96,256]{2,1,0:T(8,128)(2,1)} %broadcast_in_dim.4), calls=%async_computation | async-start | bytes 1572864 | tf_op jit(solution)/shard_map/all_to_all | solution.py:160
  10.8 6.2 %collective-permute-start = (bf16[384,1536]{1,0:T(8,128)(2,1)S(1)}, bf16[384,1536]{1,0:T(8,128)(2,1)S(1)}, u32[]{:S(2)}, u32[]{:S(2)}) collective-permute-start(bf16[384,1536]{1,0:T(8,128)(2,1)S(1)} %bitcast.23), channel_id=1, source_target_pairs={{0,1},{1,0},{2,3},{3,2},{4,5},{5,4},{6,7},{7,6},{8,9},{9,8},{10,11... | collective-permute-start | bytes 3538952 | tf_op jit(solution)/shard_map/ppermute | solution.py:177
  17.0 17.1 %copy-start.4 = (bf16[384,1536]{1,0:T(8,128)(2,1)}, bf16[384,1536]{1,0:T(8,128)(2,1)S(1)}, u32[]{:S(2)}) copy-start(bf16[384,1536]{1,0:T(8,128)(2,1)S(1)} %collective-permute-done.partner_feats_ref.partner_hbm) | copy-start | bytes 3538948
  29.0 5.1 %copy-start.3 = (bf16[16,96,256]{2,1,0:T(8,128)(2,1)}, bf16[16,96,256]{2,1,0:T(8,128)(2,1)S(1)}, u32[]{:S(2)}) copy-start(bf16[16,96,256]{2,1,0:T(8,128)(2,1)S(1)} %all-to-all-done) | copy-start | bytes 2359300
  33.1 0.9 copy-start.5
  34.1 34.1 %all-to-all-start.1 = ((bf16[16,16,1664]{2,1,0:T(8,128)(2,1)}), bf16[16,16,1664]{2,1,0:T(8,128)(2,1)S(1)}, u32[]{:S(2)}, u32[]{:S(2)}) async-start(bf16[16,16,1664]{2,1,0:T(8,128)(2,1)} %bitcast.27), calls=%async_computation.1 | async-start | bytes 1703936 | tf_op jit(solution)/shard_map/all_to_all | solution.py:213
  48.0 20.2 %copy-start.6 = (f32[1,1536]{1,0:T(1,128)S(1)}, f32[1,1536]{1,0:T(1,128)}, u32[]{:S(2)}) copy-start(f32[1,1536]{1,0:T(1,128)} %gain_ref.1) | copy-start | bytes 18436
  50.1 42.1 %collective-permute-start.1 = (bf16[1536,256]{1,0:T(8,128)(2,1)}, bf16[1536,256]{1,0:T(8,128)(2,1)S(1)}, u32[]{:S(2)}, u32[]{:S(2)}) collective-permute-start(bf16[1536,256]{1,0:T(8,128)(2,1)} %slice_bitcast_fusion.1), channel_id=1, source_target_pairs={{0,224},{1,33},{32,0},{33,65},{64,32},{65,97},{96,64},{97,129},{12... | collective-permute-start | bytes 2359304 | tf_op jit(solution)/shard_map/ppermute | solution.py:184
  54.7 37.5 %collective-permute-start.3 = (bf16[256,1536]{1,0:T(8,128)(2,1)}, bf16[256,1536]{1,0:T(8,128)(2,1)S(1)}, u32[]{:S(2)}, u32[]{:S(2)}) collective-permute-start(bf16[256,1536]{1,0:T(8,128)(2,1)} %slice_bitcast_fusion), channel_id=1, source_target_pairs={{0,224},{1,33},{32,0},{33,65},{64,32},{65,97},{96,64},{97,129},{12... | collective-permute-start | bytes 2359304 | tf_op jit(solution)/shard_map/ppermute | solution.py:185
  59.2 24.2 %collective-permute-start.2 = (bf16[1536,128]{1,0:T(8,128)(2,1)S(1)}, bf16[1536,128]{1,0:T(8,128)(2,1)S(1)}, u32[]{:S(2)}, u32[]{:S(2)}) collective-permute-start(bf16[1536,128]{1,0:T(8,128)(2,1)S(1)} %slice_bitcast_fusion.3), channel_id=1, source_target_pairs={{0,32},{1,225},{32,64},{33,1},{64,96},{65,33},{96,128},{97,65},{12... | collective-permute-start | bytes 1179656 | tf_op jit(solution)/shard_map/ppermute | solution.py:184
  69.4 22.9 %all-to-all-start.2 = ((bf16[8,16,1536]{2,1,0:T(8,128)(2,1)}), bf16[8,16,1536]{2,1,0:T(8,128)(2,1)S(1)}, u32[]{:S(2)}, u32[]{:S(2)}) async-start(bf16[8,16,1536]{2,1,0:T(8,128)(2,1)} %shard_map.57), calls=%async_computation.2 | async-start | bytes 786432 | tf_op jit(solution)/shard_map/all_to_all | solution.py:242
  77.7 14.5 %collective-permute-start.4 = (bf16[128,1536]{1,0:T(8,128)(2,1)S(1)}, bf16[128,1536]{1,0:T(8,128)(2,1)S(1)}, u32[]{:S(2)}, u32[]{:S(2)}) collective-permute-start(bf16[128,1536]{1,0:T(8,128)(2,1)S(1)} %slice_bitcast_fusion.2), channel_id=1, source_target_pairs={{0,32},{1,225},{32,64},{33,1},{64,96},{65,33},{96,128},{97,65},{12... | collective-permute-start | bytes 1179656 | tf_op jit(solution)/shard_map/ppermute | solution.py:185
  115.8 24.6 %all-to-all-start.4 = ((bf16[16,16,1536]{2,1,0:T(8,128)(2,1)}), bf16[16,16,1536]{2,1,0:T(8,128)(2,1)S(1)}, u32[]{:S(2)}, u32[]{:S(2)}) async-start(bf16[16,16,1536]{2,1,0:T(8,128)(2,1)} %shard_map.59), calls=%async_computation.4 | async-start | bytes 1572864 | tf_op jit(solution)/shard_map/all_to_all | solution.py:270
  126.7 23.1 %collective-permute-start.5 = (bf16[384,384]{1,0:T(8,128)(2,1)}, bf16[384,384]{1,0:T(8,128)(2,1)S(1)}, u32[]{:S(2)}, u32[]{:S(2)}) collective-permute-start(bf16[384,384]{1,0:T(8,128)(2,1)} %get-tuple-element.8), channel_id=1, source_target_pairs={{0,1},{1,0},{2,3},{3,2},{4,5},{5,4},{6,7},{7,6},{8,9},{9,8},{10,11... | collective-permute-start | bytes 884744 | tf_op jit(solution)/shard_map/ppermute | solution.py:228
  140.4 10.2 %collective-permute-start.6 = (bf16[256,1536]{1,0:T(8,128)(2,1)S(1)}, bf16[256,1536]{1,0:T(8,128)(2,1)S(1)}, u32[]{:S(2)}, u32[]{:S(2)}) collective-permute-start(bf16[256,1536]{1,0:T(8,128)(2,1)S(1)} %bitcast.30), channel_id=1, source_target_pairs={{0,1},{1,0},{2,3},{3,2},{4,5},{5,4},{6,7},{7,6},{8,9},{9,8},{10,11... | collective-permute-start | bytes 2359304 | tf_op jit(solution)/shard_map/ppermute | solution.py:271
  150.4 1.3 copy-start.2
  150.4 1.3 copy-start.7

commit v10 on v9

--- a/solution.py
+++ b/solution.py
@@ -1,3 +1,5 @@
+import functools
+
 import jax
 import jax.numpy as jnp
 from jax import lax
@@ -119,28 +121,56 @@
         copy.wait()
 
 
+def pack_kernel(first, count, in_hbm, out_hbm, before_hbm, packed_ref, semaphores):
+    width = in_hbm.shape[0]
+    copies = [started(in_hbm.at[:, pl.ds(first, count)], packed_ref.at[pl.ds(0, width)], semaphores, 0)]
+    for k in range(width // count):
+        block = out_hbm.at[pl.ds(first, count), pl.ds(k * count, count)]
+        copies.append(started(block, packed_ref.at[pl.ds(width + k * count, count)], semaphores, 1 + k))
+    for copy in copies:
+        copy.wait()
+
+
 def expert_kernel(rows_ref, *refs):
-    sources, partial_ref, targets, semaphores = refs[:6], refs[6], refs[7:13], refs[13]
+    sources, partial_ref, targets, semaphores = refs[:4], refs[4], refs[5:9], refs[9]
     rows = rows_ref[...].reshape(-1, rows_ref.shape[-1])
     width = rows.shape[1]
     loads = [started(source, target, semaphores, k) for k, (source, target) in enumerate(zip(sources, targets))]
+    in_ref, *packed, out_ref = targets
     hidden = []
-    for load, in_ref in zip(loads[:3], targets[:3]):
+    for load, ref in zip(loads, (in_ref, *packed)):
         load.wait()
-        one = jnp.dot(rows, in_ref[...], preferred_element_type=F32)
+        one = jnp.dot(rows, ref[:width, :], preferred_element_type=F32)
         hidden.append(jax.nn.gelu(one).astype(BF16))
-    for load in loads[3:]:
-        load.wait()
+    loads[3].wait()
     step = 512
-    for k in range(width // step):
-        part = pl.ds(k * step, step)
-        sums = jnp.dot(hidden[0], targets[3][:, part], preferred_element_type=F32)
-        sums += jnp.dot(hidden[1], targets[4][:, part], preferred_element_type=F32)
-        sums += jnp.dot(hidden[2], targets[5][:, part], preferred_element_type=F32)
-        partial_ref[:, :, part] = sums.astype(BF16).reshape(*rows_ref.shape[:2], step)
-
-
-def sum_kernel(blocks_ref, copies_hbm, total_ref, semaphores):
+    for start in range(0, width, step):
+        sums = jnp.dot(hidden[0], out_ref[:, start : start + step], preferred_element_type=F32)
+        for one, ref in zip(hidden[1:], packed):
+            count = ref.shape[1]
+            blocks = [
+                jnp.dot(one, ref[width + k : width + k + count, :], preferred_element_type=F32)
+                for k in range(start, start + step, count)
+            ]
+            sums += jnp.concatenate(blocks, axis=1)
+        partial_ref[:, :, start : start + step] = sums.astype(BF16).reshape(*rows_ref.shape[:2], step)
+
+
+def scale_kernel(own_ref, core_ref, own_weights_ref, core_weights_ref):
+    slots = own_weights_ref.shape[1]
+    blocks = (own_ref, core_ref)
+    stats = [ref[:, slots:].astype(F32) for ref in blocks]
+    lane = lax.broadcasted_iota(jnp.int32, stats[0].shape, 1)
+    highs = [jnp.sum(jnp.where(lane < 3, one, 0.0), axis=1, keepdims=True) for one in stats]
+    sums = [jnp.sum(jnp.where(lane < 3, 0.0, one), axis=1, keepdims=True) for one in stats]
+    top = jnp.maximum(highs[0], highs[1])
+    factors = [jnp.exp(high - top) for high in highs]
+    total = sums[0] * factors[0] + sums[1] * factors[1]
+    for ref, out_ref, factor in zip(blocks, (own_weights_ref, core_weights_ref), factors):
+        out_ref[...] = (ref[:, :slots].astype(F32) * (factor / total)).astype(BF16)
+
+
+def sum_kernel(blocks_ref, before_hbm, copies_hbm, total_ref, semaphores):
     total = blocks_ref[0].astype(F32)
     for k in range(1, blocks_ref.shape[0]):
         total += blocks_ref[k].astype(F32)
@@ -148,11 +178,6 @@
     copies = [started(total_ref, copies_hbm.at[k], semaphores, k) for k in range(copies_hbm.shape[0])]
     for copy in copies:
         copy.wait()
-
-
-def piece_sum(block, which):
-    part = block[:, 3 * which : 3 * which + 3].astype(F32)
-    return part[:, 0] + part[:, 1] + part[:, 2]
 
 
 def sent_to_all(value, axes):
@@ -180,9 +205,21 @@
     most = [(2 * k + c, (k + 2 * c - 1) % ring * 2 + c) for k in range(ring) for c in range(2)]
     least = [(2 * k + c, (k + 1 - 2 * c) % ring * 2 + c) for k in range(ring) for c in range(2)]
     cut = hidden_units * 2 // 3
-    pairs = [(slice(0, cut), most), (slice(cut, hidden_units), least)]
-    given_in = [w_in[0]] + [lax.ppermute(w_in[0, :, part], (*Y, "core"), perm) for part, perm in pairs]
-    given_out = [w_out[0]] + [lax.ppermute(w_out[0, part], (*Y, "core"), perm) for part, perm in pairs]
+    given = []
+    for first, units, perm in ((0, cut, most), (cut, hidden_units - cut, least)):
+        packed = kernel_call(
+            functools.partial(pack_kernel, first, units),
+            shape((2 * width, units), BF16),
+            0,
+            8 * width * units,
+            [HBM] * 3,
+            w_in[0],
+            w_out[0],
+            given[0] if given else router,
+            scratch=[pltpu.SemaphoreType.DMA((1 + width // units,))],
+            room=16,
+        )
+        given.append(lax.ppermute(packed, (*Y, "core"), perm))
 
     row = lax.broadcasted_iota(jnp.int32, (slot_count, half), 0)
     col = lax.broadcasted_iota(jnp.int32, (slot_count, half), 1)
@@ -208,13 +245,13 @@
             pltpu.VMEM((half, width + EXTRA), BF16),
             pltpu.SemaphoreType.DMA((8,)),
         ],
-        room=50,
+        room=56,
     )
     received = lax.all_to_all(
         message.reshape(owners, per_owner, width + EXTRA), ("xhi", "z"), 0, 0, tiled=True
     )
 
-    weights, answer = kernel_call(
+    exps, answer = kernel_call(
         softmax_kernel,
         (shape((count, half + EXTRA), BF16), shape((count, half + EXTRA), BF16)),
         4 * count * width * half,
@@ -225,7 +262,17 @@
         partner_feats,
         room=58,
     )
-    weights_b = lax.ppermute(answer, "core", other())
+    answer = lax.ppermute(answer, "core", other())
+    weights, weights_b = kernel_call(
+        scale_kernel,
+        (shape((count, half), BF16), shape((count, half), BF16)),
+        8 * count * half,
+        8 * count * half,
+        [VMEM] * 2,
+        exps,
+        answer,
+        room=16,
+    )
 
     slots = kernel_call(
         pool_kernel,
@@ -245,13 +292,16 @@
         shape((groups, per_owner, width), BF16),
         8 * groups * per_owner * width * hidden_units,
         8 * width * hidden_units,
-        [VMEM, *[HBM] * 6],
+        [VMEM, *[HBM] * 4],
         rows,
-        *given_in,
-        *given_out,
+        w_in[0],
+        *given,
+        w_out[0],
         scratch=[
-            *[pltpu.VMEM(block.shape, BF16) for block in given_in + given_out],
-            pltpu.SemaphoreType.DMA((6,)),
+            pltpu.VMEM((width, hidden_units), BF16),
+            *[pltpu.VMEM(block.shape, BF16) for block in given],
+            pltpu.VMEM((hidden_units, width), BF16),
+            pltpu.SemaphoreType.DMA((4,)),
         ],
         room=50,
     )
@@ -261,8 +311,9 @@
         shape((owners, per_owner, width), BF16),
         groups * per_owner * width,
         2 * half * width,
-        [VMEM],
+        [VMEM, HBM],
         blocks,
+        weights,
         out_specs=HBM,
         scratch=[pltpu.VMEM((per_owner, width), BF16), pltpu.SemaphoreType.DMA((owners,))],
         room=16,
@@ -270,15 +321,8 @@
     outs = lax.all_to_all(copies, ("xhi", "z"), 0, 0, tiled=True).reshape(half, width)
     outs_b = lax.ppermute(outs, "core", other())
 
-    stats, stats_b = weights[:, half:], weights_b[:, half:]
-    row_high, row_sum = piece_sum(stats, 0), piece_sum(stats, 1)
-    row_high_b, row_sum_b = piece_sum(stats_b, 0), piece_sum(stats_b, 1)
-    top = jnp.maximum(row_high, row_high_b)
-    factor = jnp.exp(row_high - top)
-    factor_b = jnp.exp(row_high_b - top)
-    total = row_sum * factor + row_sum_b * factor_b
-    mixed = jnp.dot(weights[:, :half], outs, preferred_element_type=F32) * (factor / total)[:, None]
-    mixed += jnp.dot(weights_b[:, :half], outs_b, preferred_element_type=F32) * (factor_b / total)[:, None]
+    mixed = jnp.dot(weights, outs, preferred_element_type=F32)
+    mixed += jnp.dot(weights_b, outs_b, preferred_element_type=F32)
     return (feats.astype(F32) + mixed).astype(BF16)[None]
 
 

time: 154 us -> 150 us (0.974); the launches traced: 153 us -> 147 us
  starting transfers between devices: 68.6 us -> 59.7 us
  blocking collectives: 19.5 us -> 25.1 us
  local copies, waits for them, and re-layouts: 9.54 us -> 4.37 us
  Pallas kernels: 13.3 us -> 17.7 us
  other arithmetic: 1.85 us -> 0.02 us
    all_to_all x1, waiting for transfers between devices: 0.01 us -> 9.34 us  [local(): rows = lax.all_to_all(slots, ('xlo', 'yh'), 0, 0, tiled=True)]
    all_to_all x1, waiting for transfers between devices: 8.84 us -> 0.01 us  [local(): blocks = lax.all_to_all(partial, ('xlo', 'yh'), 0, 0, tiled=True)]
    all_to_all x1, waiting for transfers between devices: 5.9 us -> 14.3 us  [local(): lax.all_to_all(message.reshape(owners, per_owner, width + EXTRA), ('xhi',...]
    ppermute x5 -> x3, waiting for transfers between devices: 8.81 us -> 1.4 us  [the longest x1 1.4 us: local(): answer = lax.ppermute(answer, 'core', other())]
    ppermute x5 -> x3, starting transfers between devices: 19.5 us -> 12.4 us  [the longest x2 6.43 us: local(): given.append(lax.ppermute(packed, (*Y, 'core'), perm))]
    squeeze x4 -> x0, local copies, waits for them, and re-layouts: 6.2 us -> none  [the longest x2 3.12 us: local(): w_in[0, :, part]]
    all_to_all x1, blocking collectives: 19.5 us -> 25.1 us  [local(): lax.all_to_all(copies, ('xhi', 'z'), 0, 0, tiled=True).reshape(half, width)]
    pallas_call x5 -> x8, Pallas kernels: 13.3 us -> 17.7 us  [kernel_call(): pl.pallas_call(body, out_shape=outs, in_specs=specs, out_specs=jax.tree.m...]
  transfers between devices with their start and end apart: 11 -> 9, of which waited for: 5 -> 5; matrix products, arithmetic and copies ran while one was open for 5% -> 0% of each run, Pallas kernels for 3% -> 9%
where the time goes in v10:
time: 150 us; the launch traced here: 147 us
  starting transfers between devices  59.7 us (40%)
  waiting for transfers between devices  36.7 us (24%)
  blocking collectives  25.1 us (17%)
  Pallas kernels  17.7 us (12%)
  local copies, waits for them, and re-layouts  4.37 us (3%)
  matrix products  3.26 us (2%)
    all_to_all x1, blocking collectives, local(): lax.all_to_all(copies, ('xhi', 'z'), 0, 0, tiled=True).reshape(half, width)  25.1 us
    pallas_call x8, Pallas kernels, kernel_call(): pl.pallas_call(body, out_shape=outs, in_specs=specs, out_specs=jax.tree.m...  17.7 us
    all_to_all x1, waiting for transfers between devices, local(): lax.all_to_all(message.reshape(owners, per_owner, width + EXTRA), ('xhi',...  14.3 us
    all_to_all x1, starting transfers between devices, local(): lax.all_to_all(message.reshape(owners, per_owner, width + EXTRA), ('xhi',...  13.8 us
    all_to_all x1, waiting for transfers between devices, sent_to_all(): lax.all_to_all(jnp.broadcast_to(value[None], (length, *value.shape)), axe...  9.76 us
    all_to_all x1, waiting for transfers between devices, local(): rows = lax.all_to_all(slots, ('xlo', 'yh'), 0, 0, tiled=True)  9.34 us
    all_to_all x1, starting transfers between devices, sent_to_all(): lax.all_to_all(jnp.broadcast_to(value[None], (length, *value.shape)), axe...  8.68 us
    all_to_all x1, starting transfers between devices, local(): rows = lax.all_to_all(slots, ('xlo', 'yh'), 0, 0, tiled=True)  8.46 us
  transfers between devices with their start and end apart: 9, of which 5 were waited for; matrix products, arithmetic and copies ran while one was open for 0% of the time, Pallas kernels for 9%

profile of v10, /device:TPU:1, one launch (start us, length us, event | category | flops | bytes accessed | tf_op | source)
XLA Modules:
  0.0 147.1 jit_solution(18171831186584354592)
XLA Ops:
  0.0 0.0 copy-start
  0.0 0.0 copy-start.1
  0.1 0.0 copy-start.4
  0.1 1.3 fusion.3
  1.4 1.0 broadcast_in_dim.4
  2.3 8.7 %all-to-all-start = ((bf16[16,96,256]{2,1,0:T(8,128)(2,1)}), bf16[16,96,256]{2,1,0:T(8,128)(2,1)S(1)}, u32[]{:S(2)}, u32[]{:S(2)}) async-start(bf16[16,96,256]{2,1,0:T(8,128)(2,1)} %broadcast_in_dim.4), calls=%async_computation | async-start | bytes 1572864 | tf_op jit(solution)/shard_map/all_to_all | solution.py:185
  11.0 3.7 %collective-permute-start = (bf16[384,1536]{1,0:T(8,128)(2,1)}, bf16[384,1536]{1,0:T(8,128)(2,1)}, u32[]{:S(2)}, u32[]{:S(2)}) collective-permute-start(bf16[384,1536]{1,0:T(8,128)(2,1)} %bitcast.22), channel_id=1, source_target_pairs={{0,1},{1,0},{2,3},{3,2},{4,5},{5,4},{6,7},{7,6},{8,9},{9,8},{10,11... | collective-permute-start | bytes 3538952 | tf_op jit(solution)/shard_map/ppermute | solution.py:202
  14.7 0.0 copy-done
  14.7 0.0 copy-done.1
  14.8 0.0 copy-done.4
  14.8 1.3 shard_map.59
  16.1 3.4 %collective-permute-start.2 = (bf16[3072,256]{1,0:T(8,128)(2,1)}, bf16[3072,256]{1,0:T(8,128)(2,1)}, u32[]{:S(2)}, u32[]{:S(2)}) collective-permute-start(bf16[3072,256]{1,0:T(8,128)(2,1)} %shard_map.59), channel_id=1, source_target_pairs={{0,224},{1,33},{32,0},{33,65},{64,32},{65,97},{96,64},{97,129},{12... | collective-permute-start | bytes 4718600 | tf_op jit(solution)/shard_map/ppermute | solution.py:222
  19.5 0.0 collective-permute-done.partner_feats_ref.partner_hbm
  19.5 9.8 %all-to-all-done = bf16[16,96,256]{2,1,0:T(8,128)(2,1)S(1)} async-done(((bf16[16,96,256]{2,1,0:T(8,128)(2,1)}), bf16[16,96,256]{2,1,0:T(8,128)(2,1)S(1)}, u32[]{:S(2)}, u32[]{:S(2)}) %all-to-all-start) | async-done | bytes 786464 | tf_op jit(solution)/shard_map/all_to_all | solution.py:185
  29.3 0.0 copy-start.7
  29.3 0.9 copy-done.7
  30.2 5.0 %shard_map.57 = bf16[256,1664]{1,0:T(8,128)(2,1)} custom-call(bf16[1536,256]{1,0:T(8,128)(2,1)} %bitcast.25, bf16[384,1536]{1,0:T(8,128)(2,1)} %bitcast.23, bf16[384,1536]{1,0:T(8,128)(2,1)} %collective-permute-done.partner_feats_ref.partner_hbm), custom_call_target="tpu_custom_call" | custom-call | flops 1207959552 | bytes 3932160 | tf_op jit(solution)/shard_map/pallas_call | solution.py:23
  35.2 13.8 %all-to-all-start.1 = ((bf16[16,16,1664]{2,1,0:T(8,128)(2,1)}), bf16[16,16,1664]{2,1,0:T(8,128)(2,1)S(1)}, u32[]{:S(2)}, u32[]{:S(2)}) async-start(bf16[16,16,1664]{2,1,0:T(8,128)(2,1)} %bitcast.29), calls=%async_computation.1 | async-start | bytes 1703936 | tf_op jit(solution)/shard_map/all_to_all | solution.py:250
  49.0 0.0 copy-start.5
  49.0 0.0 collective-permute-done.2.before_hbm.refs_1_
  49.0 1.2 shard_map.60
  50.2 3.0 %collective-permute-start.3 = (bf16[3072,128]{1,0:T(8,128)(2,1)}, bf16[3072,128]{1,0:T(8,128)(2,1)}, u32[]{:S(2)}, u32[]{:S(2)}) collective-permute-start(bf16[3072,128]{1,0:T(8,128)(2,1)} %shard_map.60), channel_id=1, source_target_pairs={{0,32},{1,225},{32,64},{33,1},{64,96},{65,33},{96,128},{97,65},{12... | collective-permute-start | bytes 2359304 | tf_op jit(solution)/shard_map/ppermute | solution.py:222
  53.2 14.3 %all-to-all-done.1.received_ref = bf16[16,16,1664]{2,1,0:T(8,128)(2,1)S(1)} async-done(((bf16[16,16,1664]{2,1,0:T(8,128)(2,1)}), bf16[16,16,1664]{2,1,0:T(8,128)(2,1)S(1)}, u32[]{:S(2)}, u32[]{:S(2)}) %all-to-all-start.1) | async-done | bytes 852000 | tf_op jit(solution)/shard_map/all_to_all | solution.py:250
  67.5 0.0 copy-done.5
  67.5 0.9 shard_map.58
  68.5 0.0 copy-start.2
  68.5 0.7 copy-done.2
  69.2 8.5 %all-to-all-start.2 = ((bf16[8,16,1536]{2,1,0:T(8,128)(2,1)}), bf16[8,16,1536]{2,1,0:T(8,128)(2,1)S(1)}, u32[]{:S(2)}, u32[]{:S(2)}) async-start(bf16[8,16,1536]{2,1,0:T(8,128)(2,1)} %copy-done.2), calls=%async_computation.2 | async-start | bytes 786432 | tf_op jit(solution)/shard_map/all_to_all | solution.py:289
  77.7 0.0 collective-permute-done.3.refs_2_
  77.7 9.3 %all-to-all-done.2.rows_ref = bf16[8,16,1536]{2,1,0:T(8,128)(2,1)S(1)} async-done(((bf16[8,16,1536]{2,1,0:T(8,128)(2,1)}), bf16[8,16,1536]{2,1,0:T(8,128)(2,1)S(1)}, u32[]{:S(2)}, u32[]{:S(2)}) %all-to-all-start.2) | async-done | bytes 393248 | tf_op jit(solution)/shard_map/all_to_all | solution.py:289
  87.0 3.9 %shard_map.61 = bf16[8,16,1536]{2,1,0:T(8,128)(2,1)} custom-call(bf16[8,16,1536]{2,1,0:T(8,128)(2,1)S(1)} %all-to-all-done.2.rows_ref, bf16[1536,384]{1,0:T(8,128)(2,1)S(1)} %bitcast.18, bf16[3072,256]{1,0:T(8,128)(2,1)} %collective-permute-done.2.before_hbm.refs_1_, bf16[3072,128]{1,0:T(8,128)(2,1)} %collective-permute-done.3.refs_2_, ...), custom_call_target="tpu_custom_call" | custom-call | flops 603979776 | bytes 4718592 | tf_op jit(solution)/shard_map/pallas_call | solution.py:23
  90.9 5.1 %all-to-all-start.3 = ((bf16[8,16,1536]{2,1,0:T(8,128)(2,1)}), bf16[8,16,1536]{2,1,0:T(8,128)(2,1)S(1)}, u32[]{:S(2)}, u32[]{:S(2)}) async-start(bf16[8,16,1536]{2,1,0:T(8,128)(2,1)} %shard_map.61), calls=%async_computation.3 | async-start | bytes 786432 | tf_op jit(solution)/shard_map/all_to_all | solution.py:308
  96.0 3.9 %shard_map.55 = (bf16[384,384]{1,0:T(8,128)(2,1)}, bf16[384,384]{1,0:T(8,128)(2,1)}) custom-call(bf16[1536,256]{1,0:T(8,128)(2,1)} %bitcast.26, bf16[384,1536]{1,0:T(8,128)(2,1)} %bitcast.24, bf16[384,1536]{1,0:T(8,128)(2,1)} %collective-permute-done.partner_feats_ref.partner_hbm), custom_call_target="tpu_custom_call" | custom-call | flops 603979776 | bytes 2359296 | tf_op jit(solution)/shard_map/pallas_call | solution.py:23
  99.8 6.0 %collective-permute-start.1 = (bf16[384,384]{1,0:T(8,128)(2,1)}, bf16[384,384]{1,0:T(8,128)(2,1)S(1)}, u32[]{:S(2)}, u32[]{:S(2)}) collective-permute-start(bf16[384,384]{1,0:T(8,128)(2,1)} %get-tuple-element.10), channel_id=1, source_target_pairs={{0,1},{1,0},{2,3},{3,2},{4,5},{5,4},{6,7},{7,6},{8,9},{9,8},{10,11... | collective-permute-start | bytes 884744 | tf_op jit(solution)/shard_map/ppermute | solution.py:265
  105.9 1.4 collective-permute-done.1.core_ref
  107.3 0.0 copy-start.3
  107.3 1.0 copy-done.3
  108.2 0.3 shard_map.56
  108.6 0.0 all-to-all-done.3.blocks_ref
  108.6 1.2 shard_map.62
  109.8 25.1 %all_to_all.25 = bf16[16,16,1536]{2,1,0:T(8,128)(2,1)S(1)} all-to-all(bf16[16,16,1536]{2,1,0:T(8,128)(2,1)S(1)} %shard_map.62), channel_id=1, replica_groups=mesh['xlo'=2,'yh'=4,'yl'=2,'xhi'=2,'z'=8,'core'=2] {'xhi','z'}, dimensions={0} | all-to-all | bytes 1572864 | tf_op jit(solution)/shard_map/all_to_all | solution.py:321
  134.9 7.5 %collective-permute-start.4 = (bf16[256,1536]{1,0:T(8,128)(2,1)S(1)}, bf16[256,1536]{1,0:T(8,128)(2,1)S(1)}, u32[]{:S(2)}, u32[]{:S(2)}) collective-permute-start(bf16[256,1536]{1,0:T(8,128)(2,1)S(1)} %bitcast.27), channel_id=1, source_target_pairs={{0,1},{1,0},{2,3},{3,2},{4,5},{5,4},{6,7},{7,6},{8,9},{9,8},{10,11... | collective-permute-start | bytes 2359304 | tf_op jit(solution)/shard_map/ppermute | solution.py:322
  142.4 1.9 %collective-permute-done.4 = bf16[256,1536]{1,0:T(8,128)(2,1)S(1)} collective-permute-done((bf16[256,1536]{1,0:T(8,128)(2,1)S(1)}, bf16[256,1536]{1,0:T(8,128)(2,1)S(1)}, u32[]{:S(2)}, u32[]{:S(2)}) %collective-permute-start.4) | collective-permute-done | bytes 786464 | tf_op jit(solution)/shard_map/ppermute | solution.py:322
  144.3 0.0 copy-start.6
  144.3 0.5 fusion.17
  144.8 0.8 copy-done.6
  145.6 1.5 %fusion.2 = bf16[1,384,1536]{2,1,0:T(8,128)(2,1)} fusion(f32[384,1536]{1,0:T(8,128)S(1)} %fusion.17, bf16[384,256]{1,0:T(8,128)(2,1)S(1)} %get-tuple-element.11.before_hbm, bf16[256,1536]{1,0:T(8,128)(2,1)S(1)} %bitcast.28, bf16[1,384,1536]{2,1,0:T(8,128)(2,1)S(1)} %copy-done.6), kind=kOutput, calls=%fused_computation.3 | convolution fusion | flops 304349184 | bytes 5701632 | tf_op jit(solution)/shard_map/dot_general | solution.py:324
  (3 shorter events, 0.0 us)
Async XLA Ops:
  0.0 14.7 %copy-start = (bf16[1,1536,384]{2,1,0:T(8,128)(2,1)S(1)}, bf16[1,1536,384]{2,1,0:T(8,128)(2,1)}, u32[]{:S(2)}) copy-start(bf16[1,1536,384]{2,1,0:T(8,128)(2,1)} %param.8) | copy-start | bytes 3538948
  0.0 14.7 %copy-start.1 = (bf16[1,384,1536]{2,1,0:T(8,128)(2,1)S(1)}, bf16[1,384,1536]{2,1,0:T(8,128)(2,1)}, u32[]{:S(2)}) copy-start(bf16[1,384,1536]{2,1,0:T(8,128)(2,1)} %param.9) | copy-start | bytes 3538948
  0.1 14.7 %copy-start.4 = (bf16[96,512]{1,0:T(8,128)(2,1)S(1)}, bf16[96,512]{1,0:T(8,128)(2,1)}, u32[]{:S(2)}) copy-start(bf16[96,512]{1,0:T(8,128)(2,1)} %before_hbm.1) | copy-start | bytes 294916
  2.3 27.0 %all-to-all-start = ((bf16[16,96,256]{2,1,0:T(8,128)(2,1)}), bf16[16,96,256]{2,1,0:T(8,128)(2,1)S(1)}, u32[]{:S(2)}, u32[]{:S(2)}) async-start(bf16[16,96,256]{2,1,0:T(8,128)(2,1)} %broadcast_in_dim.4), calls=%async_computation | async-start | bytes 1572864 | tf_op jit(solution)/shard_map/all_to_all | solution.py:185
  11.0 8.5 %collective-permute-start = (bf16[384,1536]{1,0:T(8,128)(2,1)}, bf16[384,1536]{1,0:T(8,128)(2,1)}, u32[]{:S(2)}, u32[]{:S(2)}) collective-permute-start(bf16[384,1536]{1,0:T(8,128)(2,1)} %bitcast.22), channel_id=1, source_target_pairs={{0,1},{1,0},{2,3},{3,2},{4,5},{5,4},{6,7},{7,6},{8,9},{9,8},{10,11... | collective-permute-start | bytes 3538952 | tf_op jit(solution)/shard_map/ppermute | solution.py:202
  16.1 32.9 %collective-permute-start.2 = (bf16[3072,256]{1,0:T(8,128)(2,1)}, bf16[3072,256]{1,0:T(8,128)(2,1)}, u32[]{:S(2)}, u32[]{:S(2)}) collective-permute-start(bf16[3072,256]{1,0:T(8,128)(2,1)} %shard_map.59), channel_id=1, source_target_pairs={{0,224},{1,33},{32,0},{33,65},{64,32},{65,97},{96,64},{97,129},{12... | collective-permute-start | bytes 4718600 | tf_op jit(solution)/shard_map/ppermute | solution.py:222
  29.3 0.9 copy-start.7
  35.2 32.4 %all-to-all-start.1 = ((bf16[16,16,1664]{2,1,0:T(8,128)(2,1)}), bf16[16,16,1664]{2,1,0:T(8,128)(2,1)S(1)}, u32[]{:S(2)}, u32[]{:S(2)}) async-start(bf16[16,16,1664]{2,1,0:T(8,128)(2,1)} %bitcast.29), calls=%async_computation.1 | async-start | bytes 1703936 | tf_op jit(solution)/shard_map/all_to_all | solution.py:250
  49.0 18.6 %copy-start.5 = (f32[1,1536]{1,0:T(1,128)S(1)}, f32[1,1536]{1,0:T(1,128)}, u32[]{:S(2)}) copy-start(f32[1,1536]{1,0:T(1,128)} %gain_ref.1) | copy-start | bytes 18436
  50.2 27.5 %collective-permute-start.3 = (bf16[3072,128]{1,0:T(8,128)(2,1)}, bf16[3072,128]{1,0:T(8,128)(2,1)}, u32[]{:S(2)}, u32[]{:S(2)}) collective-permute-start(bf16[3072,128]{1,0:T(8,128)(2,1)} %shard_map.60), channel_id=1, source_target_pairs={{0,32},{1,225},{32,64},{33,1},{64,96},{65,33},{96,128},{97,65},{12... | collective-permute-start | bytes 2359304 | tf_op jit(solution)/shard_map/ppermute | solution.py:222
  68.5 0.7 copy-start.2
  69.2 17.8 %all-to-all-start.2 = ((bf16[8,16,1536]{2,1,0:T(8,128)(2,1)}), bf16[8,16,1536]{2,1,0:T(8,128)(2,1)S(1)}, u32[]{:S(2)}, u32[]{:S(2)}) async-start(bf16[8,16,1536]{2,1,0:T(8,128)(2,1)} %copy-done.2), calls=%async_computation.2 | async-start | bytes 786432 | tf_op jit(solution)/shard_map/all_to_all | solution.py:289
  90.9 17.7 %all-to-all-start.3 = ((bf16[8,16,1536]{2,1,0:T(8,128)(2,1)}), bf16[8,16,1536]{2,1,0:T(8,128)(2,1)S(1)}, u32[]{:S(2)}, u32[]{:S(2)}) async-start(bf16[8,16,1536]{2,1,0:T(8,128)(2,1)} %shard_map.61), calls=%async_computation.3 | async-start | bytes 786432 | tf_op jit(solution)/shard_map/all_to_all | solution.py:308
  99.8 7.4 %collective-permute-start.1 = (bf16[384,384]{1,0:T(8,128)(2,1)}, bf16[384,384]{1,0:T(8,128)(2,1)S(1)}, u32[]{:S(2)}, u32[]{:S(2)}) collective-permute-start(bf16[384,384]{1,0:T(8,128)(2,1)} %get-tuple-element.10), channel_id=1, source_target_pairs={{0,1},{1,0},{2,3},{3,2},{4,5},{5,4},{6,7},{7,6},{8,9},{9,8},{10,11... | collective-permute-start | bytes 884744 | tf_op jit(solution)/shard_map/ppermute | solution.py:265
  107.3 1.0 copy-start.3
  134.9 9.4 %collective-permute-start.4 = (bf16[256,1536]{1,0:T(8,128)(2,1)S(1)}, bf16[256,1536]{1,0:T(8,128)(2,1)S(1)}, u32[]{:S(2)}, u32[]{:S(2)}) collective-permute-start(bf16[256,1536]{1,0:T(8,128)(2,1)S(1)} %bitcast.27), channel_id=1, source_target_pairs={{0,1},{1,0},{2,3},{3,2},{4,5},{5,4},{6,7},{7,6},{8,9},{9,8},{10,11... | collective-permute-start | bytes 2359304 | tf_op jit(solution)/shard_map/ppermute | solution.py:322
  144.3 1.3 copy-start.6

commit v11 on v10

--- a/solution.py
+++ b/solution.py
@@ -321,9 +321,10 @@
     outs = lax.all_to_all(copies, ("xhi", "z"), 0, 0, tiled=True).reshape(half, width)
     outs_b = lax.ppermute(outs, "core", other())
 
-    mixed = jnp.dot(weights, outs, preferred_element_type=F32)
-    mixed += jnp.dot(weights_b, outs_b, preferred_element_type=F32)
-    return (feats.astype(F32) + mixed).astype(BF16)[None]
+    near = feats.astype(F32) + jnp.dot(weights, outs, preferred_element_type=F32)
+    near = lax.optimization_barrier(near)
+    far = jnp.dot(weights_b, outs_b, preferred_element_type=F32)
+    return (near + far).astype(BF16)[None]
 
 
 def solution(mesh):

time: 150 us -> 149 us (level)
  no operation moved by 1% of the time
where the time goes in v11:
time: 149 us; the launch traced here: 146 us
  starting transfers between devices  59.8 us (40%)
  waiting for transfers between devices  36.3 us (24%)
  blocking collectives  24.9 us (17%)
  Pallas kernels  17.8 us (12%)
  local copies, waits for them, and re-layouts  3.57 us (2%)
  matrix products  2.23 us (1%)
    all_to_all x1, blocking collectives, local(): lax.all_to_all(copies, ('xhi', 'z'), 0, 0, tiled=True).reshape(half, width)  24.9 us
    pallas_call x8, Pallas kernels, kernel_call(): pl.pallas_call(body, out_shape=outs, in_specs=specs, out_specs=jax.tree.m...  17.8 us
    all_to_all x1, waiting for transfers between devices, local(): lax.all_to_all(message.reshape(owners, per_owner, width + EXTRA), ('xhi',...  14.3 us
    all_to_all x1, starting transfers between devices, local(): lax.all_to_all(message.reshape(owners, per_owner, width + EXTRA), ('xhi',...  13.8 us
    all_to_all x1, waiting for transfers between devices, sent_to_all(): lax.all_to_all(jnp.broadcast_to(value[None], (length, *value.shape)), axe...  9.77 us
    all_to_all x1, waiting for transfers between devices, local(): rows = lax.all_to_all(slots, ('xlo', 'yh'), 0, 0, tiled=True)  9.34 us
    all_to_all x1, starting transfers between devices, sent_to_all(): lax.all_to_all(jnp.broadcast_to(value[None], (length, *value.shape)), axe...  8.68 us
    all_to_all x1, starting transfers between devices, local(): rows = lax.all_to_all(slots, ('xlo', 'yh'), 0, 0, tiled=True)  8.45 us
  transfers between devices with their start and end apart: 9, of which 5 were waited for; matrix products, arithmetic and copies ran while one was open for 0% of the time, Pallas kernels for 9%

profile of v11, /device:TPU:1, one launch (start us, length us, event | category | flops | bytes accessed | tf_op | source)
XLA Modules:
  0.0 146.1 jit_solution(148420928379384413)
XLA Ops:
  0.0 0.0 copy-start.4
  0.0 0.0 copy-start.1
  0.0 0.0 copy-start
  0.1 1.3 fusion.1
  1.3 1.0 broadcast_in_dim.4
  2.3 8.7 %all-to-all-start = ((bf16[16,96,256]{2,1,0:T(8,128)(2,1)}), bf16[16,96,256]{2,1,0:T(8,128)(2,1)S(1)}, u32[]{:S(2)}, u32[]{:S(2)}) async-start(bf16[16,96,256]{2,1,0:T(8,128)(2,1)} %broadcast_in_dim.4), calls=%async_computation | async-start | bytes 1572864 | tf_op jit(solution)/shard_map/all_to_all | solution.py:185
  11.0 3.7 %collective-permute-start = (bf16[384,1536]{1,0:T(8,128)(2,1)}, bf16[384,1536]{1,0:T(8,128)(2,1)}, u32[]{:S(2)}, u32[]{:S(2)}) collective-permute-start(bf16[384,1536]{1,0:T(8,128)(2,1)} %bitcast.22), channel_id=1, source_target_pairs={{0,1},{1,0},{2,3},{3,2},{4,5},{5,4},{6,7},{7,6},{8,9},{9,8},{10,11... | collective-permute-start | bytes 3538952 | tf_op jit(solution)/shard_map/ppermute | solution.py:202
  14.7 0.0 copy-done.4
  14.7 0.0 copy-done.1
  14.7 0.0 copy-done
  14.7 1.3 shard_map.59
  16.1 3.4 %collective-permute-start.2 = (bf16[3072,256]{1,0:T(8,128)(2,1)}, bf16[3072,256]{1,0:T(8,128)(2,1)}, u32[]{:S(2)}, u32[]{:S(2)}) collective-permute-start(bf16[3072,256]{1,0:T(8,128)(2,1)} %shard_map.59), channel_id=1, source_target_pairs={{0,224},{1,33},{32,0},{33,65},{64,32},{65,97},{96,64},{97,129},{12... | collective-permute-start | bytes 4718600 | tf_op jit(solution)/shard_map/ppermute | solution.py:222
  19.5 0.0 collective-permute-done.partner_feats_ref.partner_hbm
  19.5 9.8 %all-to-all-done = bf16[16,96,256]{2,1,0:T(8,128)(2,1)S(1)} async-done(((bf16[16,96,256]{2,1,0:T(8,128)(2,1)}), bf16[16,96,256]{2,1,0:T(8,128)(2,1)S(1)}, u32[]{:S(2)}, u32[]{:S(2)}) %all-to-all-start) | async-done | bytes 786464 | tf_op jit(solution)/shard_map/all_to_all | solution.py:185
  29.3 0.0 copy-start.7
  29.3 0.9 copy-done.7
  30.2 5.0 %shard_map.57 = bf16[256,1664]{1,0:T(8,128)(2,1)} custom-call(bf16[1536,256]{1,0:T(8,128)(2,1)} %bitcast.25, bf16[384,1536]{1,0:T(8,128)(2,1)} %bitcast.23, bf16[384,1536]{1,0:T(8,128)(2,1)} %collective-permute-done.partner_feats_ref.partner_hbm), custom_call_target="tpu_custom_call" | custom-call | flops 1207959552 | bytes 3932160 | tf_op jit(solution)/shard_map/pallas_call | solution.py:23
  35.1 13.8 %all-to-all-start.1 = ((bf16[16,16,1664]{2,1,0:T(8,128)(2,1)}), bf16[16,16,1664]{2,1,0:T(8,128)(2,1)S(1)}, u32[]{:S(2)}, u32[]{:S(2)}) async-start(bf16[16,16,1664]{2,1,0:T(8,128)(2,1)} %bitcast.29), calls=%async_computation.1 | async-start | bytes 1703936 | tf_op jit(solution)/shard_map/all_to_all | solution.py:250
  49.0 0.0 copy-start.5
  49.0 0.0 collective-permute-done.2.before_hbm.refs_1_
  49.0 1.2 shard_map.60
  50.2 3.0 %collective-permute-start.3 = (bf16[3072,128]{1,0:T(8,128)(2,1)}, bf16[3072,128]{1,0:T(8,128)(2,1)}, u32[]{:S(2)}, u32[]{:S(2)}) collective-permute-start(bf16[3072,128]{1,0:T(8,128)(2,1)} %shard_map.60), channel_id=1, source_target_pairs={{0,32},{1,225},{32,64},{33,1},{64,96},{65,33},{96,128},{97,65},{12... | collective-permute-start | bytes 2359304 | tf_op jit(solution)/shard_map/ppermute | solution.py:222
  53.2 14.3 %all-to-all-done.1.received_ref = bf16[16,16,1664]{2,1,0:T(8,128)(2,1)S(1)} async-done(((bf16[16,16,1664]{2,1,0:T(8,128)(2,1)}), bf16[16,16,1664]{2,1,0:T(8,128)(2,1)S(1)}, u32[]{:S(2)}, u32[]{:S(2)}) %all-to-all-start.1) | async-done | bytes 852000 | tf_op jit(solution)/shard_map/all_to_all | solution.py:250
  67.5 0.0 copy-done.5
  67.5 0.9 shard_map.58
  68.5 0.0 copy-start.2
  68.5 0.7 copy-done.2
  69.2 8.4 %all-to-all-start.2 = ((bf16[8,16,1536]{2,1,0:T(8,128)(2,1)}), bf16[8,16,1536]{2,1,0:T(8,128)(2,1)S(1)}, u32[]{:S(2)}, u32[]{:S(2)}) async-start(bf16[8,16,1536]{2,1,0:T(8,128)(2,1)} %copy-done.2), calls=%async_computation.2 | async-start | bytes 786432 | tf_op jit(solution)/shard_map/all_to_all | solution.py:289
  77.7 0.0 collective-permute-done.3.refs_2_
  77.7 9.3 %all-to-all-done.2.rows_ref = bf16[8,16,1536]{2,1,0:T(8,128)(2,1)S(1)} async-done(((bf16[8,16,1536]{2,1,0:T(8,128)(2,1)}), bf16[8,16,1536]{2,1,0:T(8,128)(2,1)S(1)}, u32[]{:S(2)}, u32[]{:S(2)}) %all-to-all-start.2) | async-done | bytes 393248 | tf_op jit(solution)/shard_map/all_to_all | solution.py:289
  87.0 3.9 %shard_map.61 = bf16[8,16,1536]{2,1,0:T(8,128)(2,1)} custom-call(bf16[8,16,1536]{2,1,0:T(8,128)(2,1)S(1)} %all-to-all-done.2.rows_ref, bf16[1536,384]{1,0:T(8,128)(2,1)S(1)} %bitcast.18, bf16[3072,256]{1,0:T(8,128)(2,1)} %collective-permute-done.2.before_hbm.refs_1_, bf16[3072,128]{1,0:T(8,128)(2,1)} %collective-permute-done.3.refs_2_, ...), custom_call_target="tpu_custom_call" | custom-call | flops 603979776 | bytes 4718592 | tf_op jit(solution)/shard_map/pallas_call | solution.py:23
  90.9 5.1 %all-to-all-start.3 = ((bf16[8,16,1536]{2,1,0:T(8,128)(2,1)}), bf16[8,16,1536]{2,1,0:T(8,128)(2,1)S(1)}, u32[]{:S(2)}, u32[]{:S(2)}) async-start(bf16[8,16,1536]{2,1,0:T(8,128)(2,1)} %shard_map.61), calls=%async_computation.3 | async-start | bytes 786432 | tf_op jit(solution)/shard_map/all_to_all | solution.py:308
  96.0 0.0 copy-start.6
  96.0 4.0 %shard_map.55 = (bf16[384,384]{1,0:T(8,128)(2,1)}, bf16[384,384]{1,0:T(8,128)(2,1)}) custom-call(bf16[1536,256]{1,0:T(8,128)(2,1)} %bitcast.26, bf16[384,1536]{1,0:T(8,128)(2,1)} %bitcast.24, bf16[384,1536]{1,0:T(8,128)(2,1)} %collective-permute-done.partner_feats_ref.partner_hbm), custom_call_target="tpu_custom_call" | custom-call | flops 603979776 | bytes 2359296 | tf_op jit(solution)/shard_map/pallas_call | solution.py:23
  99.9 6.0 %collective-permute-start.1 = (bf16[384,384]{1,0:T(8,128)(2,1)}, bf16[384,384]{1,0:T(8,128)(2,1)S(1)}, u32[]{:S(2)}, u32[]{:S(2)}) collective-permute-start(bf16[384,384]{1,0:T(8,128)(2,1)} %get-tuple-element.10), channel_id=1, source_target_pairs={{0,1},{1,0},{2,3},{3,2},{4,5},{5,4},{6,7},{7,6},{8,9},{9,8},{10,11... | collective-permute-start | bytes 884744 | tf_op jit(solution)/shard_map/ppermute | solution.py:265
  105.9 1.4 collective-permute-done.1.core_ref
  107.3 0.0 copy-start.3
  107.3 1.0 copy-done.3
  108.3 0.3 shard_map.56
  108.6 0.0 all-to-all-done.3.blocks_ref
  108.7 1.2 shard_map.62
  109.9 24.9 %all_to_all.25 = bf16[16,16,1536]{2,1,0:T(8,128)(2,1)S(1)} all-to-all(bf16[16,16,1536]{2,1,0:T(8,128)(2,1)S(1)} %shard_map.62), channel_id=1, replica_groups=mesh['xlo'=2,'yh'=4,'yl'=2,'xhi'=2,'z'=8,'core'=2] {'xhi','z'}, dimensions={0} | all-to-all | bytes 1572864 | tf_op jit(solution)/shard_map/all_to_all | solution.py:321
  134.8 7.6 %collective-permute-start.4 = (bf16[256,1536]{1,0:T(8,128)(2,1)S(1)}, bf16[256,1536]{1,0:T(8,128)(2,1)S(1)}, u32[]{:S(2)}, u32[]{:S(2)}) collective-permute-start(bf16[256,1536]{1,0:T(8,128)(2,1)S(1)} %bitcast.27), channel_id=1, source_target_pairs={{0,1},{1,0},{2,3},{3,2},{4,5},{5,4},{6,7},{7,6},{8,9},{9,8},{10,11... | collective-permute-start | bytes 2359304 | tf_op jit(solution)/shard_map/ppermute | solution.py:322
  142.4 0.0 copy-done.6
  142.4 0.5 convolution_add_fusion
  142.9 1.4 collective-permute-done.4
  144.3 0.5 fusion.15
  144.8 1.3 fusion
  (3 shorter events, 0.0 us)
Async XLA Ops:
  0.0 14.7 %copy-start.4 = (bf16[96,512]{1,0:T(8,128)(2,1)S(1)}, bf16[96,512]{1,0:T(8,128)(2,1)}, u32[]{:S(2)}) copy-start(bf16[96,512]{1,0:T(8,128)(2,1)} %before_hbm.1) | copy-start | bytes 294916
  0.0 14.7 %copy-start.1 = (bf16[1,384,1536]{2,1,0:T(8,128)(2,1)S(1)}, bf16[1,384,1536]{2,1,0:T(8,128)(2,1)}, u32[]{:S(2)}) copy-start(bf16[1,384,1536]{2,1,0:T(8,128)(2,1)} %param.9) | copy-start | bytes 3538948
  0.0 14.7 %copy-start = (bf16[1,1536,384]{2,1,0:T(8,128)(2,1)S(1)}, bf16[1,1536,384]{2,1,0:T(8,128)(2,1)}, u32[]{:S(2)}) copy-start(bf16[1,1536,384]{2,1,0:T(8,128)(2,1)} %param.8) | copy-start | bytes 3538948
  2.3 27.0 %all-to-all-start = ((bf16[16,96,256]{2,1,0:T(8,128)(2,1)}), bf16[16,96,256]{2,1,0:T(8,128)(2,1)S(1)}, u32[]{:S(2)}, u32[]{:S(2)}) async-start(bf16[16,96,256]{2,1,0:T(8,128)(2,1)} %broadcast_in_dim.4), calls=%async_computation | async-start | bytes 1572864 | tf_op jit(solution)/shard_map/all_to_all | solution.py:185
  11.0 8.5 %collective-permute-start = (bf16[384,1536]{1,0:T(8,128)(2,1)}, bf16[384,1536]{1,0:T(8,128)(2,1)}, u32[]{:S(2)}, u32[]{:S(2)}) collective-permute-start(bf16[384,1536]{1,0:T(8,128)(2,1)} %bitcast.22), channel_id=1, source_target_pairs={{0,1},{1,0},{2,3},{3,2},{4,5},{5,4},{6,7},{7,6},{8,9},{9,8},{10,11... | collective-permute-start | bytes 3538952 | tf_op jit(solution)/shard_map/ppermute | solution.py:202
  16.1 32.9 %collective-permute-start.2 = (bf16[3072,256]{1,0:T(8,128)(2,1)}, bf16[3072,256]{1,0:T(8,128)(2,1)}, u32[]{:S(2)}, u32[]{:S(2)}) collective-permute-start(bf16[3072,256]{1,0:T(8,128)(2,1)} %shard_map.59), channel_id=1, source_target_pairs={{0,224},{1,33},{32,0},{33,65},{64,32},{65,97},{96,64},{97,129},{12... | collective-permute-start | bytes 4718600 | tf_op jit(solution)/shard_map/ppermute | solution.py:222
  29.3 0.9 copy-start.7
  35.1 32.4 %all-to-all-start.1 = ((bf16[16,16,1664]{2,1,0:T(8,128)(2,1)}), bf16[16,16,1664]{2,1,0:T(8,128)(2,1)S(1)}, u32[]{:S(2)}, u32[]{:S(2)}) async-start(bf16[16,16,1664]{2,1,0:T(8,128)(2,1)} %bitcast.29), calls=%async_computation.1 | async-start | bytes 1703936 | tf_op jit(solution)/shard_map/all_to_all | solution.py:250
  49.0 18.6 %copy-start.5 = (f32[1,1536]{1,0:T(1,128)S(1)}, f32[1,1536]{1,0:T(1,128)}, u32[]{:S(2)}) copy-start(f32[1,1536]{1,0:T(1,128)} %gain_ref.1) | copy-start | bytes 18436
  50.2 27.5 %collective-permute-start.3 = (bf16[3072,128]{1,0:T(8,128)(2,1)}, bf16[3072,128]{1,0:T(8,128)(2,1)}, u32[]{:S(2)}, u32[]{:S(2)}) collective-permute-start(bf16[3072,128]{1,0:T(8,128)(2,1)} %shard_map.60), channel_id=1, source_target_pairs={{0,32},{1,225},{32,64},{33,1},{64,96},{65,33},{96,128},{97,65},{12... | collective-permute-start | bytes 2359304 | tf_op jit(solution)/shard_map/ppermute | solution.py:222
  68.5 0.7 copy-start.2
  69.2 17.8 %all-to-all-start.2 = ((bf16[8,16,1536]{2,1,0:T(8,128)(2,1)}), bf16[8,16,1536]{2,1,0:T(8,128)(2,1)S(1)}, u32[]{:S(2)}, u32[]{:S(2)}) async-start(bf16[8,16,1536]{2,1,0:T(8,128)(2,1)} %copy-done.2), calls=%async_computation.2 | async-start | bytes 786432 | tf_op jit(solution)/shard_map/all_to_all | solution.py:289
  90.9 17.8 %all-to-all-start.3 = ((bf16[8,16,1536]{2,1,0:T(8,128)(2,1)}), bf16[8,16,1536]{2,1,0:T(8,128)(2,1)S(1)}, u32[]{:S(2)}, u32[]{:S(2)}) async-start(bf16[8,16,1536]{2,1,0:T(8,128)(2,1)} %shard_map.61), calls=%async_computation.3 | async-start | bytes 786432 | tf_op jit(solution)/shard_map/all_to_all | solution.py:308
  96.0 46.5 %copy-start.6 = (bf16[1,384,1536]{2,1,0:T(8,128)(2,1)S(1)}, bf16[1,384,1536]{2,1,0:T(8,128)(2,1)}, u32[]{:S(2)}) copy-start(bf16[1,384,1536]{2,1,0:T(8,128)(2,1)} %param.5) | copy-start | bytes 3538948
  99.9 7.4 %collective-permute-start.1 = (bf16[384,384]{1,0:T(8,128)(2,1)}, bf16[384,384]{1,0:T(8,128)(2,1)S(1)}, u32[]{:S(2)}, u32[]{:S(2)}) collective-permute-start(bf16[384,384]{1,0:T(8,128)(2,1)} %get-tuple-element.10), channel_id=1, source_target_pairs={{0,1},{1,0},{2,3},{3,2},{4,5},{5,4},{6,7},{7,6},{8,9},{9,8},{10,11... | collective-permute-start | bytes 884744 | tf_op jit(solution)/shard_map/ppermute | solution.py:265
  107.3 1.0 copy-start.3
  134.8 9.5 %collective-permute-start.4 = (bf16[256,1536]{1,0:T(8,128)(2,1)S(1)}, bf16[256,1536]{1,0:T(8,128)(2,1)S(1)}, u32[]{:S(2)}, u32[]{:S(2)}) collective-permute-start(bf16[256,1536]{1,0:T(8,128)(2,1)S(1)} %bitcast.27), channel_id=1, source_target_pairs={{0,1},{1,0},{2,3},{3,2},{4,5},{5,4},{6,7},{7,6},{8,9},{9,8},{10,11... | collective-permute-start | bytes 2359304 | tf_op jit(solution)/shard_map/ppermute | solution.py:322

commit v12 on v11

--- a/solution.py
+++ b/solution.py
@@ -57,6 +57,19 @@
         for j, piece in enumerate((first, second, column - first - second)):
             packed = jnp.where(lane == 3 * k + j, piece, packed)
     return packed.astype(BF16)
+
+
+def columns_kernel(per_owner, core_ref, router_ref, copies_hbm, own_ref, semaphores):
+    half = own_ref.shape[1]
+    shape = (router_ref.shape[1], half)
+    row = lax.broadcasted_iota(jnp.int32, shape, 0)
+    col = lax.broadcasted_iota(jnp.int32, shape, 1)
+    wanted = (col // per_owner * 2 + core_ref[0]) * per_owner + col % per_owner
+    pick = jnp.where(row == wanted, 1.0, 0.0).astype(BF16)
+    own_ref[...] = jnp.dot(router_ref[...], pick, preferred_element_type=F32).astype(BF16)
+    copies = [started(own_ref, copies_hbm.at[k], semaphores, k) for k in range(copies_hbm.shape[0])]
+    for copy in copies:
+        copy.wait()
 
 
 def dispatch_kernel(
@@ -180,13 +193,6 @@
         copy.wait()
 
 
-def sent_to_all(value, axes):
-    length = lax.axis_size(axes)
-    return lax.all_to_all(
-        jnp.broadcast_to(value[None], (length, *value.shape)), axes, 0, 0, tiled=True
-    )
-
-
 def local(tokens, router, norm_gain, w_in, w_out):
     feats = tokens[0]
     count, width = feats.shape
@@ -221,12 +227,19 @@
         )
         given.append(lax.ppermute(packed, (*Y, "core"), perm))
 
-    row = lax.broadcasted_iota(jnp.int32, (slot_count, half), 0)
-    col = lax.broadcasted_iota(jnp.int32, (slot_count, half), 1)
-    wanted = (col // per_owner * 2 + core) * per_owner + col % per_owner
-    pick = (row == wanted).astype(BF16)
-    own_columns = jnp.dot(router, pick, preferred_element_type=F32).astype(BF16)
-    columns = sent_to_all(own_columns, ("xlo", *Y)).reshape(width, half)
+    copies = kernel_call(
+        functools.partial(columns_kernel, per_owner),
+        shape((2 * groups, router.shape[0], half), BF16),
+        2 * router.shape[0] * slot_count * half,
+        4 * width * half,
+        [pl.BlockSpec(memory_space=pltpu.SMEM), VMEM],
+        jnp.full((1,), core, jnp.int32),
+        router,
+        out_specs=HBM,
+        scratch=[pltpu.VMEM((router.shape[0], half), BF16), pltpu.SemaphoreType.DMA((2 * groups,))],
+        room=58,
+    )
+    columns = lax.all_to_all(copies, ("xlo", *Y), 0, 0, tiled=True).reshape(width, half)
 
     message = kernel_call(
         dispatch_kernel,

time: 149 us -> 149 us (level)
  Pallas kernels: 17.8 us -> 20 us
    pallas_call x8 -> x9, Pallas kernels: 17.8 us -> 20 us  [kernel_call(): pl.pallas_call(body, out_shape=outs, in_specs=specs, out_specs=jax.tree.m...]
where the time goes in v12:
time: 149 us; the launch traced here: 146 us
  starting transfers between devices  59.9 us (40%)
  waiting for transfers between devices  36.2 us (24%)
  blocking collectives  25.1 us (17%)
  Pallas kernels  20 us (13%)
  local copies, waits for them, and re-layouts  2.62 us (2%)
    all_to_all x1, blocking collectives, local(): lax.all_to_all(copies, ('xhi', 'z'), 0, 0, tiled=True).reshape(half, width)  25.1 us
    pallas_call x9, Pallas kernels, kernel_call(): pl.pallas_call(body, out_shape=outs, in_specs=specs, out_specs=jax.tree.m...  20 us
    all_to_all x1, waiting for transfers between devices, local(): lax.all_to_all(message.reshape(owners, per_owner, width + EXTRA), ('xhi',...  14.3 us
    all_to_all x1, starting transfers between devices, local(): lax.all_to_all(message.reshape(owners, per_owner, width + EXTRA), ('xhi',...  13.8 us
    all_to_all x1, waiting for transfers between devices, local(): lax.all_to_all(copies, ('xlo', *Y), 0, 0, tiled=True).reshape(width, half)  9.77 us
    all_to_all x1, waiting for transfers between devices, local(): rows = lax.all_to_all(slots, ('xlo', 'yh'), 0, 0, tiled=True)  9.31 us
    all_to_all x1, starting transfers between devices, local(): lax.all_to_all(copies, ('xlo', *Y), 0, 0, tiled=True).reshape(width, half)  8.69 us
    all_to_all x1, starting transfers between devices, local(): rows = lax.all_to_all(slots, ('xlo', 'yh'), 0, 0, tiled=True)  8.45 us
  transfers between devices with their start and end apart: 9, of which 5 were waited for; matrix products, arithmetic and copies ran while one was open for 0% of the time, Pallas kernels for 9%

profile of v12, /device:TPU:1, one launch (start us, length us, event | category | flops | bytes accessed | tf_op | source)
XLA Modules:
  0.0 146.3 jit_solution(9229012172444720826)
XLA Ops:
  0.0 0.0 copy-start.3
  0.0 0.0 copy-start.1
  0.0 0.0 copy-start
  0.0 2.2 %shard_map.55 = bf16[16,96,256]{2,1,0:T(8,128)(2,1)} custom-call(s32[1]{0:T(128)} %bitcast.1.core_ref, bf16[96,512]{1,0:T(8,128)(2,1)} %before_hbm.1), custom_call_target="tpu_custom_call" | custom-call | flops 25165824 | bytes 1572864 | tf_op jit(solution)/shard_map/pallas_call | solution.py:23
  2.3 8.7 %all-to-all-start = ((bf16[16,96,256]{2,1,0:T(8,128)(2,1)}), bf16[16,96,256]{2,1,0:T(8,128)(2,1)S(1)}, u32[]{:S(2)}, u32[]{:S(2)}) async-start(bf16[16,96,256]{2,1,0:T(8,128)(2,1)} %shard_map.55), calls=%async_computation | async-start | bytes 1572864 | tf_op jit(solution)/shard_map/all_to_all | solution.py:242
  11.0 3.7 %collective-permute-start = (bf16[384,1536]{1,0:T(8,128)(2,1)}, bf16[384,1536]{1,0:T(8,128)(2,1)}, u32[]{:S(2)}, u32[]{:S(2)}) collective-permute-start(bf16[384,1536]{1,0:T(8,128)(2,1)} %bitcast.20), channel_id=1, source_target_pairs={{0,1},{1,0},{2,3},{3,2},{4,5},{5,4},{6,7},{7,6},{8,9},{9,8},{10,11... | collective-permute-start | bytes 3538952 | tf_op jit(solution)/shard_map/ppermute | solution.py:208
  14.7 0.0 copy-done.3
  14.7 0.0 copy-done.1
  14.7 0.0 copy-done
  14.7 1.3 shard_map.60
  16.0 3.4 %collective-permute-start.2 = (bf16[3072,256]{1,0:T(8,128)(2,1)}, bf16[3072,256]{1,0:T(8,128)(2,1)}, u32[]{:S(2)}, u32[]{:S(2)}) collective-permute-start(bf16[3072,256]{1,0:T(8,128)(2,1)} %shard_map.60), channel_id=1, source_target_pairs={{0,224},{1,33},{32,0},{33,65},{64,32},{65,97},{96,64},{97,129},{12... | collective-permute-start | bytes 4718600 | tf_op jit(solution)/shard_map/ppermute | solution.py:228
  19.5 0.0 collective-permute-done.partner_feats_ref.partner_hbm
  19.5 9.8 %all-to-all-done = bf16[16,96,256]{2,1,0:T(8,128)(2,1)S(1)} async-done(((bf16[16,96,256]{2,1,0:T(8,128)(2,1)}), bf16[16,96,256]{2,1,0:T(8,128)(2,1)S(1)}, u32[]{:S(2)}, u32[]{:S(2)}) %all-to-all-start) | async-done | bytes 786464 | tf_op jit(solution)/shard_map/all_to_all | solution.py:242
  29.3 0.0 copy-start.7
  29.3 0.9 copy-done.7
  30.1 5.0 %shard_map.58 = bf16[256,1664]{1,0:T(8,128)(2,1)} custom-call(bf16[1536,256]{1,0:T(8,128)(2,1)} %bitcast.23, bf16[384,1536]{1,0:T(8,128)(2,1)} %bitcast.21, bf16[384,1536]{1,0:T(8,128)(2,1)} %collective-permute-done.partner_feats_ref.partner_hbm), custom_call_target="tpu_custom_call" | custom-call | flops 1207959552 | bytes 3932160 | tf_op jit(solution)/shard_map/pallas_call | solution.py:23
  35.1 13.8 %all-to-all-start.1 = ((bf16[16,16,1664]{2,1,0:T(8,128)(2,1)}), bf16[16,16,1664]{2,1,0:T(8,128)(2,1)S(1)}, u32[]{:S(2)}, u32[]{:S(2)}) async-start(bf16[16,16,1664]{2,1,0:T(8,128)(2,1)} %bitcast.27), calls=%async_computation.1 | async-start | bytes 1703936 | tf_op jit(solution)/shard_map/all_to_all | solution.py:263
  48.9 0.0 copy-start.5
  48.9 0.0 collective-permute-done.2.before_hbm.refs_1_
  48.9 1.2 shard_map.61
  50.1 3.0 %collective-permute-start.3 = (bf16[3072,128]{1,0:T(8,128)(2,1)}, bf16[3072,128]{1,0:T(8,128)(2,1)}, u32[]{:S(2)}, u32[]{:S(2)}) collective-permute-start(bf16[3072,128]{1,0:T(8,128)(2,1)} %shard_map.61), channel_id=1, source_target_pairs={{0,32},{1,225},{32,64},{33,1},{64,96},{65,33},{96,128},{97,65},{12... | collective-permute-start | bytes 2359304 | tf_op jit(solution)/shard_map/ppermute | solution.py:228
  53.1 14.3 %all-to-all-done.1.received_ref = bf16[16,16,1664]{2,1,0:T(8,128)(2,1)S(1)} async-done(((bf16[16,16,1664]{2,1,0:T(8,128)(2,1)}), bf16[16,16,1664]{2,1,0:T(8,128)(2,1)S(1)}, u32[]{:S(2)}, u32[]{:S(2)}) %all-to-all-start.1) | async-done | bytes 852000 | tf_op jit(solution)/shard_map/all_to_all | solution.py:263
  67.5 0.0 copy-done.5
  67.5 0.9 shard_map.59
  68.4 0.0 copy-start.2
  68.5 0.7 copy-done.2
  69.2 8.5 %all-to-all-start.2 = ((bf16[8,16,1536]{2,1,0:T(8,128)(2,1)}), bf16[8,16,1536]{2,1,0:T(8,128)(2,1)S(1)}, u32[]{:S(2)}, u32[]{:S(2)}) async-start(bf16[8,16,1536]{2,1,0:T(8,128)(2,1)} %copy-done.2), calls=%async_computation.2 | async-start | bytes 786432 | tf_op jit(solution)/shard_map/all_to_all | solution.py:302
  77.6 0.0 collective-permute-done.3.refs_2_
  77.6 9.3 %all-to-all-done.2.rows_ref = bf16[8,16,1536]{2,1,0:T(8,128)(2,1)S(1)} async-done(((bf16[8,16,1536]{2,1,0:T(8,128)(2,1)}), bf16[8,16,1536]{2,1,0:T(8,128)(2,1)S(1)}, u32[]{:S(2)}, u32[]{:S(2)}) %all-to-all-start.2) | async-done | bytes 393248 | tf_op jit(solution)/shard_map/all_to_all | solution.py:302
  87.0 3.8 %shard_map.62 = bf16[8,16,1536]{2,1,0:T(8,128)(2,1)} custom-call(bf16[8,16,1536]{2,1,0:T(8,128)(2,1)S(1)} %all-to-all-done.2.rows_ref, bf16[1536,384]{1,0:T(8,128)(2,1)S(1)} %bitcast.16, bf16[3072,256]{1,0:T(8,128)(2,1)} %collective-permute-done.2.before_hbm.refs_1_, bf16[3072,128]{1,0:T(8,128)(2,1)} %collective-permute-done.3.refs_2_, ...), custom_call_target="tpu_custom_call" | custom-call | flops 603979776 | bytes 4718592 | tf_op jit(solution)/shard_map/pallas_call | solution.py:23
  90.8 5.1 %all-to-all-start.3 = ((bf16[8,16,1536]{2,1,0:T(8,128)(2,1)}), bf16[8,16,1536]{2,1,0:T(8,128)(2,1)S(1)}, u32[]{:S(2)}, u32[]{:S(2)}) async-start(bf16[8,16,1536]{2,1,0:T(8,128)(2,1)} %shard_map.62), calls=%async_computation.3 | async-start | bytes 786432 | tf_op jit(solution)/shard_map/all_to_all | solution.py:321
  95.9 0.0 copy-start.6
  95.9 3.9 %shard_map.56 = (bf16[384,384]{1,0:T(8,128)(2,1)}, bf16[384,384]{1,0:T(8,128)(2,1)}) custom-call(bf16[1536,256]{1,0:T(8,128)(2,1)} %bitcast.24, bf16[384,1536]{1,0:T(8,128)(2,1)} %bitcast.22, bf16[384,1536]{1,0:T(8,128)(2,1)} %collective-permute-done.partner_feats_ref.partner_hbm), custom_call_target="tpu_custom_call" | custom-call | flops 603979776 | bytes 2359296 | tf_op jit(solution)/shard_map/pallas_call | solution.py:23
  99.8 6.1 %collective-permute-start.1 = (bf16[384,384]{1,0:T(8,128)(2,1)}, bf16[384,384]{1,0:T(8,128)(2,1)S(1)}, u32[]{:S(2)}, u32[]{:S(2)}) collective-permute-start(bf16[384,384]{1,0:T(8,128)(2,1)} %get-tuple-element.10), channel_id=1, source_target_pairs={{0,1},{1,0},{2,3},{3,2},{4,5},{5,4},{6,7},{7,6},{8,9},{9,8},{10,11... | collective-permute-start | bytes 884744 | tf_op jit(solution)/shard_map/ppermute | solution.py:278
  105.9 1.4 collective-permute-done.1.core_ref
  107.3 0.0 copy-start.4
  107.3 1.0 copy-done.4
  108.3 0.3 shard_map.57
  108.6 0.0 all-to-all-done.3.blocks_ref
  108.6 1.2 shard_map.63
  109.9 25.1 %all_to_all.25 = bf16[16,16,1536]{2,1,0:T(8,128)(2,1)S(1)} all-to-all(bf16[16,16,1536]{2,1,0:T(8,128)(2,1)S(1)} %shard_map.63), channel_id=1, replica_groups=mesh['xlo'=2,'yh'=4,'yl'=2,'xhi'=2,'z'=8,'core'=2] {'xhi','z'}, dimensions={0} | all-to-all | bytes 1572864 | tf_op jit(solution)/shard_map/all_to_all | solution.py:334
  135.0 7.7 %collective-permute-start.4 = (bf16[256,1536]{1,0:T(8,128)(2,1)S(1)}, bf16[256,1536]{1,0:T(8,128)(2,1)S(1)}, u32[]{:S(2)}, u32[]{:S(2)}) collective-permute-start(bf16[256,1536]{1,0:T(8,128)(2,1)S(1)} %bitcast.25), channel_id=1, source_target_pairs={{0,1},{1,0},{2,3},{3,2},{4,5},{5,4},{6,7},{7,6},{8,9},{9,8},{10,11... | collective-permute-start | bytes 2359304 | tf_op jit(solution)/shard_map/ppermute | solution.py:335
  142.6 0.0 copy-done.6
  142.6 0.5 convolution_add_fusion
  143.1 1.4 collective-permute-done.4
  144.5 0.5 fusion.1
  145.0 1.3 fusion
Async XLA Ops:
  0.0 14.7 %copy-start.3 = (bf16[96,512]{1,0:T(8,128)(2,1)S(1)}, bf16[96,512]{1,0:T(8,128)(2,1)}, u32[]{:S(2)}) copy-start(bf16[96,512]{1,0:T(8,128)(2,1)} %before_hbm.1) | copy-start | bytes 294916
  0.0 14.7 %copy-start.1 = (bf16[1,384,1536]{2,1,0:T(8,128)(2,1)S(1)}, bf16[1,384,1536]{2,1,0:T(8,128)(2,1)}, u32[]{:S(2)}) copy-start(bf16[1,384,1536]{2,1,0:T(8,128)(2,1)} %param.9) | copy-start | bytes 3538948
  0.0 14.7 %copy-start = (bf16[1,1536,384]{2,1,0:T(8,128)(2,1)S(1)}, bf16[1,1536,384]{2,1,0:T(8,128)(2,1)}, u32[]{:S(2)}) copy-start(bf16[1,1536,384]{2,1,0:T(8,128)(2,1)} %param.8) | copy-start | bytes 3538948
  2.3 27.0 %all-to-all-start = ((bf16[16,96,256]{2,1,0:T(8,128)(2,1)}), bf16[16,96,256]{2,1,0:T(8,128)(2,1)S(1)}, u32[]{:S(2)}, u32[]{:S(2)}) async-start(bf16[16,96,256]{2,1,0:T(8,128)(2,1)} %shard_map.55), calls=%async_computation | async-start | bytes 1572864 | tf_op jit(solution)/shard_map/all_to_all | solution.py:242
  11.0 8.5 %collective-permute-start = (bf16[384,1536]{1,0:T(8,128)(2,1)}, bf16[384,1536]{1,0:T(8,128)(2,1)}, u32[]{:S(2)}, u32[]{:S(2)}) collective-permute-start(bf16[384,1536]{1,0:T(8,128)(2,1)} %bitcast.20), channel_id=1, source_target_pairs={{0,1},{1,0},{2,3},{3,2},{4,5},{5,4},{6,7},{7,6},{8,9},{9,8},{10,11... | collective-permute-start | bytes 3538952 | tf_op jit(solution)/shard_map/ppermute | solution.py:208
  16.0 32.9 %collective-permute-start.2 = (bf16[3072,256]{1,0:T(8,128)(2,1)}, bf16[3072,256]{1,0:T(8,128)(2,1)}, u32[]{:S(2)}, u32[]{:S(2)}) collective-permute-start(bf16[3072,256]{1,0:T(8,128)(2,1)} %shard_map.60), channel_id=1, source_target_pairs={{0,224},{1,33},{32,0},{33,65},{64,32},{65,97},{96,64},{97,129},{12... | collective-permute-start | bytes 4718600 | tf_op jit(solution)/shard_map/ppermute | solution.py:228
  29.3 0.9 copy-start.7
  35.1 32.4 %all-to-all-start.1 = ((bf16[16,16,1664]{2,1,0:T(8,128)(2,1)}), bf16[16,16,1664]{2,1,0:T(8,128)(2,1)S(1)}, u32[]{:S(2)}, u32[]{:S(2)}) async-start(bf16[16,16,1664]{2,1,0:T(8,128)(2,1)} %bitcast.27), calls=%async_computation.1 | async-start | bytes 1703936 | tf_op jit(solution)/shard_map/all_to_all | solution.py:263
  48.9 18.6 %copy-start.5 = (f32[1,1536]{1,0:T(1,128)S(1)}, f32[1,1536]{1,0:T(1,128)}, u32[]{:S(2)}) copy-start(f32[1,1536]{1,0:T(1,128)} %gain_ref.1) | copy-start | bytes 18436
  50.1 27.5 %collective-permute-start.3 = (bf16[3072,128]{1,0:T(8,128)(2,1)}, bf16[3072,128]{1,0:T(8,128)(2,1)}, u32[]{:S(2)}, u32[]{:S(2)}) collective-permute-start(bf16[3072,128]{1,0:T(8,128)(2,1)} %shard_map.61), channel_id=1, source_target_pairs={{0,32},{1,225},{32,64},{33,1},{64,96},{65,33},{96,128},{97,65},{12... | collective-permute-start | bytes 2359304 | tf_op jit(solution)/shard_map/ppermute | solution.py:228
  68.4 0.7 copy-start.2
  69.2 17.8 %all-to-all-start.2 = ((bf16[8,16,1536]{2,1,0:T(8,128)(2,1)}), bf16[8,16,1536]{2,1,0:T(8,128)(2,1)S(1)}, u32[]{:S(2)}, u32[]{:S(2)}) async-start(bf16[8,16,1536]{2,1,0:T(8,128)(2,1)} %copy-done.2), calls=%async_computation.2 | async-start | bytes 786432 | tf_op jit(solution)/shard_map/all_to_all | solution.py:302
  90.8 17.8 %all-to-all-start.3 = ((bf16[8,16,1536]{2,1,0:T(8,128)(2,1)}), bf16[8,16,1536]{2,1,0:T(8,128)(2,1)S(1)}, u32[]{:S(2)}, u32[]{:S(2)}) async-start(bf16[8,16,1536]{2,1,0:T(8,128)(2,1)} %shard_map.62), calls=%async_computation.3 | async-start | bytes 786432 | tf_op jit(solution)/shard_map/all_to_all | solution.py:321
  95.9 46.7 %copy-start.6 = (bf16[1,384,1536]{2,1,0:T(8,128)(2,1)S(1)}, bf16[1,384,1536]{2,1,0:T(8,128)(2,1)}, u32[]{:S(2)}) copy-start(bf16[1,384,1536]{2,1,0:T(8,128)(2,1)} %param.5) | copy-start | bytes 3538948
  99.8 7.5 %collective-permute-start.1 = (bf16[384,384]{1,0:T(8,128)(2,1)}, bf16[384,384]{1,0:T(8,128)(2,1)S(1)}, u32[]{:S(2)}, u32[]{:S(2)}) collective-permute-start(bf16[384,384]{1,0:T(8,128)(2,1)} %get-tuple-element.10), channel_id=1, source_target_pairs={{0,1},{1,0},{2,3},{3,2},{4,5},{5,4},{6,7},{7,6},{8,9},{9,8},{10,11... | collective-permute-start | bytes 884744 | tf_op jit(solution)/shard_map/ppermute | solution.py:278
  107.3 1.0 copy-start.4
  135.0 9.6 %collective-permute-start.4 = (bf16[256,1536]{1,0:T(8,128)(2,1)S(1)}, bf16[256,1536]{1,0:T(8,128)(2,1)S(1)}, u32[]{:S(2)}, u32[]{:S(2)}) collective-permute-start(bf16[256,1536]{1,0:T(8,128)(2,1)S(1)} %bitcast.25), channel_id=1, source_target_pairs={{0,1},{1,0},{2,3},{3,2},{4,5},{5,4},{6,7},{7,6},{8,9},{9,8},{10,11... | collective-permute-start | bytes 2359304 | tf_op jit(solution)/shard_map/ppermute | solution.py:335

commit v13 on v12

--- a/solution.py
+++ b/solution.py
@@ -64,7 +64,8 @@
     shape = (router_ref.shape[1], half)
     row = lax.broadcasted_iota(jnp.int32, shape, 0)
     col = lax.broadcasted_iota(jnp.int32, shape, 1)
-    wanted = (col // per_owner * 2 + core_ref[0]) * per_owner + col % per_owner
+    bits = per_owner.bit_length() - 1
+    wanted = ((((col >> bits) << 1) + core_ref[0]) << bits) + (col & (per_owner - 1))
     pick = jnp.where(row == wanted, 1.0, 0.0).astype(BF16)
     own_ref[...] = jnp.dot(router_ref[...], pick, preferred_element_type=F32).astype(BF16)
     copies = [started(own_ref, copies_hbm.at[k], semaphores, k) for k in range(copies_hbm.shape[0])]
@@ -193,6 +194,19 @@
         copy.wait()
 
 
+def last_kernel(near_ref, weights_ref, outs_ref, output_hbm, output_ref, semaphores):
+    weights = weights_ref[...]
+    step = 384
+    copies = []
+    for k in range(near_ref.shape[1] // step):
+        part = pl.ds(k * step, step)
+        far = jnp.dot(weights, outs_ref[:, part], preferred_element_type=F32)
+        output_ref[:, part] = (near_ref[:, part] + far).astype(BF16)
+        copies.append(started(output_ref.at[:, part], output_hbm.at[:, part], semaphores, k))
+    for copy in copies:
+        copy.wait()
+
+
 def local(tokens, router, norm_gain, w_in, w_out):
     feats = tokens[0]
     count, width = feats.shape
@@ -335,9 +349,19 @@
     outs_b = lax.ppermute(outs, "core", other())
 
     near = feats.astype(F32) + jnp.dot(weights, outs, preferred_element_type=F32)
-    near = lax.optimization_barrier(near)
-    far = jnp.dot(weights_b, outs_b, preferred_element_type=F32)
-    return (near + far).astype(BF16)[None]
+    return kernel_call(
+        last_kernel,
+        shape((count, width), BF16),
+        2 * count * width * half,
+        6 * count * width,
+        [VMEM] * 3,
+        near,
+        weights_b,
+        outs_b,
+        out_specs=HBM,
+        scratch=[pltpu.VMEM((count, width), BF16), pltpu.SemaphoreType.DMA((4,))],
+        room=16,
+    )[None]
 
 
 def solution(mesh):

time: 149 us -> 148 us (level)
    pallas_call x9 -> x10, Pallas kernels: 20 us -> 21.2 us  [kernel_call(): pl.pallas_call(body, out_shape=outs, in_specs=specs, out_specs=jax.tree.m...]
where the time goes in v13:
time: 148 us; the launch traced here: 146 us
  starting transfers between devices  59.9 us (40%)
  waiting for transfers between devices  36.2 us (24%)
  blocking collectives  25.2 us (17%)
  Pallas kernels  21.2 us (14%)
  local copies, waits for them, and re-layouts  2.62 us (2%)
    all_to_all x1, blocking collectives, local(): lax.all_to_all(copies, ('xhi', 'z'), 0, 0, tiled=True).reshape(half, width)  25.2 us
    pallas_call x10, Pallas kernels, kernel_call(): pl.pallas_call(body, out_shape=outs, in_specs=specs, out_specs=jax.tree.m...  21.2 us
    all_to_all x1, waiting for transfers between devices, local(): lax.all_to_all(message.reshape(owners, per_owner, width + EXTRA), ('xhi',...  14.3 us
    all_to_all x1, starting transfers between devices, local(): lax.all_to_all(message.reshape(owners, per_owner, width + EXTRA), ('xhi',...  13.8 us
    all_to_all x1, waiting for transfers between devices, local(): lax.all_to_all(copies, ('xlo', *Y), 0, 0, tiled=True).reshape(width, half)  9.77 us
    all_to_all x1, waiting for transfers between devices, local(): rows = lax.all_to_all(slots, ('xlo', 'yh'), 0, 0, tiled=True)  9.32 us
    all_to_all x1, starting transfers between devices, local(): lax.all_to_all(copies, ('xlo', *Y), 0, 0, tiled=True).reshape(width, half)  8.69 us
    all_to_all x1, starting transfers between devices, local(): rows = lax.all_to_all(slots, ('xlo', 'yh'), 0, 0, tiled=True)  8.46 us
  transfers between devices with their start and end apart: 9, of which 5 were waited for; matrix products, arithmetic and copies ran while one was open for 0% of the time, Pallas kernels for 9%

profile of v13, /device:TPU:1, one launch (start us, length us, event | category | flops | bytes accessed | tf_op | source)
XLA Modules:
  0.0 145.9 jit_solution(17492341366648968456)
XLA Ops:
  0.0 0.0 copy-start.3
  0.0 0.0 copy-start.1
  0.0 0.0 copy-start
  0.0 2.2 %shard_map.55 = bf16[16,96,256]{2,1,0:T(8,128)(2,1)} custom-call(s32[1]{0:T(128)} %bitcast.1.core_ref, bf16[96,512]{1,0:T(8,128)(2,1)} %before_hbm.1), custom_call_target="tpu_custom_call" | custom-call | flops 25165824 | bytes 1572864 | tf_op jit(solution)/shard_map/pallas_call | solution.py:23
  2.3 8.7 %all-to-all-start = ((bf16[16,96,256]{2,1,0:T(8,128)(2,1)}), bf16[16,96,256]{2,1,0:T(8,128)(2,1)S(1)}, u32[]{:S(2)}, u32[]{:S(2)}) async-start(bf16[16,96,256]{2,1,0:T(8,128)(2,1)} %shard_map.55), calls=%async_computation | async-start | bytes 1572864 | tf_op jit(solution)/shard_map/all_to_all | solution.py:256
  11.0 3.7 %collective-permute-start = (bf16[384,1536]{1,0:T(8,128)(2,1)}, bf16[384,1536]{1,0:T(8,128)(2,1)}, u32[]{:S(2)}, u32[]{:S(2)}) collective-permute-start(bf16[384,1536]{1,0:T(8,128)(2,1)} %bitcast.17), channel_id=1, source_target_pairs={{0,1},{1,0},{2,3},{3,2},{4,5},{5,4},{6,7},{7,6},{8,9},{9,8},{10,11... | collective-permute-start | bytes 3538952 | tf_op jit(solution)/shard_map/ppermute | solution.py:222
  14.7 0.0 copy-done.3
  14.7 0.0 copy-done.1
  14.7 0.0 copy-done
  14.7 1.3 shard_map.60
  16.0 3.4 %collective-permute-start.2 = (bf16[3072,256]{1,0:T(8,128)(2,1)}, bf16[3072,256]{1,0:T(8,128)(2,1)}, u32[]{:S(2)}, u32[]{:S(2)}) collective-permute-start(bf16[3072,256]{1,0:T(8,128)(2,1)} %shard_map.60), channel_id=1, source_target_pairs={{0,224},{1,33},{32,0},{33,65},{64,32},{65,97},{96,64},{97,129},{12... | collective-permute-start | bytes 4718600 | tf_op jit(solution)/shard_map/ppermute | solution.py:242
  19.5 0.0 collective-permute-done.partner_feats_ref.partner_hbm
  19.5 9.8 %all-to-all-done = bf16[16,96,256]{2,1,0:T(8,128)(2,1)S(1)} async-done(((bf16[16,96,256]{2,1,0:T(8,128)(2,1)}), bf16[16,96,256]{2,1,0:T(8,128)(2,1)S(1)}, u32[]{:S(2)}, u32[]{:S(2)}) %all-to-all-start) | async-done | bytes 786464 | tf_op jit(solution)/shard_map/all_to_all | solution.py:256
  29.3 0.0 copy-start.7
  29.3 0.9 copy-done.7
  30.1 5.0 %shard_map.58 = bf16[256,1664]{1,0:T(8,128)(2,1)} custom-call(bf16[1536,256]{1,0:T(8,128)(2,1)} %bitcast.20, bf16[384,1536]{1,0:T(8,128)(2,1)} %bitcast.18, bf16[384,1536]{1,0:T(8,128)(2,1)} %collective-permute-done.partner_feats_ref.partner_hbm), custom_call_target="tpu_custom_call" | custom-call | flops 1207959552 | bytes 3932160 | tf_op jit(solution)/shard_map/pallas_call | solution.py:23
  35.1 13.8 %all-to-all-start.1 = ((bf16[16,16,1664]{2,1,0:T(8,128)(2,1)}), bf16[16,16,1664]{2,1,0:T(8,128)(2,1)S(1)}, u32[]{:S(2)}, u32[]{:S(2)}) async-start(bf16[16,16,1664]{2,1,0:T(8,128)(2,1)} %bitcast.24), calls=%async_computation.1 | async-start | bytes 1703936 | tf_op jit(solution)/shard_map/all_to_all | solution.py:277
  48.9 0.0 copy-start.5
  48.9 0.0 collective-permute-done.2.before_hbm.refs_1_
  48.9 1.2 shard_map.61
  50.1 3.0 %collective-permute-start.3 = (bf16[3072,128]{1,0:T(8,128)(2,1)}, bf16[3072,128]{1,0:T(8,128)(2,1)}, u32[]{:S(2)}, u32[]{:S(2)}) collective-permute-start(bf16[3072,128]{1,0:T(8,128)(2,1)} %shard_map.61), channel_id=1, source_target_pairs={{0,32},{1,225},{32,64},{33,1},{64,96},{65,33},{96,128},{97,65},{12... | collective-permute-start | bytes 2359304 | tf_op jit(solution)/shard_map/ppermute | solution.py:242
  53.1 14.3 %all-to-all-done.1.received_ref = bf16[16,16,1664]{2,1,0:T(8,128)(2,1)S(1)} async-done(((bf16[16,16,1664]{2,1,0:T(8,128)(2,1)}), bf16[16,16,1664]{2,1,0:T(8,128)(2,1)S(1)}, u32[]{:S(2)}, u32[]{:S(2)}) %all-to-all-start.1) | async-done | bytes 852000 | tf_op jit(solution)/shard_map/all_to_all | solution.py:277
  67.5 0.0 copy-done.5
  67.5 0.9 shard_map.59
  68.4 0.0 copy-start.2
  68.5 0.7 copy-done.2
  69.2 8.5 %all-to-all-start.2 = ((bf16[8,16,1536]{2,1,0:T(8,128)(2,1)}), bf16[8,16,1536]{2,1,0:T(8,128)(2,1)S(1)}, u32[]{:S(2)}, u32[]{:S(2)}) async-start(bf16[8,16,1536]{2,1,0:T(8,128)(2,1)} %copy-done.2), calls=%async_computation.2 | async-start | bytes 786432 | tf_op jit(solution)/shard_map/all_to_all | solution.py:316
  77.6 0.0 collective-permute-done.3.refs_2_
  77.7 9.3 %all-to-all-done.2.rows_ref = bf16[8,16,1536]{2,1,0:T(8,128)(2,1)S(1)} async-done(((bf16[8,16,1536]{2,1,0:T(8,128)(2,1)}), bf16[8,16,1536]{2,1,0:T(8,128)(2,1)S(1)}, u32[]{:S(2)}, u32[]{:S(2)}) %all-to-all-start.2) | async-done | bytes 393248 | tf_op jit(solution)/shard_map/all_to_all | solution.py:316
  87.0 3.8 %shard_map.62 = bf16[8,16,1536]{2,1,0:T(8,128)(2,1)} custom-call(bf16[8,16,1536]{2,1,0:T(8,128)(2,1)S(1)} %all-to-all-done.2.rows_ref, bf16[1536,384]{1,0:T(8,128)(2,1)S(1)} %bitcast.13, bf16[3072,256]{1,0:T(8,128)(2,1)} %collective-permute-done.2.before_hbm.refs_1_, bf16[3072,128]{1,0:T(8,128)(2,1)} %collective-permute-done.3.refs_2_, ...), custom_call_target="tpu_custom_call" | custom-call | flops 603979776 | bytes 4718592 | tf_op jit(solution)/shard_map/pallas_call | solution.py:23
  90.8 5.1 %all-to-all-start.3 = ((bf16[8,16,1536]{2,1,0:T(8,128)(2,1)}), bf16[8,16,1536]{2,1,0:T(8,128)(2,1)S(1)}, u32[]{:S(2)}, u32[]{:S(2)}) async-start(bf16[8,16,1536]{2,1,0:T(8,128)(2,1)} %shard_map.62), calls=%async_computation.3 | async-start | bytes 786432 | tf_op jit(solution)/shard_map/all_to_all | solution.py:335
  95.9 3.8 %shard_map.56 = (bf16[384,384]{1,0:T(8,128)(2,1)}, bf16[384,384]{1,0:T(8,128)(2,1)}) custom-call(bf16[1536,256]{1,0:T(8,128)(2,1)} %bitcast.21, bf16[384,1536]{1,0:T(8,128)(2,1)} %bitcast.19, bf16[384,1536]{1,0:T(8,128)(2,1)} %collective-permute-done.partner_feats_ref.partner_hbm), custom_call_target="tpu_custom_call" | custom-call | flops 603979776 | bytes 2359296 | tf_op jit(solution)/shard_map/pallas_call | solution.py:23
  99.8 6.0 %collective-permute-start.1 = (bf16[384,384]{1,0:T(8,128)(2,1)}, bf16[384,384]{1,0:T(8,128)(2,1)S(1)}, u32[]{:S(2)}, u32[]{:S(2)}) collective-permute-start(bf16[384,384]{1,0:T(8,128)(2,1)} %get-tuple-element.10), channel_id=1, source_target_pairs={{0,1},{1,0},{2,3},{3,2},{4,5},{5,4},{6,7},{7,6},{8,9},{9,8},{10,11... | collective-permute-start | bytes 884744 | tf_op jit(solution)/shard_map/ppermute | solution.py:292
  105.8 1.4 collective-permute-done.1.core_ref
  107.2 0.0 copy-start.4
  107.2 1.0 copy-done.4
  108.2 0.3 shard_map.57
  108.5 0.0 copy-start.6
  108.5 0.0 all-to-all-done.3.blocks_ref
  108.5 1.2 shard_map.63
  109.8 25.2 %all_to_all.25 = bf16[16,16,1536]{2,1,0:T(8,128)(2,1)S(1)} all-to-all(bf16[16,16,1536]{2,1,0:T(8,128)(2,1)S(1)} %shard_map.63), channel_id=1, replica_groups=mesh['xlo'=2,'yh'=4,'yl'=2,'xhi'=2,'z'=8,'core'=2] {'xhi','z'}, dimensions={0} | all-to-all | bytes 1572864 | tf_op jit(solution)/shard_map/all_to_all | solution.py:348
  135.0 7.6 %collective-permute-start.4 = (bf16[256,1536]{1,0:T(8,128)(2,1)S(1)}, bf16[256,1536]{1,0:T(8,128)(2,1)S(1)}, u32[]{:S(2)}, u32[]{:S(2)}) collective-permute-start(bf16[256,1536]{1,0:T(8,128)(2,1)S(1)} %bitcast.22), channel_id=1, source_target_pairs={{0,1},{1,0},{2,3},{3,2},{4,5},{5,4},{6,7},{7,6},{8,9},{9,8},{10,11... | collective-permute-start | bytes 2359304 | tf_op jit(solution)/shard_map/ppermute | solution.py:349
  142.6 0.0 copy-done.6
  142.7 0.5 convolution_add_fusion.near_ref
  143.1 1.4 collective-permute-done.4.outs_ref
  144.5 1.3 shard_map.64
Async XLA Ops:
  0.0 14.7 %copy-start.3 = (bf16[96,512]{1,0:T(8,128)(2,1)S(1)}, bf16[96,512]{1,0:T(8,128)(2,1)}, u32[]{:S(2)}) copy-start(bf16[96,512]{1,0:T(8,128)(2,1)} %before_hbm.1) | copy-start | bytes 294916
  0.0 14.7 %copy-start.1 = (bf16[1,384,1536]{2,1,0:T(8,128)(2,1)S(1)}, bf16[1,384,1536]{2,1,0:T(8,128)(2,1)}, u32[]{:S(2)}) copy-start(bf16[1,384,1536]{2,1,0:T(8,128)(2,1)} %param.9) | copy-start | bytes 3538948
  0.0 14.7 %copy-start = (bf16[1,1536,384]{2,1,0:T(8,128)(2,1)S(1)}, bf16[1,1536,384]{2,1,0:T(8,128)(2,1)}, u32[]{:S(2)}) copy-start(bf16[1,1536,384]{2,1,0:T(8,128)(2,1)} %param.8) | copy-start | bytes 3538948
  2.3 27.0 %all-to-all-start = ((bf16[16,96,256]{2,1,0:T(8,128)(2,1)}), bf16[16,96,256]{2,1,0:T(8,128)(2,1)S(1)}, u32[]{:S(2)}, u32[]{:S(2)}) async-start(bf16[16,96,256]{2,1,0:T(8,128)(2,1)} %shard_map.55), calls=%async_computation | async-start | bytes 1572864 | tf_op jit(solution)/shard_map/all_to_all | solution.py:256
  11.0 8.5 %collective-permute-start = (bf16[384,1536]{1,0:T(8,128)(2,1)}, bf16[384,1536]{1,0:T(8,128)(2,1)}, u32[]{:S(2)}, u32[]{:S(2)}) collective-permute-start(bf16[384,1536]{1,0:T(8,128)(2,1)} %bitcast.17), channel_id=1, source_target_pairs={{0,1},{1,0},{2,3},{3,2},{4,5},{5,4},{6,7},{7,6},{8,9},{9,8},{10,11... | collective-permute-start | bytes 3538952 | tf_op jit(solution)/shard_map/ppermute | solution.py:222
  16.0 32.9 %collective-permute-start.2 = (bf16[3072,256]{1,0:T(8,128)(2,1)}, bf16[3072,256]{1,0:T(8,128)(2,1)}, u32[]{:S(2)}, u32[]{:S(2)}) collective-permute-start(bf16[3072,256]{1,0:T(8,128)(2,1)} %shard_map.60), channel_id=1, source_target_pairs={{0,224},{1,33},{32,0},{33,65},{64,32},{65,97},{96,64},{97,129},{12... | collective-permute-start | bytes 4718600 | tf_op jit(solution)/shard_map/ppermute | solution.py:242
  29.3 0.9 copy-start.7
  35.1 32.4 %all-to-all-start.1 = ((bf16[16,16,1664]{2,1,0:T(8,128)(2,1)}), bf16[16,16,1664]{2,1,0:T(8,128)(2,1)S(1)}, u32[]{:S(2)}, u32[]{:S(2)}) async-start(bf16[16,16,1664]{2,1,0:T(8,128)(2,1)} %bitcast.24), calls=%async_computation.1 | async-start | bytes 1703936 | tf_op jit(solution)/shard_map/all_to_all | solution.py:277
  48.9 18.6 %copy-start.5 = (f32[1,1536]{1,0:T(1,128)S(1)}, f32[1,1536]{1,0:T(1,128)}, u32[]{:S(2)}) copy-start(f32[1,1536]{1,0:T(1,128)} %gain_ref.1) | copy-start | bytes 18436
  50.1 27.5 %collective-permute-start.3 = (bf16[3072,128]{1,0:T(8,128)(2,1)}, bf16[3072,128]{1,0:T(8,128)(2,1)}, u32[]{:S(2)}, u32[]{:S(2)}) collective-permute-start(bf16[3072,128]{1,0:T(8,128)(2,1)} %shard_map.61), channel_id=1, source_target_pairs={{0,32},{1,225},{32,64},{33,1},{64,96},{65,33},{96,128},{97,65},{12... | collective-permute-start | bytes 2359304 | tf_op jit(solution)/shard_map/ppermute | solution.py:242
  68.4 0.7 copy-start.2
  69.2 17.8 %all-to-all-start.2 = ((bf16[8,16,1536]{2,1,0:T(8,128)(2,1)}), bf16[8,16,1536]{2,1,0:T(8,128)(2,1)S(1)}, u32[]{:S(2)}, u32[]{:S(2)}) async-start(bf16[8,16,1536]{2,1,0:T(8,128)(2,1)} %copy-done.2), calls=%async_computation.2 | async-start | bytes 786432 | tf_op jit(solution)/shard_map/all_to_all | solution.py:316
  90.8 17.7 %all-to-all-start.3 = ((bf16[8,16,1536]{2,1,0:T(8,128)(2,1)}), bf16[8,16,1536]{2,1,0:T(8,128)(2,1)S(1)}, u32[]{:S(2)}, u32[]{:S(2)}) async-start(bf16[8,16,1536]{2,1,0:T(8,128)(2,1)} %shard_map.62), calls=%async_computation.3 | async-start | bytes 786432 | tf_op jit(solution)/shard_map/all_to_all | solution.py:335
  99.8 7.4 %collective-permute-start.1 = (bf16[384,384]{1,0:T(8,128)(2,1)}, bf16[384,384]{1,0:T(8,128)(2,1)S(1)}, u32[]{:S(2)}, u32[]{:S(2)}) collective-permute-start(bf16[384,384]{1,0:T(8,128)(2,1)} %get-tuple-element.10), channel_id=1, source_target_pairs={{0,1},{1,0},{2,3},{3,2},{4,5},{5,4},{6,7},{7,6},{8,9},{9,8},{10,11... | collective-permute-start | bytes 884744 | tf_op jit(solution)/shard_map/ppermute | solution.py:292
  107.2 1.0 copy-start.4
  108.5 34.1 %copy-start.6 = (bf16[1,384,1536]{2,1,0:T(8,128)(2,1)S(1)}, bf16[1,384,1536]{2,1,0:T(8,128)(2,1)}, u32[]{:S(2)}) copy-start(bf16[1,384,1536]{2,1,0:T(8,128)(2,1)} %param.5) | copy-start | bytes 3538948
  135.0 9.5 %collective-permute-start.4 = (bf16[256,1536]{1,0:T(8,128)(2,1)S(1)}, bf16[256,1536]{1,0:T(8,128)(2,1)S(1)}, u32[]{:S(2)}, u32[]{:S(2)}) collective-permute-start(bf16[256,1536]{1,0:T(8,128)(2,1)S(1)} %bitcast.22), channel_id=1, source_target_pairs={{0,1},{1,0},{2,3},{3,2},{4,5},{5,4},{6,7},{7,6},{8,9},{9,8},{10,11... | collective-permute-start | bytes 2359304 | tf_op jit(solution)/shard_map/ppermute | solution.py:349

commit v14 on v13

--- a/solution.py
+++ b/solution.py
@@ -272,7 +272,7 @@
             pltpu.VMEM((half, width + EXTRA), BF16),
             pltpu.SemaphoreType.DMA((8,)),
         ],
-        room=56,
+        room=50,
     )
     received = lax.all_to_all(
         message.reshape(owners, per_owner, width + EXTRA), ("xhi", "z"), 0, 0, tiled=True

time: 148 us -> 148 us (level)
  waiting for transfers between devices: 36.2 us -> 32.8 us
  local copies, waits for them, and re-layouts: 2.62 us -> 5.78 us
  starting transfers between devices: 59.9 us -> 61.4 us
    all_to_all x1, waiting for transfers between devices: 9.77 us -> 6.51 us  [local(): lax.all_to_all(copies, ('xlo', *Y), 0, 0, tiled=True).reshape(width, half)]
    unnamed x16 -> x22, local copies, waits for them, and re-layouts: 2.62 us -> 5.78 us
  transfers between devices with their start and end apart: 9 -> 9, of which waited for: 5 -> 5; matrix products, arithmetic and copies ran while one was open for 0% -> 0% of each run, Pallas kernels for 9% -> 8%
where the time goes in v14:
time: 148 us; the launch traced here: 147 us
  starting transfers between devices  61.4 us (41%)
  waiting for transfers between devices  32.8 us (22%)
  blocking collectives  25 us (17%)
  Pallas kernels  21.1 us (14%)
  local copies, waits for them, and re-layouts  5.78 us (4%)
    all_to_all x1, blocking collectives, local(): lax.all_to_all(copies, ('xhi', 'z'), 0, 0, tiled=True).reshape(half, width)  25 us
    pallas_call x10, Pallas kernels, kernel_call(): pl.pallas_call(body, out_shape=outs, in_specs=specs, out_specs=jax.tree.m...  21.1 us
    all_to_all x1, starting transfers between devices, local(): lax.all_to_all(message.reshape(owners, per_owner, width + EXTRA), ('xhi',...  14.6 us
    all_to_all x1, waiting for transfers between devices, local(): lax.all_to_all(message.reshape(owners, per_owner, width + EXTRA), ('xhi',...  14.3 us
    all_to_all x1, waiting for transfers between devices, local(): rows = lax.all_to_all(slots, ('xlo', 'yh'), 0, 0, tiled=True)  9.17 us
    all_to_all x1, starting transfers between devices, local(): lax.all_to_all(copies, ('xlo', *Y), 0, 0, tiled=True).reshape(width, half)  8.74 us
    all_to_all x1, starting transfers between devices, local(): rows = lax.all_to_all(slots, ('xlo', 'yh'), 0, 0, tiled=True)  8.29 us
    ppermute x1, starting transfers between devices, local(): outs_b = lax.ppermute(outs, 'core', other())  7.75 us
  transfers between devices with their start and end apart: 9, of which 5 were waited for; matrix products, arithmetic and copies ran while one was open for 0% of the time, Pallas kernels for 8%

profile of v14, /device:TPU:1, one launch (start us, length us, event | category | flops | bytes accessed | tf_op | source)
XLA Modules:
  0.0 146.8 jit_solution(3943128504162397642)
XLA Ops:
  0.0 0.0 copy-start.1
  0.0 2.3 %shard_map.55 = bf16[16,96,256]{2,1,0:T(8,128)(2,1)} custom-call(s32[1]{0:T(128)} %bitcast.1.core_ref, bf16[96,512]{1,0:T(8,128)(2,1)} %before_hbm.1), custom_call_target="tpu_custom_call" | custom-call | flops 25165824 | bytes 1572864 | tf_op jit(solution)/shard_map/pallas_call | solution.py:23
  2.3 8.7 %all-to-all-start = ((bf16[16,96,256]{2,1,0:T(8,128)(2,1)}), bf16[16,96,256]{2,1,0:T(8,128)(2,1)}, u32[]{:S(2)}, u32[]{:S(2)}) async-start(bf16[16,96,256]{2,1,0:T(8,128)(2,1)} %shard_map.55), calls=%async_computation | async-start | bytes 1572864 | tf_op jit(solution)/shard_map/all_to_all | solution.py:256
  11.0 4.3 %collective-permute-start = (bf16[384,1536]{1,0:T(8,128)(2,1)}, bf16[384,1536]{1,0:T(8,128)(2,1)S(1)}, u32[]{:S(2)}, u32[]{:S(2)}) collective-permute-start(bf16[384,1536]{1,0:T(8,128)(2,1)} %bitcast.17), channel_id=1, source_target_pairs={{0,1},{1,0},{2,3},{3,2},{4,5},{5,4},{6,7},{7,6},{8,9},{9,8},{10,11... | collective-permute-start | bytes 3538952 | tf_op jit(solution)/shard_map/ppermute | solution.py:222
  15.4 0.0 copy-done.1
  15.4 0.0 copy-done
  15.4 0.0 copy-start.8
  15.4 0.9 copy-done.8
  16.3 1.3 shard_map.60
  17.6 3.4 %collective-permute-start.2 = (bf16[3072,256]{1,0:T(8,128)(2,1)}, bf16[3072,256]{1,0:T(8,128)(2,1)}, u32[]{:S(2)}, u32[]{:S(2)}) collective-permute-start(bf16[3072,256]{1,0:T(8,128)(2,1)} %shard_map.60), channel_id=1, source_target_pairs={{0,224},{1,33},{32,0},{33,65},{64,32},{65,97},{96,64},{97,129},{12... | collective-permute-start | bytes 4718600 | tf_op jit(solution)/shard_map/ppermute | solution.py:242
  21.0 0.0 collective-permute-done.partner_feats_ref.partner_hbm
  21.0 0.0 copy-start.5
  21.0 1.0 copy-done.5
  22.0 6.5 %all-to-all-done = bf16[16,96,256]{2,1,0:T(8,128)(2,1)} async-done(((bf16[16,96,256]{2,1,0:T(8,128)(2,1)}), bf16[16,96,256]{2,1,0:T(8,128)(2,1)}, u32[]{:S(2)}, u32[]{:S(2)}) %all-to-all-start) | async-done | bytes 786464 | tf_op jit(solution)/shard_map/all_to_all | solution.py:256
  28.5 0.0 copy-done.2
  28.5 1.3 copy-done.6
  29.8 4.8 %shard_map.58 = bf16[256,1664]{1,0:T(8,128)(2,1)S(1)} custom-call(bf16[1536,256]{1,0:T(8,128)(2,1)} %bitcast.2.columns_ref.columns_hbm, bf16[384,1536]{1,0:T(8,128)(2,1)S(1)} %bitcast.19, bf16[384,1536]{1,0:T(8,128)(2,1)S(1)} %copy-done.6), custom_call_target="tpu_custom_call" | custom-call | flops 1207959552 | bytes 3932160 | tf_op jit(solution)/shard_map/pallas_call | solution.py:23
  34.6 0.0 copy-start.7
  34.6 0.9 copy-done.7
  35.5 14.6 %all-to-all-start.1 = ((bf16[16,16,1664]{2,1,0:T(8,128)(2,1)}), bf16[16,16,1664]{2,1,0:T(8,128)(2,1)S(1)}, u32[]{:S(2)}, u32[]{:S(2)}) async-start(bf16[16,16,1664]{2,1,0:T(8,128)(2,1)} %bitcast.20), calls=%async_computation.1 | async-start | bytes 1703936 | tf_op jit(solution)/shard_map/all_to_all | solution.py:277
  50.1 0.0 copy-start.10
  50.2 0.0 collective-permute-done.2.before_hbm.refs_1_
  50.2 1.2 shard_map.61
  51.4 3.0 %collective-permute-start.3 = (bf16[3072,128]{1,0:T(8,128)(2,1)}, bf16[3072,128]{1,0:T(8,128)(2,1)}, u32[]{:S(2)}, u32[]{:S(2)}) collective-permute-start(bf16[3072,128]{1,0:T(8,128)(2,1)} %shard_map.61), channel_id=1, source_target_pairs={{0,32},{1,225},{32,64},{33,1},{64,96},{65,33},{96,128},{97,65},{12... | collective-permute-start | bytes 2359304 | tf_op jit(solution)/shard_map/ppermute | solution.py:242
  54.4 14.3 %all-to-all-done.1.received_ref = bf16[16,16,1664]{2,1,0:T(8,128)(2,1)S(1)} async-done(((bf16[16,16,1664]{2,1,0:T(8,128)(2,1)}), bf16[16,16,1664]{2,1,0:T(8,128)(2,1)S(1)}, u32[]{:S(2)}, u32[]{:S(2)}) %all-to-all-start.1) | async-done | bytes 852000 | tf_op jit(solution)/shard_map/all_to_all | solution.py:277
  68.7 0.0 copy-done.10
  68.7 0.9 shard_map.59
  69.7 0.0 copy-start.4
  69.7 0.7 copy-done.4
  70.4 8.3 %all-to-all-start.2 = ((bf16[8,16,1536]{2,1,0:T(8,128)(2,1)}), bf16[8,16,1536]{2,1,0:T(8,128)(2,1)S(1)}, u32[]{:S(2)}, u32[]{:S(2)}) async-start(bf16[8,16,1536]{2,1,0:T(8,128)(2,1)} %copy-done.4), calls=%async_computation.2 | async-start | bytes 786432 | tf_op jit(solution)/shard_map/all_to_all | solution.py:316
  78.7 0.0 collective-permute-done.3.refs_2_
  78.7 9.2 %all-to-all-done.2.rows_ref = bf16[8,16,1536]{2,1,0:T(8,128)(2,1)S(1)} async-done(((bf16[8,16,1536]{2,1,0:T(8,128)(2,1)}), bf16[8,16,1536]{2,1,0:T(8,128)(2,1)S(1)}, u32[]{:S(2)}, u32[]{:S(2)}) %all-to-all-start.2) | async-done | bytes 393248 | tf_op jit(solution)/shard_map/all_to_all | solution.py:316
  87.9 3.9 %shard_map.62 = bf16[8,16,1536]{2,1,0:T(8,128)(2,1)} custom-call(bf16[8,16,1536]{2,1,0:T(8,128)(2,1)S(1)} %all-to-all-done.2.rows_ref, bf16[1536,384]{1,0:T(8,128)(2,1)S(1)} %bitcast.13, bf16[3072,256]{1,0:T(8,128)(2,1)} %collective-permute-done.2.before_hbm.refs_1_, bf16[3072,128]{1,0:T(8,128)(2,1)} %collective-permute-done.3.refs_2_, ...), custom_call_target="tpu_custom_call" | custom-call | flops 603979776 | bytes 4718592 | tf_op jit(solution)/shard_map/pallas_call | solution.py:23
  91.7 4.8 %all-to-all-start.3 = ((bf16[8,16,1536]{2,1,0:T(8,128)(2,1)}), bf16[8,16,1536]{2,1,0:T(8,128)(2,1)S(1)}, u32[]{:S(2)}, u32[]{:S(2)}) async-start(bf16[8,16,1536]{2,1,0:T(8,128)(2,1)} %shard_map.62), calls=%async_computation.3 | async-start | bytes 786432 | tf_op jit(solution)/shard_map/all_to_all | solution.py:335
  96.6 3.8 %shard_map.56 = (bf16[384,384]{1,0:T(8,128)(2,1)}, bf16[384,384]{1,0:T(8,128)(2,1)}) custom-call(bf16[1536,256]{1,0:T(8,128)(2,1)} %bitcast.2.columns_ref.columns_hbm, bf16[384,1536]{1,0:T(8,128)(2,1)} %bitcast.18, bf16[384,1536]{1,0:T(8,128)(2,1)} %copy-done.5), custom_call_target="tpu_custom_call" | custom-call | flops 603979776 | bytes 2359296 | tf_op jit(solution)/shard_map/pallas_call | solution.py:23
  100.4 6.4 %collective-permute-start.1 = (bf16[384,384]{1,0:T(8,128)(2,1)}, bf16[384,384]{1,0:T(8,128)(2,1)S(1)}, u32[]{:S(2)}, u32[]{:S(2)}) collective-permute-start(bf16[384,384]{1,0:T(8,128)(2,1)} %get-tuple-element.10), channel_id=1, source_target_pairs={{0,1},{1,0},{2,3},{3,2},{4,5},{5,4},{6,7},{7,6},{8,9},{9,8},{10,11... | collective-permute-start | bytes 884744 | tf_op jit(solution)/shard_map/ppermute | solution.py:292
  106.8 1.4 collective-permute-done.1.core_ref
  108.2 1.0 copy-done.9
  109.2 0.3 shard_map.57
  109.5 0.0 copy-start.3
  109.5 0.0 all-to-all-done.3.blocks_ref
  109.6 1.2 shard_map.63
  110.8 25.0 %all_to_all.25 = bf16[16,16,1536]{2,1,0:T(8,128)(2,1)S(1)} all-to-all(bf16[16,16,1536]{2,1,0:T(8,128)(2,1)S(1)} %shard_map.63), channel_id=1, replica_groups=mesh['xlo'=2,'yh'=4,'yl'=2,'xhi'=2,'z'=8,'core'=2] {'xhi','z'}, dimensions={0} | all-to-all | bytes 1572864 | tf_op jit(solution)/shard_map/all_to_all | solution.py:348
  135.8 7.8 %collective-permute-start.4 = (bf16[256,1536]{1,0:T(8,128)(2,1)S(1)}, bf16[256,1536]{1,0:T(8,128)(2,1)S(1)}, u32[]{:S(2)}, u32[]{:S(2)}) collective-permute-start(bf16[256,1536]{1,0:T(8,128)(2,1)S(1)} %bitcast.21), channel_id=1, source_target_pairs={{0,1},{1,0},{2,3},{3,2},{4,5},{5,4},{6,7},{7,6},{8,9},{9,8},{10,11... | collective-permute-start | bytes 2359304 | tf_op jit(solution)/shard_map/ppermute | solution.py:349
  143.5 0.0 copy-done.3
  143.5 0.5 convolution_add_fusion.near_ref
  144.0 1.4 collective-permute-done.4.outs_ref
  145.4 1.3 shard_map.64
  (4 shorter events, 0.0 us)
Async XLA Ops:
  0.0 15.4 %copy-start.1 = (bf16[1,384,1536]{2,1,0:T(8,128)(2,1)S(1)}, bf16[1,384,1536]{2,1,0:T(8,128)(2,1)}, u32[]{:S(2)}) copy-start(bf16[1,384,1536]{2,1,0:T(8,128)(2,1)} %param.9) | copy-start | bytes 3538948
  0.0 15.4 %copy-start = (bf16[1,1536,384]{2,1,0:T(8,128)(2,1)S(1)}, bf16[1,1536,384]{2,1,0:T(8,128)(2,1)}, u32[]{:S(2)}) copy-start(bf16[1,1536,384]{2,1,0:T(8,128)(2,1)} %param.8) | copy-start | bytes 3538948
  2.3 26.3 %all-to-all-start = ((bf16[16,96,256]{2,1,0:T(8,128)(2,1)}), bf16[16,96,256]{2,1,0:T(8,128)(2,1)}, u32[]{:S(2)}, u32[]{:S(2)}) async-start(bf16[16,96,256]{2,1,0:T(8,128)(2,1)} %shard_map.55), calls=%async_computation | async-start | bytes 1572864 | tf_op jit(solution)/shard_map/all_to_all | solution.py:256
  11.0 10.0 %collective-permute-start = (bf16[384,1536]{1,0:T(8,128)(2,1)}, bf16[384,1536]{1,0:T(8,128)(2,1)S(1)}, u32[]{:S(2)}, u32[]{:S(2)}) collective-permute-start(bf16[384,1536]{1,0:T(8,128)(2,1)} %bitcast.17), channel_id=1, source_target_pairs={{0,1},{1,0},{2,3},{3,2},{4,5},{5,4},{6,7},{7,6},{8,9},{9,8},{10,11... | collective-permute-start | bytes 3538952 | tf_op jit(solution)/shard_map/ppermute | solution.py:222
  15.4 0.9 copy-start.8
  16.3 12.3 %copy-start.2 = (bf16[1,384,1536]{2,1,0:T(8,128)(2,1)S(1)}, bf16[1,384,1536]{2,1,0:T(8,128)(2,1)}, u32[]{:S(2)}) copy-start(bf16[1,384,1536]{2,1,0:T(8,128)(2,1)} %param.5) | copy-start | bytes 3538948
  17.6 32.5 %collective-permute-start.2 = (bf16[3072,256]{1,0:T(8,128)(2,1)}, bf16[3072,256]{1,0:T(8,128)(2,1)}, u32[]{:S(2)}, u32[]{:S(2)}) collective-permute-start(bf16[3072,256]{1,0:T(8,128)(2,1)} %shard_map.60), channel_id=1, source_target_pairs={{0,224},{1,33},{32,0},{33,65},{64,32},{65,97},{96,64},{97,129},{12... | collective-permute-start | bytes 4718600 | tf_op jit(solution)/shard_map/ppermute | solution.py:242
  21.0 1.0 copy-start.5
  28.5 1.3 copy-start.6
  34.6 0.9 copy-start.7
  35.5 33.2 %all-to-all-start.1 = ((bf16[16,16,1664]{2,1,0:T(8,128)(2,1)}), bf16[16,16,1664]{2,1,0:T(8,128)(2,1)S(1)}, u32[]{:S(2)}, u32[]{:S(2)}) async-start(bf16[16,16,1664]{2,1,0:T(8,128)(2,1)} %bitcast.20), calls=%async_computation.1 | async-start | bytes 1703936 | tf_op jit(solution)/shard_map/all_to_all | solution.py:277
  50.1 18.6 %copy-start.10 = (f32[1,1536]{1,0:T(1,128)S(1)}, f32[1,1536]{1,0:T(1,128)}, u32[]{:S(2)}) copy-start(f32[1,1536]{1,0:T(1,128)} %gain_ref.1) | copy-start | bytes 18436
  51.4 27.3 %collective-permute-start.3 = (bf16[3072,128]{1,0:T(8,128)(2,1)}, bf16[3072,128]{1,0:T(8,128)(2,1)}, u32[]{:S(2)}, u32[]{:S(2)}) collective-permute-start(bf16[3072,128]{1,0:T(8,128)(2,1)} %shard_map.61), channel_id=1, source_target_pairs={{0,32},{1,225},{32,64},{33,1},{64,96},{65,33},{96,128},{97,65},{12... | collective-permute-start | bytes 2359304 | tf_op jit(solution)/shard_map/ppermute | solution.py:242
  69.7 0.7 copy-start.4
  70.4 17.5 %all-to-all-start.2 = ((bf16[8,16,1536]{2,1,0:T(8,128)(2,1)}), bf16[8,16,1536]{2,1,0:T(8,128)(2,1)S(1)}, u32[]{:S(2)}, u32[]{:S(2)}) async-start(bf16[8,16,1536]{2,1,0:T(8,128)(2,1)} %copy-done.4), calls=%async_computation.2 | async-start | bytes 786432 | tf_op jit(solution)/shard_map/all_to_all | solution.py:316
  91.7 17.8 %all-to-all-start.3 = ((bf16[8,16,1536]{2,1,0:T(8,128)(2,1)}), bf16[8,16,1536]{2,1,0:T(8,128)(2,1)S(1)}, u32[]{:S(2)}, u32[]{:S(2)}) async-start(bf16[8,16,1536]{2,1,0:T(8,128)(2,1)} %shard_map.62), calls=%async_computation.3 | async-start | bytes 786432 | tf_op jit(solution)/shard_map/all_to_all | solution.py:335
  100.4 7.8 %collective-permute-start.1 = (bf16[384,384]{1,0:T(8,128)(2,1)}, bf16[384,384]{1,0:T(8,128)(2,1)S(1)}, u32[]{:S(2)}, u32[]{:S(2)}) collective-permute-start(bf16[384,384]{1,0:T(8,128)(2,1)} %get-tuple-element.10), channel_id=1, source_target_pairs={{0,1},{1,0},{2,3},{3,2},{4,5},{5,4},{6,7},{7,6},{8,9},{9,8},{10,11... | collective-permute-start | bytes 884744 | tf_op jit(solution)/shard_map/ppermute | solution.py:292
  108.2 1.0 copy-start.9
  109.5 34.0 %copy-start.3 = (bf16[1,384,1536]{2,1,0:T(8,128)(2,1)S(1)}, bf16[1,384,1536]{2,1,0:T(8,128)(2,1)}, u32[]{:S(2)}) copy-start(bf16[1,384,1536]{2,1,0:T(8,128)(2,1)} %param.5) | copy-start | bytes 3538948
  135.8 9.6 %collective-permute-start.4 = (bf16[256,1536]{1,0:T(8,128)(2,1)S(1)}, bf16[256,1536]{1,0:T(8,128)(2,1)S(1)}, u32[]{:S(2)}, u32[]{:S(2)}) collective-permute-start(bf16[256,1536]{1,0:T(8,128)(2,1)S(1)} %bitcast.21), channel_id=1, source_target_pairs={{0,1},{1,0},{2,3},{3,2},{4,5},{5,4},{6,7},{7,6},{8,9},{9,8},{10,11... | collective-permute-start | bytes 2359304 | tf_op jit(solution)/shard_map/ppermute | solution.py:349
